TPU v7x, 32 devices: a whole 2x2x4 slice. The times are simulated.
32 devices in a mesh: grp: 2 (over x), lat: 4 (over z), lon: 4 (over y, core).
Axes of the slice: x: 2, y: 2, z: 4, core: 2. Of those that a mesh axis runs over, the one named last changes fastest.
Arguments:
- coupled_state: bfloat16 [2, 80, 64, 512], P('grp', None, 'lat', 'lon'), may hold values from -6 to 6
- land_mask: int32 [64, 512], P('lat', 'lon'), may hold values 0 or 1
- regrid_offsets: int32 [2, 2, 4, 64, 512], P('grp', None, None, 'lat', 'lon'), may hold values from -8 to 8
- regrid_weights: float32 [2, 4, 64, 512], P('grp', None, 'lat', 'lon'), may hold values from 0.1 to 0.4
- surface_proj: float32 [2, 4, 80], replicated, may hold values from -0.625 to 0.625
- atm_in: bfloat16 [384, 84], replicated, may hold values from -0.625 to 0.625
- atm_bias: float32 [384], replicated, may hold values from -3 to 3
- atm_out: bfloat16 [80, 384], replicated, may hold values from -0.3125 to 0.3125
- ocn_in: bfloat16 [200, 9, 84], replicated, may hold values from -0.21875 to 0.21875
- ocn_bias: float32 [200], replicated, may hold values from -3 to 3
- ocn_out: bfloat16 [80, 9, 200], replicated, may hold values from -0.125 to 0.125
Outputs:
- next_state: bfloat16 [2, 80, 64, 512], P('grp', None, 'lat', 'lon')
All inputs are finite; a program needn't handle non-finite values. No bound on the sum of `land_mask` on one device may be relied on, other than what follows from the above.
Results may differ from a plain program's by a relative error of at most 0.008.
Values may be sent and summed in bfloat16 or wider, within the bound.
No kernel may reach another device: no remote copies, remote signals or barrier semaphores. Data moves between devices by JAX's collectives and lax.ppermute only.
A program may use at most 64 MiB of HBM per device.

v0:
```python
import functools

import jax
import jax.numpy as jnp
from jax import lax
from jax.experimental import pallas as pl
from jax.experimental.pallas import tpu as pltpu
from jax.sharding import PartitionSpec as P

CH = 80
NS = 4
NK = 4
HW = 8
SPAN = 2 * HW + 1
HIDP = 208
F32 = jnp.float32
BF16 = jnp.bfloat16


def roll(x, shift, axis=1):
    size = x.shape[axis]
    if isinstance(shift, int):
        shift = shift % size
        if shift == 0:
            return x
    return pltpu.roll(x, shift, axis)


def lanes(shape):
    return lax.broadcasted_iota(jnp.int32, shape, len(shape) - 1)


def subs(shape):
    return lax.broadcasted_iota(jnp.int32, shape, len(shape) - 2)


class Dims:
    def __init__(self, rows):
        self.rows = rows
        self.block = 32 if rows + 4 <= 32 else 64
        self.edge = 4 * self.block
        self.pieces = self.edge // 128
        self.edge_rows = CH * self.pieces
        self.tiles = -(-(rows + 4) // 8)
        self.tall = 8 * self.tiles
        self.strip = 2 * CH + self.edge_rows


def put_edges(ref, at, edges, d):
    for piece in range(d.pieces):
        ref[at + piece * CH : at + (piece + 1) * CH, :] = edges[:, piece * 128 : (piece + 1) * 128]


def get_edges(ref, at, d):
    return jnp.concatenate(
        [ref[at + piece * CH : at + (piece + 1) * CH, :] for piece in range(d.pieces)], axis=1
    )


def edge_columns(state, d):
    lane = lanes((1, d.edge))
    block = lane // d.block
    row = lane % d.block - 2
    column = jnp.where(block == 0, 126, jnp.where(block == 1, 0, jnp.where(block == 2, 127, 1)))
    half = d.rows // 2
    own = (row >= 0) & (row < d.rows)
    target = jnp.where(own, column + 128 * (row // half), -1)
    turn = row % half

    def body(step, total):
        place = subs((256, d.edge)) == jnp.where(turn == step, target, -1)
        pair = jnp.concatenate([state[step], state[step + half]], axis=1)
        return total + jnp.dot(
            pair, place.astype(F32).astype(BF16), preferred_element_type=F32
        )

    total = lax.fori_loop(0, half, body, jnp.zeros((CH, d.edge), F32))
    return total.astype(BF16)


def emit(state, proj, keeping, fields, own_edges, top, bottom, raw, d):
    half = d.rows // 2

    def body(step, carry):
        pair = jnp.concatenate([state[step], state[step + half]], axis=1)
        parts = jnp.dot(proj[...], pair, preferred_element_type=F32)
        whole = parts[0:8] + parts[8:16] + parts[16:24]
        raw[pl.ds(pl.multiple_of(step * 8, 8), 8), :] = whole[:, :128]
        raw[pl.ds(pl.multiple_of((step + half) * 8, 8), 8), :] = whole[:, 128:]
        return carry

    lax.fori_loop(0, half, body, 0)
    for field in range(NS):
        fields[field] = (raw[pl.ds(field, d.rows, stride=8), :] * keeping[...]).astype(BF16)
    edges = edge_columns(state, d)
    put_edges(own_edges, 0, edges, d)
    for ref, first in ((top, 0), (bottom, d.rows - 2)):
        ref[0:CH, :] = state[first]
        ref[CH : 2 * CH, :] = state[first + 1]
        put_edges(ref, 2 * CH, edges, d)


def start_kernel(d, state, planes, proj, keeping, fields, own_edges, top, bottom, raw, tall):
    emit(state, proj, keeping, fields, own_edges, top, bottom, raw, d)
    for plane in range(2 * NK):
        tall[plane * d.rows : (plane + 1) * d.rows, :] = planes[plane].astype(F32)
    for ref, first in ((top, 0), (bottom, d.rows - 2)):
        strip = [tall[pl.ds(first + step, 2 * NK, stride=d.rows), :] for step in range(2)]
        ref[d.strip : d.strip + 16, :] = jnp.concatenate(strip, axis=0).astype(BF16)


def decode(code):
    shifted = code.astype(jnp.int32) + (HW * SPAN + HW)
    rows = lax.shift_right_logical(shifted * 241, 12)
    return rows - HW, shifted - rows * SPAN - HW


def select_rows(sources_x, sources_y, start, picks):
    chosen = [[jnp.zeros((8, 128), F32) for _ in range(NS)] for _ in picks]
    for shift in range(-HW, HW + 1):
        at = pl.ds(start + shift, 8)
        inside = [sources_x[field, at, :] for field in range(NS)]
        beside = [sources_y[field, at, :] for field in range(NS)]
        for slot, (rows, index, within) in enumerate(picks):
            here = rows == shift
            here_x = here & within
            here_y = here & jnp.logical_not(within)
            for field in range(NS):
                from_x = jnp.take_along_axis(inside[field], index, axis=1)
                from_y = jnp.take_along_axis(beside[field], index, axis=1)
                value = jnp.where(here_x, from_x, chosen[slot][field])
                chosen[slot][field] = jnp.where(here_y, from_y, value)
    return chosen


def regrid(fields_x, fields_y, plan_x, plan_y, forcing_x, forcing_y, first, tiles, tall, sides):
    def tile(step, carry):
        at = first + step * 8
        lane = lanes((8, 128))
        picks = []
        weights = []
        for k in range(NK):
            rows, cols = decode(plan_x[pl.ds(k * tall + at, 8), :])
            column = lane + cols
            picks.append((rows, column & 127, (column >= 0) & (column < 128)))
            weights.append(plan_x[pl.ds((NK + k) * tall + at, 8), :])
        if sides:
            part = ((lane + 16) & 127) // 32
            codes = plan_y[pl.ds(at, 8), :]
            weight = plan_y[pl.ds(NK * tall + at, 8), :]
            for k in range(1, NK):
                codes = jnp.where(part == k, roll(plan_y[pl.ds(k * tall + at, 8), :], 32 * k), codes)
                weight = jnp.where(
                    part == k, roll(plan_y[pl.ds((NK + k) * tall + at, 8), :], 32 * k), weight
                )
            rows, cols = decode(codes)
            place = (lane - 32 * part) & 127
            column = jnp.where(place >= 64, place - 128, place + 128) + cols
            picks.append((rows, column & 127, (column >= 0) & (column < 128)))
            weights.append(weight)
        chosen = select_rows(fields_x, fields_y, at + 14, picks)
        for field in range(NS):
            total = chosen[0][field] * weights[0]
            for k in range(1, NK):
                total = total + chosen[k][field] * weights[k]
            forcing_x[pl.ds(at * 8 + field, 8, stride=8), :] = total
            forcing_x[pl.ds(at * 8 + field + 4, 8, stride=8), :] = total
            if sides:
                part_sum = chosen[NK][field] * weights[NK]
                total = part_sum
                for k in range(1, NK):
                    total = total + roll(part_sum, -32 * k)
                forcing_y[pl.ds(at * 8 + field, 8, stride=8), :] = total
                forcing_y[pl.ds(at * 8 + field + 4, 8, stride=8), :] = total
        return carry

    lax.fori_loop(0, tiles, tile, 0)


def place_columns(middle, left, right):
    lane = lanes(middle.shape)
    return jnp.where(lane < 64, right, left)


def gelu(x):
    return jax.nn.gelu(x)


def air(state, out, forcing_x, atm_in, atm_bias, atm_out, d):
    half = d.rows // 2
    blank = jnp.zeros((8, 128), F32)

    def inputs(row):
        at = pl.multiple_of((row + 2) * 8, 8)
        forced = jnp.concatenate([forcing_x[pl.ds(at, 8), :], blank], axis=0)
        return jnp.concatenate([state[row], forced.astype(BF16)], axis=0)

    def body(step, carry):
        pair = jnp.concatenate([inputs(step), inputs(step + half)], axis=1)
        hidden = gelu(jnp.dot(atm_in[...], pair, preferred_element_type=F32) + atm_bias[...])
        update = jnp.dot(atm_out[...], hidden.astype(BF16), preferred_element_type=F32)
        out[step] = (state[step].astype(F32) + update[:, :128]).astype(BF16)
        out[step + half] = (state[step + half].astype(F32) + update[:, 128:]).astype(BF16)
        return carry

    lax.fori_loop(0, half, body, 0)


def edge_forcing(forcing_x, forcing_y, d):
    lane = lanes((8, d.edge))
    block = lane // d.block
    row = lane % d.block

    def body(step, carry):
        inner, outer = carry
        at = pl.ds(pl.multiple_of(step * 8, 8), 8)
        pad = [jnp.zeros((8, 128), F32)] * (d.pieces - 1)
        here = jnp.concatenate([forcing_x[at, :]] + pad, axis=1)
        there = jnp.concatenate([forcing_y[at, :]] + pad, axis=1)
        for index, column in enumerate((126, 0, 127, 1)):
            shift = (step + index * d.block - column) % d.edge
            match = (block == index) & (row == step)
            inner = jnp.where(match, roll(here, shift), inner)
            outer = jnp.where(match, roll(there, shift), outer)
        return inner, outer

    blank = jnp.zeros((8, d.edge), F32)
    return lax.fori_loop(0, d.rows + 4, body, (blank, blank))


def sea(
    state, upper, lower, edges, left, right, out, forcing_x, forcing_y, ocn_in, ocn_bias, ocn_out,
    wet, at_top, at_bottom, stack, hidden, side, d,
):
    rows, block = d.rows, d.block
    lane = lanes((CH, 128))
    spot = lanes((CH, d.edge))
    part = spot // block
    inner = edges
    outer = jnp.where((part == 0) | (part == 2), left, right)

    def sides_of(inner, outer, spot):
        first = spot < block
        return (
            jnp.where(first, outer, roll(inner, -block)),
            jnp.where(first, roll(outer, -2 * block), outer),
            jnp.where(first, roll(inner, -block), roll(outer, -2 * block)),
        )

    beside = sides_of(inner, outer, spot)
    middle = beside[1]
    force_in, force_out = edge_forcing(forcing_x, forcing_y, d)
    beside_forcing = sides_of(force_in, force_out, lanes((8, d.edge)))
    sub = subs((8, d.edge))
    blank = jnp.zeros((8, d.edge), F32)
    forced = jnp.concatenate(
        [
            jnp.where(sub < 4, beside_forcing[0], beside_forcing[1]),
            jnp.where(sub < 4, beside_forcing[2], blank),
        ],
        axis=0,
    ).astype(BF16)
    columns = jnp.concatenate(list(beside) + [forced], axis=0)
    for tap in range(3):
        side[tap * 256 : (tap + 1) * 256, :] = roll(columns, -tap)

    sub_row = subs((8, 128))
    lane_row = lanes((8, 128))

    def build(row, values):
        entry = roll(middle, (127 - row) % d.edge)[:, :128]
        stack[row, 0:CH, :] = roll(jnp.where(lane == 127, entry, values), 1)
        stack[row, CH : 2 * CH, :] = values
        entry = roll(middle, (2 * d.edge - block - row) % d.edge)[:, :128]
        stack[row, 2 * CH : 3 * CH, :] = roll(jnp.where(lane == 0, entry, values), -1)
        at = pl.ds(pl.multiple_of(row * 8, 8), 8)
        here, there = forcing_x[at, :], forcing_y[at, :]
        before = roll(jnp.where(lane_row == 127, there, here), 1)
        after = roll(jnp.where(lane_row == 0, there, here), -1)
        stack[row, 3 * CH : 256, :] = jnp.concatenate(
            [jnp.where(sub_row < 4, before, here), jnp.where(sub_row < 4, after, jnp.zeros_like(after))],
            axis=0,
        ).astype(BF16)

    for step in range(2):
        build(jnp.int32(step), upper[step * CH : (step + 1) * CH, :])
        build(jnp.int32(rows + 2 + step), lower[step * CH : (step + 1) * CH, :])

    def build_own(step, carry):
        build(step + 2, state[step])
        return carry

    lax.fori_loop(0, rows, build_own, 0)

    pairs = (rows + 2) // 2

    def first(step, carry):
        taps = jnp.concatenate(
            [
                stack[pl.ds(step, 3)].reshape(3 * 256, 128),
                stack[pl.ds(step + pairs, 3)].reshape(3 * 256, 128),
            ],
            axis=1,
        )
        product = jnp.dot(ocn_in[...], taps, preferred_element_type=F32) + ocn_bias[...]
        active = gelu(product)
        keep_low = jnp.where((step == 0) & (at_top != 0), 0.0, 1.0).astype(F32)
        keep_high = jnp.where((step == pairs - 1) & (at_bottom != 0), 0.0, 1.0).astype(F32)
        hidden[step] = (active[:, :128] * keep_low).astype(BF16)
        hidden[step + pairs] = (active[:, 128:] * keep_high).astype(BF16)
        return carry

    lax.fori_loop(0, pairs, first, 0)

    product = jnp.dot(ocn_in[...], side[...], preferred_element_type=F32) + ocn_bias[...]
    spot = lanes((1, d.edge)) % block
    gone = ((spot == 0) & (at_top != 0)) | ((spot == rows + 1) & (at_bottom != 0))
    active = jnp.where(gone, 0.0, gelu(product)).astype(BF16)
    taps = jnp.concatenate([roll(active, -tap) for tap in range(3)], axis=0)
    partial = jnp.dot(ocn_out[...], taps, preferred_element_type=F32)
    from_left, from_right = partial[0:CH], partial[2 * CH : 3 * CH]
    half = rows // 2

    def second(step, carry):
        taps = jnp.concatenate(
            [
                hidden[pl.ds(step, 3)].reshape(3 * HIDP, 128),
                hidden[pl.ds(step + half, 3)].reshape(3 * HIDP, 128),
            ],
            axis=1,
        )
        product = jnp.dot(ocn_out[...], taps, preferred_element_type=F32)
        for offset in range(2):
            row = step + offset * half
            sums = product[:, offset * 128 : (offset + 1) * 128]
            entry = roll(from_left, (127 - row) % d.edge)[:, :128]
            total = sums[CH : 2 * CH] + roll(jnp.where(lane == 127, entry, sums[0:CH]), 1)
            entry = roll(from_right, (2 * d.edge - block - row) % d.edge)[:, :128]
            total = total + roll(jnp.where(lane == 0, entry, sums[2 * CH : 3 * CH]), -1)
            update = total * wet[pl.ds(row, 1), :]
            out[row] = (state[row].astype(F32) + update).astype(BF16)
        return carry

    lax.fori_loop(0, half, second, 0)


def join_rows(edge_up, edge_own, edge_down, d):
    row = lanes(edge_own.shape) % d.block
    above = roll(edge_up, -d.rows)
    below = roll(edge_down, d.rows)
    return jnp.where(row < 2, above, jnp.where(row < d.rows + 2, edge_own, below))


def step_kernel(d, opening, closing, *refs):
    refs = list(refs)
    take = lambda count: [refs.pop(0) for _ in range(count)]
    (flags,) = take(1)
    state, wet, above, beside, below, from_up, from_down, own_edges, from_left, from_right = take(10)
    if opening:
        (planes,) = take(1)
    else:
        plan_x, plan_y = take(2)
    atm_in, atm_bias, atm_out, ocn_in, ocn_bias, ocn_out, proj, keeping = take(8)
    (out,) = take(1)
    if not closing:
        fields, new_edges, top, bottom = take(4)
    if opening:
        plan_x, plan_y = take(2)
    fields_x, fields_y, forcing_x, forcing_y, stack, hidden, side, raw = take(8)
    rows, tall = d.rows, d.tall
    is_ocean, at_top, at_bottom = flags[0], flags[1], flags[2]

    if opening:

        @pl.when(is_ocean != 0)
        def _():
            plan_x[...] = jnp.zeros_like(plan_x)
            plan_y[...] = jnp.zeros_like(plan_y)
            base = d.strip
            side_base = 4 * (rows + 32) + 3 * d.edge_rows
            for step, ref in ((0, from_up), (rows + 2, from_down)):
                strip = ref[base : base + 16, :].astype(F32)
                for index in range(2):
                    plan_x[pl.ds(step + index, 2 * NK, stride=tall), :] = strip[index * 8 : (index + 1) * 8]
            for step, at in ((0, side_base), (rows + 2, side_base + 16 + 2 * NK * rows)):
                strip = place_columns(
                    from_left[at : at + 16, :],
                    from_left[at : at + 16, :].astype(F32),
                    from_right[at : at + 16, :].astype(F32),
                )
                for index in range(2):
                    plan_y[pl.ds(step + index, 2 * NK, stride=tall), :] = strip[index * 8 : (index + 1) * 8]
            for plane in range(2 * NK):
                at = side_base + 16 + plane * rows
                plan_y[plane * tall + 2 : plane * tall + 2 + rows, :] = place_columns(
                    from_left[at : at + rows, :],
                    from_left[at : at + rows, :].astype(F32),
                    from_right[at : at + rows, :].astype(F32),
                )

        for plane in range(2 * NK):
            plan_x[plane * tall + 2 : plane * tall + 2 + rows, :] = planes[plane].astype(F32)

    for field in range(NS):
        fields_x[field, 0:16, :] = above[field, rows - 16 : rows, :].astype(F32)
        fields_x[field, 16 : 16 + rows, :] = beside[field].astype(F32)
        fields_x[field, 16 + rows : 32 + rows, :] = below[field, 0:16, :].astype(F32)
        for at, start, count in (
            (0, field * 16, 16),
            (16, 64 + field * rows, rows),
            (16 + rows, 64 + 4 * rows + field * 16, 16),
        ):
            fields_y[field, at : at + count, :] = place_columns(
                from_left[start : start + count, :],
                from_left[start : start + count, :].astype(F32),
                from_right[start : start + count, :].astype(F32),
            )

    @pl.when(is_ocean == 0)
    def _():
        regrid(fields_x, fields_y, plan_x, plan_y, forcing_x, forcing_y, 2, rows // 8, tall, False)
        air(state, out, forcing_x, atm_in, atm_bias, atm_out, d)

    @pl.when(is_ocean != 0)
    def _():
        regrid(fields_x, fields_y, plan_x, plan_y, forcing_x, forcing_y, 0, d.tiles, tall, True)
        at = 4 * (rows + 32)
        size = d.edge_rows
        edges = join_rows(
            get_edges(from_up, 2 * CH, d), get_edges(own_edges, 0, d), get_edges(from_down, 2 * CH, d), d
        )
        left, right = [
            join_rows(*[get_edges(ref, at + index * size, d) for index in range(3)], d)
            for ref in (from_left, from_right)
        ]
        sea(
            state, from_up, from_down, edges, left, right, out, forcing_x, forcing_y,
            ocn_in, ocn_bias, ocn_out, wet, at_top, at_bottom, stack, hidden, side, d,
        )

    if not closing:
        emit(out, proj, keeping, fields, new_edges, top, bottom, raw, d)


VMEM = pl.BlockSpec(memory_space=pltpu.VMEM)
SMEM = pl.BlockSpec(memory_space=pltpu.SMEM)
PARAMS = pltpu.CompilerParams(vmem_limit_bytes=48 * 1024 * 1024)


def shape(*dims, dtype=BF16):
    return jax.ShapeDtypeStruct(dims, dtype)


def send(x, move):
    names = ("grp", "lat", "lon")
    sizes = [lax.axis_size(name) for name in names]
    pairs = []
    for group in range(sizes[0]):
        for lat in range(sizes[1]):
            for lon in range(sizes[2]):
                to = move(group, lat, lon)
                if to is None or not 0 <= to[1] < sizes[1]:
                    continue
                target = (to[0] * sizes[1] + to[1]) * sizes[2] + to[2] % sizes[2]
                pairs.append(((group * sizes[1] + lat) * sizes[2] + lon, target))
    return lax.ppermute(x, names, pairs)


def exchange(fields, own_edges, top, bottom, planes, d):
    rows = d.rows
    beside = send(fields, lambda g, i, j: (1 - g, i, j))
    above = send(fields, lambda g, i, j: (1 - g, i + 1, j))
    below = send(fields, lambda g, i, j: (1 - g, i - 1, j))
    from_up = send(bottom, lambda g, i, j: (1, i + 1, j) if g == 1 else None)
    from_down = send(top, lambda g, i, j: (1, i - 1, j) if g == 1 else None)
    edge_at = slice(2 * CH, d.strip)
    packed = [
        above[:, rows - 16 :].reshape(64, 128),
        beside.reshape(4 * rows, 128),
        below[:, :16].reshape(64, 128),
        from_up[edge_at],
        own_edges,
        from_down[edge_at],
    ]
    if planes is not None:
        packed += [from_up[d.strip :], planes.reshape(2 * NK * rows, 128), from_down[d.strip :]]
    packed = jnp.concatenate(packed, axis=0)
    from_left = send(packed, lambda g, i, j: (g, i, j + 1))
    from_right = send(packed, lambda g, i, j: (g, i, j - 1))
    return above, beside, below, from_up, from_down, own_edges, from_left, from_right


def local(
    coupled_state, land_mask, regrid_offsets, regrid_weights, surface_proj,
    atm_in, atm_bias, atm_out, ocn_in, ocn_bias, ocn_out,
):
    rows = coupled_state.shape[2]
    assert coupled_state.shape[3] == 128
    d = Dims(rows)
    group = lax.axis_index("grp")
    lat = lax.axis_index("lat")
    is_ocean = group == 1
    flags = jnp.stack([group, lat == 0, lat == lax.axis_size("lat") - 1]).astype(jnp.int32)
    state = jnp.transpose(coupled_state[0], (1, 0, 2))
    wet = land_mask.astype(F32)
    keeping = jnp.where(is_ocean, wet, 1.0)
    projector = lax.dynamic_index_in_dim(surface_proj, group, 0, keepdims=False)
    high = projector.astype(BF16)
    rest = projector - high.astype(F32)
    mid = rest.astype(BF16)
    low = (rest - mid.astype(F32)).astype(BF16)
    gap = jnp.zeros((4, CH), BF16)
    proj = jnp.concatenate([high, gap, mid, gap, low, gap], axis=0)
    codes = regrid_offsets[0, 0] * SPAN + regrid_offsets[0, 1]
    planes = jnp.concatenate([codes.astype(BF16), regrid_weights[0].astype(BF16)], axis=0)

    hidden_count = ocn_in.shape[0]
    taps = ocn_in.reshape(hidden_count, 3, 3, CH + NS)
    first = jnp.concatenate(
        [
            taps[..., :CH].reshape(hidden_count, 3, 3 * CH),
            taps[..., CH:].reshape(hidden_count, 3, 3 * NS),
            jnp.zeros((hidden_count, 3, 256 - 3 * (CH + NS)), BF16),
        ],
        axis=2,
    ).reshape(hidden_count, 768)
    extra = HIDP - hidden_count
    first = jnp.pad(first, ((0, extra), (0, 0)))
    first_bias = jnp.pad(ocn_bias, (0, extra))[:, None]
    second = jnp.transpose(ocn_out.reshape(CH, 3, 3, hidden_count), (2, 0, 1, 3))
    second = jnp.pad(second, ((0, 0), (0, 0), (0, 0), (0, extra))).reshape(3 * CH, 3 * HIDP)
    air_in = jnp.pad(atm_in, ((0, 0), (0, 16 - NS)))
    constants = (air_in, atm_bias[:, None], atm_out, first, first_bias, second, proj, keeping)

    emitted = [
        shape(NS, rows, 128),
        shape(d.edge_rows, 128),
        shape(d.strip, 128),
        shape(d.strip, 128),
    ]
    raw = pltpu.VMEM((rows * 8, 128), F32)
    fields, edges, top, bottom = pl.pallas_call(
        functools.partial(start_kernel, d),
        out_shape=emitted[:2] + [shape(d.strip + 16, 128)] * 2,
        in_specs=[VMEM] * 4,
        out_specs=[VMEM] * 4,
        scratch_shapes=[raw, pltpu.VMEM((2 * NK * rows, 128), F32)],
        compiler_params=PARAMS,
        name="start",
    )(state, planes, proj, keeping)

    scratch = [
        pltpu.VMEM((NS, rows + 32, 128), F32),
        pltpu.VMEM((NS, rows + 32, 128), F32),
        pltpu.VMEM((d.tall * 8, 128), F32),
        pltpu.VMEM((d.tall * 8, 128), F32),
        pltpu.VMEM((rows + 4, 256, 128), BF16),
        pltpu.VMEM((rows + 2, HIDP, 128), BF16),
        pltpu.VMEM((768, d.edge), BF16),
        raw,
    ]
    plans = [shape(2 * NK * d.tall, 128, dtype=F32)] * 2
    state_shape = shape(rows, CH, 128)

    received = exchange(fields, edges, top, bottom, planes, d)
    outs = [state_shape] + emitted + plans
    state, fields, edges, top, bottom, plan_x, plan_y = pl.pallas_call(
        functools.partial(step_kernel, d, True, False),
        out_shape=outs,
        in_specs=[SMEM] + [VMEM] * 19,
        out_specs=[VMEM] * len(outs),
        scratch_shapes=scratch,
        compiler_params=PARAMS,
        name="first_step",
    )(flags, state, wet, *received, planes, *constants)

    received = exchange(fields, edges, top, bottom, None, d)
    state = pl.pallas_call(
        functools.partial(step_kernel, d, False, True),
        out_shape=state_shape,
        in_specs=[SMEM] + [VMEM] * 20,
        out_specs=VMEM,
        scratch_shapes=scratch,
        compiler_params=PARAMS,
        name="second_step",
    )(flags, state, wet, *received, plan_x, plan_y, *constants)
    return jnp.transpose(state, (1, 0, 2))[None]


def solution(mesh):
    return jax.shard_map(
        local,
        mesh=mesh,
        in_specs=(
            P("grp", None, "lat", "lon"),
            P("lat", "lon"),
            P("grp", None, None, "lat", "lon"),
            P("grp", None, "lat", "lon"),
            P(),
            P(),
            P(),
            P(),
            P(),
            P(),
            P(),
        ),
        out_specs=P("grp", None, "lat", "lon"),
        check_vma=False,
    )
```

profile of v0, /device:TPU:2, one launch (start us, length us, event | category | flops | bytes accessed | tf_op | source)
XLA Modules:
  0.0 80.9 jit_solution(11038542536207713729)
XLA Ops:
  0.0 0.8 fusion
  0.8 1.1 %copy.31 = bf16[1,80,16,128]{3,1,2,0:T(8,128)(2,1)S(1)} copy(bf16[1,80,16,128]{3,2,1,0:T(8,128)(2,1)} %param.11) | data formatting | bytes 655360 | tf_op args[0]
  2.1 2.2 %start.1 = (bf16[4,16,128]{2,1,0:T(8,128)(2,1)S(1)}, bf16[80,128]{1,0:T(8,128)(2,1)S(1)}, bf16[256,128]{1,0:T(8,128)(2,1)S(1)}, bf16[256,128]{1,0:T(8,128)(2,1)S(1)}) custom-call(bf16[16,80,128]{2,1,0:T(8,128)(2,1)S(1)} %bitcast.41, bf16[8,16,128]{2,1,0:T(8,128)(2,1)S(1)} %pad_maximum_fusion.planes.refs_11_, ...), custom_call_target="tpu_custom_call" | custom-call | tf_op jit(solution)/shard_map/start/pallas_call | solution.py:542
  4.3 3.5 %collective-permute-start = (bf16[4,16,128]{2,1,0:T(8,128)(2,1)S(1)}, bf16[4,16,128]{2,1,0:T(8,128)(2,1)S(1)}, u32[]{:S(2)}, u32[]{:S(2)}) collective-permute-start(bf16[4,16,128]{2,1,0:T(8,128)(2,1)S(1)} %get-tuple-element.16), channel_id=1, source_target_pairs={{0,20},{1,21},{2,22},{3,23},{4,24},{5,25},{6,26},{7,27},{8,28},{9,... | collective-permute-start | bytes 49160 | tf_op jit(solution)/shard_map/ppermute | solution.py:466
  7.8 1.3 %collective-permute-start.2 = (bf16[4,16,128]{2,1,0:T(8,128)(2,1)S(1)}, bf16[4,16,128]{2,1,0:T(8,128)(2,1)S(1)}, u32[]{:S(2)}, u32[]{:S(2)}) collective-permute-start(bf16[4,16,128]{2,1,0:T(8,128)(2,1)S(1)} %get-tuple-element.16), channel_id=1, source_target_pairs={{4,16},{5,17},{6,18},{7,19},{8,20},{9,21},{10,22},{11,23},{12,24},... | collective-permute-start | bytes 49160 | tf_op jit(solution)/shard_map/ppermute | solution.py:466
  9.1 1.6 %collective-permute-start.1 = (bf16[4,16,128]{2,1,0:T(8,128)(2,1)S(1)}, bf16[4,16,128]{2,1,0:T(8,128)(2,1)S(1)}, u32[]{:S(2)}, u32[]{:S(2)}) collective-permute-start(bf16[4,16,128]{2,1,0:T(8,128)(2,1)S(1)} %get-tuple-element.16), channel_id=1, source_target_pairs={{0,16},{1,17},{2,18},{3,19},{4,20},{5,21},{6,22},{7,23},{8,24},{9,... | collective-permute-start | bytes 49160 | tf_op jit(solution)/shard_map/ppermute | solution.py:466
  10.6 4.5 %collective-permute-start.3 = (bf16[256,128]{1,0:T(8,128)(2,1)S(1)}, bf16[256,128]{1,0:T(8,128)(2,1)S(1)}, u32[]{:S(2)}, u32[]{:S(2)}) collective-permute-start(bf16[256,128]{1,0:T(8,128)(2,1)S(1)} %get-tuple-element.17), channel_id=1, source_target_pairs={{16,20},{17,21},{18,22},{19,23},{20,24},{21,25},{22,26},{23,27},{2... | collective-permute-start | bytes 196616 | tf_op jit(solution)/shard_map/ppermute | solution.py:466
  15.1 1.3 %collective-permute-start.4 = (bf16[256,128]{1,0:T(8,128)(2,1)S(1)}, bf16[256,128]{1,0:T(8,128)(2,1)S(1)}, u32[]{:S(2)}, u32[]{:S(2)}) collective-permute-start(bf16[256,128]{1,0:T(8,128)(2,1)S(1)} %get-tuple-element.18), channel_id=1, source_target_pairs={{20,16},{21,17},{22,18},{23,19},{24,20},{25,21},{26,22},{27,23},{2... | collective-permute-start | bytes 196616 | tf_op jit(solution)/shard_map/ppermute | solution.py:466
  17.0 4.3 %collective-permute-done.4.refs_7_ = bf16[256,128]{1,0:T(8,128)(2,1)S(1)} collective-permute-done((bf16[256,128]{1,0:T(8,128)(2,1)S(1)}, bf16[256,128]{1,0:T(8,128)(2,1)S(1)}, u32[]{:S(2)}, u32[]{:S(2)}) %collective-permute-start.4) | collective-permute-done | bytes 65568 | tf_op jit(solution)/shard_map/ppermute | solution.py:466
  22.1 0.7 copy-done.3
  23.0 0.6 copy-done.8
  24.6 0.9 %copy-done.2 = bf16[80,9,200]{2,0,1:T(8,128)(2,1)S(1)} copy-done((bf16[80,9,200]{2,0,1:T(8,128)(2,1)S(1)}, bf16[80,9,200]{2,0,1:T(8,128)(2,1)}, u32[]{:S(2)}) %copy-start.2) | copy-done | bytes 288024
  26.4 1.3 %collective-permute-done.5.refs_9_ = bf16[592,128]{1,0:T(8,128)(2,1)S(1)} collective-permute-done((bf16[592,128]{1,0:T(8,128)(2,1)S(1)}, bf16[592,128]{1,0:T(8,128)(2,1)S(1)}, u32[]{:S(2)}, u32[]{:S(2)}) %collective-permute-start.5) | collective-permute-done | bytes 151584 | tf_op jit(solution)/shard_map/ppermute | solution.py:466
  27.7 16.7 %first_step.1 = (bf16[16,80,128]{2,1,0:T(8,128)(2,1)S(1)}, bf16[4,16,128]{2,1,0:T(8,128)(2,1)S(1)}, bf16[80,128]{1,0:T(8,128)(2,1)S(1)}, bf16[240,128]{1,0:T(8,1...) custom-call(s32[3]{0:T(128)S(1)} %pad_add_fusion.refs_0_, ...), custom_call_target="tpu_custom_call" | custom-call | tf_op jit(solution)/shard_map/first_step/pallas_call | solution.py:567
  44.4 1.3 %collective-permute-start.7 = (bf16[4,16,128]{2,1,0:T(8,128)(2,1)S(1)}, bf16[4,16,128]{2,1,0:T(8,128)(2,1)S(1)}, u32[]{:S(2)}, u32[]{:S(2)}) collective-permute-start(bf16[4,16,128]{2,1,0:T(8,128)(2,1)S(1)} %get-tuple-element.21), channel_id=1, source_target_pairs={{0,20},{1,21},{2,22},{3,23},{4,24},{5,25},{6,26},{7,27},{8,28},{9,... | collective-permute-start | bytes 49160 | tf_op jit(solution)/shard_map/ppermute | solution.py:466
  45.7 1.3 %collective-permute-start.9 = (bf16[4,16,128]{2,1,0:T(8,128)(2,1)S(1)}, bf16[4,16,128]{2,1,0:T(8,128)(2,1)S(1)}, u32[]{:S(2)}, u32[]{:S(2)}) collective-permute-start(bf16[4,16,128]{2,1,0:T(8,128)(2,1)S(1)} %get-tuple-element.21), channel_id=1, source_target_pairs={{4,16},{5,17},{6,18},{7,19},{8,20},{9,21},{10,22},{11,23},{12,24},... | collective-permute-start | bytes 49160 | tf_op jit(solution)/shard_map/ppermute | solution.py:466
  47.0 3.7 %collective-permute-start.8 = (bf16[4,16,128]{2,1,0:T(8,128)(2,1)S(1)}, bf16[4,16,128]{2,1,0:T(8,128)(2,1)S(1)}, u32[]{:S(2)}, u32[]{:S(2)}) collective-permute-start(bf16[4,16,128]{2,1,0:T(8,128)(2,1)S(1)} %get-tuple-element.21), channel_id=1, source_target_pairs={{0,16},{1,17},{2,18},{3,19},{4,20},{5,21},{6,22},{7,23},{8,24},{9,... | collective-permute-start | bytes 49160 | tf_op jit(solution)/shard_map/ppermute | solution.py:466
  50.8 4.1 %collective-permute-start.10 = (bf16[240,128]{1,0:T(8,128)(2,1)S(1)}, bf16[240,128]{1,0:T(8,128)(2,1)S(1)}, u32[]{:S(2)}, u32[]{:S(2)}) collective-permute-start(bf16[240,128]{1,0:T(8,128)(2,1)S(1)} %get-tuple-element.22), channel_id=1, source_target_pairs={{16,20},{17,21},{18,22},{19,23},{20,24},{21,25},{22,26},{23,27},{2... | collective-permute-start | bytes 184328 | tf_op jit(solution)/shard_map/ppermute | solution.py:466
  54.9 1.3 %collective-permute-start.11 = (bf16[240,128]{1,0:T(8,128)(2,1)S(1)}, bf16[240,128]{1,0:T(8,128)(2,1)S(1)}, u32[]{:S(2)}, u32[]{:S(2)}) collective-permute-start(bf16[240,128]{1,0:T(8,128)(2,1)S(1)} %get-tuple-element.23), channel_id=1, source_target_pairs={{20,16},{21,17},{22,18},{23,19},{24,20},{25,21},{26,22},{27,23},{2... | collective-permute-start | bytes 184328 | tf_op jit(solution)/shard_map/ppermute | solution.py:466
  56.7 4.3 %collective-permute-done.11.refs_7_ = bf16[240,128]{1,0:T(8,128)(2,1)S(1)} collective-permute-done((bf16[240,128]{1,0:T(8,128)(2,1)S(1)}, bf16[240,128]{1,0:T(8,128)(2,1)S(1)}, u32[]{:S(2)}, u32[]{:S(2)}) %collective-permute-start.11) | collective-permute-done | bytes 61472 | tf_op jit(solution)/shard_map/ppermute | solution.py:466
  61.5 2.8 %collective-permute-done.13.refs_10_ = bf16[432,128]{1,0:T(8,128)(2,1)S(1)} collective-permute-done((bf16[432,128]{1,0:T(8,128)(2,1)S(1)}, bf16[432,128]{1,0:T(8,128)(2,1)S(1)}, u32[]{:S(2)}, u32[]{:S(2)}) %collective-permute-start.13) | collective-permute-done | bytes 110624 | tf_op jit(solution)/shard_map/ppermute | solution.py:466
  64.3 1.3 %collective-permute-done.12.refs_9_ = bf16[432,128]{1,0:T(8,128)(2,1)S(1)} collective-permute-done((bf16[432,128]{1,0:T(8,128)(2,1)S(1)}, bf16[432,128]{1,0:T(8,128)(2,1)S(1)}, u32[]{:S(2)}, u32[]{:S(2)}) %collective-permute-start.12) | collective-permute-done | bytes 110624 | tf_op jit(solution)/shard_map/ppermute | solution.py:466
  65.6 14.5 %second_step.1 = bf16[16,80,128]{2,1,0:T(8,128)(2,1)S(1)} custom-call(s32[3]{0:T(128)S(1)} %pad_add_fusion.refs_0_, bf16[16,80,128]{2,1,0:T(8,128)(2,1)S(1)} %get-tuple-element.20.refs_1_, f32[16,128]{1,0:T(8,128)S(1)} %convert_element_type.40.refs_2_, bf16[4,16,128]{2,1,0:T(8,128)(2,1)S(1)} %collective-permute-done.7.refs_3_, ...), custom_call_target="tpu_custom_call" | custom-call | tf_op jit(solution)/shard_map/second_step/pallas_call | solution.py:578
  80.1 0.8 %copy.26 = bf16[1,80,16,128]{3,2,1,0:T(8,128)(2,1)} copy(bf16[1,80,16,128]{3,1,2,0:T(8,128)(2,1)S(1)} %bitcast.43) | data formatting | bytes 655360 | tf_op jit(solution)/shard_map/broadcast_in_dim | solution.py:587
  (67 shorter events, 4.4 us)
Async XLA Ops:
  0.0 0.8 copy-start.4
  0.8 1.1 %copy-start.6 = (f32[2,4,80]{2,1,0:T(4,128)S(1)}, f32[2,4,80]{2,1,0:T(4,128)}, u32[]{:S(2)}) copy-start(f32[2,4,80]{2,1,0:T(4,128)} %param.15) | copy-start | bytes 7684
  0.8 1.1 %copy-start.5 = (s32[16,128]{1,0:T(8,128)S(1)}, s32[16,128]{1,0:T(8,128)}, u32[]{:S(2)}) copy-start(s32[16,128]{1,0:T(8,128)} %param.12) | copy-start | bytes 24580
  1.9 14.5 %copy-start.1 = (bf16[200,9,84]{0,2,1:T(8,128)(2,1)S(1)}, bf16[200,9,84]{0,2,1:T(8,128)(2,1)}, u32[]{:S(2)}) copy-start(bf16[200,9,84]{0,2,1:T(8,128)(2,1)} %param.19) | copy-start | bytes 907204
  4.3 12.3 %collective-permute-start = (bf16[4,16,128]{2,1,0:T(8,128)(2,1)S(1)}, bf16[4,16,128]{2,1,0:T(8,128)(2,1)S(1)}, u32[]{:S(2)}, u32[]{:S(2)}) collective-permute-start(bf16[4,16,128]{2,1,0:T(8,128)(2,1)S(1)} %get-tuple-element.16), channel_id=1, source_target_pairs={{0,20},{1,21},{2,22},{3,23},{4,24},{5,25},{6,26},{7,27},{8,28},{9,... | collective-permute-start | bytes 49160 | tf_op jit(solution)/shard_map/ppermute | solution.py:466
  7.8 8.9 %collective-permute-start.2 = (bf16[4,16,128]{2,1,0:T(8,128)(2,1)S(1)}, bf16[4,16,128]{2,1,0:T(8,128)(2,1)S(1)}, u32[]{:S(2)}, u32[]{:S(2)}) collective-permute-start(bf16[4,16,128]{2,1,0:T(8,128)(2,1)S(1)} %get-tuple-element.16), channel_id=1, source_target_pairs={{4,16},{5,17},{6,18},{7,19},{8,20},{9,21},{10,22},{11,23},{12,24},... | collective-permute-start | bytes 49160 | tf_op jit(solution)/shard_map/ppermute | solution.py:466
  9.1 7.6 %collective-permute-start.1 = (bf16[4,16,128]{2,1,0:T(8,128)(2,1)S(1)}, bf16[4,16,128]{2,1,0:T(8,128)(2,1)S(1)}, u32[]{:S(2)}, u32[]{:S(2)}) collective-permute-start(bf16[4,16,128]{2,1,0:T(8,128)(2,1)S(1)} %get-tuple-element.16), channel_id=1, source_target_pairs={{0,16},{1,17},{2,18},{3,19},{4,20},{5,21},{6,22},{7,23},{8,24},{9,... | collective-permute-start | bytes 49160 | tf_op jit(solution)/shard_map/ppermute | solution.py:466
  10.6 6.4 %collective-permute-start.3 = (bf16[256,128]{1,0:T(8,128)(2,1)S(1)}, bf16[256,128]{1,0:T(8,128)(2,1)S(1)}, u32[]{:S(2)}, u32[]{:S(2)}) collective-permute-start(bf16[256,128]{1,0:T(8,128)(2,1)S(1)} %get-tuple-element.17), channel_id=1, source_target_pairs={{16,20},{17,21},{18,22},{19,23},{20,24},{21,25},{22,26},{23,27},{2... | collective-permute-start | bytes 196616 | tf_op jit(solution)/shard_map/ppermute | solution.py:466
  15.1 6.2 %collective-permute-start.4 = (bf16[256,128]{1,0:T(8,128)(2,1)S(1)}, bf16[256,128]{1,0:T(8,128)(2,1)S(1)}, u32[]{:S(2)}, u32[]{:S(2)}) collective-permute-start(bf16[256,128]{1,0:T(8,128)(2,1)S(1)} %get-tuple-element.18), channel_id=1, source_target_pairs={{20,16},{21,17},{22,18},{23,19},{24,20},{25,21},{26,22},{27,23},{2... | collective-permute-start | bytes 196616 | tf_op jit(solution)/shard_map/ppermute | solution.py:466
  21.3 5.1 %collective-permute-start.6 = (bf16[592,128]{1,0:T(8,128)(2,1)S(1)}, bf16[592,128]{1,0:T(8,128)(2,1)S(1)}, u32[]{:S(2)}, u32[]{:S(2)}) collective-permute-start(bf16[592,128]{1,0:T(8,128)(2,1)S(1)} %constant_dynamic-update-slice_fusion), channel_id=1, source_target_pairs={{0,3},{1,0},{2,1},{3,2},{4,7},{5,4},{6,5},{7,6},{8,11},{9,8},{10,9... | collective-permute-start | bytes 454664 | tf_op jit(solution)/shard_map/ppermute | solution.py:466
  21.4 6.3 %collective-permute-start.5 = (bf16[592,128]{1,0:T(8,128)(2,1)S(1)}, bf16[592,128]{1,0:T(8,128)(2,1)S(1)}, u32[]{:S(2)}, u32[]{:S(2)}) collective-permute-start(bf16[592,128]{1,0:T(8,128)(2,1)S(1)} %constant_dynamic-update-slice_fusion), channel_id=1, source_target_pairs={{0,1},{1,2},{2,3},{3,0},{4,5},{5,6},{6,7},{7,4},{8,9},{9,10},{10,1... | collective-permute-start | bytes 454664 | tf_op jit(solution)/shard_map/ppermute | solution.py:466
  21.9 0.9 %copy-start.3 = (bf16[384,84]{0,1:T(8,128)(2,1)S(1)}, bf16[384,84]{0,1:T(8,128)(2,1)}, u32[]{:S(2)}) copy-start(bf16[384,84]{0,1:T(8,128)(2,1)} %param.16) | copy-start | bytes 193540
  22.9 0.7 copy-start.8
  23.6 0.7 copy-start.7
  24.6 1.0 %copy-start.2 = (bf16[80,9,200]{2,0,1:T(8,128)(2,1)S(1)}, bf16[80,9,200]{2,0,1:T(8,128)(2,1)}, u32[]{:S(2)}) copy-start(bf16[80,9,200]{2,0,1:T(8,128)(2,1)} %param.21) | copy-start | bytes 864004
  26.1 1.6 %copy-start = (bf16[80,384]{1,0:T(8,128)(2,1)S(1)}, bf16[80,384]{1,0:T(8,128)(2,1)}, u32[]{:S(2)}) copy-start(bf16[80,384]{1,0:T(8,128)(2,1)} %refs_15_.1) | copy-start | bytes 184324
  44.4 11.8 %collective-permute-start.7 = (bf16[4,16,128]{2,1,0:T(8,128)(2,1)S(1)}, bf16[4,16,128]{2,1,0:T(8,128)(2,1)S(1)}, u32[]{:S(2)}, u32[]{:S(2)}) collective-permute-start(bf16[4,16,128]{2,1,0:T(8,128)(2,1)S(1)} %get-tuple-element.21), channel_id=1, source_target_pairs={{0,20},{1,21},{2,22},{3,23},{4,24},{5,25},{6,26},{7,27},{8,28},{9,... | collective-permute-start | bytes 49160 | tf_op jit(solution)/shard_map/ppermute | solution.py:466
  45.7 10.5 %collective-permute-start.9 = (bf16[4,16,128]{2,1,0:T(8,128)(2,1)S(1)}, bf16[4,16,128]{2,1,0:T(8,128)(2,1)S(1)}, u32[]{:S(2)}, u32[]{:S(2)}) collective-permute-start(bf16[4,16,128]{2,1,0:T(8,128)(2,1)S(1)} %get-tuple-element.21), channel_id=1, source_target_pairs={{4,16},{5,17},{6,18},{7,19},{8,20},{9,21},{10,22},{11,23},{12,24},... | collective-permute-start | bytes 49160 | tf_op jit(solution)/shard_map/ppermute | solution.py:466
  47.0 9.2 %collective-permute-start.8 = (bf16[4,16,128]{2,1,0:T(8,128)(2,1)S(1)}, bf16[4,16,128]{2,1,0:T(8,128)(2,1)S(1)}, u32[]{:S(2)}, u32[]{:S(2)}) collective-permute-start(bf16[4,16,128]{2,1,0:T(8,128)(2,1)S(1)} %get-tuple-element.21), channel_id=1, source_target_pairs={{0,16},{1,17},{2,18},{3,19},{4,20},{5,21},{6,22},{7,23},{8,24},{9,... | collective-permute-start | bytes 49160 | tf_op jit(solution)/shard_map/ppermute | solution.py:466
  50.8 6.0 %collective-permute-start.10 = (bf16[240,128]{1,0:T(8,128)(2,1)S(1)}, bf16[240,128]{1,0:T(8,128)(2,1)S(1)}, u32[]{:S(2)}, u32[]{:S(2)}) collective-permute-start(bf16[240,128]{1,0:T(8,128)(2,1)S(1)} %get-tuple-element.22), channel_id=1, source_target_pairs={{16,20},{17,21},{18,22},{19,23},{20,24},{21,25},{22,26},{23,27},{2... | collective-permute-start | bytes 184328 | tf_op jit(solution)/shard_map/ppermute | solution.py:466
  54.9 6.1 %collective-permute-start.11 = (bf16[240,128]{1,0:T(8,128)(2,1)S(1)}, bf16[240,128]{1,0:T(8,128)(2,1)S(1)}, u32[]{:S(2)}, u32[]{:S(2)}) collective-permute-start(bf16[240,128]{1,0:T(8,128)(2,1)S(1)} %get-tuple-element.23), channel_id=1, source_target_pairs={{20,16},{21,17},{22,18},{23,19},{24,20},{25,21},{26,22},{27,23},{2... | collective-permute-start | bytes 184328 | tf_op jit(solution)/shard_map/ppermute | solution.py:466
  61.0 3.3 %collective-permute-start.13 = (bf16[432,128]{1,0:T(8,128)(2,1)S(1)}, bf16[432,128]{1,0:T(8,128)(2,1)S(1)}, u32[]{:S(2)}, u32[]{:S(2)}) collective-permute-start(bf16[432,128]{1,0:T(8,128)(2,1)S(1)} %constant_dynamic-update-slice_fusion.9), channel_id=1, source_target_pairs={{0,3},{1,0},{2,1},{3,2},{4,7},{5,4},{6,5},{7,6},{8,11},{9,8},{10,9... | collective-permute-start | bytes 331784 | tf_op jit(solution)/shard_map/ppermute | solution.py:466
  61.0 4.6 %collective-permute-start.12 = (bf16[432,128]{1,0:T(8,128)(2,1)S(1)}, bf16[432,128]{1,0:T(8,128)(2,1)S(1)}, u32[]{:S(2)}, u32[]{:S(2)}) collective-permute-start(bf16[432,128]{1,0:T(8,128)(2,1)S(1)} %constant_dynamic-update-slice_fusion.9), channel_id=1, source_target_pairs={{0,1},{1,2},{2,3},{3,0},{4,5},{5,6},{6,7},{7,4},{8,9},{9,10},{10,1... | collective-permute-start | bytes 331784 | tf_op jit(solution)/shard_map/ppermute | solution.py:466
where the time goes:
time: 81.5 us; the launch traced here: 80.9 us
  Pallas kernels  33.4 us (41%)
  starting transfers between devices  24.9 us (31%)
  waiting for transfers between devices  14.7 us (18%)
  local copies, waits for them, and re-layouts  6.46 us (8%)
  other arithmetic  1.02 us (1%)
    ppermute x14, starting transfers between devices, send(): return lax.ppermute(x, names, pairs)  24.9 us
    pallas_call x1, Pallas kernels, local(): pl.pallas_call(functools.partial(step_kernel, d, True, False), out_shape=...  16.7 us
    ppermute x14, waiting for transfers between devices, send(): return lax.ppermute(x, names, pairs)  14.7 us
    pallas_call x1, Pallas kernels, local(): pl.pallas_call(functools.partial(step_kernel, d, False, True), out_shape=...  14.5 us
    unnamed x33, local copies, waits for them, and re-layouts  4.21 us
    pallas_call x1, Pallas kernels, local(): pl.pallas_call(functools.partial(start_kernel, d), out_shape=emitted[:2]...  2.22 us
  transfers between devices with their start and end apart: 14, of which 7 were waited for; matrix products, arithmetic and copies ran while one was open for 2% of the time, Pallas kernels for 0%

commit v1 on v0

--- a/solution.py
+++ b/solution.py
@@ -78,7 +78,12 @@
     return total.astype(BF16)
 
 
-def emit(state, proj, keeping, fields, own_edges, top, bottom, raw, d):
+def strips(one, two, even, d):
+    last = d.rows - 2
+    return (one, jnp.where(even, last, 0)), (two, jnp.where(even, 0, last))
+
+
+def emit(state, proj, keeping, fields, own_edges, one, two, even, raw, d):
     half = d.rows // 2
 
     def body(step, carry):
@@ -94,17 +99,18 @@
         fields[field] = (raw[pl.ds(field, d.rows, stride=8), :] * keeping[...]).astype(BF16)
     edges = edge_columns(state, d)
     put_edges(own_edges, 0, edges, d)
-    for ref, first in ((top, 0), (bottom, d.rows - 2)):
+    for ref, first in strips(one, two, even, d):
         ref[0:CH, :] = state[first]
         ref[CH : 2 * CH, :] = state[first + 1]
         put_edges(ref, 2 * CH, edges, d)
 
 
-def start_kernel(d, state, planes, proj, keeping, fields, own_edges, top, bottom, raw, tall):
-    emit(state, proj, keeping, fields, own_edges, top, bottom, raw, d)
+def start_kernel(d, flags, state, planes, proj, keeping, fields, own_edges, one, two, raw, tall):
+    even = flags[3] == 0
+    emit(state, proj, keeping, fields, own_edges, one, two, even, raw, d)
     for plane in range(2 * NK):
         tall[plane * d.rows : (plane + 1) * d.rows, :] = planes[plane].astype(F32)
-    for ref, first in ((top, 0), (bottom, d.rows - 2)):
+    for ref, first in strips(one, two, even, d):
         strip = [tall[pl.ds(first + step, 2 * NK, stride=d.rows), :] for step in range(2)]
         ref[d.strip : d.strip + 16, :] = jnp.concatenate(strip, axis=0).astype(BF16)
 
@@ -115,21 +121,33 @@
     return rows - HW, shifted - rows * SPAN - HW
 
 
-def select_rows(sources_x, sources_y, start, picks):
+def along_lanes(values, index):
+    numbers = lax.GatherDimensionNumbers(
+        offset_dims=(),
+        collapsed_slice_dims=(1,),
+        start_index_map=(1,),
+        operand_batching_dims=(0,),
+        start_indices_batching_dims=(0,),
+    )
+    return lax.gather(
+        values, index[..., None], numbers, (1, 1), mode=lax.GatherScatterMode.PROMISE_IN_BOUNDS
+    )
+
+
+def select_rows(sources, start, picks):
     chosen = [[jnp.zeros((8, 128), F32) for _ in range(NS)] for _ in picks]
     for shift in range(-HW, HW + 1):
         at = pl.ds(start + shift, 8)
-        inside = [sources_x[field, at, :] for field in range(NS)]
-        beside = [sources_y[field, at, :] for field in range(NS)]
-        for slot, (rows, index, within) in enumerate(picks):
+        values = [[source[field, at, :] for field in range(NS)] for source in sources]
+        for slot, (rows, index, allowed) in enumerate(picks):
             here = rows == shift
-            here_x = here & within
-            here_y = here & jnp.logical_not(within)
-            for field in range(NS):
-                from_x = jnp.take_along_axis(inside[field], index, axis=1)
-                from_y = jnp.take_along_axis(beside[field], index, axis=1)
-                value = jnp.where(here_x, from_x, chosen[slot][field])
-                chosen[slot][field] = jnp.where(here_y, from_y, value)
+            for source, within in enumerate(allowed):
+                if within is None:
+                    continue
+                mask = here & within
+                for field in range(NS):
+                    picked = along_lanes(values[source][field], index)
+                    chosen[slot][field] = jnp.where(mask, picked, chosen[slot][field])
     return chosen
 
 
@@ -139,47 +157,64 @@
         lane = lanes((8, 128))
         picks = []
         weights = []
+        codes = []
         for k in range(NK):
-            rows, cols = decode(plan_x[pl.ds(k * tall + at, 8), :])
+            code = plan_x[pl.ds(k * tall + at, 8), :]
+            weight = plan_x[pl.ds((NK + k) * tall + at, 8), :]
+            codes.append(code)
+            weights.append(weight)
+            rows, cols = decode(code)
             column = lane + cols
-            picks.append((rows, column & 127, (column >= 0) & (column < 128)))
-            weights.append(plan_x[pl.ds((NK + k) * tall + at, 8), :])
-        if sides:
-            part = ((lane + 16) & 127) // 32
-            codes = plan_y[pl.ds(at, 8), :]
-            weight = plan_y[pl.ds(NK * tall + at, 8), :]
-            for k in range(1, NK):
-                codes = jnp.where(part == k, roll(plan_y[pl.ds(k * tall + at, 8), :], 32 * k), codes)
-                weight = jnp.where(
-                    part == k, roll(plan_y[pl.ds((NK + k) * tall + at, 8), :], 32 * k), weight
+            picks.append((rows, column & 127, ((column >= 0) & (column < 128), None)))
+        part = ((lane + 8) & 127) // 32
+        place = ((lane + 8) & 31) - 8
+        outer = place >= 8
+        code = jnp.zeros((8, 128), F32)
+        weight = jnp.zeros((8, 128), F32)
+        for k in range(NK):
+            edge_code = roll(codes[k], 32 * k)
+            edge_weight = roll(weights[k], 32 * k)
+            if sides:
+                edge_code = jnp.where(
+                    outer, roll(plan_y[pl.ds(k * tall + at, 8), :], 32 * k + 16), edge_code
                 )
-            rows, cols = decode(codes)
-            place = (lane - 32 * part) & 127
-            column = jnp.where(place >= 64, place - 128, place + 128) + cols
-            picks.append((rows, column & 127, (column >= 0) & (column < 128)))
-            weights.append(weight)
-        chosen = select_rows(fields_x, fields_y, at + 14, picks)
+                edge_weight = jnp.where(
+                    outer, roll(plan_y[pl.ds((NK + k) * tall + at, 8), :], 32 * k + 16), edge_weight
+                )
+            code = jnp.where(part == k, edge_code, code)
+            weight = jnp.where(part == k, edge_weight, weight)
+        rows, cols = decode(code)
+        inner_column = place & 127
+        outer_column = jnp.where(place < 16, place - 16, place + 112)
+        column = jnp.where(outer, outer_column, inner_column) + cols
+        within = (column >= 0) & (column < 128)
+        picks.append(
+            (rows, column & 127, (within & outer if sides else None, jnp.logical_not(within)))
+        )
+        chosen = select_rows((fields_x, fields_y), at + 14, picks)
+        edge = (lane < 8) | (lane >= 120)
         for field in range(NS):
             total = chosen[0][field] * weights[0]
             for k in range(1, NK):
                 total = total + chosen[k][field] * weights[k]
+            part_sum = chosen[NK][field] * weight
+            extra = part_sum
+            for k in range(1, NK):
+                extra = extra + roll(part_sum, -32 * k)
+            total = total + jnp.where(edge, extra, 0.0)
             forcing_x[pl.ds(at * 8 + field, 8, stride=8), :] = total
             forcing_x[pl.ds(at * 8 + field + 4, 8, stride=8), :] = total
             if sides:
-                part_sum = chosen[NK][field] * weights[NK]
-                total = part_sum
-                for k in range(1, NK):
-                    total = total + roll(part_sum, -32 * k)
-                forcing_y[pl.ds(at * 8 + field, 8, stride=8), :] = total
-                forcing_y[pl.ds(at * 8 + field + 4, 8, stride=8), :] = total
+                extra = roll(extra, -16)
+                forcing_y[pl.ds(at * 8 + field, 8, stride=8), :] = extra
+                forcing_y[pl.ds(at * 8 + field + 4, 8, stride=8), :] = extra
         return carry
 
     lax.fori_loop(0, tiles, tile, 0)
 
 
-def place_columns(middle, left, right):
-    lane = lanes(middle.shape)
-    return jnp.where(lane < 64, right, left)
+def place_columns(left, right):
+    return jnp.where(lanes(left.shape) < 64, right.astype(F32), left.astype(F32))
 
 
 def gelu(x):
@@ -355,7 +390,7 @@
     refs = list(refs)
     take = lambda count: [refs.pop(0) for _ in range(count)]
     (flags,) = take(1)
-    state, wet, above, beside, below, from_up, from_down, own_edges, from_left, from_right = take(10)
+    state, wet, field_one, beside, field_two, from_one, from_two, own_edges, from_left, from_right = take(10)
     if opening:
         (planes,) = take(1)
     else:
@@ -363,12 +398,24 @@
     atm_in, atm_bias, atm_out, ocn_in, ocn_bias, ocn_out, proj, keeping = take(8)
     (out,) = take(1)
     if not closing:
-        fields, new_edges, top, bottom = take(4)
+        fields, new_edges, one, two = take(4)
     if opening:
         plan_x, plan_y = take(2)
     fields_x, fields_y, forcing_x, forcing_y, stack, hidden, side, raw = take(8)
     rows, tall = d.rows, d.tall
     is_ocean, at_top, at_bottom = flags[0], flags[1], flags[2]
+    even = flags[3] == 0
+
+    def up(one, two):
+        values = jnp.where(even, two, one).astype(F32)
+        return jnp.where(at_top != 0, 0.0, values)
+
+    def down(one, two):
+        values = jnp.where(even, one, two).astype(F32)
+        return jnp.where(at_bottom != 0, 0.0, values)
+
+    def up_and_down(one, two):
+        return up(one, two), down(one, two)
 
     if opening:
 
@@ -378,43 +425,43 @@
             plan_y[...] = jnp.zeros_like(plan_y)
             base = d.strip
             side_base = 4 * (rows + 32) + 3 * d.edge_rows
-            for step, ref in ((0, from_up), (rows + 2, from_down)):
-                strip = ref[base : base + 16, :].astype(F32)
+            pair = up_and_down(from_one[base : base + 16, :], from_two[base : base + 16, :])
+            for step, strip in zip((0, rows + 2), pair):
                 for index in range(2):
                     plan_x[pl.ds(step + index, 2 * NK, stride=tall), :] = strip[index * 8 : (index + 1) * 8]
-            for step, at in ((0, side_base), (rows + 2, side_base + 16 + 2 * NK * rows)):
-                strip = place_columns(
-                    from_left[at : at + 16, :],
-                    from_left[at : at + 16, :].astype(F32),
-                    from_right[at : at + 16, :].astype(F32),
-                )
+            ends = [
+                place_columns(from_left[at : at + 16, :], from_right[at : at + 16, :])
+                for at in (side_base, side_base + 16 + 2 * NK * rows)
+            ]
+            for step, strip in zip((0, rows + 2), up_and_down(*ends)):
                 for index in range(2):
                     plan_y[pl.ds(step + index, 2 * NK, stride=tall), :] = strip[index * 8 : (index + 1) * 8]
             for plane in range(2 * NK):
                 at = side_base + 16 + plane * rows
                 plan_y[plane * tall + 2 : plane * tall + 2 + rows, :] = place_columns(
-                    from_left[at : at + rows, :],
-                    from_left[at : at + rows, :].astype(F32),
-                    from_right[at : at + rows, :].astype(F32),
+                    from_left[at : at + rows, :], from_right[at : at + rows, :]
                 )
 
         for plane in range(2 * NK):
             plan_x[plane * tall + 2 : plane * tall + 2 + rows, :] = planes[plane].astype(F32)
 
+    lower_at = 64 + 4 * rows
     for field in range(NS):
-        fields_x[field, 0:16, :] = above[field, rows - 16 : rows, :].astype(F32)
+        ends = up_and_down(field_one[field], field_two[field])
+        fields_x[field, 0:16, :] = ends[0][rows - 16 : rows]
         fields_x[field, 16 : 16 + rows, :] = beside[field].astype(F32)
-        fields_x[field, 16 + rows : 32 + rows, :] = below[field, 0:16, :].astype(F32)
-        for at, start, count in (
-            (0, field * 16, 16),
-            (16, 64 + field * rows, rows),
-            (16 + rows, 64 + 4 * rows + field * 16, 16),
-        ):
-            fields_y[field, at : at + count, :] = place_columns(
-                from_left[start : start + count, :],
-                from_left[start : start + count, :].astype(F32),
-                from_right[start : start + count, :].astype(F32),
-            )
+        fields_x[field, 16 + rows : 32 + rows, :] = ends[1][0:16]
+        start = 64 + field * rows
+        fields_y[field, 16 : 16 + rows, :] = place_columns(
+            from_left[start : start + rows, :], from_right[start : start + rows, :]
+        )
+        ends = [
+            place_columns(from_left[at : at + 16, :], from_right[at : at + 16, :])
+            for at in (field * 16, lower_at + field * 16)
+        ]
+        ends = up_and_down(*ends)
+        fields_y[field, 0:16, :] = ends[0]
+        fields_y[field, 16 + rows : 32 + rows, :] = ends[1]
 
     @pl.when(is_ocean == 0)
     def _():
@@ -426,20 +473,25 @@
         regrid(fields_x, fields_y, plan_x, plan_y, forcing_x, forcing_y, 0, d.tiles, tall, True)
         at = 4 * (rows + 32)
         size = d.edge_rows
-        edges = join_rows(
-            get_edges(from_up, 2 * CH, d), get_edges(own_edges, 0, d), get_edges(from_down, 2 * CH, d), d
+        def joined(one, own, two):
+            above, below = up_and_down(one, two)
+            return join_rows(above.astype(BF16), own, below.astype(BF16), d)
+
+        edges = joined(
+            get_edges(from_one, 2 * CH, d), get_edges(own_edges, 0, d), get_edges(from_two, 2 * CH, d)
         )
         left, right = [
-            join_rows(*[get_edges(ref, at + index * size, d) for index in range(3)], d)
+            joined(*[get_edges(ref, at + index * size, d) for index in range(3)])
             for ref in (from_left, from_right)
         ]
+        upper, lower = up_and_down(from_one[0 : 2 * CH, :], from_two[0 : 2 * CH, :])
         sea(
-            state, from_up, from_down, edges, left, right, out, forcing_x, forcing_y,
+            state, upper.astype(BF16), lower.astype(BF16), edges, left, right, out, forcing_x, forcing_y,
             ocn_in, ocn_bias, ocn_out, wet, at_top, at_bottom, stack, hidden, side, d,
         )
 
     if not closing:
-        emit(out, proj, keeping, fields, new_edges, top, bottom, raw, d)
+        emit(out, proj, keeping, fields, new_edges, one, two, even, raw, d)
 
 
 VMEM = pl.BlockSpec(memory_space=pltpu.VMEM)
@@ -466,28 +518,49 @@
     return lax.ppermute(x, names, pairs)
 
 
-def exchange(fields, own_edges, top, bottom, planes, d):
+def swap_rows(x, turn, across):
+    count = lax.axis_size("lat")
+
+    def move(group, lat, lon):
+        other = ((lat + turn) ^ 1) - turn
+        to = 1 - group if across else group
+        return to, other if 0 <= other < count else lat, lon
+
+    return send(x, move)
+
+
+def exchange(fields, own_edges, one, two, planes, d, hold):
     rows = d.rows
     beside = send(fields, lambda g, i, j: (1 - g, i, j))
-    above = send(fields, lambda g, i, j: (1 - g, i + 1, j))
-    below = send(fields, lambda g, i, j: (1 - g, i - 1, j))
-    from_up = send(bottom, lambda g, i, j: (1, i + 1, j) if g == 1 else None)
-    from_down = send(top, lambda g, i, j: (1, i - 1, j) if g == 1 else None)
+    field_one = swap_rows(fields, 0, True)
+    field_two = swap_rows(fields, 1, True)
+    from_one = swap_rows(one, 0, False)
+    from_two = swap_rows(two, 1, False)
+    (beside, field_one, field_two, from_one, from_two), hold = lax.optimization_barrier(
+        ((beside, field_one, field_two, from_one, from_two), hold)
+    )
     edge_at = slice(2 * CH, d.strip)
+    odd = lax.axis_index("lat") % 2
+    if rows == 16:
+        ends = [field_one, field_two]
+    else:
+        last = [field[:, rows - 16 :] for field in (field_one, field_two)]
+        first = [field[:, :16] for field in (field_one, field_two)]
+        ends = [jnp.where(odd == 1, last[0], first[0]), jnp.where(odd == 1, first[1], last[1])]
     packed = [
-        above[:, rows - 16 :].reshape(64, 128),
+        ends[0].reshape(64, 128),
         beside.reshape(4 * rows, 128),
-        below[:, :16].reshape(64, 128),
-        from_up[edge_at],
+        ends[1].reshape(64, 128),
+        from_one[edge_at],
         own_edges,
-        from_down[edge_at],
+        from_two[edge_at],
     ]
     if planes is not None:
-        packed += [from_up[d.strip :], planes.reshape(2 * NK * rows, 128), from_down[d.strip :]]
+        packed += [from_one[d.strip :], planes.reshape(2 * NK * rows, 128), from_two[d.strip :]]
     packed = jnp.concatenate(packed, axis=0)
     from_left = send(packed, lambda g, i, j: (g, i, j + 1))
     from_right = send(packed, lambda g, i, j: (g, i, j - 1))
-    return above, beside, below, from_up, from_down, own_edges, from_left, from_right
+    return (field_one, beside, field_two, from_one, from_two, own_edges, from_left, from_right), hold
 
 
 def local(
@@ -500,7 +573,9 @@
     group = lax.axis_index("grp")
     lat = lax.axis_index("lat")
     is_ocean = group == 1
-    flags = jnp.stack([group, lat == 0, lat == lax.axis_size("lat") - 1]).astype(jnp.int32)
+    flags = jnp.stack(
+        [group, lat == 0, lat == lax.axis_size("lat") - 1, lat % 2]
+    ).astype(jnp.int32)
     state = jnp.transpose(coupled_state[0], (1, 0, 2))
     wet = land_mask.astype(F32)
     keeping = jnp.where(is_ocean, wet, 1.0)
@@ -539,15 +614,15 @@
         shape(d.strip, 128),
     ]
     raw = pltpu.VMEM((rows * 8, 128), F32)
-    fields, edges, top, bottom = pl.pallas_call(
+    fields, edges, one, two = pl.pallas_call(
         functools.partial(start_kernel, d),
         out_shape=emitted[:2] + [shape(d.strip + 16, 128)] * 2,
-        in_specs=[VMEM] * 4,
+        in_specs=[SMEM] + [VMEM] * 4,
         out_specs=[VMEM] * 4,
         scratch_shapes=[raw, pltpu.VMEM((2 * NK * rows, 128), F32)],
         compiler_params=PARAMS,
         name="start",
-    )(state, planes, proj, keeping)
+    )(flags, state, planes, proj, keeping)
 
     scratch = [
         pltpu.VMEM((NS, rows + 32, 128), F32),
@@ -562,9 +637,9 @@
     plans = [shape(2 * NK * d.tall, 128, dtype=F32)] * 2
     state_shape = shape(rows, CH, 128)
 
-    received = exchange(fields, edges, top, bottom, planes, d)
+    received, constants = exchange(fields, edges, one, two, planes, d, constants)
     outs = [state_shape] + emitted + plans
-    state, fields, edges, top, bottom, plan_x, plan_y = pl.pallas_call(
+    state, fields, edges, one, two, plan_x, plan_y = pl.pallas_call(
         functools.partial(step_kernel, d, True, False),
         out_shape=outs,
         in_specs=[SMEM] + [VMEM] * 19,
@@ -574,7 +649,7 @@
         name="first_step",
     )(flags, state, wet, *received, planes, *constants)
 
-    received = exchange(fields, edges, top, bottom, None, d)
+    received, _ = exchange(fields, edges, one, two, None, d, ())
     state = pl.pallas_call(
         functools.partial(step_kernel, d, False, True),
         out_shape=state_shape,

time: 81.5 us -> 69.4 us (0.85)
  the two profiles are of different devices: /device:TPU:2 before, /device:TPU:7 now
where the time goes in v1:
time: 69.4 us; the launch traced here: 69 us
  Pallas kernels  33.2 us (48%)
  starting transfers between devices  18.7 us (27%)
  waiting for transfers between devices  10 us (14%)
  local copies, waits for them, and re-layouts  5.74 us (8%)
  other arithmetic  1.02 us (1%)
    ppermute x14, starting transfers between devices, send(): return lax.ppermute(x, names, pairs)  18.7 us
    pallas_call x1, Pallas kernels, local(): pl.pallas_call(functools.partial(step_kernel, d, True, False), out_shape=...  16.4 us
    pallas_call x1, Pallas kernels, local(): pl.pallas_call(functools.partial(step_kernel, d, False, True), out_shape=...  14.1 us
    ppermute x14, waiting for transfers between devices, send(): return lax.ppermute(x, names, pairs)  10 us
    unnamed x33, local copies, waits for them, and re-layouts  3.46 us
    pallas_call x1, Pallas kernels, local(): pl.pallas_call(functools.partial(start_kernel, d), out_shape=emitted[:2]...  2.77 us
  transfers between devices with their start and end apart: 14, of which 4 were waited for; matrix products, arithmetic and copies ran while one was open for 2% of the time, Pallas kernels for 0%

profile of v1, /device:TPU:7, one launch (start us, length us, event | category | flops | bytes accessed | tf_op | source)
XLA Modules:
  0.0 69.0 jit_solution(3587386213539879049)
XLA Ops:
  0.0 0.8 %fusion = bf16[4,16,128]{2,1,0:T(8,128)(2,1)S(1)} fusion(s32[1,2,4,16,128]{4,3,2,1,0:T(8,128)} %param.13), kind=kLoop, calls=%fused_computation.20 | loop fusion | flops 24576 | bytes 81920 | tf_op jit(solution)/shard_map/convert_element_type | solution.py:590
  0.8 1.1 %copy.31 = bf16[1,80,16,128]{3,1,2,0:T(8,128)(2,1)S(1)} copy(bf16[1,80,16,128]{3,2,1,0:T(8,128)(2,1)} %param.11) | data formatting | bytes 655360 | tf_op args[0]
  2.2 2.8 %start.1 = (bf16[4,16,128]{2,1,0:T(8,128)(2,1)S(1)}, bf16[80,128]{1,0:T(8,128)(2,1)S(1)}, bf16[256,128]{1,0:T(8,128)(2,1)S(1)}, bf16[256,128]{1,0:T(8,128)(2,1)S(1)}) custom-call(s32[4]{0:T(128)S(1)} %pad_add_fusion.flags.refs_0_, bf16[16,80,128]{2,1,0:T(8,128)(2,1)S(1)} %bitcast.42, bf16[8,16,128]{2,1,0:T(8,128)(2,1)S(1)} %pad_maximum_fusion.planes.refs_11_, ...), custom_call_target="tpu_custom_call" | custom-call | tf_op jit(solution)/shard_map/start/pallas_call | solution.py:617
  4.9 0.3 collective-permute-start.2
  5.3 3.2 %collective-permute-start.1 = (bf16[4,16,128]{2,1,0:T(8,128)(2,1)S(1)}, bf16[4,16,128]{2,1,0:T(8,128)(2,1)S(1)}, u32[]{:S(2)}, u32[]{:S(2)}) collective-permute-start(bf16[4,16,128]{2,1,0:T(8,128)(2,1)S(1)} %get-tuple-element.34), channel_id=1, source_target_pairs={{0,20},{1,21},{2,22},{3,23},{4,16},{5,17},{6,18},{7,19},{8,28},{9,... | collective-permute-start | bytes 49160 | tf_op jit(solution)/shard_map/ppermute | solution.py:518
  8.5 0.3 collective-permute-start
  8.8 0.7 collective-permute-start.4
  9.7 0.6 copy-done.7
  10.9 0.9 %copy-done.2 = bf16[80,9,200]{2,0,1:T(8,128)(2,1)S(1)} copy-done((bf16[80,9,200]{2,0,1:T(8,128)(2,1)S(1)}, bf16[80,9,200]{2,0,1:T(8,128)(2,1)}, u32[]{:S(2)}) %copy-start.2) | copy-done | bytes 288024
  12.4 0.3 reshape.49.refs_17_.refs_18_
  12.6 0.4 copy-done.8
  13.2 1.6 %collective-permute-start.6 = (bf16[592,128]{1,0:T(8,128)(2,1)S(1)}, bf16[592,128]{1,0:T(8,128)(2,1)S(1)}, u32[]{:S(2)}, u32[]{:S(2)}) collective-permute-start(bf16[592,128]{1,0:T(8,128)(2,1)S(1)} %constant_dynamic-update-slice_fusion), channel_id=1, source_target_pairs={{0,3},{1,0},{2,1},{3,2},{4,7},{5,4},{6,5},{7,6},{8,11},{9,8},{10,9... | collective-permute-start | bytes 454664 | tf_op jit(solution)/shard_map/ppermute | solution.py:518
  15.3 3.6 %collective-permute-done.6.refs_10_ = bf16[592,128]{1,0:T(8,128)(2,1)S(1)} collective-permute-done((bf16[592,128]{1,0:T(8,128)(2,1)S(1)}, bf16[592,128]{1,0:T(8,128)(2,1)S(1)}, u32[]{:S(2)}, u32[]{:S(2)}) %collective-permute-start.6) | collective-permute-done | bytes 151584 | tf_op jit(solution)/shard_map/ppermute | solution.py:518
  18.9 16.4 %first_step.1 = (bf16[16,80,128]{2,1,0:T(8,128)(2,1)S(1)}, bf16[4,16,128]{2,1,0:T(8,128)(2,1)S(1)}, bf16[80,128]{1,0:T(8,128)(2,1)S(1)}, bf16[240,128]{1,0:T(8,1...) custom-call(s32[4]{0:T(128)S(1)} %pad_add_fusion.flags.refs_0_, ...), custom_call_target="tpu_custom_call" | custom-call | tf_op jit(solution)/shard_map/first_step/pallas_call | solution.py:642
  35.3 3.4 %collective-permute-start.10 = (bf16[240,128]{1,0:T(8,128)(2,1)S(1)}, bf16[240,128]{1,0:T(8,128)(2,1)S(1)}, u32[]{:S(2)}, u32[]{:S(2)}) collective-permute-start(bf16[240,128]{1,0:T(8,128)(2,1)S(1)} %get-tuple-element.53), channel_id=1, source_target_pairs={{0,4},{1,5},{2,6},{3,7},{4,0},{5,1},{6,2},{7,3},{8,12},{9,13},{10,... | collective-permute-start | bytes 184328 | tf_op jit(solution)/shard_map/ppermute | solution.py:518
  38.7 0.7 collective-permute-start.11
  39.4 3.6 %collective-permute-start.8 = (bf16[4,16,128]{2,1,0:T(8,128)(2,1)S(1)}, bf16[4,16,128]{2,1,0:T(8,128)(2,1)S(1)}, u32[]{:S(2)}, u32[]{:S(2)}) collective-permute-start(bf16[4,16,128]{2,1,0:T(8,128)(2,1)S(1)} %get-tuple-element.52), channel_id=1, source_target_pairs={{0,20},{1,21},{2,22},{3,23},{4,16},{5,17},{6,18},{7,19},{8,28},{9,... | collective-permute-start | bytes 49160 | tf_op jit(solution)/shard_map/ppermute | solution.py:518
  43.1 1.2 %collective-permute-done.8.refs_3_ = bf16[4,16,128]{2,1,0:T(8,128)(2,1)S(1)} collective-permute-done((bf16[4,16,128]{2,1,0:T(8,128)(2,1)S(1)}, bf16[4,16,128]{2,1,0:T(8,128)(2,1)S(1)}, u32[]{:S(2)}, u32[]{:S(2)}) %collective-permute-start.8) | collective-permute-done | bytes 16416 | tf_op jit(solution)/shard_map/ppermute | solution.py:518
  44.3 1.4 %collective-permute-done.7.refs_4_ = bf16[4,16,128]{2,1,0:T(8,128)(2,1)S(1)} collective-permute-done((bf16[4,16,128]{2,1,0:T(8,128)(2,1)S(1)}, bf16[4,16,128]{2,1,0:T(8,128)(2,1)S(1)}, u32[]{:S(2)}, u32[]{:S(2)}) %collective-permute-start.7) | collective-permute-done | bytes 16416 | tf_op jit(solution)/shard_map/ppermute | solution.py:518
  45.7 3.4 %collective-permute-start.13 = (bf16[432,128]{1,0:T(8,128)(2,1)S(1)}, bf16[432,128]{1,0:T(8,128)(2,1)S(1)}, u32[]{:S(2)}, u32[]{:S(2)}) collective-permute-start(bf16[432,128]{1,0:T(8,128)(2,1)S(1)} %constant_dynamic-update-slice_fusion.9), channel_id=1, source_target_pairs={{0,3},{1,0},{2,1},{3,2},{4,7},{5,4},{6,5},{7,6},{8,11},{9,8},{10,9... | collective-permute-start | bytes 331784 | tf_op jit(solution)/shard_map/ppermute | solution.py:518
  49.1 1.2 %collective-permute-start.12 = (bf16[432,128]{1,0:T(8,128)(2,1)S(1)}, bf16[432,128]{1,0:T(8,128)(2,1)S(1)}, u32[]{:S(2)}, u32[]{:S(2)}) collective-permute-start(bf16[432,128]{1,0:T(8,128)(2,1)S(1)} %constant_dynamic-update-slice_fusion.9), channel_id=1, source_target_pairs={{0,1},{1,2},{2,3},{3,0},{4,5},{5,6},{6,7},{7,4},{8,9},{9,10},{10,1... | collective-permute-start | bytes 331784 | tf_op jit(solution)/shard_map/ppermute | solution.py:518
  50.3 3.8 %collective-permute-done.13.refs_10_ = bf16[432,128]{1,0:T(8,128)(2,1)S(1)} collective-permute-done((bf16[432,128]{1,0:T(8,128)(2,1)S(1)}, bf16[432,128]{1,0:T(8,128)(2,1)S(1)}, u32[]{:S(2)}, u32[]{:S(2)}) %collective-permute-start.13) | collective-permute-done | bytes 110624 | tf_op jit(solution)/shard_map/ppermute | solution.py:518
  54.1 14.1 %second_step.1 = bf16[16,80,128]{2,1,0:T(8,128)(2,1)S(1)} custom-call(s32[4]{0:T(128)S(1)} %pad_add_fusion.flags.refs_0_, bf16[16,80,128]{2,1,0:T(8,128)(2,1)S(1)} %get-tuple-element.51.refs_1_, f32[16,128]{1,0:T(8,128)S(1)} %convert_element_type.40.refs_2_, bf16[4,16,128]{2,1,0:T(8,128)(2,1)S(1)} %collective-permute-done.8.refs_3_, ...), custom_call_target="tpu_custom_call" | custom-call | tf_op jit(solution)/shard_map/second_step/pallas_call | solution.py:653
  68.2 0.8 %copy.26 = bf16[1,80,16,128]{3,2,1,0:T(8,128)(2,1)} copy(bf16[1,80,16,128]{3,1,2,0:T(8,128)(2,1)S(1)} %bitcast.44) | data formatting | bytes 655360 | tf_op jit(solution)/shard_map/broadcast_in_dim | solution.py:662
  (68 shorter events, 2.3 us)
Async XLA Ops:
  0.0 0.8 %copy-start.4 = (f32[1,4,16,128]{3,2,1,0:T(8,128)S(1)}, f32[1,4,16,128]{3,2,1,0:T(8,128)}, u32[]{:S(2)}) copy-start(f32[1,4,16,128]{3,2,1,0:T(8,128)} %param.14) | copy-start | bytes 98308
  0.8 1.1 %copy-start.6 = (f32[2,4,80]{2,1,0:T(4,128)S(1)}, f32[2,4,80]{2,1,0:T(4,128)}, u32[]{:S(2)}) copy-start(f32[2,4,80]{2,1,0:T(4,128)} %param.15) | copy-start | bytes 7684
  0.8 1.1 %copy-start.5 = (s32[16,128]{1,0:T(8,128)S(1)}, s32[16,128]{1,0:T(8,128)}, u32[]{:S(2)}) copy-start(s32[16,128]{1,0:T(8,128)} %param.12) | copy-start | bytes 24580
  1.9 7.5 %copy-start.1 = (bf16[200,9,84]{0,2,1:T(8,128)(2,1)S(1)}, bf16[200,9,84]{0,2,1:T(8,128)(2,1)}, u32[]{:S(2)}) copy-start(bf16[200,9,84]{0,2,1:T(8,128)(2,1)} %param.19) | copy-start | bytes 907204
  4.9 8.1 %collective-permute-start.2 = (bf16[4,16,128]{2,1,0:T(8,128)(2,1)S(1)}, bf16[4,16,128]{2,1,0:T(8,128)(2,1)S(1)}, u32[]{:S(2)}, u32[]{:S(2)}) collective-permute-start(bf16[4,16,128]{2,1,0:T(8,128)(2,1)S(1)} %get-tuple-element.34), channel_id=1, source_target_pairs={{0,16},{1,17},{2,18},{3,19},{4,24},{5,25},{6,26},{7,27},{8,20},{9,... | collective-permute-start | bytes 49160 | tf_op jit(solution)/shard_map/ppermute | solution.py:518
  5.3 7.8 %collective-permute-start.1 = (bf16[4,16,128]{2,1,0:T(8,128)(2,1)S(1)}, bf16[4,16,128]{2,1,0:T(8,128)(2,1)S(1)}, u32[]{:S(2)}, u32[]{:S(2)}) collective-permute-start(bf16[4,16,128]{2,1,0:T(8,128)(2,1)S(1)} %get-tuple-element.34), channel_id=1, source_target_pairs={{0,20},{1,21},{2,22},{3,23},{4,16},{5,17},{6,18},{7,19},{8,28},{9,... | collective-permute-start | bytes 49160 | tf_op jit(solution)/shard_map/ppermute | solution.py:518
  8.5 4.5 %collective-permute-start = (bf16[4,16,128]{2,1,0:T(8,128)(2,1)S(1)}, bf16[4,16,128]{2,1,0:T(8,128)(2,1)S(1)}, u32[]{:S(2)}, u32[]{:S(2)}) collective-permute-start(bf16[4,16,128]{2,1,0:T(8,128)(2,1)S(1)} %get-tuple-element.34), channel_id=1, source_target_pairs={{0,16},{1,17},{2,18},{3,19},{4,20},{5,21},{6,22},{7,23},{8,24},{9,... | collective-permute-start | bytes 49160 | tf_op jit(solution)/shard_map/ppermute | solution.py:518
  8.8 4.3 %collective-permute-start.3 = (bf16[256,128]{1,0:T(8,128)(2,1)S(1)}, bf16[256,128]{1,0:T(8,128)(2,1)S(1)}, u32[]{:S(2)}, u32[]{:S(2)}) collective-permute-start(bf16[256,128]{1,0:T(8,128)(2,1)S(1)} %get-tuple-element.35), channel_id=1, source_target_pairs={{0,4},{1,5},{2,6},{3,7},{4,0},{5,1},{6,2},{7,3},{8,12},{9,13},{10,... | collective-permute-start | bytes 196616 | tf_op jit(solution)/shard_map/ppermute | solution.py:518
  8.8 4.3 %collective-permute-start.4 = (bf16[256,128]{1,0:T(8,128)(2,1)S(1)}, bf16[256,128]{1,0:T(8,128)(2,1)S(1)}, u32[]{:S(2)}, u32[]{:S(2)}) collective-permute-start(bf16[256,128]{1,0:T(8,128)(2,1)S(1)} %get-tuple-element.36), channel_id=1, source_target_pairs={{0,0},{1,1},{2,2},{3,3},{4,8},{5,9},{6,10},{7,11},{8,4},{9,5},{10,... | collective-permute-start | bytes 196616 | tf_op jit(solution)/shard_map/ppermute | solution.py:518
  9.6 0.7 copy-start.7
  9.6 0.9 %copy-start.3 = (bf16[384,84]{0,1:T(8,128)(2,1)S(1)}, bf16[384,84]{0,1:T(8,128)(2,1)}, u32[]{:S(2)}) copy-start(bf16[384,84]{0,1:T(8,128)(2,1)} %param.16) | copy-start | bytes 193540
  10.9 1.0 %copy-start.2 = (bf16[80,9,200]{2,0,1:T(8,128)(2,1)S(1)}, bf16[80,9,200]{2,0,1:T(8,128)(2,1)}, u32[]{:S(2)}) copy-start(bf16[80,9,200]{2,0,1:T(8,128)(2,1)} %param.21) | copy-start | bytes 864004
  12.3 0.7 copy-start.8
  13.2 5.7 %collective-permute-start.6 = (bf16[592,128]{1,0:T(8,128)(2,1)S(1)}, bf16[592,128]{1,0:T(8,128)(2,1)S(1)}, u32[]{:S(2)}, u32[]{:S(2)}) collective-permute-start(bf16[592,128]{1,0:T(8,128)(2,1)S(1)} %constant_dynamic-update-slice_fusion), channel_id=1, source_target_pairs={{0,3},{1,0},{2,1},{3,2},{4,7},{5,4},{6,5},{7,6},{8,11},{9,8},{10,9... | collective-permute-start | bytes 454664 | tf_op jit(solution)/shard_map/ppermute | solution.py:518
  14.8 4.1 %collective-permute-start.5 = (bf16[592,128]{1,0:T(8,128)(2,1)S(1)}, bf16[592,128]{1,0:T(8,128)(2,1)S(1)}, u32[]{:S(2)}, u32[]{:S(2)}) collective-permute-start(bf16[592,128]{1,0:T(8,128)(2,1)S(1)} %constant_dynamic-update-slice_fusion), channel_id=1, source_target_pairs={{0,1},{1,2},{2,3},{3,0},{4,5},{5,6},{6,7},{7,4},{8,9},{9,10},{10,1... | collective-permute-start | bytes 454664 | tf_op jit(solution)/shard_map/ppermute | solution.py:518
  15.1 3.8 %copy-start = (bf16[80,384]{1,0:T(8,128)(2,1)S(1)}, bf16[80,384]{1,0:T(8,128)(2,1)}, u32[]{:S(2)}) copy-start(bf16[80,384]{1,0:T(8,128)(2,1)} %refs_15_) | copy-start | bytes 184324
  35.3 10.4 %collective-permute-start.10 = (bf16[240,128]{1,0:T(8,128)(2,1)S(1)}, bf16[240,128]{1,0:T(8,128)(2,1)S(1)}, u32[]{:S(2)}, u32[]{:S(2)}) collective-permute-start(bf16[240,128]{1,0:T(8,128)(2,1)S(1)} %get-tuple-element.53), channel_id=1, source_target_pairs={{0,4},{1,5},{2,6},{3,7},{4,0},{5,1},{6,2},{7,3},{8,12},{9,13},{10,... | collective-permute-start | bytes 184328 | tf_op jit(solution)/shard_map/ppermute | solution.py:518
  38.7 7.0 %collective-permute-start.11 = (bf16[240,128]{1,0:T(8,128)(2,1)S(1)}, bf16[240,128]{1,0:T(8,128)(2,1)S(1)}, u32[]{:S(2)}, u32[]{:S(2)}) collective-permute-start(bf16[240,128]{1,0:T(8,128)(2,1)S(1)} %get-tuple-element.54), channel_id=1, source_target_pairs={{0,0},{1,1},{2,2},{3,3},{4,8},{5,9},{6,10},{7,11},{8,4},{9,5},{10,... | collective-permute-start | bytes 184328 | tf_op jit(solution)/shard_map/ppermute | solution.py:518
  39.3 3.7 %collective-permute-start.9 = (bf16[4,16,128]{2,1,0:T(8,128)(2,1)S(1)}, bf16[4,16,128]{2,1,0:T(8,128)(2,1)S(1)}, u32[]{:S(2)}, u32[]{:S(2)}) collective-permute-start(bf16[4,16,128]{2,1,0:T(8,128)(2,1)S(1)} %get-tuple-element.52), channel_id=1, source_target_pairs={{0,16},{1,17},{2,18},{3,19},{4,24},{5,25},{6,26},{7,27},{8,20},{9,... | collective-permute-start | bytes 49160 | tf_op jit(solution)/shard_map/ppermute | solution.py:518
  39.4 4.9 %collective-permute-start.8 = (bf16[4,16,128]{2,1,0:T(8,128)(2,1)S(1)}, bf16[4,16,128]{2,1,0:T(8,128)(2,1)S(1)}, u32[]{:S(2)}, u32[]{:S(2)}) collective-permute-start(bf16[4,16,128]{2,1,0:T(8,128)(2,1)S(1)} %get-tuple-element.52), channel_id=1, source_target_pairs={{0,20},{1,21},{2,22},{3,23},{4,16},{5,17},{6,18},{7,19},{8,28},{9,... | collective-permute-start | bytes 49160 | tf_op jit(solution)/shard_map/ppermute | solution.py:518
  43.0 2.6 %collective-permute-start.7 = (bf16[4,16,128]{2,1,0:T(8,128)(2,1)S(1)}, bf16[4,16,128]{2,1,0:T(8,128)(2,1)S(1)}, u32[]{:S(2)}, u32[]{:S(2)}) collective-permute-start(bf16[4,16,128]{2,1,0:T(8,128)(2,1)S(1)} %get-tuple-element.52), channel_id=1, source_target_pairs={{0,16},{1,17},{2,18},{3,19},{4,20},{5,21},{6,22},{7,23},{8,24},{9,... | collective-permute-start | bytes 49160 | tf_op jit(solution)/shard_map/ppermute | solution.py:518
  45.7 8.4 %collective-permute-start.13 = (bf16[432,128]{1,0:T(8,128)(2,1)S(1)}, bf16[432,128]{1,0:T(8,128)(2,1)S(1)}, u32[]{:S(2)}, u32[]{:S(2)}) collective-permute-start(bf16[432,128]{1,0:T(8,128)(2,1)S(1)} %constant_dynamic-update-slice_fusion.9), channel_id=1, source_target_pairs={{0,3},{1,0},{2,1},{3,2},{4,7},{5,4},{6,5},{7,6},{8,11},{9,8},{10,9... | collective-permute-start | bytes 331784 | tf_op jit(solution)/shard_map/ppermute | solution.py:518
  49.1 5.0 %collective-permute-start.12 = (bf16[432,128]{1,0:T(8,128)(2,1)S(1)}, bf16[432,128]{1,0:T(8,128)(2,1)S(1)}, u32[]{:S(2)}, u32[]{:S(2)}) collective-permute-start(bf16[432,128]{1,0:T(8,128)(2,1)S(1)} %constant_dynamic-update-slice_fusion.9), channel_id=1, source_target_pairs={{0,1},{1,2},{2,3},{3,0},{4,5},{5,6},{6,7},{7,4},{8,9},{9,10},{10,1... | collective-permute-start | bytes 331784 | tf_op jit(solution)/shard_map/ppermute | solution.py:518

commit v2 on v1

--- a/solution.py
+++ b/solution.py
@@ -62,20 +62,28 @@
     block = lane // d.block
     row = lane % d.block - 2
     column = jnp.where(block == 0, 126, jnp.where(block == 1, 0, jnp.where(block == 2, 127, 1)))
-    half = d.rows // 2
     own = (row >= 0) & (row < d.rows)
-    target = jnp.where(own, column + 128 * (row // half), -1)
-    turn = row % half
-
-    def body(step, total):
-        place = subs((256, d.edge)) == jnp.where(turn == step, target, -1)
-        pair = jnp.concatenate([state[step], state[step + half]], axis=1)
-        return total + jnp.dot(
-            pair, place.astype(F32).astype(BF16), preferred_element_type=F32
-        )
-
-    total = lax.fori_loop(0, half, body, jnp.zeros((CH, d.edge), F32))
+    target = jnp.where(own, column, -1)
+    position = subs((128, d.edge))
+    places = [
+        (position == jnp.where(row == step, target, -1)).astype(F32).astype(BF16)
+        for step in range(d.rows)
+    ]
+    whole = jnp.concatenate([state[step] for step in range(d.rows)], axis=1)
+    total = jnp.dot(whole, jnp.concatenate(places, axis=0), preferred_element_type=F32)
     return total.astype(BF16)
+
+
+def loop(count, unroll, body):
+    while count % unroll:
+        unroll -= 1
+
+    def several(step, carry):
+        for offset in range(unroll):
+            body(step * unroll + offset)
+        return carry
+
+    lax.fori_loop(0, count // unroll, several, 0)
 
 
 def strips(one, two, even, d):
@@ -86,15 +94,14 @@
 def emit(state, proj, keeping, fields, own_edges, one, two, even, raw, d):
     half = d.rows // 2
 
-    def body(step, carry):
+    def body(step):
         pair = jnp.concatenate([state[step], state[step + half]], axis=1)
         parts = jnp.dot(proj[...], pair, preferred_element_type=F32)
         whole = parts[0:8] + parts[8:16] + parts[16:24]
         raw[pl.ds(pl.multiple_of(step * 8, 8), 8), :] = whole[:, :128]
         raw[pl.ds(pl.multiple_of((step + half) * 8, 8), 8), :] = whole[:, 128:]
-        return carry
-
-    lax.fori_loop(0, half, body, 0)
+
+    loop(half, 8, body)
     for field in range(NS):
         fields[field] = (raw[pl.ds(field, d.rows, stride=8), :] * keeping[...]).astype(BF16)
     edges = edge_columns(state, d)
@@ -230,15 +237,14 @@
         forced = jnp.concatenate([forcing_x[pl.ds(at, 8), :], blank], axis=0)
         return jnp.concatenate([state[row], forced.astype(BF16)], axis=0)
 
-    def body(step, carry):
+    def body(step):
         pair = jnp.concatenate([inputs(step), inputs(step + half)], axis=1)
         hidden = gelu(jnp.dot(atm_in[...], pair, preferred_element_type=F32) + atm_bias[...])
         update = jnp.dot(atm_out[...], hidden.astype(BF16), preferred_element_type=F32)
         out[step] = (state[step].astype(F32) + update[:, :128]).astype(BF16)
         out[step + half] = (state[step + half].astype(F32) + update[:, 128:]).astype(BF16)
-        return carry
-
-    lax.fori_loop(0, half, body, 0)
+
+    loop(half, 2, body)
 
 
 def edge_forcing(forcing_x, forcing_y, d):
@@ -246,21 +252,19 @@
     block = lane // d.block
     row = lane % d.block
 
-    def body(step, carry):
-        inner, outer = carry
-        at = pl.ds(pl.multiple_of(step * 8, 8), 8)
+    inner = outer = jnp.zeros((8, d.edge), F32)
+    for step in range(d.rows + 4):
+        at = pl.ds(step * 8, 8)
         pad = [jnp.zeros((8, 128), F32)] * (d.pieces - 1)
         here = jnp.concatenate([forcing_x[at, :]] + pad, axis=1)
         there = jnp.concatenate([forcing_y[at, :]] + pad, axis=1)
         for index, column in enumerate((126, 0, 127, 1)):
-            shift = (step + index * d.block - column) % d.edge
+            shift = step + index * d.block - column
             match = (block == index) & (row == step)
-            inner = jnp.where(match, roll(here, shift), inner)
+            if column in (0, 127):
+                inner = jnp.where(match, roll(here, shift), inner)
             outer = jnp.where(match, roll(there, shift), outer)
-        return inner, outer
-
-    blank = jnp.zeros((8, d.edge), F32)
-    return lax.fori_loop(0, d.rows + 4, body, (blank, blank))
+    return inner, outer
 
 
 def sea(
@@ -303,11 +307,11 @@
     lane_row = lanes((8, 128))
 
     def build(row, values):
-        entry = roll(middle, (127 - row) % d.edge)[:, :128]
-        stack[row, 0:CH, :] = roll(jnp.where(lane == 127, entry, values), 1)
+        entry = roll(middle, (d.edge - row) % d.edge)[:, :128]
+        stack[row, 0:CH, :] = jnp.where(lane == 0, entry, roll(values, 1))
         stack[row, CH : 2 * CH, :] = values
-        entry = roll(middle, (2 * d.edge - block - row) % d.edge)[:, :128]
-        stack[row, 2 * CH : 3 * CH, :] = roll(jnp.where(lane == 0, entry, values), -1)
+        entry = roll(middle, (2 * d.edge + 127 - block - row) % d.edge)[:, :128]
+        stack[row, 2 * CH : 3 * CH, :] = jnp.where(lane == 127, entry, roll(values, -1))
         at = pl.ds(pl.multiple_of(row * 8, 8), 8)
         here, there = forcing_x[at, :], forcing_y[at, :]
         before = roll(jnp.where(lane_row == 127, there, here), 1)
@@ -321,15 +325,11 @@
         build(jnp.int32(step), upper[step * CH : (step + 1) * CH, :])
         build(jnp.int32(rows + 2 + step), lower[step * CH : (step + 1) * CH, :])
 
-    def build_own(step, carry):
-        build(step + 2, state[step])
-        return carry
-
-    lax.fori_loop(0, rows, build_own, 0)
+    loop(rows, 4, lambda step: build(step + 2, state[step]))
 
     pairs = (rows + 2) // 2
 
-    def first(step, carry):
+    def first(step):
         taps = jnp.concatenate(
             [
                 stack[pl.ds(step, 3)].reshape(3 * 256, 128),
@@ -343,9 +343,8 @@
         keep_high = jnp.where((step == pairs - 1) & (at_bottom != 0), 0.0, 1.0).astype(F32)
         hidden[step] = (active[:, :128] * keep_low).astype(BF16)
         hidden[step + pairs] = (active[:, 128:] * keep_high).astype(BF16)
-        return carry
-
-    lax.fori_loop(0, pairs, first, 0)
+
+    loop(pairs, 3, first)
 
     product = jnp.dot(ocn_in[...], side[...], preferred_element_type=F32) + ocn_bias[...]
     spot = lanes((1, d.edge)) % block
@@ -356,7 +355,7 @@
     from_left, from_right = partial[0:CH], partial[2 * CH : 3 * CH]
     half = rows // 2
 
-    def second(step, carry):
+    def second(step):
         taps = jnp.concatenate(
             [
                 hidden[pl.ds(step, 3)].reshape(3 * HIDP, 128),
@@ -368,15 +367,14 @@
         for offset in range(2):
             row = step + offset * half
             sums = product[:, offset * 128 : (offset + 1) * 128]
-            entry = roll(from_left, (127 - row) % d.edge)[:, :128]
-            total = sums[CH : 2 * CH] + roll(jnp.where(lane == 127, entry, sums[0:CH]), 1)
-            entry = roll(from_right, (2 * d.edge - block - row) % d.edge)[:, :128]
-            total = total + roll(jnp.where(lane == 0, entry, sums[2 * CH : 3 * CH]), -1)
+            entry = roll(from_left, (d.edge - row) % d.edge)[:, :128]
+            total = sums[CH : 2 * CH] + jnp.where(lane == 0, entry, roll(sums[0:CH], 1))
+            entry = roll(from_right, (2 * d.edge + 127 - block - row) % d.edge)[:, :128]
+            total = total + jnp.where(lane == 127, entry, roll(sums[2 * CH : 3 * CH], -1))
             update = total * wet[pl.ds(row, 1), :]
             out[row] = (state[row].astype(F32) + update).astype(BF16)
-        return carry
-
-    lax.fori_loop(0, half, second, 0)
+
+    loop(half, 2, second)
 
 
 def join_rows(edge_up, edge_own, edge_down, d):
@@ -529,16 +527,13 @@
     return send(x, move)
 
 
-def exchange(fields, own_edges, one, two, planes, d, hold):
+def exchange(fields, own_edges, one, two, planes, d):
     rows = d.rows
     beside = send(fields, lambda g, i, j: (1 - g, i, j))
     field_one = swap_rows(fields, 0, True)
     field_two = swap_rows(fields, 1, True)
     from_one = swap_rows(one, 0, False)
     from_two = swap_rows(two, 1, False)
-    (beside, field_one, field_two, from_one, from_two), hold = lax.optimization_barrier(
-        ((beside, field_one, field_two, from_one, from_two), hold)
-    )
     edge_at = slice(2 * CH, d.strip)
     odd = lax.axis_index("lat") % 2
     if rows == 16:
@@ -560,7 +555,7 @@
     packed = jnp.concatenate(packed, axis=0)
     from_left = send(packed, lambda g, i, j: (g, i, j + 1))
     from_right = send(packed, lambda g, i, j: (g, i, j - 1))
-    return (field_one, beside, field_two, from_one, from_two, own_edges, from_left, from_right), hold
+    return field_one, beside, field_two, from_one, from_two, own_edges, from_left, from_right
 
 
 def local(
@@ -637,7 +632,7 @@
     plans = [shape(2 * NK * d.tall, 128, dtype=F32)] * 2
     state_shape = shape(rows, CH, 128)
 
-    received, constants = exchange(fields, edges, one, two, planes, d, constants)
+    received = exchange(fields, edges, one, two, planes, d)
     outs = [state_shape] + emitted + plans
     state, fields, edges, one, two, plan_x, plan_y = pl.pallas_call(
         functools.partial(step_kernel, d, True, False),
@@ -649,7 +644,7 @@
         name="first_step",
     )(flags, state, wet, *received, planes, *constants)
 
-    received, _ = exchange(fields, edges, one, two, None, d, ())
+    received = exchange(fields, edges, one, two, None, d)
     state = pl.pallas_call(
         functools.partial(step_kernel, d, False, True),
         out_shape=state_shape,

time: 69.4 us -> 53.2 us (0.77)
  the two profiles are of different devices: /device:TPU:7 before, /device:TPU:15 now
where the time goes in v2:
time: 53.2 us; the launch traced here: 52.8 us
  starting transfers between devices  18.5 us (35%)
  Pallas kernels  18.3 us (34%)
  waiting for transfers between devices  8.12 us (15%)
  local copies, waits for them, and re-layouts  6.54 us (12%)
  other arithmetic  1.02 us (2%)
    ppermute x14, starting transfers between devices, send(): return lax.ppermute(x, names, pairs)  18.5 us
    pallas_call x1, Pallas kernels, local(): pl.pallas_call(functools.partial(step_kernel, d, True, False), out_shape=...  8.88 us
    pallas_call x1, Pallas kernels, local(): pl.pallas_call(functools.partial(step_kernel, d, False, True), out_shape=...  8.54 us
    ppermute x14, waiting for transfers between devices, send(): return lax.ppermute(x, names, pairs)  8.12 us
    unnamed x33, local copies, waits for them, and re-layouts  4.3 us
  transfers between devices with their start and end apart: 14, of which 4 were waited for; matrix products, arithmetic and copies ran while one was open for 3% of the time, Pallas kernels for 0%

profile of v2, /device:TPU:15, one launch (start us, length us, event | category | flops | bytes accessed | tf_op | source)
XLA Modules:
  0.0 52.8 jit_solution(10800217723817976762)
XLA Ops:
  0.0 0.8 %fusion = bf16[4,16,128]{2,1,0:T(8,128)(2,1)S(1)} fusion(s32[1,2,4,16,128]{4,3,2,1,0:T(8,128)} %param.13), kind=kLoop, calls=%fused_computation.20 | loop fusion | flops 24576 | bytes 81920 | tf_op jit(solution)/shard_map/convert_element_type | solution.py:585
  0.8 1.1 %copy.31 = bf16[1,80,16,128]{3,1,2,0:T(8,128)(2,1)S(1)} copy(bf16[1,80,16,128]{3,2,1,0:T(8,128)(2,1)} %param.11) | data formatting | bytes 655360 | tf_op args[0]
  2.2 0.8 %start.1 = (bf16[4,16,128]{2,1,0:T(8,128)(2,1)S(1)}, bf16[80,128]{1,0:T(8,128)(2,1)S(1)}, bf16[256,128]{1,0:T(8,128)(2,1)S(1)}, bf16[256,128]{1,0:T(8,128)(2,1)S(1)}) custom-call(s32[4]{0:T(128)S(1)} %pad_add_fusion.flags.refs_0_, bf16[16,80,128]{2,1,0:T(8,128)(2,1)S(1)} %bitcast.42, bf16[8,16,128]{2,1,0:T(8,128)(2,1)S(1)} %pad_maximum_fusion.planes.refs_11_, ...), custom_call_target="tpu_custom_call" | custom-call | tf_op jit(solution)/shard_map/start/pallas_call | solution.py:612
  3.2 3.3 %collective-permute-start.2 = (bf16[4,16,128]{2,1,0:T(8,128)(2,1)S(1)}, bf16[4,16,128]{2,1,0:T(8,128)(2,1)S(1)}, u32[]{:S(2)}, u32[]{:S(2)}) collective-permute-start(bf16[4,16,128]{2,1,0:T(8,128)(2,1)S(1)} %get-tuple-element.16), channel_id=1, source_target_pairs={{0,16},{1,17},{2,18},{3,19},{4,24},{5,25},{6,26},{7,27},{8,20},{9,... | collective-permute-start | bytes 49160 | tf_op jit(solution)/shard_map/ppermute | solution.py:516
  6.6 0.3 collective-permute-start.1
  6.8 2.3 %collective-permute-start.4 = (bf16[256,128]{1,0:T(8,128)(2,1)S(1)}, bf16[256,128]{1,0:T(8,128)(2,1)S(1)}, u32[]{:S(2)}, u32[]{:S(2)}) collective-permute-start(bf16[256,128]{1,0:T(8,128)(2,1)S(1)} %get-tuple-element.18), channel_id=1, source_target_pairs={{0,0},{1,1},{2,2},{3,3},{4,8},{5,9},{6,10},{7,11},{8,4},{9,5},{10,... | collective-permute-start | bytes 196616 | tf_op jit(solution)/shard_map/ppermute | solution.py:516
  9.3 0.8 %copy-done.3 = bf16[384,84]{0,1:T(8,128)(2,1)S(1)} copy-done((bf16[384,84]{0,1:T(8,128)(2,1)S(1)}, bf16[384,84]{0,1:T(8,128)(2,1)}, u32[]{:S(2)}) %copy-start.3) | copy-done | bytes 64536
  10.3 0.6 %copy-done.8 = f32[200]{0:T(256)S(1)} copy-done((f32[200]{0:T(256)S(1)}, f32[200]{0:T(256)}, u32[]{:S(2)}) %copy-start.8) | copy-done | bytes 824
  11.1 0.6 %copy-done.7 = f32[384]{0:T(512)S(1)} copy-done((f32[384]{0:T(512)S(1)}, f32[384]{0:T(512)}, u32[]{:S(2)}) %copy-start.7) | copy-done | bytes 1560
  12.2 2.4 %collective-permute-start.6 = (bf16[592,128]{1,0:T(8,128)(2,1)S(1)}, bf16[592,128]{1,0:T(8,128)(2,1)S(1)}, u32[]{:S(2)}, u32[]{:S(2)}) collective-permute-start(bf16[592,128]{1,0:T(8,128)(2,1)S(1)} %constant_dynamic-update-slice_fusion), channel_id=1, source_target_pairs={{0,3},{1,0},{2,1},{3,2},{4,7},{5,4},{6,5},{7,6},{8,11},{9,8},{10,9... | collective-permute-start | bytes 454664 | tf_op jit(solution)/shard_map/ppermute | solution.py:516
  15.1 0.9 %copy-done.2 = bf16[80,9,200]{2,0,1:T(8,128)(2,1)S(1)} copy-done((bf16[80,9,200]{2,0,1:T(8,128)(2,1)S(1)}, bf16[80,9,200]{2,0,1:T(8,128)(2,1)}, u32[]{:S(2)}) %copy-start.2) | copy-done | bytes 288024
  16.0 0.3 copy.30
  16.5 0.3 reshape.53.refs_17_.refs_18_
  16.8 1.7 %collective-permute-done.6.refs_10_ = bf16[592,128]{1,0:T(8,128)(2,1)S(1)} collective-permute-done((bf16[592,128]{1,0:T(8,128)(2,1)S(1)}, bf16[592,128]{1,0:T(8,128)(2,1)S(1)}, u32[]{:S(2)}, u32[]{:S(2)}) %collective-permute-start.6) | collective-permute-done | bytes 151584 | tf_op jit(solution)/shard_map/ppermute | solution.py:516
  18.5 8.9 %first_step.1 = (bf16[16,80,128]{2,1,0:T(8,128)(2,1)S(1)}, bf16[4,16,128]{2,1,0:T(8,128)(2,1)S(1)}, bf16[80,128]{1,0:T(8,128)(2,1)S(1)}, bf16[240,128]{1,0:T(8,1...) custom-call(s32[4]{0:T(128)S(1)} %pad_add_fusion.flags.refs_0_, ...), custom_call_target="tpu_custom_call" | custom-call | tf_op jit(solution)/shard_map/first_step/pallas_call | solution.py:637
  27.6 1.9 %collective-permute-start.8 = (bf16[4,16,128]{2,1,0:T(8,128)(2,1)S(1)}, bf16[4,16,128]{2,1,0:T(8,128)(2,1)S(1)}, u32[]{:S(2)}, u32[]{:S(2)}) collective-permute-start(bf16[4,16,128]{2,1,0:T(8,128)(2,1)S(1)} %get-tuple-element.21), channel_id=1, source_target_pairs={{0,16},{1,17},{2,18},{3,19},{4,20},{5,21},{6,22},{7,23},{8,24},{9,... | collective-permute-start | bytes 49160 | tf_op jit(solution)/shard_map/ppermute | solution.py:516
  29.5 0.7 %collective-permute-start.10 = (bf16[240,128]{1,0:T(8,128)(2,1)S(1)}, bf16[240,128]{1,0:T(8,128)(2,1)S(1)}, u32[]{:S(2)}, u32[]{:S(2)}) collective-permute-start(bf16[240,128]{1,0:T(8,128)(2,1)S(1)} %get-tuple-element.22), channel_id=1, source_target_pairs={{0,4},{1,5},{2,6},{3,7},{4,0},{5,1},{6,2},{7,3},{8,12},{9,13},{10,... | collective-permute-start | bytes 184328 | tf_op jit(solution)/shard_map/ppermute | solution.py:516
  30.1 2.6 %collective-permute-start.11 = (bf16[240,128]{1,0:T(8,128)(2,1)S(1)}, bf16[240,128]{1,0:T(8,128)(2,1)S(1)}, u32[]{:S(2)}, u32[]{:S(2)}) collective-permute-start(bf16[240,128]{1,0:T(8,128)(2,1)S(1)} %get-tuple-element.23), channel_id=1, source_target_pairs={{0,0},{1,1},{2,2},{3,3},{4,8},{5,9},{6,10},{7,11},{8,4},{9,5},{10,... | collective-permute-start | bytes 184328 | tf_op jit(solution)/shard_map/ppermute | solution.py:516
  32.9 2.3 %collective-permute-done.11.refs_7_ = bf16[240,128]{1,0:T(8,128)(2,1)S(1)} collective-permute-done((bf16[240,128]{1,0:T(8,128)(2,1)S(1)}, bf16[240,128]{1,0:T(8,128)(2,1)S(1)}, u32[]{:S(2)}, u32[]{:S(2)}) %collective-permute-start.11) | collective-permute-done | bytes 61472 | tf_op jit(solution)/shard_map/ppermute | solution.py:516
  35.2 3.2 %collective-permute-start.13 = (bf16[432,128]{1,0:T(8,128)(2,1)S(1)}, bf16[432,128]{1,0:T(8,128)(2,1)S(1)}, u32[]{:S(2)}, u32[]{:S(2)}) collective-permute-start(bf16[432,128]{1,0:T(8,128)(2,1)S(1)} %constant_dynamic-update-slice_fusion.9), channel_id=1, source_target_pairs={{0,3},{1,0},{2,1},{3,2},{4,7},{5,4},{6,5},{7,6},{8,11},{9,8},{10,9... | collective-permute-start | bytes 331784 | tf_op jit(solution)/shard_map/ppermute | solution.py:516
  38.5 1.2 %collective-permute-start.12 = (bf16[432,128]{1,0:T(8,128)(2,1)S(1)}, bf16[432,128]{1,0:T(8,128)(2,1)S(1)}, u32[]{:S(2)}, u32[]{:S(2)}) collective-permute-start(bf16[432,128]{1,0:T(8,128)(2,1)S(1)} %constant_dynamic-update-slice_fusion.9), channel_id=1, source_target_pairs={{0,1},{1,2},{2,3},{3,0},{4,5},{5,6},{6,7},{7,4},{8,9},{9,10},{10,1... | collective-permute-start | bytes 331784 | tf_op jit(solution)/shard_map/ppermute | solution.py:516
  39.6 3.9 %collective-permute-done.13.refs_10_ = bf16[432,128]{1,0:T(8,128)(2,1)S(1)} collective-permute-done((bf16[432,128]{1,0:T(8,128)(2,1)S(1)}, bf16[432,128]{1,0:T(8,128)(2,1)S(1)}, u32[]{:S(2)}, u32[]{:S(2)}) %collective-permute-start.13) | collective-permute-done | bytes 110624 | tf_op jit(solution)/shard_map/ppermute | solution.py:516
  43.5 8.5 %second_step.1 = bf16[16,80,128]{2,1,0:T(8,128)(2,1)S(1)} custom-call(s32[4]{0:T(128)S(1)} %pad_add_fusion.flags.refs_0_, bf16[16,80,128]{2,1,0:T(8,128)(2,1)S(1)} %get-tuple-element.20.refs_1_, f32[16,128]{1,0:T(8,128)S(1)} %convert_element_type.40.refs_2_, bf16[4,16,128]{2,1,0:T(8,128)(2,1)S(1)} %collective-permute-done.7.refs_3_, ...), custom_call_target="tpu_custom_call" | custom-call | tf_op jit(solution)/shard_map/second_step/pallas_call | solution.py:648
  52.0 0.8 %copy.26 = bf16[1,80,16,128]{3,2,1,0:T(8,128)(2,1)} copy(bf16[1,80,16,128]{3,1,2,0:T(8,128)(2,1)S(1)} %bitcast.44) | data formatting | bytes 655360 | tf_op jit(solution)/shard_map/broadcast_in_dim | solution.py:657
  (67 shorter events, 2.2 us)
Async XLA Ops:
  0.0 0.8 %copy-start.4 = (f32[1,4,16,128]{3,2,1,0:T(8,128)S(1)}, f32[1,4,16,128]{3,2,1,0:T(8,128)}, u32[]{:S(2)}) copy-start(f32[1,4,16,128]{3,2,1,0:T(8,128)} %param.14) | copy-start | bytes 98308
  0.8 1.1 %copy-start.6 = (f32[2,4,80]{2,1,0:T(4,128)S(1)}, f32[2,4,80]{2,1,0:T(4,128)}, u32[]{:S(2)}) copy-start(f32[2,4,80]{2,1,0:T(4,128)} %param.15) | copy-start | bytes 7684
  0.8 1.1 %copy-start.5 = (s32[16,128]{1,0:T(8,128)S(1)}, s32[16,128]{1,0:T(8,128)}, u32[]{:S(2)}) copy-start(s32[16,128]{1,0:T(8,128)} %param.12) | copy-start | bytes 24580
  1.9 7.3 %copy-start.1 = (bf16[200,9,84]{0,2,1:T(8,128)(2,1)S(1)}, bf16[200,9,84]{0,2,1:T(8,128)(2,1)}, u32[]{:S(2)}) copy-start(bf16[200,9,84]{0,2,1:T(8,128)(2,1)} %param.19) | copy-start | bytes 907204
  3.0 8.8 %collective-permute-start = (bf16[4,16,128]{2,1,0:T(8,128)(2,1)S(1)}, bf16[4,16,128]{2,1,0:T(8,128)(2,1)S(1)}, u32[]{:S(2)}, u32[]{:S(2)}) collective-permute-start(bf16[4,16,128]{2,1,0:T(8,128)(2,1)S(1)} %get-tuple-element.16), channel_id=1, source_target_pairs={{0,20},{1,21},{2,22},{3,23},{4,16},{5,17},{6,18},{7,19},{8,28},{9,... | collective-permute-start | bytes 49160 | tf_op jit(solution)/shard_map/ppermute | solution.py:516
  3.2 8.6 %collective-permute-start.2 = (bf16[4,16,128]{2,1,0:T(8,128)(2,1)S(1)}, bf16[4,16,128]{2,1,0:T(8,128)(2,1)S(1)}, u32[]{:S(2)}, u32[]{:S(2)}) collective-permute-start(bf16[4,16,128]{2,1,0:T(8,128)(2,1)S(1)} %get-tuple-element.16), channel_id=1, source_target_pairs={{0,16},{1,17},{2,18},{3,19},{4,24},{5,25},{6,26},{7,27},{8,20},{9,... | collective-permute-start | bytes 49160 | tf_op jit(solution)/shard_map/ppermute | solution.py:516
  6.6 5.2 %collective-permute-start.1 = (bf16[4,16,128]{2,1,0:T(8,128)(2,1)S(1)}, bf16[4,16,128]{2,1,0:T(8,128)(2,1)S(1)}, u32[]{:S(2)}, u32[]{:S(2)}) collective-permute-start(bf16[4,16,128]{2,1,0:T(8,128)(2,1)S(1)} %get-tuple-element.16), channel_id=1, source_target_pairs={{0,16},{1,17},{2,18},{3,19},{4,20},{5,21},{6,22},{7,23},{8,24},{9,... | collective-permute-start | bytes 49160 | tf_op jit(solution)/shard_map/ppermute | solution.py:516
  6.8 5.0 %collective-permute-start.3 = (bf16[256,128]{1,0:T(8,128)(2,1)S(1)}, bf16[256,128]{1,0:T(8,128)(2,1)S(1)}, u32[]{:S(2)}, u32[]{:S(2)}) collective-permute-start(bf16[256,128]{1,0:T(8,128)(2,1)S(1)} %get-tuple-element.17), channel_id=1, source_target_pairs={{0,4},{1,5},{2,6},{3,7},{4,0},{5,1},{6,2},{7,3},{8,12},{9,13},{10,... | collective-permute-start | bytes 196616 | tf_op jit(solution)/shard_map/ppermute | solution.py:516
  6.8 5.3 %collective-permute-start.4 = (bf16[256,128]{1,0:T(8,128)(2,1)S(1)}, bf16[256,128]{1,0:T(8,128)(2,1)S(1)}, u32[]{:S(2)}, u32[]{:S(2)}) collective-permute-start(bf16[256,128]{1,0:T(8,128)(2,1)S(1)} %get-tuple-element.18), channel_id=1, source_target_pairs={{0,0},{1,1},{2,2},{3,3},{4,8},{5,9},{6,10},{7,11},{8,4},{9,5},{10,... | collective-permute-start | bytes 196616 | tf_op jit(solution)/shard_map/ppermute | solution.py:516
  9.2 0.9 %copy-start.3 = (bf16[384,84]{0,1:T(8,128)(2,1)S(1)}, bf16[384,84]{0,1:T(8,128)(2,1)}, u32[]{:S(2)}) copy-start(bf16[384,84]{0,1:T(8,128)(2,1)} %param.16) | copy-start | bytes 193540
  10.2 0.7 %copy-start.8 = (f32[200]{0:T(256)S(1)}, f32[200]{0:T(256)}, u32[]{:S(2)}) copy-start(f32[200]{0:T(256)} %param.20) | copy-start | bytes 2404
  10.9 0.7 %copy-start.7 = (f32[384]{0:T(512)S(1)}, f32[384]{0:T(512)}, u32[]{:S(2)}) copy-start(f32[384]{0:T(512)} %param.17) | copy-start | bytes 4612
  12.2 6.3 %collective-permute-start.6 = (bf16[592,128]{1,0:T(8,128)(2,1)S(1)}, bf16[592,128]{1,0:T(8,128)(2,1)S(1)}, u32[]{:S(2)}, u32[]{:S(2)}) collective-permute-start(bf16[592,128]{1,0:T(8,128)(2,1)S(1)} %constant_dynamic-update-slice_fusion), channel_id=1, source_target_pairs={{0,3},{1,0},{2,1},{3,2},{4,7},{5,4},{6,5},{7,6},{8,11},{9,8},{10,9... | collective-permute-start | bytes 454664 | tf_op jit(solution)/shard_map/ppermute | solution.py:516
  14.6 3.9 %collective-permute-start.5 = (bf16[592,128]{1,0:T(8,128)(2,1)S(1)}, bf16[592,128]{1,0:T(8,128)(2,1)S(1)}, u32[]{:S(2)}, u32[]{:S(2)}) collective-permute-start(bf16[592,128]{1,0:T(8,128)(2,1)S(1)} %constant_dynamic-update-slice_fusion), channel_id=1, source_target_pairs={{0,1},{1,2},{2,3},{3,0},{4,5},{5,6},{6,7},{7,4},{8,9},{9,10},{10,1... | collective-permute-start | bytes 454664 | tf_op jit(solution)/shard_map/ppermute | solution.py:516
  15.0 1.0 %copy-start.2 = (bf16[80,9,200]{2,0,1:T(8,128)(2,1)S(1)}, bf16[80,9,200]{2,0,1:T(8,128)(2,1)}, u32[]{:S(2)}) copy-start(bf16[80,9,200]{2,0,1:T(8,128)(2,1)} %param.21) | copy-start | bytes 864004
  16.5 2.0 %copy-start = (bf16[80,384]{1,0:T(8,128)(2,1)S(1)}, bf16[80,384]{1,0:T(8,128)(2,1)}, u32[]{:S(2)}) copy-start(bf16[80,384]{1,0:T(8,128)(2,1)} %refs_15_.1) | copy-start | bytes 184324
  27.4 5.4 %collective-permute-start.7 = (bf16[4,16,128]{2,1,0:T(8,128)(2,1)S(1)}, bf16[4,16,128]{2,1,0:T(8,128)(2,1)S(1)}, u32[]{:S(2)}, u32[]{:S(2)}) collective-permute-start(bf16[4,16,128]{2,1,0:T(8,128)(2,1)S(1)} %get-tuple-element.21), channel_id=1, source_target_pairs={{0,20},{1,21},{2,22},{3,23},{4,16},{5,17},{6,18},{7,19},{8,28},{9,... | collective-permute-start | bytes 49160 | tf_op jit(solution)/shard_map/ppermute | solution.py:516
  27.5 5.4 %collective-permute-start.9 = (bf16[4,16,128]{2,1,0:T(8,128)(2,1)S(1)}, bf16[4,16,128]{2,1,0:T(8,128)(2,1)S(1)}, u32[]{:S(2)}, u32[]{:S(2)}) collective-permute-start(bf16[4,16,128]{2,1,0:T(8,128)(2,1)S(1)} %get-tuple-element.21), channel_id=1, source_target_pairs={{0,16},{1,17},{2,18},{3,19},{4,24},{5,25},{6,26},{7,27},{8,20},{9,... | collective-permute-start | bytes 49160 | tf_op jit(solution)/shard_map/ppermute | solution.py:516
  27.6 5.3 %collective-permute-start.8 = (bf16[4,16,128]{2,1,0:T(8,128)(2,1)S(1)}, bf16[4,16,128]{2,1,0:T(8,128)(2,1)S(1)}, u32[]{:S(2)}, u32[]{:S(2)}) collective-permute-start(bf16[4,16,128]{2,1,0:T(8,128)(2,1)S(1)} %get-tuple-element.21), channel_id=1, source_target_pairs={{0,16},{1,17},{2,18},{3,19},{4,20},{5,21},{6,22},{7,23},{8,24},{9,... | collective-permute-start | bytes 49160 | tf_op jit(solution)/shard_map/ppermute | solution.py:516
  29.5 3.4 %collective-permute-start.10 = (bf16[240,128]{1,0:T(8,128)(2,1)S(1)}, bf16[240,128]{1,0:T(8,128)(2,1)S(1)}, u32[]{:S(2)}, u32[]{:S(2)}) collective-permute-start(bf16[240,128]{1,0:T(8,128)(2,1)S(1)} %get-tuple-element.22), channel_id=1, source_target_pairs={{0,4},{1,5},{2,6},{3,7},{4,0},{5,1},{6,2},{7,3},{8,12},{9,13},{10,... | collective-permute-start | bytes 184328 | tf_op jit(solution)/shard_map/ppermute | solution.py:516
  30.1 5.1 %collective-permute-start.11 = (bf16[240,128]{1,0:T(8,128)(2,1)S(1)}, bf16[240,128]{1,0:T(8,128)(2,1)S(1)}, u32[]{:S(2)}, u32[]{:S(2)}) collective-permute-start(bf16[240,128]{1,0:T(8,128)(2,1)S(1)} %get-tuple-element.23), channel_id=1, source_target_pairs={{0,0},{1,1},{2,2},{3,3},{4,8},{5,9},{6,10},{7,11},{8,4},{9,5},{10,... | collective-permute-start | bytes 184328 | tf_op jit(solution)/shard_map/ppermute | solution.py:516
  35.2 8.3 %collective-permute-start.13 = (bf16[432,128]{1,0:T(8,128)(2,1)S(1)}, bf16[432,128]{1,0:T(8,128)(2,1)S(1)}, u32[]{:S(2)}, u32[]{:S(2)}) collective-permute-start(bf16[432,128]{1,0:T(8,128)(2,1)S(1)} %constant_dynamic-update-slice_fusion.9), channel_id=1, source_target_pairs={{0,3},{1,0},{2,1},{3,2},{4,7},{5,4},{6,5},{7,6},{8,11},{9,8},{10,9... | collective-permute-start | bytes 331784 | tf_op jit(solution)/shard_map/ppermute | solution.py:516
  38.5 5.0 %collective-permute-start.12 = (bf16[432,128]{1,0:T(8,128)(2,1)S(1)}, bf16[432,128]{1,0:T(8,128)(2,1)S(1)}, u32[]{:S(2)}, u32[]{:S(2)}) collective-permute-start(bf16[432,128]{1,0:T(8,128)(2,1)S(1)} %constant_dynamic-update-slice_fusion.9), channel_id=1, source_target_pairs={{0,1},{1,2},{2,3},{3,0},{4,5},{5,6},{6,7},{7,4},{8,9},{9,10},{10,1... | collective-permute-start | bytes 331784 | tf_op jit(solution)/shard_map/ppermute | solution.py:516

commit v3 on v2

v3 whole, which is shorter than its diff:
```python
import functools

import jax
import jax.numpy as jnp
from jax import lax
from jax.experimental import pallas as pl
from jax.experimental.pallas import tpu as pltpu
from jax.sharding import PartitionSpec as P

CH = 80
NS = 4
NK = 4
HA = 384
HW = 8
SPAN = 2 * HW + 1
HIDK = 208
HIDP = 256
F32 = jnp.float32
BF16 = jnp.bfloat16


def roll(x, shift, axis=1):
    size = x.shape[axis]
    if isinstance(shift, int):
        shift = shift % size
        if shift == 0:
            return x
    return pltpu.roll(x, shift, axis)


def lanes(shape):
    return lax.broadcasted_iota(jnp.int32, shape, len(shape) - 1)


def subs(shape):
    return lax.broadcasted_iota(jnp.int32, shape, len(shape) - 2)


class Dims:
    def __init__(self, rows):
        self.rows = rows
        self.block = 32 if rows + 4 <= 32 else 64
        self.edge = 4 * self.block
        self.pieces = self.edge // 128
        self.edge_rows = CH * self.pieces
        self.tiles = -(-(rows + 4) // 8)
        self.tall = 8 * self.tiles
        self.strip = 2 * CH + self.edge_rows


def put_edges(ref, at, edges, d):
    for piece in range(d.pieces):
        ref[at + piece * CH : at + (piece + 1) * CH, :] = edges[:, piece * 128 : (piece + 1) * 128]


def get_edges(ref, at, d):
    return jnp.concatenate(
        [ref[at + piece * CH : at + (piece + 1) * CH, :] for piece in range(d.pieces)], axis=1
    )


def edge_columns(state, d):
    lane = lanes((1, d.edge))
    block = lane // d.block
    row = lane % d.block - 2
    column = jnp.where(block == 0, 126, jnp.where(block == 1, 0, jnp.where(block == 2, 127, 1)))
    own = (row >= 0) & (row < d.rows)
    target = jnp.where(own, column, -1)
    position = subs((128, d.edge))
    places = [
        (position == jnp.where(row == step, target, -1)).astype(F32).astype(BF16)
        for step in range(d.rows)
    ]
    whole = jnp.concatenate([state[step] for step in range(d.rows)], axis=1)
    total = jnp.dot(whole, jnp.concatenate(places, axis=0), preferred_element_type=F32)
    return total.astype(BF16)


def loop(count, unroll, body):
    while count % unroll:
        unroll -= 1

    def several(step, carry):
        for offset in range(unroll):
            body(step * unroll + offset)
        return carry

    lax.fori_loop(0, count // unroll, several, 0)


def strips(one, two, even, d):
    last = d.rows - 2
    return (one, jnp.where(even, last, 0)), (two, jnp.where(even, 0, last))


def split_bf16(values):
    high = values.astype(BF16).astype(F32)
    mid = (values - high).astype(BF16).astype(F32)
    return high, mid, values - high - mid


def emit(state, surface, wet, flags, fields, own_edges, one, two, raw, d):
    half = d.rows // 2
    is_ocean, even = flags[0] != 0, flags[3] == 0
    gap = jnp.zeros((4, CH), F32)
    terms = []
    for term in split_bf16(surface[flags[0]]):
        terms += [term, gap]
    proj = jnp.concatenate(terms + [gap, gap], axis=0).astype(BF16)
    for step in range(half):
        pair = jnp.concatenate([state[step], state[step + half]], axis=1)
        parts = jnp.dot(proj, pair, preferred_element_type=F32)
        whole = parts[0:8] + parts[8:16] + parts[16:24]
        raw[step * 8 : step * 8 + 8, :] = whole[:, :128]
        raw[(step + half) * 8 : (step + half) * 8 + 8, :] = whole[:, 128:]
    keeping = jnp.where(is_ocean, wet[...].astype(F32), 1.0)
    for field in range(NS):
        fields[field] = (raw[pl.ds(field, d.rows, stride=8), :] * keeping).astype(BF16)
    edges = edge_columns(state, d)
    put_edges(own_edges, 0, edges, d)
    for ref, first in strips(one, two, even, d):
        ref[0:CH, :] = state[first]
        ref[CH : 2 * CH, :] = state[first + 1]
        put_edges(ref, 2 * CH, edges, d)


def start_kernel(
    d, flags, given, offsets, weights, surface, wet, state, planes, fields, own_edges, one, two,
    raw, tall, turned,
):
    rows = d.rows
    turned[...] = given[...].astype(F32).reshape(CH * rows, 128)
    for row in range(rows):
        state[row] = turned[pl.ds(row, CH, stride=rows), :].astype(BF16)
    emit(state, surface, wet, flags, fields, own_edges, one, two, raw, d)
    for k in range(NK):
        code = (offsets[0, k] * SPAN + offsets[1, k]).astype(F32)
        tall[k * rows : (k + 1) * rows, :] = code
        tall[(NK + k) * rows : (NK + k + 1) * rows, :] = weights[k]
        planes[k] = code.astype(BF16)
        planes[NK + k] = weights[k].astype(BF16)
    for ref, first in strips(one, two, flags[3] == 0, d):
        strip = [tall[pl.ds(first + step, 2 * NK, stride=rows), :] for step in range(2)]
        ref[d.strip : d.strip + 16, :] = jnp.concatenate(strip, axis=0).astype(BF16)


def decode(code):
    shifted = code.astype(jnp.int32) + (HW * SPAN + HW)
    rows = lax.shift_right_logical(shifted * 241, 12)
    return rows - HW, shifted - rows * SPAN - HW


def along_lanes(values, index):
    numbers = lax.GatherDimensionNumbers(
        offset_dims=(),
        collapsed_slice_dims=(1,),
        start_index_map=(1,),
        operand_batching_dims=(0,),
        start_indices_batching_dims=(0,),
    )
    return lax.gather(
        values, index[..., None], numbers, (1, 1), mode=lax.GatherScatterMode.PROMISE_IN_BOUNDS
    )


def select_rows(sources, start, picks):
    chosen = [[jnp.zeros((8, 128), F32) for _ in range(NS)] for _ in picks]
    for shift in range(-HW, HW + 1):
        at = pl.ds(start + shift, 8)
        used = [any(pick[2][index] is not None for pick in picks) for index in range(len(sources))]
        values = [
            [source[field, at, :] for field in range(NS)] if use else None
            for source, use in zip(sources, used)
        ]
        for slot, (rows, index, allowed) in enumerate(picks):
            here = rows == shift
            for source, within in enumerate(allowed):
                if within is None:
                    continue
                mask = here & within
                for field in range(NS):
                    picked = along_lanes(values[source][field], index)
                    chosen[slot][field] = jnp.where(mask, picked, chosen[slot][field])
    return chosen


def regrid_inside(fields_x, plan_x, part_x, first, tiles, tall):
    lane = lanes((8, 128))
    for step in range(tiles):
        at = first + step * 8
        picks = []
        weights = []
        for k in range(NK):
            rows, cols = decode(plan_x[pl.ds(k * tall + at, 8), :])
            weights.append(plan_x[pl.ds((NK + k) * tall + at, 8), :])
            column = lane + cols
            picks.append((rows, column & 127, ((column >= 0) & (column < 128),)))
        chosen = select_rows((fields_x,), at + 14, picks)
        for field in range(NS):
            total = chosen[0][field] * weights[0]
            for k in range(1, NK):
                total = total + chosen[k][field] * weights[k]
            part_x[pl.ds(field * tall + at, 8), :] = total


def regrid_beside(
    fields_x, fields_y, plan_x, plan_y, part_x, forcing_x, forcing_y, first, tiles, tall, sides
):
    lane = lanes((8, 128))
    part = ((lane + 8) & 127) // 32
    place = ((lane + 8) & 31) - 8
    outer = place >= 8
    inner_column = place & 127
    outer_column = jnp.where(place < 16, place - 16, place + 112)
    edge = (lane < 8) | (lane >= 120)
    for step in range(tiles):
        at = first + step * 8
        code = jnp.zeros((8, 128), F32)
        weight = jnp.zeros((8, 128), F32)
        for k in range(NK):
            edge_code = roll(plan_x[pl.ds(k * tall + at, 8), :], 32 * k)
            edge_weight = roll(plan_x[pl.ds((NK + k) * tall + at, 8), :], 32 * k)
            if sides:
                edge_code = jnp.where(
                    outer, roll(plan_y[pl.ds(k * tall + at, 8), :], 32 * k + 16), edge_code
                )
                edge_weight = jnp.where(
                    outer, roll(plan_y[pl.ds((NK + k) * tall + at, 8), :], 32 * k + 16), edge_weight
                )
            code = jnp.where(part == k, edge_code, code)
            weight = jnp.where(part == k, edge_weight, weight)
        rows, cols = decode(code)
        column = jnp.where(outer, outer_column, inner_column) + cols
        within = (column >= 0) & (column < 128)
        picks = [(rows, column & 127, (within & outer if sides else None, jnp.logical_not(within)))]
        (chosen,) = select_rows((fields_x, fields_y), at + 14, picks)
        for field in range(NS):
            part_sum = chosen[field] * weight
            extra = part_sum
            for k in range(1, NK):
                extra = extra + roll(part_sum, -32 * k)
            total = part_x[pl.ds(field * tall + at, 8), :] + jnp.where(edge, extra, 0.0)
            forcing_x[pl.ds(at * 8 + field, 8, stride=8), :] = total
            forcing_x[pl.ds(at * 8 + field + 4, 8, stride=8), :] = total
            if sides:
                extra = roll(extra, -16)
                forcing_y[pl.ds(at * 8 + field, 8, stride=8), :] = extra
                forcing_y[pl.ds(at * 8 + field + 4, 8, stride=8), :] = extra


def place_columns(left, right):
    return jnp.where(lanes(left.shape) < 64, right.astype(F32), left.astype(F32))


def gelu(x):
    scale = (2 / jnp.pi) ** 0.5
    half = 0.5 * x
    return half + half * jnp.tanh(x * (scale + (scale * 0.044715) * (x * x)))


def air(state, out, forcing_x, air_in, atm_out, d):
    half = d.rows // 2
    first = subs((8, 128)) < 4
    blank = jnp.zeros((32, 128), BF16)

    def inputs(row):
        at = (row + 2) * 8
        forced = jnp.where(first, forcing_x[at : at + 8, :], 1.0)
        forced = jnp.concatenate([forced, jnp.zeros_like(forced)], axis=0).astype(BF16)
        return jnp.concatenate([state[row], forced, blank], axis=0)

    for step in range(half):
        pair = jnp.concatenate([inputs(step), inputs(step + half)], axis=1)
        hidden = gelu(jnp.dot(air_in[...], pair, preferred_element_type=F32)).astype(BF16)
        update = jnp.dot(atm_out[...], hidden, preferred_element_type=F32)
        for offset in range(2):
            row = step + offset * half
            change = update[:, offset * 128 : (offset + 1) * 128]
            out(row, state[row].astype(F32) + change)


def edge_forcing(forcing_x, forcing_y, d):
    lane = lanes((8, d.edge))
    block = lane // d.block
    row = lane % d.block

    inner = outer = jnp.zeros((8, d.edge), F32)
    for step in range(d.rows + 4):
        at = pl.ds(step * 8, 8)
        pad = [jnp.zeros((8, 128), F32)] * (d.pieces - 1)
        here = jnp.concatenate([forcing_x[at, :]] + pad, axis=1)
        there = jnp.concatenate([forcing_y[at, :]] + pad, axis=1)
        for index, column in enumerate((126, 0, 127, 1)):
            shift = step + index * d.block - column
            match = (block == index) & (row == step)
            if column in (0, 127):
                inner = jnp.where(match, roll(here, shift), inner)
            outer = jnp.where(match, roll(there, shift), outer)
    return inner, outer


def roll_rows(state, upper, lower, rolled, d):
    def put(row, values):
        rolled[row, 0:CH, :] = roll(values, 1)
        rolled[row, CH : 2 * CH, :] = values
        rolled[row, 2 * CH : 3 * CH, :] = roll(values, -1)

    for step in range(2):
        put(step, upper[step * CH : (step + 1) * CH, :])
        put(d.rows + 2 + step, lower[step * CH : (step + 1) * CH, :])
    for row in range(d.rows):
        put(row + 2, state[row])


def sea(
    state, rolled, edges, left, right, out, forcing_x, forcing_y, ocn_in, ocn_out, wet,
    at_top, at_bottom, stack, hidden, side, d,
):
    rows, block = d.rows, d.block
    lane = lanes((CH, 128))
    spot = lanes((CH, d.edge))
    part = spot // block
    inner = edges
    outer = jnp.where((part == 0) | (part == 2), left, right)

    def sides_of(inner, outer, spot):
        first = spot < block
        return (
            jnp.where(first, outer, roll(inner, -block)),
            jnp.where(first, roll(outer, -2 * block), outer),
            jnp.where(first, roll(inner, -block), roll(outer, -2 * block)),
        )

    beside = sides_of(inner, outer, spot)
    middle = beside[1]
    force_in, force_out = edge_forcing(forcing_x, forcing_y, d)
    beside_forcing = sides_of(force_in, force_out, lanes((8, d.edge)))
    sub = subs((8, d.edge))
    ones = jnp.ones((8, d.edge), F32)
    forced = jnp.concatenate(
        [
            jnp.where(sub < 4, beside_forcing[0], beside_forcing[1]),
            jnp.where(sub < 4, beside_forcing[2], ones),
        ],
        axis=0,
    ).astype(BF16)
    columns = jnp.concatenate(list(beside) + [forced], axis=0)
    for tap in range(3):
        side[tap * 256 : (tap + 1) * 256, :] = roll(columns, -tap)

    sub_row = subs((8, 128))
    lane_row = lanes((8, 128))

    for row in range(rows + 4):
        entry = roll(middle, -row)[:, :128]
        stack[row, 0:CH, :] = jnp.where(lane == 0, entry, rolled[row, 0:CH, :])
        stack[row, CH : 2 * CH, :] = rolled[row, CH : 2 * CH, :]
        entry = roll(middle, 127 - block - row)[:, :128]
        stack[row, 2 * CH : 3 * CH, :] = jnp.where(lane == 127, entry, rolled[row, 2 * CH : 3 * CH, :])
        here, there = forcing_x[row * 8 : row * 8 + 8, :], forcing_y[row * 8 : row * 8 + 8, :]
        before = roll(jnp.where(lane_row == 127, there, here), 1)
        after = roll(jnp.where(lane_row == 0, there, here), -1)
        stack[row, 3 * CH : 256, :] = jnp.concatenate(
            [jnp.where(sub_row < 4, before, here), jnp.where(sub_row < 4, after, 1.0)], axis=0
        ).astype(BF16)

    pairs = (rows + 2) // 2

    for step in range(pairs):
        taps = jnp.concatenate(
            [
                stack[step : step + 3].reshape(3 * 256, 128),
                stack[step + pairs : step + pairs + 3].reshape(3 * 256, 128),
            ],
            axis=1,
        )
        active = gelu(jnp.dot(ocn_in[...], taps, preferred_element_type=F32))
        low, high = active[:, :128], active[:, 128:]
        if step == 0:
            low = jnp.where(at_top != 0, 0.0, low)
        if step == pairs - 1:
            high = jnp.where(at_bottom != 0, 0.0, high)
        hidden[step, 0:HIDK, :] = low.astype(BF16)
        hidden[step + pairs, 0:HIDK, :] = high.astype(BF16)
        blank = jnp.zeros((HIDP - HIDK, 128), BF16)
        hidden[step, HIDK:HIDP, :] = blank
        hidden[step + pairs, HIDK:HIDP, :] = blank

    product = jnp.dot(ocn_in[...], side[...], preferred_element_type=F32)
    spot = lanes((1, d.edge)) % block
    gone = ((spot == 0) & (at_top != 0)) | ((spot == rows + 1) & (at_bottom != 0))
    active = jnp.where(gone, 0.0, gelu(product)).astype(BF16)
    active = jnp.concatenate([active, jnp.zeros((HIDP - HIDK, d.edge), BF16)], axis=0)

    def taps_of(slices):
        total = None
        for tap, values in enumerate(slices):
            weights = ocn_out[tap * 3 * CH : (tap + 1) * 3 * CH, :]
            product = jnp.dot(weights, values, preferred_element_type=F32)
            total = product if total is None else total + product
        return total

    partial = taps_of([roll(active, -tap) for tap in range(3)])
    from_left, from_right = partial[0:CH], partial[2 * CH : 3 * CH]
    half = rows // 2
    for step in range(half):
        product = taps_of(
            [
                jnp.concatenate([hidden[step + tap], hidden[step + half + tap]], axis=1)
                for tap in range(3)
            ]
        )
        for offset in range(2):
            row = step + offset * half
            sums = product[:, offset * 128 : (offset + 1) * 128]
            entry = roll(from_left, -row)[:, :128]
            total = sums[CH : 2 * CH] + jnp.where(lane == 0, entry, roll(sums[0:CH], 1))
            entry = roll(from_right, 127 - block - row)[:, :128]
            total = total + jnp.where(lane == 127, entry, roll(sums[2 * CH : 3 * CH], -1))
            update = total * wet[row : row + 1, :].astype(F32)
            out(row, state[row].astype(F32) + update)


def join_rows(edge_up, edge_own, edge_down, d):
    row = lanes(edge_own.shape) % d.block
    above = roll(edge_up, -d.rows)
    below = roll(edge_down, d.rows)
    return jnp.where(row < 2, above, jnp.where(row < d.rows + 2, edge_own, below))


def prepare(atm_in, atm_bias, ocn_in, ocn_bias, ocn_out, air_in, first, second, is_ocean):
    def bias_rows(ref, width):
        row = ref[0:1, :]
        terms = list(split_bf16(row)) + [jnp.zeros_like(row)]
        bias = jnp.concatenate(terms, axis=0)
        return jnp.pad(bias, ((0, 0), (0, width - bias.shape[1])))

    @pl.when(is_ocean == 0)
    def _():
        columns = jnp.concatenate(
            [atm_in[...].astype(F32), bias_rows(atm_bias, HA), jnp.zeros((40, HA), F32)], axis=0
        )
        air_in[...] = columns.T.astype(BF16)

    @pl.when(is_ocean != 0)
    def _():
        bias = bias_rows(ocn_bias, 256)
        count = ocn_in.shape[2]
        for tap in range(3):
            whole = [ocn_in[3 * tap + side].astype(F32) for side in range(3)]
            whole = [jnp.pad(values, ((0, 0), (0, 256 - count))) for values in whole]
            rows = [values[:CH] for values in whole] + [values[CH:] for values in whole]
            rows.append(bias if tap == 0 else jnp.zeros((4, 256), F32))
            columns = jnp.concatenate(rows, axis=0).T
            first[:, tap * 256 : (tap + 1) * 256] = columns[:HIDK].astype(BF16)
        for tap in range(9):
            values = ocn_out[tap].astype(F32)
            second[tap * CH : (tap + 1) * CH, :] = jnp.pad(
                values, ((0, 0), (0, HIDP - count))
            ).astype(BF16)


def ends(flags):
    at_top, at_bottom, even = flags[1] != 0, flags[2] != 0, flags[3] == 0

    def up_and_down(one, two):
        above = jnp.where(even, two, one).astype(F32)
        below = jnp.where(even, one, two).astype(F32)
        return jnp.where(at_top, 0.0, above), jnp.where(at_bottom, 0.0, below)

    return up_and_down


def middle_kernel(d, opening, *refs):
    refs = list(refs)
    take = lambda count: [refs.pop(0) for _ in range(count)]
    flags, state, field_one, beside, field_two, from_one, from_two, own_edges = take(8)
    if opening:
        planes, *raw_weights = take(6)
    else:
        (plan_x,) = take(1)
    part_x, fields_x, rolled, edges = take(4)
    if opening:
        plan_x, *made_weights = take(4)
    rows, tall = d.rows, d.tall
    is_ocean = flags[0]
    up_and_down = ends(flags)

    if opening:

        @pl.when(is_ocean != 0)
        def _():
            base = d.strip
            pair = up_and_down(from_one[base : base + 16, :], from_two[base : base + 16, :])
            plan_x[...] = jnp.zeros_like(plan_x)
            for step, strip in zip((0, rows + 2), pair):
                for index in range(2):
                    plan_x[pl.ds(step + index, 2 * NK, stride=tall), :] = strip[index * 8 : (index + 1) * 8]

        for plane in range(2 * NK):
            plan_x[plane * tall + 2 : plane * tall + 2 + rows, :] = planes[plane].astype(F32)

    for field in range(NS):
        pair = up_and_down(field_one[field], field_two[field])
        fields_x[field, 0:16, :] = pair[0][rows - 16 : rows]
        fields_x[field, 16 : 16 + rows, :] = beside[field].astype(F32)
        fields_x[field, 16 + rows : 32 + rows, :] = pair[1][0:16]

    @pl.when(is_ocean == 0)
    def _():
        regrid_inside(fields_x, plan_x, part_x, 2, rows // 8, tall)

    @pl.when(is_ocean != 0)
    def _():
        regrid_inside(fields_x, plan_x, part_x, 0, d.tiles, tall)
        upper, lower = up_and_down(from_one[0 : 2 * CH, :], from_two[0 : 2 * CH, :])
        roll_rows(state, upper.astype(BF16), lower.astype(BF16), rolled, d)
        above, below = up_and_down(get_edges(from_one, 2 * CH, d), get_edges(from_two, 2 * CH, d))
        joined = join_rows(above.astype(BF16), get_edges(own_edges, 0, d), below.astype(BF16), d)
        put_edges(edges, 0, joined, d)

    if opening:
        prepare(*raw_weights, *made_weights, is_ocean)


def step_kernel(d, opening, closing, *refs):
    refs = list(refs)
    take = lambda count: [refs.pop(0) for _ in range(count)]
    flags, state, wet, from_left, from_right = take(5)
    part_x, fields_x, rolled, edges, plan_x, air_in, first, second, atm_out = take(9)
    if not opening:
        (plan_y,) = take(1)
    if not closing:
        (surface,) = take(1)
    (out,) = take(1)
    if not closing:
        fields, new_edges, one, two = take(4)
    if opening:
        (plan_y,) = take(1)
    fields_y, forcing_x, forcing_y, stack, hidden, side, raw = take(7)
    rows, tall = d.rows, d.tall
    is_ocean, at_top, at_bottom = flags[0], flags[1], flags[2]
    up_and_down = ends(flags)

    if opening:

        @pl.when(is_ocean != 0)
        def _():
            plan_y[...] = jnp.zeros_like(plan_y)
            side_base = 4 * (rows + 32) + 3 * d.edge_rows
            pair = [
                place_columns(from_left[at : at + 16, :], from_right[at : at + 16, :])
                for at in (side_base, side_base + 16 + 2 * NK * rows)
            ]
            for step, strip in zip((0, rows + 2), up_and_down(*pair)):
                for index in range(2):
                    plan_y[pl.ds(step + index, 2 * NK, stride=tall), :] = strip[index * 8 : (index + 1) * 8]
            for plane in range(2 * NK):
                at = side_base + 16 + plane * rows
                plan_y[plane * tall + 2 : plane * tall + 2 + rows, :] = place_columns(
                    from_left[at : at + rows, :], from_right[at : at + rows, :]
                )

    lower_at = 64 + 4 * rows
    for field in range(NS):
        start = 64 + field * rows
        fields_y[field, 16 : 16 + rows, :] = place_columns(
            from_left[start : start + rows, :], from_right[start : start + rows, :]
        )
        pair = [
            place_columns(from_left[at : at + 16, :], from_right[at : at + 16, :])
            for at in (field * 16, lower_at + field * 16)
        ]
        pair = up_and_down(*pair)
        fields_y[field, 0:16, :] = pair[0]
        fields_y[field, 16 + rows : 32 + rows, :] = pair[1]

    def put(row, values):
        if closing:
            raw[pl.ds(row, CH, stride=rows), :] = values
        else:
            out[row] = values.astype(BF16)

    @pl.when(is_ocean == 0)
    def _():
        regrid_beside(
            fields_x, fields_y, plan_x, plan_y, part_x, forcing_x, forcing_y, 2, rows // 8, tall, False
        )
        air(state, put, forcing_x, air_in, atm_out, d)

    @pl.when(is_ocean != 0)
    def _():
        regrid_beside(
            fields_x, fields_y, plan_x, plan_y, part_x, forcing_x, forcing_y, 0, d.tiles, tall, True
        )
        at = 4 * (rows + 32)
        size = d.edge_rows
        joined = []
        for ref in (from_left, from_right):
            one_edges, middle, two_edges = [get_edges(ref, at + index * size, d) for index in range(3)]
            above, below = up_and_down(one_edges, two_edges)
            joined.append(join_rows(above.astype(BF16), middle, below.astype(BF16), d))
        sea(
            state, rolled, get_edges(edges, 0, d), *joined, put, forcing_x, forcing_y,
            first, second, wet, at_top, at_bottom, stack, hidden, side, d,
        )

    if closing:
        out[...] = raw[...].reshape(CH, rows, 128).astype(BF16)
    else:
        emit(out, surface, wet, flags, fields, new_edges, one, two, raw, d)


VMEM = pl.BlockSpec(memory_space=pltpu.VMEM)
SMEM = pl.BlockSpec(memory_space=pltpu.SMEM)
PARAMS = pltpu.CompilerParams(vmem_limit_bytes=48 * 1024 * 1024)


def shape(*dims, dtype=BF16):
    return jax.ShapeDtypeStruct(dims, dtype)


def send(x, move):
    names = ("grp", "lat", "lon")
    sizes = [lax.axis_size(name) for name in names]
    pairs = []
    for group in range(sizes[0]):
        for lat in range(sizes[1]):
            for lon in range(sizes[2]):
                to = move(group, lat, lon)
                if to is None or not 0 <= to[1] < sizes[1]:
                    continue
                target = (to[0] * sizes[1] + to[1]) * sizes[2] + to[2] % sizes[2]
                pairs.append(((group * sizes[1] + lat) * sizes[2] + lon, target))
    return lax.ppermute(x, names, pairs)


def swap_rows(x, turn, across):
    count = lax.axis_size("lat")

    def move(group, lat, lon):
        other = ((lat + turn) ^ 1) - turn
        to = 1 - group if across else group
        return to, other if 0 <= other < count else lat, lon

    return send(x, move)


def exchange(fields, own_edges, one, two, planes, d):
    rows = d.rows
    beside = send(fields, lambda g, i, j: (1 - g, i, j))
    field_one = swap_rows(fields, 0, True)
    field_two = swap_rows(fields, 1, True)
    from_one = swap_rows(one, 0, False)
    from_two = swap_rows(two, 1, False)
    edge_at = slice(2 * CH, d.strip)
    odd = lax.axis_index("lat") % 2
    if rows == 16:
        outer = [field_one, field_two]
    else:
        last = [field[:, rows - 16 :] for field in (field_one, field_two)]
        first = [field[:, :16] for field in (field_one, field_two)]
        outer = [jnp.where(odd == 1, last[0], first[0]), jnp.where(odd == 1, first[1], last[1])]
    packed = [
        outer[0].reshape(64, 128),
        beside.reshape(4 * rows, 128),
        outer[1].reshape(64, 128),
        from_one[edge_at],
        own_edges,
        from_two[edge_at],
    ]
    if planes is not None:
        packed += [from_one[d.strip :], planes.reshape(2 * NK * rows, 128), from_two[d.strip :]]
    packed = jnp.concatenate(packed, axis=0)
    from_left = send(packed, lambda g, i, j: (g, i, j + 1))
    from_right = send(packed, lambda g, i, j: (g, i, j - 1))
    return (field_one, beside, field_two, from_one, from_two), (from_left, from_right)


def local(
    coupled_state, land_mask, regrid_offsets, regrid_weights, surface_proj,
    atm_in, atm_bias, atm_out, ocn_in, ocn_bias, ocn_out,
):
    rows = coupled_state.shape[2]
    assert coupled_state.shape[3] == 128
    d = Dims(rows)
    group = lax.axis_index("grp")
    lat = lax.axis_index("lat")
    flags = jnp.stack(
        [group, lat == 0, lat == lax.axis_size("lat") - 1, lat % 2]
    ).astype(jnp.int32)
    raw_weights = (
        atm_in.T,
        atm_bias[None],
        jnp.transpose(ocn_in, (1, 2, 0)),
        ocn_bias[None],
        jnp.transpose(ocn_out, (1, 0, 2)),
    )
    state_shape = shape(rows, CH, 128)
    emitted = [
        shape(NS, rows, 128),
        shape(d.edge_rows, 128),
        shape(d.strip, 128),
        shape(d.strip, 128),
    ]
    raw = pltpu.VMEM((rows * 8, 128), F32)
    turned = pltpu.VMEM((CH * rows, 128), F32)

    def call(kernel, operands, outs, scratch, name):
        return pl.pallas_call(
            kernel,
            out_shape=outs,
            in_specs=[SMEM] + [VMEM] * len(operands),
            out_specs=[VMEM] * len(outs),
            scratch_shapes=scratch,
            compiler_params=PARAMS,
            name=name,
        )(flags, *operands)

    state, planes, fields, edges, one, two = call(
        functools.partial(start_kernel, d),
        (coupled_state[0], regrid_offsets[0], regrid_weights[0], surface_proj, land_mask),
        [state_shape, shape(2 * NK, rows, 128)] + emitted[:2] + [shape(d.strip + 16, 128)] * 2,
        [raw, pltpu.VMEM((2 * NK * rows, 128), F32), turned],
        "start",
    )

    plan = shape(2 * NK * d.tall, 128, dtype=F32)
    between = [
        shape(NS * d.tall, 128, dtype=F32),
        shape(NS, rows + 32, 128, dtype=F32),
        shape(rows + 4, 3 * CH, 128),
        shape(d.edge_rows, 128),
    ]
    made = [shape(HA, 128), shape(HIDK, 768), shape(9 * CH, HIDP)]
    scratch = [
        pltpu.VMEM((NS, rows + 32, 128), F32),
        pltpu.VMEM((d.tall * 8, 128), F32),
        pltpu.VMEM((d.tall * 8, 128), F32),
        pltpu.VMEM((rows + 4, 256, 128), BF16),
        pltpu.VMEM((rows + 2, HIDP, 128), BF16),
        pltpu.VMEM((768, d.edge), BF16),
    ]

    vertical, horizontal = exchange(fields, edges, one, two, planes, d)
    *shared, plan_x, air_in, first, second = call(
        functools.partial(middle_kernel, d, True),
        (state, *vertical, edges, planes, *raw_weights),
        between + [plan] + made,
        [],
        "first_middle",
    )
    weights = (air_in, first, second, atm_out)
    state, fields, edges, one, two, plan_y = call(
        functools.partial(step_kernel, d, True, False),
        (state, land_mask, *horizontal, *shared, plan_x, *weights, surface_proj),
        [state_shape] + emitted + [plan],
        scratch + [raw],
        "first_step",
    )

    vertical, horizontal = exchange(fields, edges, one, two, None, d)
    shared = call(
        functools.partial(middle_kernel, d, False),
        (state, *vertical, edges, plan_x),
        between,
        [],
        "second_middle",
    )
    (state,) = call(
        functools.partial(step_kernel, d, False, True),
        (state, land_mask, *horizontal, *shared, plan_x, *weights, plan_y),
        [shape(CH, rows, 128)],
        scratch + [turned],
        "second_step",
    )
    return state[None]


def solution(mesh):
    return jax.shard_map(
        local,
        mesh=mesh,
        in_specs=(
            P("grp", None, "lat", "lon"),
            P("lat", "lon"),
            P("grp", None, None, "lat", "lon"),
            P("grp", None, "lat", "lon"),
            P(),
            P(),
            P(),
            P(),
            P(),
            P(),
            P(),
        ),
        out_specs=P("grp", None, "lat", "lon"),
        check_vma=False,
    )
```

time: 53.2 us -> 49.5 us (0.930)
  the two profiles are of different devices: /device:TPU:15 before, /device:TPU:9 now
where the time goes in v3:
time: 49.5 us; the launch traced here: 49 us
  starting transfers between devices  20.7 us (42%)
  Pallas kernels  12.4 us (25%)
  local copies, waits for them, and re-layouts  8.31 us (17%)
  waiting for transfers between devices  7.26 us (15%)
    ppermute x14, starting transfers between devices, send(): return lax.ppermute(x, names, pairs)  20.7 us
    pallas_call x5, Pallas kernels, call(): pl.pallas_call(kernel, out_shape=outs, in_specs=[SMEM] + [VMEM] * len(ope...  12.4 us
    unnamed x35, local copies, waits for them, and re-layouts  7.61 us
    ppermute x14, waiting for transfers between devices, send(): return lax.ppermute(x, names, pairs)  7.26 us
  transfers between devices with their start and end apart: 14, of which 4 were waited for; matrix products, arithmetic and copies ran while one was open for 2% of the time, Pallas kernels for 7%

profile of v3, /device:TPU:9, one launch (start us, length us, event | category | flops | bytes accessed | tf_op | source)
XLA Modules:
  0.0 49.0 jit_solution(17116512925234439231)
XLA Ops:
  0.1 1.0 %copy-done.2 = bf16[1,80,16,128]{3,2,1,0:T(8,128)(2,1)S(1)} copy-done((bf16[1,80,16,128]{3,2,1,0:T(8,128)(2,1)S(1)}, bf16[1,80,16,128]{3,2,1,0:T(8,128)(2,1)}, u32[]{:S(2)}) %copy-start.2) | copy-done | bytes 327704
  4.0 1.2 %start.1 = (bf16[16,80,128]{2,1,0:T(8,128)(2,1)S(1)}, bf16[8,16,128]{2,1,0:T(8,128)(2,1)S(1)}, bf16[4,16,128]{2,1,0:T(8,128)(2,1)S(1)}, bf16[80,128]{1,0:T(8,128...) custom-call(s32[4]{0:T(128)S(1)} %pad_add_fusion.flags.refs_0_, ...), custom_call_target="tpu_custom_call" | custom-call | tf_op jit(solution)/shard_map/start/pallas_call | solution.py:710
  5.2 1.2 %collective-permute-start = (bf16[4,16,128]{2,1,0:T(8,128)(2,1)S(1)}, bf16[4,16,128]{2,1,0:T(8,128)(2,1)S(1)}, u32[]{:S(2)}, u32[]{:S(2)}) collective-permute-start(bf16[4,16,128]{2,1,0:T(8,128)(2,1)S(1)} %get-tuple-element.30), channel_id=1, source_target_pairs={{0,20},{1,21},{2,22},{3,23},{4,16},{5,17},{6,18},{7,19},{8,28},{9,... | collective-permute-start | bytes 49160 | tf_op jit(solution)/shard_map/ppermute | solution.py:635
  6.4 2.4 %collective-permute-start.2 = (bf16[4,16,128]{2,1,0:T(8,128)(2,1)S(1)}, bf16[4,16,128]{2,1,0:T(8,128)(2,1)S(1)}, u32[]{:S(2)}, u32[]{:S(2)}) collective-permute-start(bf16[4,16,128]{2,1,0:T(8,128)(2,1)S(1)} %get-tuple-element.30), channel_id=1, source_target_pairs={{0,16},{1,17},{2,18},{3,19},{4,24},{5,25},{6,26},{7,27},{8,20},{9,... | collective-permute-start | bytes 49160 | tf_op jit(solution)/shard_map/ppermute | solution.py:635
  8.8 1.2 %collective-permute-start.1 = (bf16[4,16,128]{2,1,0:T(8,128)(2,1)S(1)}, bf16[4,16,128]{2,1,0:T(8,128)(2,1)S(1)}, u32[]{:S(2)}, u32[]{:S(2)}) collective-permute-start(bf16[4,16,128]{2,1,0:T(8,128)(2,1)S(1)} %get-tuple-element.30), channel_id=1, source_target_pairs={{0,16},{1,17},{2,18},{3,19},{4,20},{5,21},{6,22},{7,23},{8,24},{9,... | collective-permute-start | bytes 49160 | tf_op jit(solution)/shard_map/ppermute | solution.py:635
  10.0 2.3 %collective-permute-start.4 = (bf16[256,128]{1,0:T(8,128)(2,1)S(1)}, bf16[256,128]{1,0:T(8,128)(2,1)S(1)}, u32[]{:S(2)}, u32[]{:S(2)}) collective-permute-start(bf16[256,128]{1,0:T(8,128)(2,1)S(1)} %get-tuple-element.33), channel_id=1, source_target_pairs={{0,0},{1,1},{2,2},{3,3},{4,8},{5,9},{6,10},{7,11},{8,4},{9,5},{10,... | collective-permute-start | bytes 196616 | tf_op jit(solution)/shard_map/ppermute | solution.py:635
  12.4 0.9 %collective-permute-done.3.refs_5_ = bf16[256,128]{1,0:T(8,128)(2,1)S(1)} collective-permute-done((bf16[256,128]{1,0:T(8,128)(2,1)S(1)}, bf16[256,128]{1,0:T(8,128)(2,1)S(1)}, u32[]{:S(2)}, u32[]{:S(2)}) %collective-permute-start.3) | collective-permute-done | bytes 65568 | tf_op jit(solution)/shard_map/ppermute | solution.py:635
  13.4 1.9 %collective-permute-done.4.refs_6_ = bf16[256,128]{1,0:T(8,128)(2,1)S(1)} collective-permute-done((bf16[256,128]{1,0:T(8,128)(2,1)S(1)}, bf16[256,128]{1,0:T(8,128)(2,1)S(1)}, u32[]{:S(2)}, u32[]{:S(2)}) %collective-permute-start.4) | collective-permute-done | bytes 65568 | tf_op jit(solution)/shard_map/ppermute | solution.py:635
  15.3 2.4 %collective-permute-start.6 = (bf16[592,128]{1,0:T(8,128)(2,1)S(1)}, bf16[592,128]{1,0:T(8,128)(2,1)S(1)}, u32[]{:S(2)}, u32[]{:S(2)}) collective-permute-start(bf16[592,128]{1,0:T(8,128)(2,1)S(1)} %constant_dynamic-update-slice_fusion), channel_id=1, source_target_pairs={{0,3},{1,0},{2,1},{3,2},{4,7},{5,4},{6,5},{7,6},{8,11},{9,8},{10,9... | collective-permute-start | bytes 454664 | tf_op jit(solution)/shard_map/ppermute | solution.py:635
  17.7 1.2 %collective-permute-start.5 = (bf16[592,128]{1,0:T(8,128)(2,1)S(1)}, bf16[592,128]{1,0:T(8,128)(2,1)S(1)}, u32[]{:S(2)}, u32[]{:S(2)}) collective-permute-start(bf16[592,128]{1,0:T(8,128)(2,1)S(1)} %constant_dynamic-update-slice_fusion), channel_id=1, source_target_pairs={{0,1},{1,2},{2,3},{3,0},{4,5},{5,6},{6,7},{7,4},{8,9},{9,10},{10,1... | collective-permute-start | bytes 454664 | tf_op jit(solution)/shard_map/ppermute | solution.py:635
  19.6 1.0 %copy-done = bf16[200,9,84]{0,2,1:T(8,128)(2,1)S(1)} copy-done((bf16[200,9,84]{0,2,1:T(8,128)(2,1)S(1)}, bf16[200,9,84]{0,2,1:T(8,128)(2,1)}, u32[]{:S(2)}) %copy-start) | copy-done | bytes 302424
  20.6 1.0 %copy-done.1 = bf16[80,9,200]{2,0,1:T(8,128)(2,1)S(1)} copy-done((bf16[80,9,200]{2,0,1:T(8,128)(2,1)S(1)}, bf16[80,9,200]{2,0,1:T(8,128)(2,1)}, u32[]{:S(2)}) %copy-start.1) | copy-done | bytes 288024
  21.6 0.9 %copy-done.6 = bf16[384,84]{0,1:T(8,128)(2,1)S(1)} copy-done((bf16[384,84]{0,1:T(8,128)(2,1)S(1)}, bf16[384,84]{0,1:T(8,128)(2,1)}, u32[]{:S(2)}) %copy-start.6) | copy-done | bytes 64536
  23.1 1.8 %first_middle.1 = (f32[96,128]{1,0:T(8,128)S(1)}, f32[4,48,128]{2,1,0:T(8,128)S(1)}, bf16[20,240,128]{2,1,0:T(8,128)(2,1)S(1)}, bf16[80,128]{1,0:T(8,128)(2,1)S(...) custom-call(s32[4]{0:T(128)S(1)} %pad_add_fusion.flags.refs_0_, ...), custom_call_target="tpu_custom_call" | custom-call | tf_op jit(solution)/shard_map/first_middle/pallas_call | solution.py:710
  24.9 3.6 %first_step.1 = (bf16[16,80,128]{2,1,0:T(8,128)(2,1)S(1)}, bf16[4,16,128]{2,1,0:T(8,128)(2,1)S(1)}, bf16[80,128]{1,0:T(8,128)(2,1)S(1)}, bf16[240,128]{1,0:T(8,1...) custom-call(s32[4]{0:T(128)S(1)} %pad_add_fusion.flags.refs_0_, ...), custom_call_target="tpu_custom_call" | custom-call | tf_op jit(solution)/shard_map/first_step/pallas_call | solution.py:710
  28.6 2.4 %collective-permute-start.9 = (bf16[4,16,128]{2,1,0:T(8,128)(2,1)S(1)}, bf16[4,16,128]{2,1,0:T(8,128)(2,1)S(1)}, u32[]{:S(2)}, u32[]{:S(2)}) collective-permute-start(bf16[4,16,128]{2,1,0:T(8,128)(2,1)S(1)} %get-tuple-element.44), channel_id=1, source_target_pairs={{0,16},{1,17},{2,18},{3,19},{4,24},{5,25},{6,26},{7,27},{8,20},{9,... | collective-permute-start | bytes 49160 | tf_op jit(solution)/shard_map/ppermute | solution.py:635
  31.0 2.1 %collective-permute-start.10 = (bf16[240,128]{1,0:T(8,128)(2,1)S(1)}, bf16[240,128]{1,0:T(8,128)(2,1)S(1)}, u32[]{:S(2)}, u32[]{:S(2)}) collective-permute-start(bf16[240,128]{1,0:T(8,128)(2,1)S(1)} %get-tuple-element.45), channel_id=1, source_target_pairs={{0,4},{1,5},{2,6},{3,7},{4,0},{5,1},{6,2},{7,3},{8,12},{9,13},{10,... | collective-permute-start | bytes 184328 | tf_op jit(solution)/shard_map/ppermute | solution.py:635
  33.2 2.6 %collective-permute-start.11 = (bf16[240,128]{1,0:T(8,128)(2,1)S(1)}, bf16[240,128]{1,0:T(8,128)(2,1)S(1)}, u32[]{:S(2)}, u32[]{:S(2)}) collective-permute-start(bf16[240,128]{1,0:T(8,128)(2,1)S(1)} %get-tuple-element.47), channel_id=1, source_target_pairs={{0,0},{1,1},{2,2},{3,3},{4,8},{5,9},{6,10},{7,11},{8,4},{9,5},{10,... | collective-permute-start | bytes 184328 | tf_op jit(solution)/shard_map/ppermute | solution.py:635
  35.9 2.2 %collective-permute-done.11.refs_6_ = bf16[240,128]{1,0:T(8,128)(2,1)S(1)} collective-permute-done((bf16[240,128]{1,0:T(8,128)(2,1)S(1)}, bf16[240,128]{1,0:T(8,128)(2,1)S(1)}, u32[]{:S(2)}, u32[]{:S(2)}) %collective-permute-start.11) | collective-permute-done | bytes 61472 | tf_op jit(solution)/shard_map/ppermute | solution.py:635
  38.1 1.6 %collective-permute-start.13 = (bf16[432,128]{1,0:T(8,128)(2,1)S(1)}, bf16[432,128]{1,0:T(8,128)(2,1)S(1)}, u32[]{:S(2)}, u32[]{:S(2)}) collective-permute-start(bf16[432,128]{1,0:T(8,128)(2,1)S(1)} %constant_dynamic-update-slice_fusion.9), channel_id=1, source_target_pairs={{0,3},{1,0},{2,1},{3,2},{4,7},{5,4},{6,5},{7,6},{8,11},{9,8},{10,9... | collective-permute-start | bytes 331784 | tf_op jit(solution)/shard_map/ppermute | solution.py:635
  39.7 1.2 %collective-permute-start.12 = (bf16[432,128]{1,0:T(8,128)(2,1)S(1)}, bf16[432,128]{1,0:T(8,128)(2,1)S(1)}, u32[]{:S(2)}, u32[]{:S(2)}) collective-permute-start(bf16[432,128]{1,0:T(8,128)(2,1)S(1)} %constant_dynamic-update-slice_fusion.9), channel_id=1, source_target_pairs={{0,1},{1,2},{2,3},{3,0},{4,5},{5,6},{6,7},{7,4},{8,9},{9,10},{10,1... | collective-permute-start | bytes 331784 | tf_op jit(solution)/shard_map/ppermute | solution.py:635
  40.9 1.6 %second_middle.1 = (f32[96,128]{1,0:T(8,128)S(1)}, f32[4,48,128]{2,1,0:T(8,128)S(1)}, bf16[20,240,128]{2,1,0:T(8,128)(2,1)S(1)}, bf16[80,128]{1,0:T(8,128)(2,1)S(1)}) custom-call(s32[4]{0:T(128)S(1)} %pad_add_fusion.flags.refs_0_, bf16[16,80,128]{2,1,0:T(8,128)(2,1)S(1)} %get-tuple-element.43.refs_1_, ...), custom_call_target="tpu_custom_call" | custom-call | tf_op jit(solution)/shard_map/second_middle/pallas_call | solution.py:710
  42.5 2.2 %collective-permute-done.13.refs_4_ = bf16[432,128]{1,0:T(8,128)(2,1)S(1)} collective-permute-done((bf16[432,128]{1,0:T(8,128)(2,1)S(1)}, bf16[432,128]{1,0:T(8,128)(2,1)S(1)}, u32[]{:S(2)}, u32[]{:S(2)}) %collective-permute-start.13) | collective-permute-done | bytes 110624 | tf_op jit(solution)/shard_map/ppermute | solution.py:635
  44.7 4.3 %second_step.1 = bf16[80,16,128]{2,1,0:T(8,128)(2,1)} custom-call(s32[4]{0:T(128)S(1)} %pad_add_fusion.flags.refs_0_, bf16[16,80,128]{2,1,0:T(8,128)(2,1)S(1)} %get-tuple-element.43.refs_1_, s32[16,128]{1,0:T(8,128)S(1)} %copy-done.5, bf16[432,128]{1,0:T(8,128)(2,1)S(1)} %collective-permute-done.12.refs_3_, ...), custom_call_target="tpu_custom_call" | custom-call | tf_op jit(solution)/shard_map/second_step/pallas_call | solution.py:710
  (48 shorter events, 4.7 us)
Async XLA Ops:
  0.0 24.9 %copy-start.5 = (s32[16,128]{1,0:T(8,128)S(1)}, s32[16,128]{1,0:T(8,128)}, u32[]{:S(2)}) copy-start(s32[16,128]{1,0:T(8,128)} %refs_2_.3) | copy-start | bytes 24580
  0.1 1.0 %copy-start.2 = (bf16[1,80,16,128]{3,2,1,0:T(8,128)(2,1)S(1)}, bf16[1,80,16,128]{3,2,1,0:T(8,128)(2,1)}, u32[]{:S(2)}) copy-start(bf16[1,80,16,128]{3,2,1,0:T(8,128)(2,1)} %param.11) | copy-start | bytes 983044
  1.1 0.7 %copy-start.4 = (s32[16,128]{1,0:T(8,128)S(1)}, s32[16,128]{1,0:T(8,128)}, u32[]{:S(2)}) copy-start(s32[16,128]{1,0:T(8,128)} %refs_2_.3) | copy-start | bytes 24580
  1.8 0.8 %copy-start.7 = (s32[1,2,4,16,128]{4,3,2,1,0:T(8,128)S(1)}, s32[1,2,4,16,128]{4,3,2,1,0:T(8,128)}, u32[]{:S(2)}) copy-start(s32[1,2,4,16,128]{4,3,2,1,0:T(8,128)} %param.13) | copy-start | bytes 196612
  2.6 0.8 %copy-start.8 = (f32[1,4,16,128]{3,2,1,0:T(8,128)S(1)}, f32[1,4,16,128]{3,2,1,0:T(8,128)}, u32[]{:S(2)}) copy-start(f32[1,4,16,128]{3,2,1,0:T(8,128)} %param.14) | copy-start | bytes 98308
  3.4 0.7 %copy-start.9 = (f32[2,4,80]{2,1,0:T(4,128)S(1)}, f32[2,4,80]{2,1,0:T(4,128)}, u32[]{:S(2)}) copy-start(f32[2,4,80]{2,1,0:T(4,128)} %refs_14_.1) | copy-start | bytes 7684
  4.0 20.9 %copy-start.3 = (bf16[80,384]{1,0:T(8,128)(2,1)S(1)}, bf16[80,384]{1,0:T(8,128)(2,1)}, u32[]{:S(2)}) copy-start(bf16[80,384]{1,0:T(8,128)(2,1)} %refs_13_.3) | copy-start | bytes 184324
  5.2 7.1 %collective-permute-start = (bf16[4,16,128]{2,1,0:T(8,128)(2,1)S(1)}, bf16[4,16,128]{2,1,0:T(8,128)(2,1)S(1)}, u32[]{:S(2)}, u32[]{:S(2)}) collective-permute-start(bf16[4,16,128]{2,1,0:T(8,128)(2,1)S(1)} %get-tuple-element.30), channel_id=1, source_target_pairs={{0,20},{1,21},{2,22},{3,23},{4,16},{5,17},{6,18},{7,19},{8,28},{9,... | collective-permute-start | bytes 49160 | tf_op jit(solution)/shard_map/ppermute | solution.py:635
  6.4 6.0 %collective-permute-start.2 = (bf16[4,16,128]{2,1,0:T(8,128)(2,1)S(1)}, bf16[4,16,128]{2,1,0:T(8,128)(2,1)S(1)}, u32[]{:S(2)}, u32[]{:S(2)}) collective-permute-start(bf16[4,16,128]{2,1,0:T(8,128)(2,1)S(1)} %get-tuple-element.30), channel_id=1, source_target_pairs={{0,16},{1,17},{2,18},{3,19},{4,24},{5,25},{6,26},{7,27},{8,20},{9,... | collective-permute-start | bytes 49160 | tf_op jit(solution)/shard_map/ppermute | solution.py:635
  8.8 3.6 %collective-permute-start.1 = (bf16[4,16,128]{2,1,0:T(8,128)(2,1)S(1)}, bf16[4,16,128]{2,1,0:T(8,128)(2,1)S(1)}, u32[]{:S(2)}, u32[]{:S(2)}) collective-permute-start(bf16[4,16,128]{2,1,0:T(8,128)(2,1)S(1)} %get-tuple-element.30), channel_id=1, source_target_pairs={{0,16},{1,17},{2,18},{3,19},{4,20},{5,21},{6,22},{7,23},{8,24},{9,... | collective-permute-start | bytes 49160 | tf_op jit(solution)/shard_map/ppermute | solution.py:635
  10.0 3.4 %collective-permute-start.3 = (bf16[256,128]{1,0:T(8,128)(2,1)S(1)}, bf16[256,128]{1,0:T(8,128)(2,1)S(1)}, u32[]{:S(2)}, u32[]{:S(2)}) collective-permute-start(bf16[256,128]{1,0:T(8,128)(2,1)S(1)} %get-tuple-element.31), channel_id=1, source_target_pairs={{0,4},{1,5},{2,6},{3,7},{4,0},{5,1},{6,2},{7,3},{8,12},{9,13},{10,... | collective-permute-start | bytes 196616 | tf_op jit(solution)/shard_map/ppermute | solution.py:635
  10.0 5.3 %collective-permute-start.4 = (bf16[256,128]{1,0:T(8,128)(2,1)S(1)}, bf16[256,128]{1,0:T(8,128)(2,1)S(1)}, u32[]{:S(2)}, u32[]{:S(2)}) collective-permute-start(bf16[256,128]{1,0:T(8,128)(2,1)S(1)} %get-tuple-element.33), channel_id=1, source_target_pairs={{0,0},{1,1},{2,2},{3,3},{4,8},{5,9},{6,10},{7,11},{8,4},{9,5},{10,... | collective-permute-start | bytes 196616 | tf_op jit(solution)/shard_map/ppermute | solution.py:635
  15.3 9.6 %collective-permute-start.6 = (bf16[592,128]{1,0:T(8,128)(2,1)S(1)}, bf16[592,128]{1,0:T(8,128)(2,1)S(1)}, u32[]{:S(2)}, u32[]{:S(2)}) collective-permute-start(bf16[592,128]{1,0:T(8,128)(2,1)S(1)} %constant_dynamic-update-slice_fusion), channel_id=1, source_target_pairs={{0,3},{1,0},{2,1},{3,2},{4,7},{5,4},{6,5},{7,6},{8,11},{9,8},{10,9... | collective-permute-start | bytes 454664 | tf_op jit(solution)/shard_map/ppermute | solution.py:635
  17.7 7.2 %collective-permute-start.5 = (bf16[592,128]{1,0:T(8,128)(2,1)S(1)}, bf16[592,128]{1,0:T(8,128)(2,1)S(1)}, u32[]{:S(2)}, u32[]{:S(2)}) collective-permute-start(bf16[592,128]{1,0:T(8,128)(2,1)S(1)} %constant_dynamic-update-slice_fusion), channel_id=1, source_target_pairs={{0,1},{1,2},{2,3},{3,0},{4,5},{5,6},{6,7},{7,4},{8,9},{9,10},{10,1... | collective-permute-start | bytes 454664 | tf_op jit(solution)/shard_map/ppermute | solution.py:635
  19.6 1.0 %copy-start = (bf16[200,9,84]{0,2,1:T(8,128)(2,1)S(1)}, bf16[200,9,84]{0,2,1:T(8,128)(2,1)}, u32[]{:S(2)}) copy-start(bf16[200,9,84]{0,2,1:T(8,128)(2,1)} %param.19) | copy-start | bytes 907204
  20.6 1.0 %copy-start.1 = (bf16[80,9,200]{2,0,1:T(8,128)(2,1)S(1)}, bf16[80,9,200]{2,0,1:T(8,128)(2,1)}, u32[]{:S(2)}) copy-start(bf16[80,9,200]{2,0,1:T(8,128)(2,1)} %param.21) | copy-start | bytes 864004
  21.6 0.9 %copy-start.6 = (bf16[384,84]{0,1:T(8,128)(2,1)S(1)}, bf16[384,84]{0,1:T(8,128)(2,1)}, u32[]{:S(2)}) copy-start(bf16[384,84]{0,1:T(8,128)(2,1)} %param.16) | copy-start | bytes 193540
  28.6 7.2 %collective-permute-start.7 = (bf16[4,16,128]{2,1,0:T(8,128)(2,1)S(1)}, bf16[4,16,128]{2,1,0:T(8,128)(2,1)S(1)}, u32[]{:S(2)}, u32[]{:S(2)}) collective-permute-start(bf16[4,16,128]{2,1,0:T(8,128)(2,1)S(1)} %get-tuple-element.44), channel_id=1, source_target_pairs={{0,20},{1,21},{2,22},{3,23},{4,16},{5,17},{6,18},{7,19},{8,28},{9,... | collective-permute-start | bytes 49160 | tf_op jit(solution)/shard_map/ppermute | solution.py:635
  28.6 7.2 %collective-permute-start.9 = (bf16[4,16,128]{2,1,0:T(8,128)(2,1)S(1)}, bf16[4,16,128]{2,1,0:T(8,128)(2,1)S(1)}, u32[]{:S(2)}, u32[]{:S(2)}) collective-permute-start(bf16[4,16,128]{2,1,0:T(8,128)(2,1)S(1)} %get-tuple-element.44), channel_id=1, source_target_pairs={{0,16},{1,17},{2,18},{3,19},{4,24},{5,25},{6,26},{7,27},{8,20},{9,... | collective-permute-start | bytes 49160 | tf_op jit(solution)/shard_map/ppermute | solution.py:635
  31.0 4.8 %collective-permute-start.8 = (bf16[4,16,128]{2,1,0:T(8,128)(2,1)S(1)}, bf16[4,16,128]{2,1,0:T(8,128)(2,1)S(1)}, u32[]{:S(2)}, u32[]{:S(2)}) collective-permute-start(bf16[4,16,128]{2,1,0:T(8,128)(2,1)S(1)} %get-tuple-element.44), channel_id=1, source_target_pairs={{0,16},{1,17},{2,18},{3,19},{4,20},{5,21},{6,22},{7,23},{8,24},{9,... | collective-permute-start | bytes 49160 | tf_op jit(solution)/shard_map/ppermute | solution.py:635
  31.0 4.8 %collective-permute-start.10 = (bf16[240,128]{1,0:T(8,128)(2,1)S(1)}, bf16[240,128]{1,0:T(8,128)(2,1)S(1)}, u32[]{:S(2)}, u32[]{:S(2)}) collective-permute-start(bf16[240,128]{1,0:T(8,128)(2,1)S(1)} %get-tuple-element.45), channel_id=1, source_target_pairs={{0,4},{1,5},{2,6},{3,7},{4,0},{5,1},{6,2},{7,3},{8,12},{9,13},{10,... | collective-permute-start | bytes 184328 | tf_op jit(solution)/shard_map/ppermute | solution.py:635
  33.2 5.0 %collective-permute-start.11 = (bf16[240,128]{1,0:T(8,128)(2,1)S(1)}, bf16[240,128]{1,0:T(8,128)(2,1)S(1)}, u32[]{:S(2)}, u32[]{:S(2)}) collective-permute-start(bf16[240,128]{1,0:T(8,128)(2,1)S(1)} %get-tuple-element.47), channel_id=1, source_target_pairs={{0,0},{1,1},{2,2},{3,3},{4,8},{5,9},{6,10},{7,11},{8,4},{9,5},{10,... | collective-permute-start | bytes 184328 | tf_op jit(solution)/shard_map/ppermute | solution.py:635
  38.1 6.6 %collective-permute-start.13 = (bf16[432,128]{1,0:T(8,128)(2,1)S(1)}, bf16[432,128]{1,0:T(8,128)(2,1)S(1)}, u32[]{:S(2)}, u32[]{:S(2)}) collective-permute-start(bf16[432,128]{1,0:T(8,128)(2,1)S(1)} %constant_dynamic-update-slice_fusion.9), channel_id=1, source_target_pairs={{0,3},{1,0},{2,1},{3,2},{4,7},{5,4},{6,5},{7,6},{8,11},{9,8},{10,9... | collective-permute-start | bytes 331784 | tf_op jit(solution)/shard_map/ppermute | solution.py:635
  39.7 5.0 %collective-permute-start.12 = (bf16[432,128]{1,0:T(8,128)(2,1)S(1)}, bf16[432,128]{1,0:T(8,128)(2,1)S(1)}, u32[]{:S(2)}, u32[]{:S(2)}) collective-permute-start(bf16[432,128]{1,0:T(8,128)(2,1)S(1)} %constant_dynamic-update-slice_fusion.9), channel_id=1, source_target_pairs={{0,1},{1,2},{2,3},{3,0},{4,5},{5,6},{6,7},{7,4},{8,9},{9,10},{10,1... | collective-permute-start | bytes 331784 | tf_op jit(solution)/shard_map/ppermute | solution.py:635
  (1 other events, 0.7 us)

commit v4 on v3

--- a/solution.py
+++ b/solution.py
@@ -124,14 +124,33 @@
         put_edges(ref, 2 * CH, edges, d)
 
 
+def fetch(sources, targets, sems):
+    copies = [
+        pltpu.make_async_copy(source, target, sems.at[index])
+        for index, (source, target) in enumerate(zip(sources, targets))
+    ]
+    for copy in copies:
+        copy.start()
+    return copies
+
+
 def start_kernel(
-    d, flags, given, offsets, weights, surface, wet, state, planes, fields, own_edges, one, two,
-    raw, tall, turned,
+    d, flags, far_given, far_surface, far_wet, far_offsets, far_weights,
+    state, planes, fields, own_edges, one, two,
+    raw, tall, turned, given, surface, wet, offsets, weights, sems,
 ):
     rows = d.rows
+    copies = fetch(
+        (far_given, far_surface, far_wet, far_offsets, far_weights),
+        (given, surface, wet, offsets, weights),
+        sems,
+    )
+    copies[0].wait()
     turned[...] = given[...].astype(F32).reshape(CH * rows, 128)
     for row in range(rows):
         state[row] = turned[pl.ds(row, CH, stride=rows), :].astype(BF16)
+    for copy in copies[1:]:
+        copy.wait()
     emit(state, surface, wet, flags, fields, own_edges, one, two, raw, d)
     for k in range(NK):
         code = (offsets[0, k] * SPAN + offsets[1, k]).astype(F32)
@@ -430,7 +449,7 @@
 
 def prepare(atm_in, atm_bias, ocn_in, ocn_bias, ocn_out, air_in, first, second, is_ocean):
     def bias_rows(ref, width):
-        row = ref[0:1, :]
+        row = jnp.concatenate([ref[index : index + 1, :] for index in range(ref.shape[0])], axis=1)
         terms = list(split_bf16(row)) + [jnp.zeros_like(row)]
         bias = jnp.concatenate(terms, axis=0)
         return jnp.pad(bias, ((0, 0), (0, width - bias.shape[1])))
@@ -476,12 +495,14 @@
     take = lambda count: [refs.pop(0) for _ in range(count)]
     flags, state, field_one, beside, field_two, from_one, from_two, own_edges = take(8)
     if opening:
-        planes, *raw_weights = take(6)
+        planes, *far_weights = take(6)
     else:
         (plan_x,) = take(1)
     part_x, fields_x, rolled, edges = take(4)
     if opening:
         plan_x, *made_weights = take(4)
+        *raw_weights, sems = take(6)
+        copies = fetch(far_weights, raw_weights, sems)
     rows, tall = d.rows, d.tall
     is_ocean = flags[0]
     up_and_down = ends(flags)
@@ -520,6 +541,8 @@
         put_edges(edges, 0, joined, d)
 
     if opening:
+        for copy in copies:
+            copy.wait()
         prepare(*raw_weights, *made_weights, is_ocean)
 
 
@@ -612,6 +635,7 @@
 
 
 VMEM = pl.BlockSpec(memory_space=pltpu.VMEM)
+HBM = pl.BlockSpec(memory_space=pltpu.HBM)
 SMEM = pl.BlockSpec(memory_space=pltpu.SMEM)
 PARAMS = pltpu.CompilerParams(vmem_limit_bytes=48 * 1024 * 1024)
 
@@ -691,7 +715,7 @@
     ).astype(jnp.int32)
     raw_weights = (
         atm_in.T,
-        atm_bias[None],
+        atm_bias.reshape(HA // 128, 128),
         jnp.transpose(ocn_in, (1, 2, 0)),
         ocn_bias[None],
         jnp.transpose(ocn_out, (1, 0, 2)),
@@ -706,23 +730,29 @@
     raw = pltpu.VMEM((rows * 8, 128), F32)
     turned = pltpu.VMEM((CH * rows, 128), F32)
 
-    def call(kernel, operands, outs, scratch, name):
+    def call(kernel, operands, outs, scratch, name, far=()):
+        scratch = scratch + [pltpu.VMEM(x.shape, x.dtype) for x in far]
+        if far:
+            scratch.append(pltpu.SemaphoreType.DMA((len(far),)))
+
+        far = [pltpu.with_memory_space_constraint(x, pltpu.HBM) for x in far]
         return pl.pallas_call(
             kernel,
             out_shape=outs,
-            in_specs=[SMEM] + [VMEM] * len(operands),
+            in_specs=[SMEM] + [VMEM] * len(operands) + [HBM] * len(far),
             out_specs=[VMEM] * len(outs),
             scratch_shapes=scratch,
             compiler_params=PARAMS,
             name=name,
-        )(flags, *operands)
+        )(flags, *operands, *far)
 
     state, planes, fields, edges, one, two = call(
         functools.partial(start_kernel, d),
-        (coupled_state[0], regrid_offsets[0], regrid_weights[0], surface_proj, land_mask),
+        (),
         [state_shape, shape(2 * NK, rows, 128)] + emitted[:2] + [shape(d.strip + 16, 128)] * 2,
         [raw, pltpu.VMEM((2 * NK * rows, 128), F32), turned],
         "start",
+        (coupled_state[0], surface_proj, land_mask, regrid_offsets[0], regrid_weights[0]),
     )
 
     plan = shape(2 * NK * d.tall, 128, dtype=F32)
@@ -745,10 +775,11 @@
     vertical, horizontal = exchange(fields, edges, one, two, planes, d)
     *shared, plan_x, air_in, first, second = call(
         functools.partial(middle_kernel, d, True),
-        (state, *vertical, edges, planes, *raw_weights),
+        (state, *vertical, edges, planes),
         between + [plan] + made,
         [],
         "first_middle",
+        raw_weights,
     )
     weights = (air_in, first, second, atm_out)
     state, fields, edges, one, two, plan_y = call(

time: 49.5 us -> 44.1 us (0.89)
  the two profiles are of different devices: /device:TPU:9 before, /device:TPU:13 now
where the time goes in v4:
time: 44.1 us; the launch traced here: 43.9 us
  starting transfers between devices  20.9 us (47%)
  Pallas kernels  13.5 us (31%)
  waiting for transfers between devices  9.15 us (21%)
    ppermute x14, starting transfers between devices, send(): return lax.ppermute(x, names, pairs)  20.9 us
    pallas_call x5, Pallas kernels, call(): pl.pallas_call(kernel, out_shape=outs, in_specs=[SMEM] + [VMEM] * len(ope...  13.5 us
    ppermute x14, waiting for transfers between devices, send(): return lax.ppermute(x, names, pairs)  9.15 us
  transfers between devices with their start and end apart: 14, of which 5 were waited for; matrix products, arithmetic and copies ran while one was open for 0% of the time, Pallas kernels for 8%

profile of v4, /device:TPU:13, one launch (start us, length us, event | category | flops | bytes accessed | tf_op | source)
XLA Modules:
  0.0 43.9 jit_solution(7121848427109347654)
XLA Ops:
  0.0 0.1 pad_add_fusion.flags.refs_0_
  0.1 2.1 %start.1 = (bf16[16,80,128]{2,1,0:T(8,128)(2,1)S(1)}, bf16[8,16,128]{2,1,0:T(8,128)(2,1)S(1)}, bf16[4,16,128]{2,1,0:T(8,128)(2,1)S(1)}, bf16[80,128]{1,0:T(8,128...) custom-call(s32[4]{0:T(128)S(1)} %pad_add_fusion.flags.refs_0_, bf16[80,16,128]{2,1,0:T(8,128)(2,1)} %bitcast.29, ...), custom_call_target="tpu_custom_call" | custom-call | tf_op jit(solution)/shard_map/start/pallas_call | solution.py:739
  2.2 1.2 %collective-permute-start = (bf16[4,16,128]{2,1,0:T(8,128)(2,1)S(1)}, bf16[4,16,128]{2,1,0:T(8,128)(2,1)S(1)}, u32[]{:S(2)}, u32[]{:S(2)}) collective-permute-start(bf16[4,16,128]{2,1,0:T(8,128)(2,1)S(1)} %get-tuple-element.30), channel_id=1, source_target_pairs={{0,20},{1,21},{2,22},{3,23},{4,16},{5,17},{6,18},{7,19},{8,28},{9,... | collective-permute-start | bytes 49160 | tf_op jit(solution)/shard_map/ppermute | solution.py:659
  3.4 2.4 %collective-permute-start.2 = (bf16[4,16,128]{2,1,0:T(8,128)(2,1)S(1)}, bf16[4,16,128]{2,1,0:T(8,128)(2,1)S(1)}, u32[]{:S(2)}, u32[]{:S(2)}) collective-permute-start(bf16[4,16,128]{2,1,0:T(8,128)(2,1)S(1)} %get-tuple-element.30), channel_id=1, source_target_pairs={{0,16},{1,17},{2,18},{3,19},{4,24},{5,25},{6,26},{7,27},{8,20},{9,... | collective-permute-start | bytes 49160 | tf_op jit(solution)/shard_map/ppermute | solution.py:659
  5.8 1.2 %collective-permute-start.1 = (bf16[4,16,128]{2,1,0:T(8,128)(2,1)S(1)}, bf16[4,16,128]{2,1,0:T(8,128)(2,1)S(1)}, u32[]{:S(2)}, u32[]{:S(2)}) collective-permute-start(bf16[4,16,128]{2,1,0:T(8,128)(2,1)S(1)} %get-tuple-element.30), channel_id=1, source_target_pairs={{0,16},{1,17},{2,18},{3,19},{4,20},{5,21},{6,22},{7,23},{8,24},{9,... | collective-permute-start | bytes 49160 | tf_op jit(solution)/shard_map/ppermute | solution.py:659
  7.0 2.3 %collective-permute-start.4 = (bf16[256,128]{1,0:T(8,128)(2,1)S(1)}, bf16[256,128]{1,0:T(8,128)(2,1)S(1)}, u32[]{:S(2)}, u32[]{:S(2)}) collective-permute-start(bf16[256,128]{1,0:T(8,128)(2,1)S(1)} %get-tuple-element.33), channel_id=1, source_target_pairs={{0,0},{1,1},{2,2},{3,3},{4,8},{5,9},{6,10},{7,11},{8,4},{9,5},{10,... | collective-permute-start | bytes 196616 | tf_op jit(solution)/shard_map/ppermute | solution.py:659
  9.4 0.9 %collective-permute-done.3.refs_5_ = bf16[256,128]{1,0:T(8,128)(2,1)S(1)} collective-permute-done((bf16[256,128]{1,0:T(8,128)(2,1)S(1)}, bf16[256,128]{1,0:T(8,128)(2,1)S(1)}, u32[]{:S(2)}, u32[]{:S(2)}) %collective-permute-start.3) | collective-permute-done | bytes 65568 | tf_op jit(solution)/shard_map/ppermute | solution.py:659
  10.4 1.9 %collective-permute-done.4.refs_6_ = bf16[256,128]{1,0:T(8,128)(2,1)S(1)} collective-permute-done((bf16[256,128]{1,0:T(8,128)(2,1)S(1)}, bf16[256,128]{1,0:T(8,128)(2,1)S(1)}, u32[]{:S(2)}, u32[]{:S(2)}) %collective-permute-start.4) | collective-permute-done | bytes 65568 | tf_op jit(solution)/shard_map/ppermute | solution.py:659
  12.3 2.4 %collective-permute-start.6 = (bf16[592,128]{1,0:T(8,128)(2,1)S(1)}, bf16[592,128]{1,0:T(8,128)(2,1)S(1)}, u32[]{:S(2)}, u32[]{:S(2)}) collective-permute-start(bf16[592,128]{1,0:T(8,128)(2,1)S(1)} %constant_dynamic-update-slice_fusion), channel_id=1, source_target_pairs={{0,3},{1,0},{2,1},{3,2},{4,7},{5,4},{6,5},{7,6},{8,11},{9,8},{10,9... | collective-permute-start | bytes 454664 | tf_op jit(solution)/shard_map/ppermute | solution.py:659
  14.8 0.2 collective-permute-start.5
  14.9 1.9 %first_middle.1 = (f32[96,128]{1,0:T(8,128)S(1)}, f32[4,48,128]{2,1,0:T(8,128)S(1)}, bf16[20,240,128]{2,1,0:T(8,128)(2,1)S(1)}, bf16[80,128]{1,0:T(8,128)(2,1)S(...) custom-call(s32[4]{0:T(128)S(1)} %pad_add_fusion.flags.refs_0_, ...), custom_call_target="tpu_custom_call" | custom-call | tf_op jit(solution)/shard_map/first_middle/pallas_call | solution.py:739
  16.8 1.8 %collective-permute-done.6.refs_4_ = bf16[592,128]{1,0:T(8,128)(2,1)S(1)} collective-permute-done((bf16[592,128]{1,0:T(8,128)(2,1)S(1)}, bf16[592,128]{1,0:T(8,128)(2,1)S(1)}, u32[]{:S(2)}, u32[]{:S(2)}) %collective-permute-start.6) | collective-permute-done | bytes 151584 | tf_op jit(solution)/shard_map/ppermute | solution.py:659
  18.7 3.6 %first_step.1 = (bf16[16,80,128]{2,1,0:T(8,128)(2,1)S(1)}, bf16[4,16,128]{2,1,0:T(8,128)(2,1)S(1)}, bf16[80,128]{1,0:T(8,128)(2,1)S(1)}, bf16[240,128]{1,0:T(8,1...) custom-call(s32[4]{0:T(128)S(1)} %pad_add_fusion.flags.refs_0_, ...), custom_call_target="tpu_custom_call" | custom-call | tf_op jit(solution)/shard_map/first_step/pallas_call | solution.py:739
  22.3 0.1 collective-permute-start.7
  22.4 1.5 %collective-permute-start.9 = (bf16[4,16,128]{2,1,0:T(8,128)(2,1)S(1)}, bf16[4,16,128]{2,1,0:T(8,128)(2,1)S(1)}, u32[]{:S(2)}, u32[]{:S(2)}) collective-permute-start(bf16[4,16,128]{2,1,0:T(8,128)(2,1)S(1)} %get-tuple-element.44), channel_id=1, source_target_pairs={{0,16},{1,17},{2,18},{3,19},{4,24},{5,25},{6,26},{7,27},{8,20},{9,... | collective-permute-start | bytes 49160 | tf_op jit(solution)/shard_map/ppermute | solution.py:659
  23.9 0.5 %collective-permute-start.8 = (bf16[4,16,128]{2,1,0:T(8,128)(2,1)S(1)}, bf16[4,16,128]{2,1,0:T(8,128)(2,1)S(1)}, u32[]{:S(2)}, u32[]{:S(2)}) collective-permute-start(bf16[4,16,128]{2,1,0:T(8,128)(2,1)S(1)} %get-tuple-element.44), channel_id=1, source_target_pairs={{0,16},{1,17},{2,18},{3,19},{4,20},{5,21},{6,22},{7,23},{8,24},{9,... | collective-permute-start | bytes 49160 | tf_op jit(solution)/shard_map/ppermute | solution.py:659
  24.4 1.7 %collective-permute-start.10 = (bf16[240,128]{1,0:T(8,128)(2,1)S(1)}, bf16[240,128]{1,0:T(8,128)(2,1)S(1)}, u32[]{:S(2)}, u32[]{:S(2)}) collective-permute-start(bf16[240,128]{1,0:T(8,128)(2,1)S(1)} %get-tuple-element.45), channel_id=1, source_target_pairs={{0,4},{1,5},{2,6},{3,7},{4,0},{5,1},{6,2},{7,3},{8,12},{9,13},{10,... | collective-permute-start | bytes 184328 | tf_op jit(solution)/shard_map/ppermute | solution.py:659
  26.0 2.6 %collective-permute-start.11 = (bf16[240,128]{1,0:T(8,128)(2,1)S(1)}, bf16[240,128]{1,0:T(8,128)(2,1)S(1)}, u32[]{:S(2)}, u32[]{:S(2)}) collective-permute-start(bf16[240,128]{1,0:T(8,128)(2,1)S(1)} %get-tuple-element.47), channel_id=1, source_target_pairs={{0,0},{1,1},{2,2},{3,3},{4,8},{5,9},{6,10},{7,11},{8,4},{9,5},{10,... | collective-permute-start | bytes 184328 | tf_op jit(solution)/shard_map/ppermute | solution.py:659
  28.8 2.2 %collective-permute-done.11.refs_6_ = bf16[240,128]{1,0:T(8,128)(2,1)S(1)} collective-permute-done((bf16[240,128]{1,0:T(8,128)(2,1)S(1)}, bf16[240,128]{1,0:T(8,128)(2,1)S(1)}, u32[]{:S(2)}, u32[]{:S(2)}) %collective-permute-start.11) | collective-permute-done | bytes 61472 | tf_op jit(solution)/shard_map/ppermute | solution.py:659
  31.0 3.7 %collective-permute-start.13 = (bf16[432,128]{1,0:T(8,128)(2,1)S(1)}, bf16[432,128]{1,0:T(8,128)(2,1)S(1)}, u32[]{:S(2)}, u32[]{:S(2)}) collective-permute-start(bf16[432,128]{1,0:T(8,128)(2,1)S(1)} %constant_dynamic-update-slice_fusion.9), channel_id=1, source_target_pairs={{0,3},{1,0},{2,1},{3,2},{4,7},{5,4},{6,5},{7,6},{8,11},{9,8},{10,9... | collective-permute-start | bytes 331784 | tf_op jit(solution)/shard_map/ppermute | solution.py:659
  34.7 1.2 %collective-permute-start.12 = (bf16[432,128]{1,0:T(8,128)(2,1)S(1)}, bf16[432,128]{1,0:T(8,128)(2,1)S(1)}, u32[]{:S(2)}, u32[]{:S(2)}) collective-permute-start(bf16[432,128]{1,0:T(8,128)(2,1)S(1)} %constant_dynamic-update-slice_fusion.9), channel_id=1, source_target_pairs={{0,1},{1,2},{2,3},{3,0},{4,5},{5,6},{6,7},{7,4},{8,9},{9,10},{10,1... | collective-permute-start | bytes 331784 | tf_op jit(solution)/shard_map/ppermute | solution.py:659
  35.8 1.6 %second_middle.1 = (f32[96,128]{1,0:T(8,128)S(1)}, f32[4,48,128]{2,1,0:T(8,128)S(1)}, bf16[20,240,128]{2,1,0:T(8,128)(2,1)S(1)}, bf16[80,128]{1,0:T(8,128)(2,1)S(1)}) custom-call(s32[4]{0:T(128)S(1)} %pad_add_fusion.flags.refs_0_, bf16[16,80,128]{2,1,0:T(8,128)(2,1)S(1)} %get-tuple-element.43.refs_1_, ...), custom_call_target="tpu_custom_call" | custom-call | tf_op jit(solution)/shard_map/second_middle/pallas_call | solution.py:739
  37.5 2.2 %collective-permute-done.13.refs_4_ = bf16[432,128]{1,0:T(8,128)(2,1)S(1)} collective-permute-done((bf16[432,128]{1,0:T(8,128)(2,1)S(1)}, bf16[432,128]{1,0:T(8,128)(2,1)S(1)}, u32[]{:S(2)}, u32[]{:S(2)}) %collective-permute-start.13) | collective-permute-done | bytes 110624 | tf_op jit(solution)/shard_map/ppermute | solution.py:659
  39.7 4.3 %second_step.1 = bf16[80,16,128]{2,1,0:T(8,128)(2,1)} custom-call(s32[4]{0:T(128)S(1)} %pad_add_fusion.flags.refs_0_, bf16[16,80,128]{2,1,0:T(8,128)(2,1)S(1)} %get-tuple-element.43.refs_1_, s32[16,128]{1,0:T(8,128)S(1)} %copy-done.1, bf16[432,128]{1,0:T(8,128)(2,1)S(1)} %collective-permute-done.12.refs_3_, ...), custom_call_target="tpu_custom_call" | custom-call | tf_op jit(solution)/shard_map/second_step/pallas_call | solution.py:739
  (31 shorter events, 0.2 us)
Async XLA Ops:
  0.0 18.7 %copy-start.1 = (s32[16,128]{1,0:T(8,128)S(1)}, s32[16,128]{1,0:T(8,128)}, u32[]{:S(2)}) copy-start(s32[16,128]{1,0:T(8,128)} %refs_2_.3) | copy-start | bytes 24580
  0.0 18.7 %copy-start.2 = (f32[2,4,80]{2,1,0:T(4,128)S(1)}, f32[2,4,80]{2,1,0:T(4,128)}, u32[]{:S(2)}) copy-start(f32[2,4,80]{2,1,0:T(4,128)} %refs_14_.1) | copy-start | bytes 7684
  0.0 18.7 %copy-start = (bf16[80,384]{1,0:T(8,128)(2,1)S(1)}, bf16[80,384]{1,0:T(8,128)(2,1)}, u32[]{:S(2)}) copy-start(bf16[80,384]{1,0:T(8,128)(2,1)} %refs_13_.3) | copy-start | bytes 184324
  2.2 7.1 %collective-permute-start = (bf16[4,16,128]{2,1,0:T(8,128)(2,1)S(1)}, bf16[4,16,128]{2,1,0:T(8,128)(2,1)S(1)}, u32[]{:S(2)}, u32[]{:S(2)}) collective-permute-start(bf16[4,16,128]{2,1,0:T(8,128)(2,1)S(1)} %get-tuple-element.30), channel_id=1, source_target_pairs={{0,20},{1,21},{2,22},{3,23},{4,16},{5,17},{6,18},{7,19},{8,28},{9,... | collective-permute-start | bytes 49160 | tf_op jit(solution)/shard_map/ppermute | solution.py:659
  3.4 6.0 %collective-permute-start.2 = (bf16[4,16,128]{2,1,0:T(8,128)(2,1)S(1)}, bf16[4,16,128]{2,1,0:T(8,128)(2,1)S(1)}, u32[]{:S(2)}, u32[]{:S(2)}) collective-permute-start(bf16[4,16,128]{2,1,0:T(8,128)(2,1)S(1)} %get-tuple-element.30), channel_id=1, source_target_pairs={{0,16},{1,17},{2,18},{3,19},{4,24},{5,25},{6,26},{7,27},{8,20},{9,... | collective-permute-start | bytes 49160 | tf_op jit(solution)/shard_map/ppermute | solution.py:659
  5.8 3.6 %collective-permute-start.1 = (bf16[4,16,128]{2,1,0:T(8,128)(2,1)S(1)}, bf16[4,16,128]{2,1,0:T(8,128)(2,1)S(1)}, u32[]{:S(2)}, u32[]{:S(2)}) collective-permute-start(bf16[4,16,128]{2,1,0:T(8,128)(2,1)S(1)} %get-tuple-element.30), channel_id=1, source_target_pairs={{0,16},{1,17},{2,18},{3,19},{4,20},{5,21},{6,22},{7,23},{8,24},{9,... | collective-permute-start | bytes 49160 | tf_op jit(solution)/shard_map/ppermute | solution.py:659
  7.0 3.4 %collective-permute-start.3 = (bf16[256,128]{1,0:T(8,128)(2,1)S(1)}, bf16[256,128]{1,0:T(8,128)(2,1)S(1)}, u32[]{:S(2)}, u32[]{:S(2)}) collective-permute-start(bf16[256,128]{1,0:T(8,128)(2,1)S(1)} %get-tuple-element.31), channel_id=1, source_target_pairs={{0,4},{1,5},{2,6},{3,7},{4,0},{5,1},{6,2},{7,3},{8,12},{9,13},{10,... | collective-permute-start | bytes 196616 | tf_op jit(solution)/shard_map/ppermute | solution.py:659
  7.0 5.3 %collective-permute-start.4 = (bf16[256,128]{1,0:T(8,128)(2,1)S(1)}, bf16[256,128]{1,0:T(8,128)(2,1)S(1)}, u32[]{:S(2)}, u32[]{:S(2)}) collective-permute-start(bf16[256,128]{1,0:T(8,128)(2,1)S(1)} %get-tuple-element.33), channel_id=1, source_target_pairs={{0,0},{1,1},{2,2},{3,3},{4,8},{5,9},{6,10},{7,11},{8,4},{9,5},{10,... | collective-permute-start | bytes 196616 | tf_op jit(solution)/shard_map/ppermute | solution.py:659
  12.3 6.3 %collective-permute-start.6 = (bf16[592,128]{1,0:T(8,128)(2,1)S(1)}, bf16[592,128]{1,0:T(8,128)(2,1)S(1)}, u32[]{:S(2)}, u32[]{:S(2)}) collective-permute-start(bf16[592,128]{1,0:T(8,128)(2,1)S(1)} %constant_dynamic-update-slice_fusion), channel_id=1, source_target_pairs={{0,3},{1,0},{2,1},{3,2},{4,7},{5,4},{6,5},{7,6},{8,11},{9,8},{10,9... | collective-permute-start | bytes 454664 | tf_op jit(solution)/shard_map/ppermute | solution.py:659
  14.8 3.9 %collective-permute-start.5 = (bf16[592,128]{1,0:T(8,128)(2,1)S(1)}, bf16[592,128]{1,0:T(8,128)(2,1)S(1)}, u32[]{:S(2)}, u32[]{:S(2)}) collective-permute-start(bf16[592,128]{1,0:T(8,128)(2,1)S(1)} %constant_dynamic-update-slice_fusion), channel_id=1, source_target_pairs={{0,1},{1,2},{2,3},{3,0},{4,5},{5,6},{6,7},{7,4},{8,9},{9,10},{10,1... | collective-permute-start | bytes 454664 | tf_op jit(solution)/shard_map/ppermute | solution.py:659
  22.3 6.4 %collective-permute-start.7 = (bf16[4,16,128]{2,1,0:T(8,128)(2,1)S(1)}, bf16[4,16,128]{2,1,0:T(8,128)(2,1)S(1)}, u32[]{:S(2)}, u32[]{:S(2)}) collective-permute-start(bf16[4,16,128]{2,1,0:T(8,128)(2,1)S(1)} %get-tuple-element.44), channel_id=1, source_target_pairs={{0,20},{1,21},{2,22},{3,23},{4,16},{5,17},{6,18},{7,19},{8,28},{9,... | collective-permute-start | bytes 49160 | tf_op jit(solution)/shard_map/ppermute | solution.py:659
  22.4 6.3 %collective-permute-start.9 = (bf16[4,16,128]{2,1,0:T(8,128)(2,1)S(1)}, bf16[4,16,128]{2,1,0:T(8,128)(2,1)S(1)}, u32[]{:S(2)}, u32[]{:S(2)}) collective-permute-start(bf16[4,16,128]{2,1,0:T(8,128)(2,1)S(1)} %get-tuple-element.44), channel_id=1, source_target_pairs={{0,16},{1,17},{2,18},{3,19},{4,24},{5,25},{6,26},{7,27},{8,20},{9,... | collective-permute-start | bytes 49160 | tf_op jit(solution)/shard_map/ppermute | solution.py:659
  23.9 4.8 %collective-permute-start.8 = (bf16[4,16,128]{2,1,0:T(8,128)(2,1)S(1)}, bf16[4,16,128]{2,1,0:T(8,128)(2,1)S(1)}, u32[]{:S(2)}, u32[]{:S(2)}) collective-permute-start(bf16[4,16,128]{2,1,0:T(8,128)(2,1)S(1)} %get-tuple-element.44), channel_id=1, source_target_pairs={{0,16},{1,17},{2,18},{3,19},{4,20},{5,21},{6,22},{7,23},{8,24},{9,... | collective-permute-start | bytes 49160 | tf_op jit(solution)/shard_map/ppermute | solution.py:659
  24.4 4.4 %collective-permute-start.10 = (bf16[240,128]{1,0:T(8,128)(2,1)S(1)}, bf16[240,128]{1,0:T(8,128)(2,1)S(1)}, u32[]{:S(2)}, u32[]{:S(2)}) collective-permute-start(bf16[240,128]{1,0:T(8,128)(2,1)S(1)} %get-tuple-element.45), channel_id=1, source_target_pairs={{0,4},{1,5},{2,6},{3,7},{4,0},{5,1},{6,2},{7,3},{8,12},{9,13},{10,... | collective-permute-start | bytes 184328 | tf_op jit(solution)/shard_map/ppermute | solution.py:659
  26.0 5.0 %collective-permute-start.11 = (bf16[240,128]{1,0:T(8,128)(2,1)S(1)}, bf16[240,128]{1,0:T(8,128)(2,1)S(1)}, u32[]{:S(2)}, u32[]{:S(2)}) collective-permute-start(bf16[240,128]{1,0:T(8,128)(2,1)S(1)} %get-tuple-element.47), channel_id=1, source_target_pairs={{0,0},{1,1},{2,2},{3,3},{4,8},{5,9},{6,10},{7,11},{8,4},{9,5},{10,... | collective-permute-start | bytes 184328 | tf_op jit(solution)/shard_map/ppermute | solution.py:659
  31.0 8.7 %collective-permute-start.13 = (bf16[432,128]{1,0:T(8,128)(2,1)S(1)}, bf16[432,128]{1,0:T(8,128)(2,1)S(1)}, u32[]{:S(2)}, u32[]{:S(2)}) collective-permute-start(bf16[432,128]{1,0:T(8,128)(2,1)S(1)} %constant_dynamic-update-slice_fusion.9), channel_id=1, source_target_pairs={{0,3},{1,0},{2,1},{3,2},{4,7},{5,4},{6,5},{7,6},{8,11},{9,8},{10,9... | collective-permute-start | bytes 331784 | tf_op jit(solution)/shard_map/ppermute | solution.py:659
  34.7 5.0 %collective-permute-start.12 = (bf16[432,128]{1,0:T(8,128)(2,1)S(1)}, bf16[432,128]{1,0:T(8,128)(2,1)S(1)}, u32[]{:S(2)}, u32[]{:S(2)}) collective-permute-start(bf16[432,128]{1,0:T(8,128)(2,1)S(1)} %constant_dynamic-update-slice_fusion.9), channel_id=1, source_target_pairs={{0,1},{1,2},{2,3},{3,0},{4,5},{5,6},{6,7},{7,4},{8,9},{9,10},{10,1... | collective-permute-start | bytes 331784 | tf_op jit(solution)/shard_map/ppermute | solution.py:659

commit v5 on v4

--- a/solution.py
+++ b/solution.py
@@ -493,16 +493,25 @@
 def middle_kernel(d, opening, *refs):
     refs = list(refs)
     take = lambda count: [refs.pop(0) for _ in range(count)]
-    flags, state, field_one, beside, field_two, from_one, from_two, own_edges = take(8)
+    flags, state, from_one, from_two, own_edges = take(5)
     if opening:
-        planes, *far_weights = take(6)
+        (planes,) = take(1)
     else:
         (plan_x,) = take(1)
-    part_x, fields_x, rolled, edges = take(4)
+    (gathered,) = take(1)
+    if opening:
+        far_weights = take(5)
+    part_x, fields_x, fields_y, rolled, edges = take(5)
     if opening:
         plan_x, *made_weights = take(4)
-        *raw_weights, sems = take(6)
-        copies = fetch(far_weights, raw_weights, sems)
+    tiles = take(1)[0]
+    raw_weights = take(5) if opening else []
+    (sems,) = take(1)
+    copies = fetch(
+        [gathered.at[flags[4 + index]] for index in range(9)] + (far_weights if opening else []),
+        [tiles.at[index] for index in range(9)] + raw_weights,
+        sems,
+    )
     rows, tall = d.rows, d.tall
     is_ocean = flags[0]
     up_and_down = ends(flags)
@@ -521,11 +530,17 @@
         for plane in range(2 * NK):
             plan_x[plane * tall + 2 : plane * tall + 2 + rows, :] = planes[plane].astype(F32)
 
+    for copy in copies[:9]:
+        copy.wait()
+    at_top, at_bottom = flags[1] != 0, flags[2] != 0
     for field in range(NS):
-        pair = up_and_down(field_one[field], field_two[field])
-        fields_x[field, 0:16, :] = pair[0][rows - 16 : rows]
-        fields_x[field, 16 : 16 + rows, :] = beside[field].astype(F32)
-        fields_x[field, 16 + rows : 32 + rows, :] = pair[1][0:16]
+        for target, columns in ((fields_x, [tiles[3 * row + 1, field] for row in range(3)]),
+                                (fields_y, [place_columns(tiles[3 * row, field], tiles[3 * row + 2, field])
+                                            for row in range(3)])):
+            above, own, below = [values.astype(F32) for values in columns]
+            target[field, 0:16, :] = jnp.where(at_top, 0.0, above)[rows - 16 : rows]
+            target[field, 16 : 16 + rows, :] = own
+            target[field, 16 + rows : 32 + rows, :] = jnp.where(at_bottom, 0.0, below)[0:16]
 
     @pl.when(is_ocean == 0)
     def _():
@@ -541,7 +556,7 @@
         put_edges(edges, 0, joined, d)
 
     if opening:
-        for copy in copies:
+        for copy in copies[9:]:
             copy.wait()
         prepare(*raw_weights, *made_weights, is_ocean)
 
@@ -550,7 +565,7 @@
     refs = list(refs)
     take = lambda count: [refs.pop(0) for _ in range(count)]
     flags, state, wet, from_left, from_right = take(5)
-    part_x, fields_x, rolled, edges, plan_x, air_in, first, second, atm_out = take(9)
+    part_x, fields_x, fields_y, rolled, edges, plan_x, air_in, first, second, atm_out = take(10)
     if not opening:
         (plan_y,) = take(1)
     if not closing:
@@ -560,7 +575,7 @@
         fields, new_edges, one, two = take(4)
     if opening:
         (plan_y,) = take(1)
-    fields_y, forcing_x, forcing_y, stack, hidden, side, raw = take(7)
+    forcing_x, forcing_y, stack, hidden, side, raw = take(6)
     rows, tall = d.rows, d.tall
     is_ocean, at_top, at_bottom = flags[0], flags[1], flags[2]
     up_and_down = ends(flags)
@@ -570,7 +585,7 @@
         @pl.when(is_ocean != 0)
         def _():
             plan_y[...] = jnp.zeros_like(plan_y)
-            side_base = 4 * (rows + 32) + 3 * d.edge_rows
+            side_base = 3 * d.edge_rows
             pair = [
                 place_columns(from_left[at : at + 16, :], from_right[at : at + 16, :])
                 for at in (side_base, side_base + 16 + 2 * NK * rows)
@@ -584,20 +599,6 @@
                     from_left[at : at + rows, :], from_right[at : at + rows, :]
                 )
 
-    lower_at = 64 + 4 * rows
-    for field in range(NS):
-        start = 64 + field * rows
-        fields_y[field, 16 : 16 + rows, :] = place_columns(
-            from_left[start : start + rows, :], from_right[start : start + rows, :]
-        )
-        pair = [
-            place_columns(from_left[at : at + 16, :], from_right[at : at + 16, :])
-            for at in (field * 16, lower_at + field * 16)
-        ]
-        pair = up_and_down(*pair)
-        fields_y[field, 0:16, :] = pair[0]
-        fields_y[field, 16 + rows : 32 + rows, :] = pair[1]
-
     def put(row, values):
         if closing:
             raw[pl.ds(row, CH, stride=rows), :] = values
@@ -616,7 +617,7 @@
         regrid_beside(
             fields_x, fields_y, plan_x, plan_y, part_x, forcing_x, forcing_y, 0, d.tiles, tall, True
         )
-        at = 4 * (rows + 32)
+        at = 0
         size = d.edge_rows
         joined = []
         for ref in (from_left, from_right):
@@ -659,46 +660,30 @@
     return lax.ppermute(x, names, pairs)
 
 
-def swap_rows(x, turn, across):
+def swap_rows(x, turn):
     count = lax.axis_size("lat")
 
     def move(group, lat, lon):
         other = ((lat + turn) ^ 1) - turn
-        to = 1 - group if across else group
-        return to, other if 0 <= other < count else lat, lon
+        return group, other if 0 <= other < count else lat, lon
 
     return send(x, move)
 
 
 def exchange(fields, own_edges, one, two, planes, d):
     rows = d.rows
-    beside = send(fields, lambda g, i, j: (1 - g, i, j))
-    field_one = swap_rows(fields, 0, True)
-    field_two = swap_rows(fields, 1, True)
-    from_one = swap_rows(one, 0, False)
-    from_two = swap_rows(two, 1, False)
+    gathered = lax.all_gather(fields, ("grp", "lat", "lon"))
+    from_one = swap_rows(one, 0)
+    from_two = swap_rows(two, 1)
     edge_at = slice(2 * CH, d.strip)
-    odd = lax.axis_index("lat") % 2
-    if rows == 16:
-        outer = [field_one, field_two]
-    else:
-        last = [field[:, rows - 16 :] for field in (field_one, field_two)]
-        first = [field[:, :16] for field in (field_one, field_two)]
-        outer = [jnp.where(odd == 1, last[0], first[0]), jnp.where(odd == 1, first[1], last[1])]
-    packed = [
-        outer[0].reshape(64, 128),
-        beside.reshape(4 * rows, 128),
-        outer[1].reshape(64, 128),
-        from_one[edge_at],
-        own_edges,
-        from_two[edge_at],
-    ]
+    packed = [from_one[edge_at], own_edges, from_two[edge_at]]
     if planes is not None:
         packed += [from_one[d.strip :], planes.reshape(2 * NK * rows, 128), from_two[d.strip :]]
     packed = jnp.concatenate(packed, axis=0)
     from_left = send(packed, lambda g, i, j: (g, i, j + 1))
     from_right = send(packed, lambda g, i, j: (g, i, j - 1))
-    return (field_one, beside, field_two, from_one, from_two), (from_left, from_right)
+    gathered, packed = lax.optimization_barrier((gathered, packed))
+    return (from_one, from_two), (from_left, from_right), gathered
 
 
 def local(
@@ -710,9 +695,14 @@
     d = Dims(rows)
     group = lax.axis_index("grp")
     lat = lax.axis_index("lat")
-    flags = jnp.stack(
-        [group, lat == 0, lat == lax.axis_size("lat") - 1, lat % 2]
-    ).astype(jnp.int32)
+    lon = lax.axis_index("lon")
+    counts = lax.axis_size("lat"), lax.axis_size("lon")
+    flags = [group, lat == 0, lat == counts[0] - 1, lat % 2]
+    for row in range(-1, 2):
+        for column in range(-1, 2):
+            at = (1 - group) * counts[0] + jnp.clip(lat + row, 0, counts[0] - 1)
+            flags.append(at * counts[1] + (lon + column) % counts[1])
+    flags = jnp.stack([flag.astype(jnp.int32) for flag in flags])
     raw_weights = (
         atm_in.T,
         atm_bias.reshape(HA // 128, 128),
@@ -731,9 +721,10 @@
     turned = pltpu.VMEM((CH * rows, 128), F32)
 
     def call(kernel, operands, outs, scratch, name, far=()):
-        scratch = scratch + [pltpu.VMEM(x.shape, x.dtype) for x in far]
+        gathers = name.endswith("middle")
+        scratch = scratch + [pltpu.VMEM(x.shape, x.dtype) for x in far[gathers:]]
         if far:
-            scratch.append(pltpu.SemaphoreType.DMA((len(far),)))
+            scratch.append(pltpu.SemaphoreType.DMA((len(far) + 8 * gathers,)))
 
         far = [pltpu.with_memory_space_constraint(x, pltpu.HBM) for x in far]
         return pl.pallas_call(
@@ -759,12 +750,13 @@
     between = [
         shape(NS * d.tall, 128, dtype=F32),
         shape(NS, rows + 32, 128, dtype=F32),
+        shape(NS, rows + 32, 128, dtype=F32),
         shape(rows + 4, 3 * CH, 128),
         shape(d.edge_rows, 128),
     ]
     made = [shape(HA, 128), shape(HIDK, 768), shape(9 * CH, HIDP)]
+    tiles = [pltpu.VMEM((9, NS, rows, 128), BF16)]
     scratch = [
-        pltpu.VMEM((NS, rows + 32, 128), F32),
         pltpu.VMEM((d.tall * 8, 128), F32),
         pltpu.VMEM((d.tall * 8, 128), F32),
         pltpu.VMEM((rows + 4, 256, 128), BF16),
@@ -772,14 +764,14 @@
         pltpu.VMEM((768, d.edge), BF16),
     ]
 
-    vertical, horizontal = exchange(fields, edges, one, two, planes, d)
+    vertical, horizontal, gathered = exchange(fields, edges, one, two, planes, d)
     *shared, plan_x, air_in, first, second = call(
         functools.partial(middle_kernel, d, True),
         (state, *vertical, edges, planes),
         between + [plan] + made,
-        [],
+        tiles,
         "first_middle",
-        raw_weights,
+        (gathered, *raw_weights),
     )
     weights = (air_in, first, second, atm_out)
     state, fields, edges, one, two, plan_y = call(
@@ -790,13 +782,14 @@
         "first_step",
     )
 
-    vertical, horizontal = exchange(fields, edges, one, two, None, d)
+    vertical, horizontal, gathered = exchange(fields, edges, one, two, None, d)
     shared = call(
         functools.partial(middle_kernel, d, False),
         (state, *vertical, edges, plan_x),
         between,
-        [],
+        tiles,
         "second_middle",
+        (gathered,),
     )
     (state,) = call(
         functools.partial(step_kernel, d, False, True),

time: 44.1 us -> 118 us (2.68)
  the two profiles are of different devices: /device:TPU:13 before, /device:TPU:0 now
where the time goes in v5:
time: 118 us; the launch traced here: 117 us
  blocking collectives  88.1 us (75%)
  Pallas kernels  15.3 us (13%)
  starting transfers between devices  8.06 us (7%)
  waiting for transfers between devices  5.14 us (4%)
    all_gather x2, blocking collectives, exchange(): gathered = lax.all_gather(fields, ('grp', 'lat', 'lon'))  88.1 us
    pallas_call x5, Pallas kernels, call(): pl.pallas_call(kernel, out_shape=outs, in_specs=[SMEM] + [VMEM] * len(ope...  15.3 us
    ppermute x8, starting transfers between devices, send(): return lax.ppermute(x, names, pairs)  8.06 us
    ppermute x8, waiting for transfers between devices, send(): return lax.ppermute(x, names, pairs)  5.14 us
  transfers between devices with their start and end apart: 8, of which 2 were waited for; matrix products, arithmetic and copies ran while one was open for 0% of the time, Pallas kernels for 5%

profile of v5, /device:TPU:0, one launch (start us, length us, event | category | flops | bytes accessed | tf_op | source)
XLA Modules:
  0.0 117.0 jit_solution(5003325255669665923)
XLA Ops:
  0.0 0.1 stack.63.flags.refs_0_
  0.1 2.1 %start.1 = (bf16[16,80,128]{2,1,0:T(8,128)(2,1)S(1)}, bf16[8,16,128]{2,1,0:T(8,128)(2,1)S(1)}, bf16[4,16,128]{2,1,0:T(8,128)(2,1)S(1)}, bf16[80,128]{1,0:T(8,128...) custom-call(s32[13]{0:T(128)S(1)} %stack.63.flags.refs_0_, bf16[80,16,128]{2,1,0:T(8,128)(2,1)} %bitcast.30, ...), custom_call_target="tpu_custom_call" | custom-call | tf_op jit(solution)/shard_map/start/pallas_call | solution.py:730
  2.2 3.1 %collective-permute-start = (bf16[256,128]{1,0:T(8,128)(2,1)S(1)}, bf16[256,128]{1,0:T(8,128)(2,1)S(1)}, u32[]{:S(2)}, u32[]{:S(2)}) collective-permute-start(bf16[256,128]{1,0:T(8,128)(2,1)S(1)} %get-tuple-element.34), channel_id=1, source_target_pairs={{0,4},{1,5},{2,6},{3,7},{4,0},{5,1},{6,2},{7,3},{8,12},{9,13},{10,... | collective-permute-start | bytes 196616 | tf_op jit(solution)/shard_map/ppermute | solution.py:660
  5.3 0.7 collective-permute-start.1
  6.0 1.6 %collective-permute-done.refs_2_ = bf16[256,128]{1,0:T(8,128)(2,1)S(1)} collective-permute-done((bf16[256,128]{1,0:T(8,128)(2,1)S(1)}, bf16[256,128]{1,0:T(8,128)(2,1)S(1)}, u32[]{:S(2)}, u32[]{:S(2)}) %collective-permute-start) | collective-permute-done | bytes 65568 | tf_op jit(solution)/shard_map/ppermute | solution.py:660
  7.6 0.0 copy-start
  7.6 0.0 copy-start.1
  7.6 0.0 copy-start.2
  7.7 0.1 collective-permute-start.2
  7.7 1.7 %collective-permute-start.3 = (bf16[400,128]{1,0:T(8,128)(2,1)S(1)}, bf16[400,128]{1,0:T(8,128)(2,1)S(1)}, u32[]{:S(2)}, u32[]{:S(2)}) collective-permute-start(bf16[400,128]{1,0:T(8,128)(2,1)S(1)} %constant_dynamic-update-slice_fusion), channel_id=1, source_target_pairs={{0,3},{1,0},{2,1},{3,2},{4,7},{5,4},{6,5},{7,6},{8,11},{9,8},{10,9... | collective-permute-start | bytes 307208 | tf_op jit(solution)/shard_map/ppermute | solution.py:660
  9.5 46.4 %all-gather = bf16[128,16,128]{2,1,0:T(8,128)(2,1)} all-gather(bf16[4,16,128]{2,1,0:T(8,128)(2,1)S(1)} %get-tuple-element.38), channel_id=2, replica_groups=mesh['grp'=2,'lat'=4,'lon'=4] {'grp','lat','lon'}, dimensions={0}, use_global_device_ids=true | all-gather | bytes 540672 | tf_op jit(solution)/shard_map/all_gather | solution.py:675
  55.9 2.8 %first_middle.1 = (f32[96,128]{1,0:T(8,128)S(1)}, f32[4,48,128]{2,1,0:T(8,128)S(1)}, f32[4,48,128]{2,1,0:T(8,128)S(1)}, bf16[20,240,128]{2,1,0:T(8,128)(2,1)S(1)...) custom-call(s32[13]{0:T(128)S(1)} %stack.63.flags.refs_0_, ...), custom_call_target="tpu_custom_call" | custom-call | tf_op jit(solution)/shard_map/first_middle/pallas_call | solution.py:730
  58.7 0.0 collective-permute-done.2.refs_3_
  58.7 3.6 %first_step.1 = (bf16[16,80,128]{2,1,0:T(8,128)(2,1)S(1)}, bf16[4,16,128]{2,1,0:T(8,128)(2,1)S(1)}, bf16[80,128]{1,0:T(8,128)(2,1)S(1)}, bf16[240,128]{1,0:T(8,1...) custom-call(s32[13]{0:T(128)S(1)} %stack.63.flags.refs_0_, ...), custom_call_target="tpu_custom_call" | custom-call | tf_op jit(solution)/shard_map/first_step/pallas_call | solution.py:730
  62.3 0.1 collective-permute-start.4
  62.4 0.7 collective-permute-start.5
  63.1 3.5 %collective-permute-done.4.refs_2_ = bf16[240,128]{1,0:T(8,128)(2,1)S(1)} collective-permute-done((bf16[240,128]{1,0:T(8,128)(2,1)S(1)}, bf16[240,128]{1,0:T(8,128)(2,1)S(1)}, u32[]{:S(2)}, u32[]{:S(2)}) %collective-permute-start.4) | collective-permute-done | bytes 61472 | tf_op jit(solution)/shard_map/ppermute | solution.py:660
  66.6 0.0 collective-permute-done.5.refs_3_
  66.6 0.1 collective-permute-start.6
  66.7 1.7 %collective-permute-start.7 = (bf16[240,128]{1,0:T(8,128)(2,1)S(1)}, bf16[240,128]{1,0:T(8,128)(2,1)S(1)}, u32[]{:S(2)}, u32[]{:S(2)}) collective-permute-start(bf16[240,128]{1,0:T(8,128)(2,1)S(1)} %pad_maximum_fusion), channel_id=1, source_target_pairs={{0,3},{1,0},{2,1},{3,2},{4,7},{5,4},{6,5},{7,6},{8,11},{9,8},{10,9... | collective-permute-start | bytes 184328 | tf_op jit(solution)/shard_map/ppermute | solution.py:660
  68.4 41.6 %all-gather.1 = bf16[128,16,128]{2,1,0:T(8,128)(2,1)} all-gather(bf16[4,16,128]{2,1,0:T(8,128)(2,1)S(1)} %get-tuple-element.53), channel_id=3, replica_groups=mesh['grp'=2,'lat'=4,'lon'=4] {'grp','lat','lon'}, dimensions={0}, use_global_device_ids=true | all-gather | bytes 540672 | tf_op jit(solution)/shard_map/all_gather | solution.py:675
  110.1 2.6 %second_middle.1 = (f32[96,128]{1,0:T(8,128)S(1)}, f32[4,48,128]{2,1,0:T(8,128)S(1)}, f32[4,48,128]{2,1,0:T(8,128)S(1)}, bf16[20,240,128]{2,1,0:T(8,128)(2,1)S(1)}, bf16[80,128]{1,0:T(8,128)(2,1)S(1)}) custom-call(s32[13]{0:T(128)S(1)} %stack.63.flags.refs_0_, bf16[16,80,128]{2,1,0:T(8,128)(2,1)S(1)} %get-tuple-element.49.refs_1_, ...), custom_call_target="tpu_custom_call" | custom-call | tf_op jit(solution)/shard_map/second_middle/pallas_call | solution.py:730
  112.7 0.0 collective-permute-done.6.refs_3_
  112.7 4.3 %second_step.1 = bf16[80,16,128]{2,1,0:T(8,128)(2,1)} custom-call(s32[13]{0:T(128)S(1)} %stack.63.flags.refs_0_, bf16[16,80,128]{2,1,0:T(8,128)(2,1)S(1)} %get-tuple-element.49.refs_1_, s32[16,128]{1,0:T(8,128)S(1)} %copy-done.1, bf16[240,128]{1,0:T(8,128)(2,1)S(1)} %collective-permute-done.6.refs_3_, bf16[240,128]{1,0:T(8,128)(2,1)S(1)} %collective-permute-done.7.refs_4_, ...), custom_call_target="tpu_custom_call" | custom-call | tf_op jit(solution)/shard_map/second_step/pallas_call | solution.py:730
  (15 shorter events, 0.1 us)
Async XLA Ops:
  2.2 5.3 %collective-permute-start = (bf16[256,128]{1,0:T(8,128)(2,1)S(1)}, bf16[256,128]{1,0:T(8,128)(2,1)S(1)}, u32[]{:S(2)}, u32[]{:S(2)}) collective-permute-start(bf16[256,128]{1,0:T(8,128)(2,1)S(1)} %get-tuple-element.34), channel_id=1, source_target_pairs={{0,4},{1,5},{2,6},{3,7},{4,0},{5,1},{6,2},{7,3},{8,12},{9,13},{10,... | collective-permute-start | bytes 196616 | tf_op jit(solution)/shard_map/ppermute | solution.py:660
  5.3 2.3 %collective-permute-start.1 = (bf16[256,128]{1,0:T(8,128)(2,1)S(1)}, bf16[256,128]{1,0:T(8,128)(2,1)S(1)}, u32[]{:S(2)}, u32[]{:S(2)}) collective-permute-start(bf16[256,128]{1,0:T(8,128)(2,1)S(1)} %get-tuple-element.36), channel_id=1, source_target_pairs={{0,0},{1,1},{2,2},{3,3},{4,8},{5,9},{6,10},{7,11},{8,4},{9,5},{10,... | collective-permute-start | bytes 196616 | tf_op jit(solution)/shard_map/ppermute | solution.py:660
  7.6 51.1 %copy-start = (bf16[80,384]{1,0:T(8,128)(2,1)S(1)}, bf16[80,384]{1,0:T(8,128)(2,1)}, u32[]{:S(2)}) copy-start(bf16[80,384]{1,0:T(8,128)(2,1)} %refs_14_.3) | copy-start | bytes 184324
  7.6 51.1 %copy-start.1 = (s32[16,128]{1,0:T(8,128)S(1)}, s32[16,128]{1,0:T(8,128)}, u32[]{:S(2)}) copy-start(s32[16,128]{1,0:T(8,128)} %refs_2_.3) | copy-start | bytes 24580
  7.6 51.1 %copy-start.2 = (f32[2,4,80]{2,1,0:T(4,128)S(1)}, f32[2,4,80]{2,1,0:T(4,128)}, u32[]{:S(2)}) copy-start(f32[2,4,80]{2,1,0:T(4,128)} %refs_15_.1) | copy-start | bytes 7684
  7.7 51.0 %collective-permute-start.2 = (bf16[400,128]{1,0:T(8,128)(2,1)S(1)}, bf16[400,128]{1,0:T(8,128)(2,1)S(1)}, u32[]{:S(2)}, u32[]{:S(2)}) collective-permute-start(bf16[400,128]{1,0:T(8,128)(2,1)S(1)} %constant_dynamic-update-slice_fusion), channel_id=1, source_target_pairs={{0,1},{1,2},{2,3},{3,0},{4,5},{5,6},{6,7},{7,4},{8,9},{9,10},{10,1... | collective-permute-start | bytes 307208 | tf_op jit(solution)/shard_map/ppermute | solution.py:660
  7.7 51.0 %collective-permute-start.3 = (bf16[400,128]{1,0:T(8,128)(2,1)S(1)}, bf16[400,128]{1,0:T(8,128)(2,1)S(1)}, u32[]{:S(2)}, u32[]{:S(2)}) collective-permute-start(bf16[400,128]{1,0:T(8,128)(2,1)S(1)} %constant_dynamic-update-slice_fusion), channel_id=1, source_target_pairs={{0,3},{1,0},{2,1},{3,2},{4,7},{5,4},{6,5},{7,6},{8,11},{9,8},{10,9... | collective-permute-start | bytes 307208 | tf_op jit(solution)/shard_map/ppermute | solution.py:660
  62.3 4.3 %collective-permute-start.4 = (bf16[240,128]{1,0:T(8,128)(2,1)S(1)}, bf16[240,128]{1,0:T(8,128)(2,1)S(1)}, u32[]{:S(2)}, u32[]{:S(2)}) collective-permute-start(bf16[240,128]{1,0:T(8,128)(2,1)S(1)} %get-tuple-element.50), channel_id=1, source_target_pairs={{0,4},{1,5},{2,6},{3,7},{4,0},{5,1},{6,2},{7,3},{8,12},{9,13},{10,... | collective-permute-start | bytes 184328 | tf_op jit(solution)/shard_map/ppermute | solution.py:660
  62.4 4.2 %collective-permute-start.5 = (bf16[240,128]{1,0:T(8,128)(2,1)S(1)}, bf16[240,128]{1,0:T(8,128)(2,1)S(1)}, u32[]{:S(2)}, u32[]{:S(2)}) collective-permute-start(bf16[240,128]{1,0:T(8,128)(2,1)S(1)} %get-tuple-element.52), channel_id=1, source_target_pairs={{0,0},{1,1},{2,2},{3,3},{4,8},{5,9},{6,10},{7,11},{8,4},{9,5},{10,... | collective-permute-start | bytes 184328 | tf_op jit(solution)/shard_map/ppermute | solution.py:660
  66.6 46.0 %collective-permute-start.6 = (bf16[240,128]{1,0:T(8,128)(2,1)S(1)}, bf16[240,128]{1,0:T(8,128)(2,1)S(1)}, u32[]{:S(2)}, u32[]{:S(2)}) collective-permute-start(bf16[240,128]{1,0:T(8,128)(2,1)S(1)} %pad_maximum_fusion), channel_id=1, source_target_pairs={{0,1},{1,2},{2,3},{3,0},{4,5},{5,6},{6,7},{7,4},{8,9},{9,10},{10,1... | collective-permute-start | bytes 184328 | tf_op jit(solution)/shard_map/ppermute | solution.py:660
  66.7 46.0 %collective-permute-start.7 = (bf16[240,128]{1,0:T(8,128)(2,1)S(1)}, bf16[240,128]{1,0:T(8,128)(2,1)S(1)}, u32[]{:S(2)}, u32[]{:S(2)}) collective-permute-start(bf16[240,128]{1,0:T(8,128)(2,1)S(1)} %pad_maximum_fusion), channel_id=1, source_target_pairs={{0,3},{1,0},{2,1},{3,2},{4,7},{5,4},{6,5},{7,6},{8,11},{9,8},{10,9... | collective-permute-start | bytes 184328 | tf_op jit(solution)/shard_map/ppermute | solution.py:660

commit v6 on v4

--- a/solution.py
+++ b/solution.py
@@ -664,8 +664,9 @@
 
     def move(group, lat, lon):
         other = ((lat + turn) ^ 1) - turn
-        to = 1 - group if across else group
-        return to, other if 0 <= other < count else lat, lon
+        if not 0 <= other < count:
+            return 1 - group, lat, lon
+        return (1 - group if across else group), other, lon
 
     return send(x, move)
 

time: 44.1 us -> 42.6 us (0.966)
  the two profiles are of different devices: /device:TPU:13 before, /device:TPU:0 now
where the time goes in v6:
time: 42.6 us; the launch traced here: 42.4 us
  starting transfers between devices  15.1 us (35%)
  Pallas kernels  13.5 us (32%)
  waiting for transfers between devices  13.5 us (32%)
    ppermute x14, starting transfers between devices, send(): return lax.ppermute(x, names, pairs)  15.1 us
    ppermute x14, waiting for transfers between devices, send(): return lax.ppermute(x, names, pairs)  13.5 us
    pallas_call x5, Pallas kernels, call(): pl.pallas_call(kernel, out_shape=outs, in_specs=[SMEM] + [VMEM] * len(ope...  13.5 us
  transfers between devices with their start and end apart: 14, of which 9 were waited for; matrix products, arithmetic and copies ran while one was open for 0% of the time, Pallas kernels for 8%

profile of v6, /device:TPU:0, one launch (start us, length us, event | category | flops | bytes accessed | tf_op | source)
XLA Modules:
  0.0 42.4 jit_solution(11654741843075944825)
XLA Ops:
  0.1 2.1 %start.1 = (bf16[16,80,128]{2,1,0:T(8,128)(2,1)S(1)}, bf16[8,16,128]{2,1,0:T(8,128)(2,1)S(1)}, bf16[4,16,128]{2,1,0:T(8,128)(2,1)S(1)}, bf16[80,128]{1,0:T(8,128...) custom-call(s32[4]{0:T(128)S(1)} %pad_add_fusion.flags.refs_0_, bf16[80,16,128]{2,1,0:T(8,128)(2,1)} %bitcast.29, ...), custom_call_target="tpu_custom_call" | custom-call | tf_op jit(solution)/shard_map/start/pallas_call | solution.py:740
  2.2 4.0 %collective-permute-start = (bf16[4,16,128]{2,1,0:T(8,128)(2,1)S(1)}, bf16[4,16,128]{2,1,0:T(8,128)(2,1)S(1)}, u32[]{:S(2)}, u32[]{:S(2)}) collective-permute-start(bf16[4,16,128]{2,1,0:T(8,128)(2,1)S(1)} %get-tuple-element.30), channel_id=1, source_target_pairs={{0,20},{1,21},{2,22},{3,23},{4,16},{5,17},{6,18},{7,19},{8,28},{9,... | collective-permute-start | bytes 49160 | tf_op jit(solution)/shard_map/ppermute | solution.py:659
  6.3 0.5 %collective-permute-start.2 = (bf16[4,16,128]{2,1,0:T(8,128)(2,1)S(1)}, bf16[4,16,128]{2,1,0:T(8,128)(2,1)S(1)}, u32[]{:S(2)}, u32[]{:S(2)}) collective-permute-start(bf16[4,16,128]{2,1,0:T(8,128)(2,1)S(1)} %get-tuple-element.30), channel_id=1, source_target_pairs={{0,16},{1,17},{2,18},{3,19},{4,24},{5,25},{6,26},{7,27},{8,20},{9,... | collective-permute-start | bytes 49160 | tf_op jit(solution)/shard_map/ppermute | solution.py:659
  6.8 1.5 %collective-permute-start.1 = (bf16[4,16,128]{2,1,0:T(8,128)(2,1)S(1)}, bf16[4,16,128]{2,1,0:T(8,128)(2,1)S(1)}, u32[]{:S(2)}, u32[]{:S(2)}) collective-permute-start(bf16[4,16,128]{2,1,0:T(8,128)(2,1)S(1)} %get-tuple-element.30), channel_id=1, source_target_pairs={{0,16},{1,17},{2,18},{3,19},{4,20},{5,21},{6,22},{7,23},{8,24},{9,... | collective-permute-start | bytes 49160 | tf_op jit(solution)/shard_map/ppermute | solution.py:659
  8.3 2.6 %collective-permute-start.3 = (bf16[256,128]{1,0:T(8,128)(2,1)S(1)}, bf16[256,128]{1,0:T(8,128)(2,1)S(1)}, u32[]{:S(2)}, u32[]{:S(2)}) collective-permute-start(bf16[256,128]{1,0:T(8,128)(2,1)S(1)} %get-tuple-element.31), channel_id=1, source_target_pairs={{0,4},{1,5},{2,6},{3,7},{4,0},{5,1},{6,2},{7,3},{8,12},{9,13},{10,... | collective-permute-start | bytes 196616 | tf_op jit(solution)/shard_map/ppermute | solution.py:659
  10.9 0.5 %collective-permute-start.4 = (bf16[256,128]{1,0:T(8,128)(2,1)S(1)}, bf16[256,128]{1,0:T(8,128)(2,1)S(1)}, u32[]{:S(2)}, u32[]{:S(2)}) collective-permute-start(bf16[256,128]{1,0:T(8,128)(2,1)S(1)} %get-tuple-element.33), channel_id=1, source_target_pairs={{0,16},{1,17},{2,18},{3,19},{4,8},{5,9},{6,10},{7,11},{8,4},{9,5},... | collective-permute-start | bytes 196616 | tf_op jit(solution)/shard_map/ppermute | solution.py:659
  11.4 1.7 %collective-permute-done.3.refs_5_ = bf16[256,128]{1,0:T(8,128)(2,1)S(1)} collective-permute-done((bf16[256,128]{1,0:T(8,128)(2,1)S(1)}, bf16[256,128]{1,0:T(8,128)(2,1)S(1)}, u32[]{:S(2)}, u32[]{:S(2)}) %collective-permute-start.3) | collective-permute-done | bytes 65568 | tf_op jit(solution)/shard_map/ppermute | solution.py:659
  13.1 2.0 %collective-permute-done.4.refs_6_ = bf16[256,128]{1,0:T(8,128)(2,1)S(1)} collective-permute-done((bf16[256,128]{1,0:T(8,128)(2,1)S(1)}, bf16[256,128]{1,0:T(8,128)(2,1)S(1)}, u32[]{:S(2)}, u32[]{:S(2)}) %collective-permute-start.4) | collective-permute-done | bytes 65568 | tf_op jit(solution)/shard_map/ppermute | solution.py:659
  15.7 1.9 %first_middle.1 = (f32[96,128]{1,0:T(8,128)S(1)}, f32[4,48,128]{2,1,0:T(8,128)S(1)}, bf16[20,240,128]{2,1,0:T(8,128)(2,1)S(1)}, bf16[80,128]{1,0:T(8,128)(2,1)S(...) custom-call(s32[4]{0:T(128)S(1)} %pad_add_fusion.flags.refs_0_, ...), custom_call_target="tpu_custom_call" | custom-call | tf_op jit(solution)/shard_map/first_middle/pallas_call | solution.py:740
  17.6 0.9 %collective-permute-done.6.refs_4_ = bf16[592,128]{1,0:T(8,128)(2,1)S(1)} collective-permute-done((bf16[592,128]{1,0:T(8,128)(2,1)S(1)}, bf16[592,128]{1,0:T(8,128)(2,1)S(1)}, u32[]{:S(2)}, u32[]{:S(2)}) %collective-permute-start.6) | collective-permute-done | bytes 151584 | tf_op jit(solution)/shard_map/ppermute | solution.py:659
  18.6 3.0 %collective-permute-done.5.refs_3_ = bf16[592,128]{1,0:T(8,128)(2,1)S(1)} collective-permute-done((bf16[592,128]{1,0:T(8,128)(2,1)S(1)}, bf16[592,128]{1,0:T(8,128)(2,1)S(1)}, u32[]{:S(2)}, u32[]{:S(2)}) %collective-permute-start.5) | collective-permute-done | bytes 151584 | tf_op jit(solution)/shard_map/ppermute | solution.py:659
  21.5 3.6 %first_step.1 = (bf16[16,80,128]{2,1,0:T(8,128)(2,1)S(1)}, bf16[4,16,128]{2,1,0:T(8,128)(2,1)S(1)}, bf16[80,128]{1,0:T(8,128)(2,1)S(1)}, bf16[240,128]{1,0:T(8,1...) custom-call(s32[4]{0:T(128)S(1)} %pad_add_fusion.flags.refs_0_, ...), custom_call_target="tpu_custom_call" | custom-call | tf_op jit(solution)/shard_map/first_step/pallas_call | solution.py:740
  25.2 0.8 %collective-permute-start.7 = (bf16[4,16,128]{2,1,0:T(8,128)(2,1)S(1)}, bf16[4,16,128]{2,1,0:T(8,128)(2,1)S(1)}, u32[]{:S(2)}, u32[]{:S(2)}) collective-permute-start(bf16[4,16,128]{2,1,0:T(8,128)(2,1)S(1)} %get-tuple-element.44), channel_id=1, source_target_pairs={{0,20},{1,21},{2,22},{3,23},{4,16},{5,17},{6,18},{7,19},{8,28},{9,... | collective-permute-start | bytes 49160 | tf_op jit(solution)/shard_map/ppermute | solution.py:659
  26.0 0.7 %collective-permute-start.9 = (bf16[4,16,128]{2,1,0:T(8,128)(2,1)S(1)}, bf16[4,16,128]{2,1,0:T(8,128)(2,1)S(1)}, u32[]{:S(2)}, u32[]{:S(2)}) collective-permute-start(bf16[4,16,128]{2,1,0:T(8,128)(2,1)S(1)} %get-tuple-element.44), channel_id=1, source_target_pairs={{0,16},{1,17},{2,18},{3,19},{4,24},{5,25},{6,26},{7,27},{8,20},{9,... | collective-permute-start | bytes 49160 | tf_op jit(solution)/shard_map/ppermute | solution.py:659
  26.7 1.3 %collective-permute-start.8 = (bf16[4,16,128]{2,1,0:T(8,128)(2,1)S(1)}, bf16[4,16,128]{2,1,0:T(8,128)(2,1)S(1)}, u32[]{:S(2)}, u32[]{:S(2)}) collective-permute-start(bf16[4,16,128]{2,1,0:T(8,128)(2,1)S(1)} %get-tuple-element.44), channel_id=1, source_target_pairs={{0,16},{1,17},{2,18},{3,19},{4,20},{5,21},{6,22},{7,23},{8,24},{9,... | collective-permute-start | bytes 49160 | tf_op jit(solution)/shard_map/ppermute | solution.py:659
  28.0 1.5 %collective-permute-start.10 = (bf16[240,128]{1,0:T(8,128)(2,1)S(1)}, bf16[240,128]{1,0:T(8,128)(2,1)S(1)}, u32[]{:S(2)}, u32[]{:S(2)}) collective-permute-start(bf16[240,128]{1,0:T(8,128)(2,1)S(1)} %get-tuple-element.45), channel_id=1, source_target_pairs={{0,4},{1,5},{2,6},{3,7},{4,0},{5,1},{6,2},{7,3},{8,12},{9,13},{10,... | collective-permute-start | bytes 184328 | tf_op jit(solution)/shard_map/ppermute | solution.py:659
  29.5 0.5 %collective-permute-start.11 = (bf16[240,128]{1,0:T(8,128)(2,1)S(1)}, bf16[240,128]{1,0:T(8,128)(2,1)S(1)}, u32[]{:S(2)}, u32[]{:S(2)}) collective-permute-start(bf16[240,128]{1,0:T(8,128)(2,1)S(1)} %get-tuple-element.47), channel_id=1, source_target_pairs={{0,16},{1,17},{2,18},{3,19},{4,8},{5,9},{6,10},{7,11},{8,4},{9,5},... | collective-permute-start | bytes 184328 | tf_op jit(solution)/shard_map/ppermute | solution.py:659
  30.5 1.8 %collective-permute-done.10.refs_5_ = bf16[240,128]{1,0:T(8,128)(2,1)S(1)} collective-permute-done((bf16[240,128]{1,0:T(8,128)(2,1)S(1)}, bf16[240,128]{1,0:T(8,128)(2,1)S(1)}, u32[]{:S(2)}, u32[]{:S(2)}) %collective-permute-start.10) | collective-permute-done | bytes 61472 | tf_op jit(solution)/shard_map/ppermute | solution.py:659
  32.3 1.5 %collective-permute-done.11.refs_6_ = bf16[240,128]{1,0:T(8,128)(2,1)S(1)} collective-permute-done((bf16[240,128]{1,0:T(8,128)(2,1)S(1)}, bf16[240,128]{1,0:T(8,128)(2,1)S(1)}, u32[]{:S(2)}, u32[]{:S(2)}) %collective-permute-start.11) | collective-permute-done | bytes 61472 | tf_op jit(solution)/shard_map/ppermute | solution.py:659
  33.7 0.5 %collective-permute-start.12 = (bf16[432,128]{1,0:T(8,128)(2,1)S(1)}, bf16[432,128]{1,0:T(8,128)(2,1)S(1)}, u32[]{:S(2)}, u32[]{:S(2)}) collective-permute-start(bf16[432,128]{1,0:T(8,128)(2,1)S(1)} %constant_dynamic-update-slice_fusion.9), channel_id=1, source_target_pairs={{0,1},{1,2},{2,3},{3,0},{4,5},{5,6},{6,7},{7,4},{8,9},{9,10},{10,1... | collective-permute-start | bytes 331784 | tf_op jit(solution)/shard_map/ppermute | solution.py:659
  34.2 1.6 %second_middle.1 = (f32[96,128]{1,0:T(8,128)S(1)}, f32[4,48,128]{2,1,0:T(8,128)S(1)}, bf16[20,240,128]{2,1,0:T(8,128)(2,1)S(1)}, bf16[80,128]{1,0:T(8,128)(2,1)S(1)}) custom-call(s32[4]{0:T(128)S(1)} %pad_add_fusion.flags.refs_0_, bf16[16,80,128]{2,1,0:T(8,128)(2,1)S(1)} %get-tuple-element.43.refs_1_, ...), custom_call_target="tpu_custom_call" | custom-call | tf_op jit(solution)/shard_map/second_middle/pallas_call | solution.py:740
  35.9 1.3 %collective-permute-done.13.refs_4_ = bf16[432,128]{1,0:T(8,128)(2,1)S(1)} collective-permute-done((bf16[432,128]{1,0:T(8,128)(2,1)S(1)}, bf16[432,128]{1,0:T(8,128)(2,1)S(1)}, u32[]{:S(2)}, u32[]{:S(2)}) %collective-permute-start.13) | collective-permute-done | bytes 110624 | tf_op jit(solution)/shard_map/ppermute | solution.py:659
  37.2 1.0 %collective-permute-done.12.refs_3_ = bf16[432,128]{1,0:T(8,128)(2,1)S(1)} collective-permute-done((bf16[432,128]{1,0:T(8,128)(2,1)S(1)}, bf16[432,128]{1,0:T(8,128)(2,1)S(1)}, u32[]{:S(2)}, u32[]{:S(2)}) %collective-permute-start.12) | collective-permute-done | bytes 110624 | tf_op jit(solution)/shard_map/ppermute | solution.py:659
  38.2 4.3 %second_step.1 = bf16[80,16,128]{2,1,0:T(8,128)(2,1)} custom-call(s32[4]{0:T(128)S(1)} %pad_add_fusion.flags.refs_0_, bf16[16,80,128]{2,1,0:T(8,128)(2,1)S(1)} %get-tuple-element.43.refs_1_, s32[16,128]{1,0:T(8,128)S(1)} %copy-done.1, bf16[432,128]{1,0:T(8,128)(2,1)S(1)} %collective-permute-done.12.refs_3_, ...), custom_call_target="tpu_custom_call" | custom-call | tf_op jit(solution)/shard_map/second_step/pallas_call | solution.py:740
  (31 shorter events, 1.2 us)
Async XLA Ops:
  0.0 21.5 %copy-start.1 = (s32[16,128]{1,0:T(8,128)S(1)}, s32[16,128]{1,0:T(8,128)}, u32[]{:S(2)}) copy-start(s32[16,128]{1,0:T(8,128)} %refs_2_.3) | copy-start | bytes 24580
  0.0 21.5 %copy-start.2 = (f32[2,4,80]{2,1,0:T(4,128)S(1)}, f32[2,4,80]{2,1,0:T(4,128)}, u32[]{:S(2)}) copy-start(f32[2,4,80]{2,1,0:T(4,128)} %refs_14_.1) | copy-start | bytes 7684
  0.0 21.5 %copy-start = (bf16[80,384]{1,0:T(8,128)(2,1)S(1)}, bf16[80,384]{1,0:T(8,128)(2,1)}, u32[]{:S(2)}) copy-start(bf16[80,384]{1,0:T(8,128)(2,1)} %refs_13_.3) | copy-start | bytes 184324
  2.2 9.2 %collective-permute-start = (bf16[4,16,128]{2,1,0:T(8,128)(2,1)S(1)}, bf16[4,16,128]{2,1,0:T(8,128)(2,1)S(1)}, u32[]{:S(2)}, u32[]{:S(2)}) collective-permute-start(bf16[4,16,128]{2,1,0:T(8,128)(2,1)S(1)} %get-tuple-element.30), channel_id=1, source_target_pairs={{0,20},{1,21},{2,22},{3,23},{4,16},{5,17},{6,18},{7,19},{8,28},{9,... | collective-permute-start | bytes 49160 | tf_op jit(solution)/shard_map/ppermute | solution.py:659
  6.3 5.2 %collective-permute-start.2 = (bf16[4,16,128]{2,1,0:T(8,128)(2,1)S(1)}, bf16[4,16,128]{2,1,0:T(8,128)(2,1)S(1)}, u32[]{:S(2)}, u32[]{:S(2)}) collective-permute-start(bf16[4,16,128]{2,1,0:T(8,128)(2,1)S(1)} %get-tuple-element.30), channel_id=1, source_target_pairs={{0,16},{1,17},{2,18},{3,19},{4,24},{5,25},{6,26},{7,27},{8,20},{9,... | collective-permute-start | bytes 49160 | tf_op jit(solution)/shard_map/ppermute | solution.py:659
  6.8 4.6 %collective-permute-start.1 = (bf16[4,16,128]{2,1,0:T(8,128)(2,1)S(1)}, bf16[4,16,128]{2,1,0:T(8,128)(2,1)S(1)}, u32[]{:S(2)}, u32[]{:S(2)}) collective-permute-start(bf16[4,16,128]{2,1,0:T(8,128)(2,1)S(1)} %get-tuple-element.30), channel_id=1, source_target_pairs={{0,16},{1,17},{2,18},{3,19},{4,20},{5,21},{6,22},{7,23},{8,24},{9,... | collective-permute-start | bytes 49160 | tf_op jit(solution)/shard_map/ppermute | solution.py:659
  8.3 4.8 %collective-permute-start.3 = (bf16[256,128]{1,0:T(8,128)(2,1)S(1)}, bf16[256,128]{1,0:T(8,128)(2,1)S(1)}, u32[]{:S(2)}, u32[]{:S(2)}) collective-permute-start(bf16[256,128]{1,0:T(8,128)(2,1)S(1)} %get-tuple-element.31), channel_id=1, source_target_pairs={{0,4},{1,5},{2,6},{3,7},{4,0},{5,1},{6,2},{7,3},{8,12},{9,13},{10,... | collective-permute-start | bytes 196616 | tf_op jit(solution)/shard_map/ppermute | solution.py:659
  10.9 4.3 %collective-permute-start.4 = (bf16[256,128]{1,0:T(8,128)(2,1)S(1)}, bf16[256,128]{1,0:T(8,128)(2,1)S(1)}, u32[]{:S(2)}, u32[]{:S(2)}) collective-permute-start(bf16[256,128]{1,0:T(8,128)(2,1)S(1)} %get-tuple-element.33), channel_id=1, source_target_pairs={{0,16},{1,17},{2,18},{3,19},{4,8},{5,9},{6,10},{7,11},{8,4},{9,5},... | collective-permute-start | bytes 196616 | tf_op jit(solution)/shard_map/ppermute | solution.py:659
  15.2 3.4 %collective-permute-start.6 = (bf16[592,128]{1,0:T(8,128)(2,1)S(1)}, bf16[592,128]{1,0:T(8,128)(2,1)S(1)}, u32[]{:S(2)}, u32[]{:S(2)}) collective-permute-start(bf16[592,128]{1,0:T(8,128)(2,1)S(1)} %constant_dynamic-update-slice_fusion), channel_id=1, source_target_pairs={{0,3},{1,0},{2,1},{3,2},{4,7},{5,4},{6,5},{7,6},{8,11},{9,8},{10,9... | collective-permute-start | bytes 454664 | tf_op jit(solution)/shard_map/ppermute | solution.py:659
  15.2 6.3 %collective-permute-start.5 = (bf16[592,128]{1,0:T(8,128)(2,1)S(1)}, bf16[592,128]{1,0:T(8,128)(2,1)S(1)}, u32[]{:S(2)}, u32[]{:S(2)}) collective-permute-start(bf16[592,128]{1,0:T(8,128)(2,1)S(1)} %constant_dynamic-update-slice_fusion), channel_id=1, source_target_pairs={{0,1},{1,2},{2,3},{3,0},{4,5},{5,6},{6,7},{7,4},{8,9},{9,10},{10,1... | collective-permute-start | bytes 454664 | tf_op jit(solution)/shard_map/ppermute | solution.py:659
  25.2 4.8 %collective-permute-start.7 = (bf16[4,16,128]{2,1,0:T(8,128)(2,1)S(1)}, bf16[4,16,128]{2,1,0:T(8,128)(2,1)S(1)}, u32[]{:S(2)}, u32[]{:S(2)}) collective-permute-start(bf16[4,16,128]{2,1,0:T(8,128)(2,1)S(1)} %get-tuple-element.44), channel_id=1, source_target_pairs={{0,20},{1,21},{2,22},{3,23},{4,16},{5,17},{6,18},{7,19},{8,28},{9,... | collective-permute-start | bytes 49160 | tf_op jit(solution)/shard_map/ppermute | solution.py:659
  26.0 4.5 %collective-permute-start.9 = (bf16[4,16,128]{2,1,0:T(8,128)(2,1)S(1)}, bf16[4,16,128]{2,1,0:T(8,128)(2,1)S(1)}, u32[]{:S(2)}, u32[]{:S(2)}) collective-permute-start(bf16[4,16,128]{2,1,0:T(8,128)(2,1)S(1)} %get-tuple-element.44), channel_id=1, source_target_pairs={{0,16},{1,17},{2,18},{3,19},{4,24},{5,25},{6,26},{7,27},{8,20},{9,... | collective-permute-start | bytes 49160 | tf_op jit(solution)/shard_map/ppermute | solution.py:659
  26.7 3.7 %collective-permute-start.8 = (bf16[4,16,128]{2,1,0:T(8,128)(2,1)S(1)}, bf16[4,16,128]{2,1,0:T(8,128)(2,1)S(1)}, u32[]{:S(2)}, u32[]{:S(2)}) collective-permute-start(bf16[4,16,128]{2,1,0:T(8,128)(2,1)S(1)} %get-tuple-element.44), channel_id=1, source_target_pairs={{0,16},{1,17},{2,18},{3,19},{4,20},{5,21},{6,22},{7,23},{8,24},{9,... | collective-permute-start | bytes 49160 | tf_op jit(solution)/shard_map/ppermute | solution.py:659
  28.0 4.2 %collective-permute-start.10 = (bf16[240,128]{1,0:T(8,128)(2,1)S(1)}, bf16[240,128]{1,0:T(8,128)(2,1)S(1)}, u32[]{:S(2)}, u32[]{:S(2)}) collective-permute-start(bf16[240,128]{1,0:T(8,128)(2,1)S(1)} %get-tuple-element.45), channel_id=1, source_target_pairs={{0,4},{1,5},{2,6},{3,7},{4,0},{5,1},{6,2},{7,3},{8,12},{9,13},{10,... | collective-permute-start | bytes 184328 | tf_op jit(solution)/shard_map/ppermute | solution.py:659
  29.5 4.2 %collective-permute-start.11 = (bf16[240,128]{1,0:T(8,128)(2,1)S(1)}, bf16[240,128]{1,0:T(8,128)(2,1)S(1)}, u32[]{:S(2)}, u32[]{:S(2)}) collective-permute-start(bf16[240,128]{1,0:T(8,128)(2,1)S(1)} %get-tuple-element.47), channel_id=1, source_target_pairs={{0,16},{1,17},{2,18},{3,19},{4,8},{5,9},{6,10},{7,11},{8,4},{9,5},... | collective-permute-start | bytes 184328 | tf_op jit(solution)/shard_map/ppermute | solution.py:659
  33.7 3.5 %collective-permute-start.13 = (bf16[432,128]{1,0:T(8,128)(2,1)S(1)}, bf16[432,128]{1,0:T(8,128)(2,1)S(1)}, u32[]{:S(2)}, u32[]{:S(2)}) collective-permute-start(bf16[432,128]{1,0:T(8,128)(2,1)S(1)} %constant_dynamic-update-slice_fusion.9), channel_id=1, source_target_pairs={{0,3},{1,0},{2,1},{3,2},{4,7},{5,4},{6,5},{7,6},{8,11},{9,8},{10,9... | collective-permute-start | bytes 331784 | tf_op jit(solution)/shard_map/ppermute | solution.py:659
  33.7 4.4 %collective-permute-start.12 = (bf16[432,128]{1,0:T(8,128)(2,1)S(1)}, bf16[432,128]{1,0:T(8,128)(2,1)S(1)}, u32[]{:S(2)}, u32[]{:S(2)}) collective-permute-start(bf16[432,128]{1,0:T(8,128)(2,1)S(1)} %constant_dynamic-update-slice_fusion.9), channel_id=1, source_target_pairs={{0,1},{1,2},{2,3},{3,0},{4,5},{5,6},{6,7},{7,4},{8,9},{9,10},{10,1... | collective-permute-start | bytes 331784 | tf_op jit(solution)/shard_map/ppermute | solution.py:659

commit v7 on v6

--- a/solution.py
+++ b/solution.py
@@ -13,6 +13,7 @@
 HA = 384
 HW = 8
 SPAN = 2 * HW + 1
+REACH = HW + 2
 HIDK = 208
 HIDP = 256
 F32 = jnp.float32
@@ -88,6 +89,24 @@
     lax.fori_loop(0, count // unroll, several, 0)
 
 
+def pack_columns(values, reach):
+    lane = lanes(values[0].shape)
+    pitch = 128 // len(values)
+    packed = jnp.zeros_like(values[0])
+    for index, value in enumerate(values):
+        at = index * pitch
+        packed = jnp.where((lane >= at) & (lane < at + reach), roll(value, at), packed)
+        at += reach
+        packed = jnp.where((lane >= at) & (lane < at + reach), roll(value, at + reach - 128), packed)
+    return packed
+
+
+def unpack_columns(left, right, index, count, reach):
+    at = index * (128 // count)
+    left = roll(left.astype(F32), 128 - at - 2 * reach)
+    return jnp.where(lanes(left.shape) < 64, roll(right.astype(F32), -at), left)
+
+
 def strips(one, two, even, d):
     last = d.rows - 2
     return (one, jnp.where(even, last, 0)), (two, jnp.where(even, 0, last))
@@ -114,14 +133,21 @@
         raw[step * 8 : step * 8 + 8, :] = whole[:, :128]
         raw[(step + half) * 8 : (step + half) * 8 + 8, :] = whole[:, 128:]
     keeping = jnp.where(is_ocean, wet[...].astype(F32), 1.0)
+    whole = [raw[pl.ds(field, d.rows, stride=8), :] * keeping for field in range(NS)]
     for field in range(NS):
-        fields[field] = (raw[pl.ds(field, d.rows, stride=8), :] * keeping).astype(BF16)
+        fields[field] = whole[field].astype(BF16)
+    fields[NS] = pack_columns(whole, REACH).astype(BF16)
     edges = edge_columns(state, d)
     put_edges(own_edges, 0, edges, d)
-    for ref, first in strips(one, two, even, d):
+    row = lanes(edges.shape) % d.block
+    downward = jnp.where(row < 2, roll(edges, -d.rows), jnp.zeros_like(edges))
+    upward = jnp.where(
+        (row >= d.rows + 2) & (row < d.rows + 4), roll(edges, d.rows), jnp.zeros_like(edges)
+    )
+    for (ref, first), down in zip(strips(one, two, even, d), (even, jnp.logical_not(even))):
         ref[0:CH, :] = state[first]
         ref[CH : 2 * CH, :] = state[first + 1]
-        put_edges(ref, 2 * CH, edges, d)
+        put_edges(ref, 2 * CH, jnp.where(down, downward, upward), d)
 
 
 def fetch(sources, targets, sems):
@@ -136,20 +162,24 @@
 
 def start_kernel(
     d, flags, far_given, far_surface, far_wet, far_offsets, far_weights,
-    state, planes, fields, own_edges, one, two,
+    state, planes, sides, fields, own_edges, one, two,
     raw, tall, turned, given, surface, wet, offsets, weights, sems,
 ):
     rows = d.rows
+    pieces = [pl.ds(at, 16) for at in range(0, CH, 16)]
     copies = fetch(
-        (far_given, far_surface, far_wet, far_offsets, far_weights),
-        (given, surface, wet, offsets, weights),
+        [far_given.at[piece] for piece in pieces] + [far_surface, far_wet, far_offsets, far_weights],
+        [given.at[piece] for piece in pieces] + [surface, wet, offsets, weights],
         sems,
     )
-    copies[0].wait()
-    turned[...] = given[...].astype(F32).reshape(CH * rows, 128)
+    for index, piece in enumerate(pieces):
+        copies[index].wait()
+        turned[index * 16 * rows : (index + 1) * 16 * rows, :] = (
+            given[piece].astype(F32).reshape(16 * rows, 128)
+        )
     for row in range(rows):
         state[row] = turned[pl.ds(row, CH, stride=rows), :].astype(BF16)
-    for copy in copies[1:]:
+    for copy in copies[len(pieces) :]:
         copy.wait()
     emit(state, surface, wet, flags, fields, own_edges, one, two, raw, d)
     for k in range(NK):
@@ -158,9 +188,15 @@
         tall[(NK + k) * rows : (NK + k + 1) * rows, :] = weights[k]
         planes[k] = code.astype(BF16)
         planes[NK + k] = weights[k].astype(BF16)
-    for ref, first in strips(one, two, flags[3] == 0, d):
+    packed = pack_columns([tall[plane * rows : (plane + 1) * rows, :] for plane in range(2 * NK)], 2)
+    sides[...] = packed.astype(BF16)
+    even = flags[3] == 0
+    for (ref, first), down in zip(strips(one, two, even, d), (even, jnp.logical_not(even))):
         strip = [tall[pl.ds(first + step, 2 * NK, stride=rows), :] for step in range(2)]
         ref[d.strip : d.strip + 16, :] = jnp.concatenate(strip, axis=0).astype(BF16)
+        ref[d.strip + 16 : d.strip + 32, :] = jnp.where(
+            down, packed[rows - 16 : rows], packed[0:16]
+        ).astype(BF16)
 
 
 def decode(code):
@@ -267,10 +303,6 @@
                 forcing_y[pl.ds(at * 8 + field + 4, 8, stride=8), :] = extra
 
 
-def place_columns(left, right):
-    return jnp.where(lanes(left.shape) < 64, right.astype(F32), left.astype(F32))
-
-
 def gelu(x):
     scale = (2 / jnp.pi) ** 0.5
     half = 0.5 * x
@@ -440,13 +472,6 @@
             out(row, state[row].astype(F32) + update)
 
 
-def join_rows(edge_up, edge_own, edge_down, d):
-    row = lanes(edge_own.shape) % d.block
-    above = roll(edge_up, -d.rows)
-    below = roll(edge_down, d.rows)
-    return jnp.where(row < 2, above, jnp.where(row < d.rows + 2, edge_own, below))
-
-
 def prepare(atm_in, atm_bias, ocn_in, ocn_bias, ocn_out, air_in, first, second, is_ocean):
     def bias_rows(ref, width):
         row = jnp.concatenate([ref[index : index + 1, :] for index in range(ref.shape[0])], axis=1)
@@ -493,12 +518,12 @@
 def middle_kernel(d, opening, *refs):
     refs = list(refs)
     take = lambda count: [refs.pop(0) for _ in range(count)]
-    flags, state, field_one, beside, field_two, from_one, from_two, own_edges = take(8)
+    flags, state, field_one, beside, field_two, from_one, from_two = take(7)
     if opening:
         planes, *far_weights = take(6)
     else:
         (plan_x,) = take(1)
-    part_x, fields_x, rolled, edges = take(4)
+    part_x, fields_x, rolled = take(3)
     if opening:
         plan_x, *made_weights = take(4)
         *raw_weights, sems = take(6)
@@ -536,9 +561,6 @@
         regrid_inside(fields_x, plan_x, part_x, 0, d.tiles, tall)
         upper, lower = up_and_down(from_one[0 : 2 * CH, :], from_two[0 : 2 * CH, :])
         roll_rows(state, upper.astype(BF16), lower.astype(BF16), rolled, d)
-        above, below = up_and_down(get_edges(from_one, 2 * CH, d), get_edges(from_two, 2 * CH, d))
-        joined = join_rows(above.astype(BF16), get_edges(own_edges, 0, d), below.astype(BF16), d)
-        put_edges(edges, 0, joined, d)
 
     if opening:
         for copy in copies:
@@ -570,33 +592,34 @@
         @pl.when(is_ocean != 0)
         def _():
             plan_y[...] = jnp.zeros_like(plan_y)
-            side_base = 4 * (rows + 32) + 3 * d.edge_rows
-            pair = [
-                place_columns(from_left[at : at + 16, :], from_right[at : at + 16, :])
-                for at in (side_base, side_base + 16 + 2 * NK * rows)
+            base = rows + 32 + d.edge_rows
+            parts = [
+                (ref[base : base + 16, :], ref[base + 16 + rows : base + 32 + rows, :],
+                 ref[base + 16 : base + 16 + rows, :])
+                for ref in (from_left, from_right)
             ]
-            for step, strip in zip((0, rows + 2), up_and_down(*pair)):
-                for index in range(2):
-                    plan_y[pl.ds(step + index, 2 * NK, stride=tall), :] = strip[index * 8 : (index + 1) * 8]
             for plane in range(2 * NK):
-                at = side_base + 16 + plane * rows
-                plan_y[plane * tall + 2 : plane * tall + 2 + rows, :] = place_columns(
-                    from_left[at : at + rows, :], from_right[at : at + rows, :]
-                )
-
-    lower_at = 64 + 4 * rows
+                first_end, second_end, own = [
+                    unpack_columns(left, right, plane, 2 * NK, 2) for left, right in zip(*parts)
+                ]
+                above, below = up_and_down(first_end, second_end)
+                at = plane * tall
+                plan_y[at : at + 2, :] = above[14:16]
+                plan_y[at + 2 : at + 2 + rows, :] = own
+                plan_y[at + 2 + rows : at + 4 + rows, :] = below[0:2]
+
+    parts = [
+        (ref[0:16, :], ref[16 + rows : 32 + rows, :], ref[16 : 16 + rows, :])
+        for ref in (from_left, from_right)
+    ]
     for field in range(NS):
-        start = 64 + field * rows
-        fields_y[field, 16 : 16 + rows, :] = place_columns(
-            from_left[start : start + rows, :], from_right[start : start + rows, :]
-        )
-        pair = [
-            place_columns(from_left[at : at + 16, :], from_right[at : at + 16, :])
-            for at in (field * 16, lower_at + field * 16)
+        first_end, second_end, own = [
+            unpack_columns(left, right, field, NS, REACH) for left, right in zip(*parts)
         ]
-        pair = up_and_down(*pair)
-        fields_y[field, 0:16, :] = pair[0]
-        fields_y[field, 16 + rows : 32 + rows, :] = pair[1]
+        above, below = up_and_down(first_end, second_end)
+        fields_y[field, 0:16, :] = above
+        fields_y[field, 16 : 16 + rows, :] = own
+        fields_y[field, 16 + rows : 32 + rows, :] = below
 
     def put(row, values):
         if closing:
@@ -616,13 +639,7 @@
         regrid_beside(
             fields_x, fields_y, plan_x, plan_y, part_x, forcing_x, forcing_y, 0, d.tiles, tall, True
         )
-        at = 4 * (rows + 32)
-        size = d.edge_rows
-        joined = []
-        for ref in (from_left, from_right):
-            one_edges, middle, two_edges = [get_edges(ref, at + index * size, d) for index in range(3)]
-            above, below = up_and_down(one_edges, two_edges)
-            joined.append(join_rows(above.astype(BF16), middle, below.astype(BF16), d))
+        joined = [get_edges(ref, rows + 32, d) for ref in (from_left, from_right)]
         sea(
             state, rolled, get_edges(edges, 0, d), *joined, put, forcing_x, forcing_y,
             first, second, wet, at_top, at_bottom, stack, hidden, side, d,
@@ -671,35 +688,33 @@
     return send(x, move)
 
 
-def exchange(fields, own_edges, one, two, planes, d):
+def exchange(fields, own_edges, one, two, sides, d):
     rows = d.rows
-    beside = send(fields, lambda g, i, j: (1 - g, i, j))
+    from_one = swap_rows(one, 0, False)
+    from_two = swap_rows(two, 1, False)
     field_one = swap_rows(fields, 0, True)
     field_two = swap_rows(fields, 1, True)
-    from_one = swap_rows(one, 0, False)
-    from_two = swap_rows(two, 1, False)
-    edge_at = slice(2 * CH, d.strip)
-    odd = lax.axis_index("lat") % 2
-    if rows == 16:
-        outer = [field_one, field_two]
-    else:
-        last = [field[:, rows - 16 :] for field in (field_one, field_two)]
-        first = [field[:, :16] for field in (field_one, field_two)]
-        outer = [jnp.where(odd == 1, last[0], first[0]), jnp.where(odd == 1, first[1], last[1])]
-    packed = [
-        outer[0].reshape(64, 128),
-        beside.reshape(4 * rows, 128),
-        outer[1].reshape(64, 128),
-        from_one[edge_at],
-        own_edges,
-        from_two[edge_at],
-    ]
-    if planes is not None:
-        packed += [from_one[d.strip :], planes.reshape(2 * NK * rows, 128), from_two[d.strip :]]
+    beside = send(fields, lambda g, i, j: (1 - g, i, j))
+    lat, count = lax.axis_index("lat"), lax.axis_size("lat")
+    odd = lat % 2 == 1
+    edges = own_edges
+    for turn, ref in ((0, from_one), (1, from_two)):
+        other = ((lat + turn) ^ 1) - turn
+        there = (other >= 0) & (other < count)
+        edges = edges + jnp.where(there, ref[2 * CH : d.strip], 0)
+    outer = [field_one[NS], field_two[NS]]
+    if rows != 16:
+        outer = [
+            jnp.where(odd, outer[0][rows - 16 :], outer[0][:16]),
+            jnp.where(odd, outer[1][:16], outer[1][rows - 16 :]),
+        ]
+    packed = [outer[0], beside[NS], outer[1], edges]
+    if sides is not None:
+        packed += [from_one[d.strip + 16 :], sides, from_two[d.strip + 16 :]]
     packed = jnp.concatenate(packed, axis=0)
     from_left = send(packed, lambda g, i, j: (g, i, j + 1))
     from_right = send(packed, lambda g, i, j: (g, i, j - 1))
-    return (field_one, beside, field_two, from_one, from_two), (from_left, from_right)
+    return (field_one, beside, field_two, from_one, from_two), (from_left, from_right), edges
 
 
 def local(
@@ -723,7 +738,7 @@
     )
     state_shape = shape(rows, CH, 128)
     emitted = [
-        shape(NS, rows, 128),
+        shape(NS + 1, rows, 128),
         shape(d.edge_rows, 128),
         shape(d.strip, 128),
         shape(d.strip, 128),
@@ -734,7 +749,7 @@
     def call(kernel, operands, outs, scratch, name, far=()):
         scratch = scratch + [pltpu.VMEM(x.shape, x.dtype) for x in far]
         if far:
-            scratch.append(pltpu.SemaphoreType.DMA((len(far),)))
+            scratch.append(pltpu.SemaphoreType.DMA((len(far) + CH // 16,)))
 
         far = [pltpu.with_memory_space_constraint(x, pltpu.HBM) for x in far]
         return pl.pallas_call(
@@ -747,10 +762,12 @@
             name=name,
         )(flags, *operands, *far)
 
-    state, planes, fields, edges, one, two = call(
+    state, planes, sides, fields, edges, one, two = call(
         functools.partial(start_kernel, d),
         (),
-        [state_shape, shape(2 * NK, rows, 128)] + emitted[:2] + [shape(d.strip + 16, 128)] * 2,
+        [state_shape, shape(2 * NK, rows, 128), shape(rows, 128)]
+        + emitted[:2]
+        + [shape(d.strip + 32, 128)] * 2,
         [raw, pltpu.VMEM((2 * NK * rows, 128), F32), turned],
         "start",
         (coupled_state[0], surface_proj, land_mask, regrid_offsets[0], regrid_weights[0]),
@@ -761,7 +778,6 @@
         shape(NS * d.tall, 128, dtype=F32),
         shape(NS, rows + 32, 128, dtype=F32),
         shape(rows + 4, 3 * CH, 128),
-        shape(d.edge_rows, 128),
     ]
     made = [shape(HA, 128), shape(HIDK, 768), shape(9 * CH, HIDP)]
     scratch = [
@@ -773,10 +789,10 @@
         pltpu.VMEM((768, d.edge), BF16),
     ]
 
-    vertical, horizontal = exchange(fields, edges, one, two, planes, d)
+    vertical, horizontal, edges = exchange(fields, edges, one, two, sides, d)
     *shared, plan_x, air_in, first, second = call(
         functools.partial(middle_kernel, d, True),
-        (state, *vertical, edges, planes),
+        (state, *vertical, planes),
         between + [plan] + made,
         [],
         "first_middle",
@@ -785,23 +801,23 @@
     weights = (air_in, first, second, atm_out)
     state, fields, edges, one, two, plan_y = call(
         functools.partial(step_kernel, d, True, False),
-        (state, land_mask, *horizontal, *shared, plan_x, *weights, surface_proj),
+        (state, land_mask, *horizontal, *shared, edges, plan_x, *weights, surface_proj),
         [state_shape] + emitted + [plan],
         scratch + [raw],
         "first_step",
     )
 
-    vertical, horizontal = exchange(fields, edges, one, two, None, d)
+    vertical, horizontal, edges = exchange(fields, edges, one, two, None, d)
     shared = call(
         functools.partial(middle_kernel, d, False),
-        (state, *vertical, edges, plan_x),
+        (state, *vertical, plan_x),
         between,
         [],
         "second_middle",
     )
     (state,) = call(
         functools.partial(step_kernel, d, False, True),
-        (state, land_mask, *horizontal, *shared, plan_x, *weights, plan_y),
+        (state, land_mask, *horizontal, *shared, edges, plan_x, *weights, plan_y),
         [shape(CH, rows, 128)],
         scratch + [turned],
         "second_step",

time: 42.6 us -> 40.2 us (0.944)
  waiting for transfers between devices: 13.5 us -> 10.1 us
  starting transfers between devices: 15.1 us -> 15.9 us
    ppermute x14, waiting for transfers between devices: 13.5 us -> 10.1 us  [send(): return lax.ppermute(x, names, pairs)]
    ppermute x14, starting transfers between devices: 15.1 us -> 15.9 us  [send(): return lax.ppermute(x, names, pairs)]
  transfers between devices with their start and end apart: 14 -> 14, of which waited for: 9 -> 7; matrix products, arithmetic and copies ran while one was open for 0% -> 0% of each run, Pallas kernels for 8% -> 9%
where the time goes in v7:
time: 40.2 us; the launch traced here: 40.1 us
  starting transfers between devices  15.9 us (40%)
  Pallas kernels  13.8 us (34%)
  waiting for transfers between devices  10.1 us (25%)
    ppermute x14, starting transfers between devices, send(): return lax.ppermute(x, names, pairs)  15.9 us
    pallas_call x5, Pallas kernels, call(): pl.pallas_call(kernel, out_shape=outs, in_specs=[SMEM] + [VMEM] * len(ope...  13.8 us
    ppermute x14, waiting for transfers between devices, send(): return lax.ppermute(x, names, pairs)  10.1 us
  transfers between devices with their start and end apart: 14, of which 7 were waited for; matrix products, arithmetic and copies ran while one was open for 0% of the time, Pallas kernels for 9%

profile of v7, /device:TPU:0, one launch (start us, length us, event | category | flops | bytes accessed | tf_op | source)
XLA Modules:
  0.0 40.1 jit_solution(13460658709665312777)
XLA Ops:
  0.1 2.2 %start.1 = (bf16[16,80,128]{2,1,0:T(8,128)(2,1)S(1)}, bf16[8,16,128]{2,1,0:T(8,128)(2,1)S(1)}, bf16[16,128]{1,0:T(8,128)(2,1)S(1)}, bf16[5,16,128]{2,1,0:T(8,128...) custom-call(s32[4]{0:T(128)S(1)} %pad_add_fusion.flags.refs_0_, ...), custom_call_target="tpu_custom_call" | custom-call | tf_op jit(solution)/shard_map/start/pallas_call | solution.py:755
  2.3 4.0 %collective-permute-start = (bf16[5,16,128]{2,1,0:T(8,128)(2,1)S(1)}, bf16[5,16,128]{2,1,0:T(8,128)(2,1)S(1)}, u32[]{:S(2)}, u32[]{:S(2)}) collective-permute-start(bf16[5,16,128]{2,1,0:T(8,128)(2,1)S(1)} %get-tuple-element.29), channel_id=1, source_target_pairs={{0,20},{1,21},{2,22},{3,23},{4,16},{5,17},{6,18},{7,19},{8,28},{9,... | collective-permute-start | bytes 61448 | tf_op jit(solution)/shard_map/ppermute | solution.py:676
  6.3 0.5 %collective-permute-start.2 = (bf16[5,16,128]{2,1,0:T(8,128)(2,1)S(1)}, bf16[5,16,128]{2,1,0:T(8,128)(2,1)S(1)}, u32[]{:S(2)}, u32[]{:S(2)}) collective-permute-start(bf16[5,16,128]{2,1,0:T(8,128)(2,1)S(1)} %get-tuple-element.29), channel_id=1, source_target_pairs={{0,16},{1,17},{2,18},{3,19},{4,24},{5,25},{6,26},{7,27},{8,20},{9,... | collective-permute-start | bytes 61448 | tf_op jit(solution)/shard_map/ppermute | solution.py:676
  6.8 1.5 %collective-permute-start.1 = (bf16[5,16,128]{2,1,0:T(8,128)(2,1)S(1)}, bf16[5,16,128]{2,1,0:T(8,128)(2,1)S(1)}, u32[]{:S(2)}, u32[]{:S(2)}) collective-permute-start(bf16[5,16,128]{2,1,0:T(8,128)(2,1)S(1)} %get-tuple-element.29), channel_id=1, source_target_pairs={{0,16},{1,17},{2,18},{3,19},{4,20},{5,21},{6,22},{7,23},{8,24},{9,... | collective-permute-start | bytes 61448 | tf_op jit(solution)/shard_map/ppermute | solution.py:676
  8.3 2.6 %collective-permute-start.3 = (bf16[272,128]{1,0:T(8,128)(2,1)S(1)}, bf16[272,128]{1,0:T(8,128)(2,1)S(1)}, u32[]{:S(2)}, u32[]{:S(2)}) collective-permute-start(bf16[272,128]{1,0:T(8,128)(2,1)S(1)} %get-tuple-element.31), channel_id=1, source_target_pairs={{0,4},{1,5},{2,6},{3,7},{4,0},{5,1},{6,2},{7,3},{8,12},{9,13},{10,... | collective-permute-start | bytes 208904 | tf_op jit(solution)/shard_map/ppermute | solution.py:676
  10.9 0.5 %collective-permute-start.4 = (bf16[272,128]{1,0:T(8,128)(2,1)S(1)}, bf16[272,128]{1,0:T(8,128)(2,1)S(1)}, u32[]{:S(2)}, u32[]{:S(2)}) collective-permute-start(bf16[272,128]{1,0:T(8,128)(2,1)S(1)} %get-tuple-element.32), channel_id=1, source_target_pairs={{0,16},{1,17},{2,18},{3,19},{4,8},{5,9},{6,10},{7,11},{8,4},{9,5},... | collective-permute-start | bytes 208904 | tf_op jit(solution)/shard_map/ppermute | solution.py:676
  11.5 1.7 %collective-permute-done.3.refs_5_ = bf16[272,128]{1,0:T(8,128)(2,1)S(1)} collective-permute-done((bf16[272,128]{1,0:T(8,128)(2,1)S(1)}, bf16[272,128]{1,0:T(8,128)(2,1)S(1)}, u32[]{:S(2)}, u32[]{:S(2)}) %collective-permute-start.3) | collective-permute-done | bytes 69664 | tf_op jit(solution)/shard_map/ppermute | solution.py:676
  13.2 2.0 %collective-permute-done.4.refs_6_ = bf16[272,128]{1,0:T(8,128)(2,1)S(1)} collective-permute-done((bf16[272,128]{1,0:T(8,128)(2,1)S(1)}, bf16[272,128]{1,0:T(8,128)(2,1)S(1)}, u32[]{:S(2)}, u32[]{:S(2)}) %collective-permute-start.4) | collective-permute-done | bytes 69664 | tf_op jit(solution)/shard_map/ppermute | solution.py:676
  15.4 0.5 %collective-permute-start.5 = (bf16[176,128]{1,0:T(8,128)(2,1)S(1)}, bf16[176,128]{1,0:T(8,128)(2,1)S(1)}, u32[]{:S(2)}, u32[]{:S(2)}) collective-permute-start(bf16[176,128]{1,0:T(8,128)(2,1)S(1)} %constant_dynamic-update-slice_fusion), channel_id=1, source_target_pairs={{0,1},{1,2},{2,3},{3,0},{4,5},{5,6},{6,7},{7,4},{8,9},{9,10},{10,1... | collective-permute-start | bytes 135176 | tf_op jit(solution)/shard_map/ppermute | solution.py:676
  15.9 1.9 %first_middle.1 = (f32[96,128]{1,0:T(8,128)S(1)}, f32[4,48,128]{2,1,0:T(8,128)S(1)}, bf16[20,240,128]{2,1,0:T(8,128)(2,1)S(1)}, f32[192,128]{1,0:T(8,128)S(1)}, ...) custom-call(s32[4]{0:T(128)S(1)} %pad_add_fusion.flags.refs_0_, ...), custom_call_target="tpu_custom_call" | custom-call | tf_op jit(solution)/shard_map/first_middle/pallas_call | solution.py:755
  17.8 1.6 %collective-permute-done.5.refs_3_ = bf16[176,128]{1,0:T(8,128)(2,1)S(1)} collective-permute-done((bf16[176,128]{1,0:T(8,128)(2,1)S(1)}, bf16[176,128]{1,0:T(8,128)(2,1)S(1)}, u32[]{:S(2)}, u32[]{:S(2)}) %collective-permute-start.5) | collective-permute-done | bytes 45088 | tf_op jit(solution)/shard_map/ppermute | solution.py:676
  19.4 3.8 %first_step.1 = (bf16[16,80,128]{2,1,0:T(8,128)(2,1)S(1)}, bf16[5,16,128]{2,1,0:T(8,128)(2,1)S(1)}, bf16[80,128]{1,0:T(8,128)(2,1)S(1)}, bf16[240,128]{1,0:T(8,1...) custom-call(s32[4]{0:T(128)S(1)} %pad_add_fusion.flags.refs_0_, ...), custom_call_target="tpu_custom_call" | custom-call | tf_op jit(solution)/shard_map/first_step/pallas_call | solution.py:755
  23.1 1.4 %collective-permute-start.9 = (bf16[5,16,128]{2,1,0:T(8,128)(2,1)S(1)}, bf16[5,16,128]{2,1,0:T(8,128)(2,1)S(1)}, u32[]{:S(2)}, u32[]{:S(2)}) collective-permute-start(bf16[5,16,128]{2,1,0:T(8,128)(2,1)S(1)} %get-tuple-element.43), channel_id=1, source_target_pairs={{0,16},{1,17},{2,18},{3,19},{4,24},{5,25},{6,26},{7,27},{8,20},{9,... | collective-permute-start | bytes 61448 | tf_op jit(solution)/shard_map/ppermute | solution.py:676
  24.6 0.7 %collective-permute-start.8 = (bf16[5,16,128]{2,1,0:T(8,128)(2,1)S(1)}, bf16[5,16,128]{2,1,0:T(8,128)(2,1)S(1)}, u32[]{:S(2)}, u32[]{:S(2)}) collective-permute-start(bf16[5,16,128]{2,1,0:T(8,128)(2,1)S(1)} %get-tuple-element.43), channel_id=1, source_target_pairs={{0,16},{1,17},{2,18},{3,19},{4,20},{5,21},{6,22},{7,23},{8,24},{9,... | collective-permute-start | bytes 61448 | tf_op jit(solution)/shard_map/ppermute | solution.py:676
  25.2 1.3 %collective-permute-start.7 = (bf16[5,16,128]{2,1,0:T(8,128)(2,1)S(1)}, bf16[5,16,128]{2,1,0:T(8,128)(2,1)S(1)}, u32[]{:S(2)}, u32[]{:S(2)}) collective-permute-start(bf16[5,16,128]{2,1,0:T(8,128)(2,1)S(1)} %get-tuple-element.43), channel_id=1, source_target_pairs={{0,20},{1,21},{2,22},{3,23},{4,16},{5,17},{6,18},{7,19},{8,28},{9,... | collective-permute-start | bytes 61448 | tf_op jit(solution)/shard_map/ppermute | solution.py:676
  26.5 1.6 %collective-permute-start.10 = (bf16[240,128]{1,0:T(8,128)(2,1)S(1)}, bf16[240,128]{1,0:T(8,128)(2,1)S(1)}, u32[]{:S(2)}, u32[]{:S(2)}) collective-permute-start(bf16[240,128]{1,0:T(8,128)(2,1)S(1)} %get-tuple-element.45), channel_id=1, source_target_pairs={{0,4},{1,5},{2,6},{3,7},{4,0},{5,1},{6,2},{7,3},{8,12},{9,13},{10,... | collective-permute-start | bytes 184328 | tf_op jit(solution)/shard_map/ppermute | solution.py:676
  28.1 0.7 %collective-permute-start.11 = (bf16[240,128]{1,0:T(8,128)(2,1)S(1)}, bf16[240,128]{1,0:T(8,128)(2,1)S(1)}, u32[]{:S(2)}, u32[]{:S(2)}) collective-permute-start(bf16[240,128]{1,0:T(8,128)(2,1)S(1)} %get-tuple-element.46), channel_id=1, source_target_pairs={{0,16},{1,17},{2,18},{3,19},{4,8},{5,9},{6,10},{7,11},{8,4},{9,5},... | collective-permute-start | bytes 184328 | tf_op jit(solution)/shard_map/ppermute | solution.py:676
  28.7 1.2 %collective-permute-done.7.refs_2_ = bf16[5,16,128]{2,1,0:T(8,128)(2,1)S(1)} collective-permute-done((bf16[5,16,128]{2,1,0:T(8,128)(2,1)S(1)}, bf16[5,16,128]{2,1,0:T(8,128)(2,1)S(1)}, u32[]{:S(2)}, u32[]{:S(2)}) %collective-permute-start.7) | collective-permute-done | bytes 20512 | tf_op jit(solution)/shard_map/ppermute | solution.py:676
  29.9 0.8 %collective-permute-done.10.refs_5_ = bf16[240,128]{1,0:T(8,128)(2,1)S(1)} collective-permute-done((bf16[240,128]{1,0:T(8,128)(2,1)S(1)}, bf16[240,128]{1,0:T(8,128)(2,1)S(1)}, u32[]{:S(2)}, u32[]{:S(2)}) %collective-permute-start.10) | collective-permute-done | bytes 61472 | tf_op jit(solution)/shard_map/ppermute | solution.py:676
  30.7 1.6 %collective-permute-done.11.refs_6_ = bf16[240,128]{1,0:T(8,128)(2,1)S(1)} collective-permute-done((bf16[240,128]{1,0:T(8,128)(2,1)S(1)}, bf16[240,128]{1,0:T(8,128)(2,1)S(1)}, u32[]{:S(2)}, u32[]{:S(2)}) %collective-permute-start.11) | collective-permute-done | bytes 61472 | tf_op jit(solution)/shard_map/ppermute | solution.py:676
  32.4 0.5 %collective-permute-start.12 = (bf16[128,128]{1,0:T(8,128)(2,1)S(1)}, bf16[128,128]{1,0:T(8,128)(2,1)S(1)}, u32[]{:S(2)}, u32[]{:S(2)}) collective-permute-start(bf16[128,128]{1,0:T(8,128)(2,1)S(1)} %pad_maximum_fusion), channel_id=1, source_target_pairs={{0,1},{1,2},{2,3},{3,0},{4,5},{5,6},{6,7},{7,4},{8,9},{9,10},{10,1... | collective-permute-start | bytes 98312 | tf_op jit(solution)/shard_map/ppermute | solution.py:676
  32.9 1.6 %second_middle.1 = (f32[96,128]{1,0:T(8,128)S(1)}, f32[4,48,128]{2,1,0:T(8,128)S(1)}, bf16[20,240,128]{2,1,0:T(8,128)(2,1)S(1)}) custom-call(s32[4]{0:T(128)S(1)} %pad_add_fusion.flags.refs_0_, bf16[16,80,128]{2,1,0:T(8,128)(2,1)S(1)} %get-tuple-element.42.refs_1_, bf16[5,16,128]{2,1,0:T(8,128)(2,1)S(1)} %collective-permute-done.7.refs_2_, ...), custom_call_target="tpu_custom_call" | custom-call | tf_op jit(solution)/shard_map/second_middle/pallas_call | solution.py:755
  34.5 1.2 %collective-permute-done.12.refs_3_ = bf16[128,128]{1,0:T(8,128)(2,1)S(1)} collective-permute-done((bf16[128,128]{1,0:T(8,128)(2,1)S(1)}, bf16[128,128]{1,0:T(8,128)(2,1)S(1)}, u32[]{:S(2)}, u32[]{:S(2)}) %collective-permute-start.12) | collective-permute-done | bytes 32800 | tf_op jit(solution)/shard_map/ppermute | solution.py:676
  35.8 4.3 %second_step.1 = bf16[80,16,128]{2,1,0:T(8,128)(2,1)} custom-call(s32[4]{0:T(128)S(1)} %pad_add_fusion.flags.refs_0_, bf16[16,80,128]{2,1,0:T(8,128)(2,1)S(1)} %get-tuple-element.42.refs_1_, s32[16,128]{1,0:T(8,128)S(1)} %copy-done.1, bf16[128,128]{1,0:T(8,128)(2,1)S(1)} %collective-permute-done.12.refs_3_, ...), custom_call_target="tpu_custom_call" | custom-call | tf_op jit(solution)/shard_map/second_step/pallas_call | solution.py:755
  (28 shorter events, 0.3 us)
Async XLA Ops:
  0.0 19.4 %copy-start.1 = (s32[16,128]{1,0:T(8,128)S(1)}, s32[16,128]{1,0:T(8,128)}, u32[]{:S(2)}) copy-start(s32[16,128]{1,0:T(8,128)} %refs_2_.3) | copy-start | bytes 24580
  0.0 19.4 %copy-start.2 = (f32[2,4,80]{2,1,0:T(4,128)S(1)}, f32[2,4,80]{2,1,0:T(4,128)}, u32[]{:S(2)}) copy-start(f32[2,4,80]{2,1,0:T(4,128)} %refs_14_.1) | copy-start | bytes 7684
  0.0 19.4 %copy-start = (bf16[80,384]{1,0:T(8,128)(2,1)S(1)}, bf16[80,384]{1,0:T(8,128)(2,1)}, u32[]{:S(2)}) copy-start(bf16[80,384]{1,0:T(8,128)(2,1)} %refs_13_.3) | copy-start | bytes 184324
  2.3 9.2 %collective-permute-start = (bf16[5,16,128]{2,1,0:T(8,128)(2,1)S(1)}, bf16[5,16,128]{2,1,0:T(8,128)(2,1)S(1)}, u32[]{:S(2)}, u32[]{:S(2)}) collective-permute-start(bf16[5,16,128]{2,1,0:T(8,128)(2,1)S(1)} %get-tuple-element.29), channel_id=1, source_target_pairs={{0,20},{1,21},{2,22},{3,23},{4,16},{5,17},{6,18},{7,19},{8,28},{9,... | collective-permute-start | bytes 61448 | tf_op jit(solution)/shard_map/ppermute | solution.py:676
  6.3 5.2 %collective-permute-start.2 = (bf16[5,16,128]{2,1,0:T(8,128)(2,1)S(1)}, bf16[5,16,128]{2,1,0:T(8,128)(2,1)S(1)}, u32[]{:S(2)}, u32[]{:S(2)}) collective-permute-start(bf16[5,16,128]{2,1,0:T(8,128)(2,1)S(1)} %get-tuple-element.29), channel_id=1, source_target_pairs={{0,16},{1,17},{2,18},{3,19},{4,24},{5,25},{6,26},{7,27},{8,20},{9,... | collective-permute-start | bytes 61448 | tf_op jit(solution)/shard_map/ppermute | solution.py:676
  6.8 4.6 %collective-permute-start.1 = (bf16[5,16,128]{2,1,0:T(8,128)(2,1)S(1)}, bf16[5,16,128]{2,1,0:T(8,128)(2,1)S(1)}, u32[]{:S(2)}, u32[]{:S(2)}) collective-permute-start(bf16[5,16,128]{2,1,0:T(8,128)(2,1)S(1)} %get-tuple-element.29), channel_id=1, source_target_pairs={{0,16},{1,17},{2,18},{3,19},{4,20},{5,21},{6,22},{7,23},{8,24},{9,... | collective-permute-start | bytes 61448 | tf_op jit(solution)/shard_map/ppermute | solution.py:676
  8.3 4.9 %collective-permute-start.3 = (bf16[272,128]{1,0:T(8,128)(2,1)S(1)}, bf16[272,128]{1,0:T(8,128)(2,1)S(1)}, u32[]{:S(2)}, u32[]{:S(2)}) collective-permute-start(bf16[272,128]{1,0:T(8,128)(2,1)S(1)} %get-tuple-element.31), channel_id=1, source_target_pairs={{0,4},{1,5},{2,6},{3,7},{4,0},{5,1},{6,2},{7,3},{8,12},{9,13},{10,... | collective-permute-start | bytes 208904 | tf_op jit(solution)/shard_map/ppermute | solution.py:676
  10.9 4.3 %collective-permute-start.4 = (bf16[272,128]{1,0:T(8,128)(2,1)S(1)}, bf16[272,128]{1,0:T(8,128)(2,1)S(1)}, u32[]{:S(2)}, u32[]{:S(2)}) collective-permute-start(bf16[272,128]{1,0:T(8,128)(2,1)S(1)} %get-tuple-element.32), channel_id=1, source_target_pairs={{0,16},{1,17},{2,18},{3,19},{4,8},{5,9},{6,10},{7,11},{8,4},{9,5},... | collective-permute-start | bytes 208904 | tf_op jit(solution)/shard_map/ppermute | solution.py:676
  15.3 2.5 %collective-permute-start.6 = (bf16[176,128]{1,0:T(8,128)(2,1)S(1)}, bf16[176,128]{1,0:T(8,128)(2,1)S(1)}, u32[]{:S(2)}, u32[]{:S(2)}) collective-permute-start(bf16[176,128]{1,0:T(8,128)(2,1)S(1)} %constant_dynamic-update-slice_fusion), channel_id=1, source_target_pairs={{0,3},{1,0},{2,1},{3,2},{4,7},{5,4},{6,5},{7,6},{8,11},{9,8},{10,9... | collective-permute-start | bytes 135176 | tf_op jit(solution)/shard_map/ppermute | solution.py:676
  15.4 4.0 %collective-permute-start.5 = (bf16[176,128]{1,0:T(8,128)(2,1)S(1)}, bf16[176,128]{1,0:T(8,128)(2,1)S(1)}, u32[]{:S(2)}, u32[]{:S(2)}) collective-permute-start(bf16[176,128]{1,0:T(8,128)(2,1)S(1)} %constant_dynamic-update-slice_fusion), channel_id=1, source_target_pairs={{0,1},{1,2},{2,3},{3,0},{4,5},{5,6},{6,7},{7,4},{8,9},{9,10},{10,1... | collective-permute-start | bytes 135176 | tf_op jit(solution)/shard_map/ppermute | solution.py:676
  23.1 5.6 %collective-permute-start.9 = (bf16[5,16,128]{2,1,0:T(8,128)(2,1)S(1)}, bf16[5,16,128]{2,1,0:T(8,128)(2,1)S(1)}, u32[]{:S(2)}, u32[]{:S(2)}) collective-permute-start(bf16[5,16,128]{2,1,0:T(8,128)(2,1)S(1)} %get-tuple-element.43), channel_id=1, source_target_pairs={{0,16},{1,17},{2,18},{3,19},{4,24},{5,25},{6,26},{7,27},{8,20},{9,... | collective-permute-start | bytes 61448 | tf_op jit(solution)/shard_map/ppermute | solution.py:676
  24.6 4.2 %collective-permute-start.8 = (bf16[5,16,128]{2,1,0:T(8,128)(2,1)S(1)}, bf16[5,16,128]{2,1,0:T(8,128)(2,1)S(1)}, u32[]{:S(2)}, u32[]{:S(2)}) collective-permute-start(bf16[5,16,128]{2,1,0:T(8,128)(2,1)S(1)} %get-tuple-element.43), channel_id=1, source_target_pairs={{0,16},{1,17},{2,18},{3,19},{4,20},{5,21},{6,22},{7,23},{8,24},{9,... | collective-permute-start | bytes 61448 | tf_op jit(solution)/shard_map/ppermute | solution.py:676
  25.2 4.7 %collective-permute-start.7 = (bf16[5,16,128]{2,1,0:T(8,128)(2,1)S(1)}, bf16[5,16,128]{2,1,0:T(8,128)(2,1)S(1)}, u32[]{:S(2)}, u32[]{:S(2)}) collective-permute-start(bf16[5,16,128]{2,1,0:T(8,128)(2,1)S(1)} %get-tuple-element.43), channel_id=1, source_target_pairs={{0,20},{1,21},{2,22},{3,23},{4,16},{5,17},{6,18},{7,19},{8,28},{9,... | collective-permute-start | bytes 61448 | tf_op jit(solution)/shard_map/ppermute | solution.py:676
  26.5 4.2 %collective-permute-start.10 = (bf16[240,128]{1,0:T(8,128)(2,1)S(1)}, bf16[240,128]{1,0:T(8,128)(2,1)S(1)}, u32[]{:S(2)}, u32[]{:S(2)}) collective-permute-start(bf16[240,128]{1,0:T(8,128)(2,1)S(1)} %get-tuple-element.45), channel_id=1, source_target_pairs={{0,4},{1,5},{2,6},{3,7},{4,0},{5,1},{6,2},{7,3},{8,12},{9,13},{10,... | collective-permute-start | bytes 184328 | tf_op jit(solution)/shard_map/ppermute | solution.py:676
  28.1 4.2 %collective-permute-start.11 = (bf16[240,128]{1,0:T(8,128)(2,1)S(1)}, bf16[240,128]{1,0:T(8,128)(2,1)S(1)}, u32[]{:S(2)}, u32[]{:S(2)}) collective-permute-start(bf16[240,128]{1,0:T(8,128)(2,1)S(1)} %get-tuple-element.46), channel_id=1, source_target_pairs={{0,16},{1,17},{2,18},{3,19},{4,8},{5,9},{6,10},{7,11},{8,4},{9,5},... | collective-permute-start | bytes 184328 | tf_op jit(solution)/shard_map/ppermute | solution.py:676
  32.3 2.2 %collective-permute-start.13 = (bf16[128,128]{1,0:T(8,128)(2,1)S(1)}, bf16[128,128]{1,0:T(8,128)(2,1)S(1)}, u32[]{:S(2)}, u32[]{:S(2)}) collective-permute-start(bf16[128,128]{1,0:T(8,128)(2,1)S(1)} %pad_maximum_fusion), channel_id=1, source_target_pairs={{0,3},{1,0},{2,1},{3,2},{4,7},{5,4},{6,5},{7,6},{8,11},{9,8},{10,9... | collective-permute-start | bytes 98312 | tf_op jit(solution)/shard_map/ppermute | solution.py:676
  32.4 3.4 %collective-permute-start.12 = (bf16[128,128]{1,0:T(8,128)(2,1)S(1)}, bf16[128,128]{1,0:T(8,128)(2,1)S(1)}, u32[]{:S(2)}, u32[]{:S(2)}) collective-permute-start(bf16[128,128]{1,0:T(8,128)(2,1)S(1)} %pad_maximum_fusion), channel_id=1, source_target_pairs={{0,1},{1,2},{2,3},{3,0},{4,5},{5,6},{6,7},{7,4},{8,9},{9,10},{10,1... | collective-permute-start | bytes 98312 | tf_op jit(solution)/shard_map/ppermute | solution.py:676

commit v8 on v7

--- a/solution.py
+++ b/solution.py
@@ -592,7 +592,7 @@
         @pl.when(is_ocean != 0)
         def _():
             plan_y[...] = jnp.zeros_like(plan_y)
-            base = rows + 32 + d.edge_rows
+            base = d.edge_rows
             parts = [
                 (ref[base : base + 16, :], ref[base + 16 + rows : base + 32 + rows, :],
                  ref[base + 16 : base + 16 + rows, :])
@@ -608,8 +608,10 @@
                 plan_y[at + 2 : at + 2 + rows, :] = own
                 plan_y[at + 2 + rows : at + 4 + rows, :] = below[0:2]
 
+    base = d.edge_rows + (rows + 32 if opening else 0)
     parts = [
-        (ref[0:16, :], ref[16 + rows : 32 + rows, :], ref[16 : 16 + rows, :])
+        (ref[base : base + 16, :], ref[base + 16 + rows : base + 32 + rows, :],
+         ref[base + 16 : base + 16 + rows, :])
         for ref in (from_left, from_right)
     ]
     for field in range(NS):
@@ -639,7 +641,7 @@
         regrid_beside(
             fields_x, fields_y, plan_x, plan_y, part_x, forcing_x, forcing_y, 0, d.tiles, tall, True
         )
-        joined = [get_edges(ref, rows + 32, d) for ref in (from_left, from_right)]
+        joined = [get_edges(ref, 0, d) for ref in (from_left, from_right)]
         sea(
             state, rolled, get_edges(edges, 0, d), *joined, put, forcing_x, forcing_y,
             first, second, wet, at_top, at_bottom, stack, hidden, side, d,
@@ -702,15 +704,19 @@
         other = ((lat + turn) ^ 1) - turn
         there = (other >= 0) & (other < count)
         edges = edges + jnp.where(there, ref[2 * CH : d.strip], 0)
+    edges, beside, field_one, field_two = lax.optimization_barrier(
+        (edges, beside, field_one, field_two)
+    )
     outer = [field_one[NS], field_two[NS]]
     if rows != 16:
         outer = [
             jnp.where(odd, outer[0][rows - 16 :], outer[0][:16]),
             jnp.where(odd, outer[1][:16], outer[1][rows - 16 :]),
         ]
-    packed = [outer[0], beside[NS], outer[1], edges]
+    packed = [edges]
     if sides is not None:
         packed += [from_one[d.strip + 16 :], sides, from_two[d.strip + 16 :]]
+    packed += [outer[0], beside[NS], outer[1]]
     packed = jnp.concatenate(packed, axis=0)
     from_left = send(packed, lambda g, i, j: (g, i, j + 1))
     from_right = send(packed, lambda g, i, j: (g, i, j - 1))

time: 40.2 us -> 38.7 us (0.963)
  waiting for transfers between devices: 10.1 us -> 7.4 us
  starting transfers between devices: 15.9 us -> 17.1 us
    ppermute x14, waiting for transfers between devices: 10.1 us -> 7.4 us  [send(): return lax.ppermute(x, names, pairs)]
    ppermute x14, starting transfers between devices: 15.9 us -> 17.1 us  [send(): return lax.ppermute(x, names, pairs)]
  transfers between devices with their start and end apart: 14 -> 14, of which waited for: 7 -> 6; matrix products, arithmetic and copies ran while one was open for 0% -> 0% of each run, Pallas kernels for 9% -> 9%
where the time goes in v8:
time: 38.7 us; the launch traced here: 38.5 us
  starting transfers between devices  17.1 us (44%)
  Pallas kernels  13.8 us (36%)
  waiting for transfers between devices  7.4 us (19%)
    ppermute x14, starting transfers between devices, send(): return lax.ppermute(x, names, pairs)  17.1 us
    pallas_call x5, Pallas kernels, call(): pl.pallas_call(kernel, out_shape=outs, in_specs=[SMEM] + [VMEM] * len(ope...  13.8 us
    ppermute x14, waiting for transfers between devices, send(): return lax.ppermute(x, names, pairs)  7.4 us
  transfers between devices with their start and end apart: 14, of which 6 were waited for; matrix products, arithmetic and copies ran while one was open for 0% of the time, Pallas kernels for 9%

profile of v8, /device:TPU:0, one launch (start us, length us, event | category | flops | bytes accessed | tf_op | source)
XLA Modules:
  0.0 38.5 jit_solution(7422534513772979257)
XLA Ops:
  0.0 0.1 pad_add_fusion.flags.refs_0_
  0.1 2.2 %start.1 = (bf16[16,80,128]{2,1,0:T(8,128)(2,1)S(1)}, bf16[8,16,128]{2,1,0:T(8,128)(2,1)S(1)}, bf16[16,128]{1,0:T(8,128)(2,1)S(1)}, bf16[5,16,128]{2,1,0:T(8,128...) custom-call(s32[4]{0:T(128)S(1)} %pad_add_fusion.flags.refs_0_, ...), custom_call_target="tpu_custom_call" | custom-call | tf_op jit(solution)/shard_map/start/pallas_call | solution.py:761
  2.3 3.1 %collective-permute-start = (bf16[272,128]{1,0:T(8,128)(2,1)S(1)}, bf16[272,128]{1,0:T(8,128)(2,1)S(1)}, u32[]{:S(2)}, u32[]{:S(2)}) collective-permute-start(bf16[272,128]{1,0:T(8,128)(2,1)S(1)} %get-tuple-element.38), channel_id=1, source_target_pairs={{0,4},{1,5},{2,6},{3,7},{4,0},{5,1},{6,2},{7,3},{8,12},{9,13},{10,... | collective-permute-start | bytes 208904 | tf_op jit(solution)/shard_map/ppermute | solution.py:678
  5.4 1.5 %collective-permute-start.1 = (bf16[272,128]{1,0:T(8,128)(2,1)S(1)}, bf16[272,128]{1,0:T(8,128)(2,1)S(1)}, u32[]{:S(2)}, u32[]{:S(2)}) collective-permute-start(bf16[272,128]{1,0:T(8,128)(2,1)S(1)} %get-tuple-element.39), channel_id=1, source_target_pairs={{0,16},{1,17},{2,18},{3,19},{4,8},{5,9},{6,10},{7,11},{8,4},{9,5},... | collective-permute-start | bytes 208904 | tf_op jit(solution)/shard_map/ppermute | solution.py:678
  6.9 0.5 %collective-permute-start.4 = (bf16[5,16,128]{2,1,0:T(8,128)(2,1)S(1)}, bf16[5,16,128]{2,1,0:T(8,128)(2,1)S(1)}, u32[]{:S(2)}, u32[]{:S(2)}) collective-permute-start(bf16[5,16,128]{2,1,0:T(8,128)(2,1)S(1)} %get-tuple-element.40), channel_id=1, source_target_pairs={{0,16},{1,17},{2,18},{3,19},{4,24},{5,25},{6,26},{7,27},{8,20},{9,... | collective-permute-start | bytes 61448 | tf_op jit(solution)/shard_map/ppermute | solution.py:678
  7.4 2.1 %collective-permute-start.3 = (bf16[5,16,128]{2,1,0:T(8,128)(2,1)S(1)}, bf16[5,16,128]{2,1,0:T(8,128)(2,1)S(1)}, u32[]{:S(2)}, u32[]{:S(2)}) collective-permute-start(bf16[5,16,128]{2,1,0:T(8,128)(2,1)S(1)} %get-tuple-element.40), channel_id=1, source_target_pairs={{0,20},{1,21},{2,22},{3,23},{4,16},{5,17},{6,18},{7,19},{8,28},{9,... | collective-permute-start | bytes 61448 | tf_op jit(solution)/shard_map/ppermute | solution.py:678
  9.5 1.5 %collective-permute-start.2 = (bf16[5,16,128]{2,1,0:T(8,128)(2,1)S(1)}, bf16[5,16,128]{2,1,0:T(8,128)(2,1)S(1)}, u32[]{:S(2)}, u32[]{:S(2)}) collective-permute-start(bf16[5,16,128]{2,1,0:T(8,128)(2,1)S(1)} %get-tuple-element.40), channel_id=1, source_target_pairs={{0,16},{1,17},{2,18},{3,19},{4,20},{5,21},{6,22},{7,23},{8,24},{9,... | collective-permute-start | bytes 61448 | tf_op jit(solution)/shard_map/ppermute | solution.py:678
  11.0 1.1 %collective-permute-done.3.refs_2_ = bf16[5,16,128]{2,1,0:T(8,128)(2,1)S(1)} collective-permute-done((bf16[5,16,128]{2,1,0:T(8,128)(2,1)S(1)}, bf16[5,16,128]{2,1,0:T(8,128)(2,1)S(1)}, u32[]{:S(2)}, u32[]{:S(2)}) %collective-permute-start.3) | collective-permute-done | bytes 20512 | tf_op jit(solution)/shard_map/ppermute | solution.py:678
  12.1 1.2 %collective-permute-done.2.refs_3_ = bf16[5,16,128]{2,1,0:T(8,128)(2,1)S(1)} collective-permute-done((bf16[5,16,128]{2,1,0:T(8,128)(2,1)S(1)}, bf16[5,16,128]{2,1,0:T(8,128)(2,1)S(1)}, u32[]{:S(2)}, u32[]{:S(2)}) %collective-permute-start.2) | collective-permute-done | bytes 20512 | tf_op jit(solution)/shard_map/ppermute | solution.py:678
  13.4 0.5 %collective-permute-start.5 = (bf16[176,128]{1,0:T(8,128)(2,1)S(1)}, bf16[176,128]{1,0:T(8,128)(2,1)S(1)}, u32[]{:S(2)}, u32[]{:S(2)}) collective-permute-start(bf16[176,128]{1,0:T(8,128)(2,1)S(1)} %constant_dynamic-update-slice_fusion), channel_id=1, source_target_pairs={{0,1},{1,2},{2,3},{3,0},{4,5},{5,6},{6,7},{7,4},{8,9},{9,10},{10,1... | collective-permute-start | bytes 135176 | tf_op jit(solution)/shard_map/ppermute | solution.py:678
  13.9 1.9 %first_middle.1 = (f32[96,128]{1,0:T(8,128)S(1)}, f32[4,48,128]{2,1,0:T(8,128)S(1)}, bf16[20,240,128]{2,1,0:T(8,128)(2,1)S(1)}, f32[192,128]{1,0:T(8,128)S(1)}, ...) custom-call(s32[4]{0:T(128)S(1)} %pad_add_fusion.flags.refs_0_, ...), custom_call_target="tpu_custom_call" | custom-call | tf_op jit(solution)/shard_map/first_middle/pallas_call | solution.py:761
  15.8 1.6 %collective-permute-done.5.refs_3_ = bf16[176,128]{1,0:T(8,128)(2,1)S(1)} collective-permute-done((bf16[176,128]{1,0:T(8,128)(2,1)S(1)}, bf16[176,128]{1,0:T(8,128)(2,1)S(1)}, u32[]{:S(2)}, u32[]{:S(2)}) %collective-permute-start.5) | collective-permute-done | bytes 45088 | tf_op jit(solution)/shard_map/ppermute | solution.py:678
  17.4 3.8 %first_step.1 = (bf16[16,80,128]{2,1,0:T(8,128)(2,1)S(1)}, bf16[5,16,128]{2,1,0:T(8,128)(2,1)S(1)}, bf16[80,128]{1,0:T(8,128)(2,1)S(1)}, bf16[240,128]{1,0:T(8,1...) custom-call(s32[4]{0:T(128)S(1)} %pad_add_fusion.flags.refs_0_, ...), custom_call_target="tpu_custom_call" | custom-call | tf_op jit(solution)/shard_map/first_step/pallas_call | solution.py:761
  21.2 1.2 %collective-permute-start.7 = (bf16[240,128]{1,0:T(8,128)(2,1)S(1)}, bf16[240,128]{1,0:T(8,128)(2,1)S(1)}, u32[]{:S(2)}, u32[]{:S(2)}) collective-permute-start(bf16[240,128]{1,0:T(8,128)(2,1)S(1)} %get-tuple-element.56), channel_id=1, source_target_pairs={{0,4},{1,5},{2,6},{3,7},{4,0},{5,1},{6,2},{7,3},{8,12},{9,13},{10,... | collective-permute-start | bytes 184328 | tf_op jit(solution)/shard_map/ppermute | solution.py:678
  22.3 1.6 %collective-permute-start.8 = (bf16[240,128]{1,0:T(8,128)(2,1)S(1)}, bf16[240,128]{1,0:T(8,128)(2,1)S(1)}, u32[]{:S(2)}, u32[]{:S(2)}) collective-permute-start(bf16[240,128]{1,0:T(8,128)(2,1)S(1)} %get-tuple-element.57), channel_id=1, source_target_pairs={{0,16},{1,17},{2,18},{3,19},{4,8},{5,9},{6,10},{7,11},{8,4},{9,5},... | collective-permute-start | bytes 184328 | tf_op jit(solution)/shard_map/ppermute | solution.py:678
  23.9 0.4 %collective-permute-start.11 = (bf16[5,16,128]{2,1,0:T(8,128)(2,1)S(1)}, bf16[5,16,128]{2,1,0:T(8,128)(2,1)S(1)}, u32[]{:S(2)}, u32[]{:S(2)}) collective-permute-start(bf16[5,16,128]{2,1,0:T(8,128)(2,1)S(1)} %get-tuple-element.58), channel_id=1, source_target_pairs={{0,16},{1,17},{2,18},{3,19},{4,24},{5,25},{6,26},{7,27},{8,20},{9,... | collective-permute-start | bytes 61448 | tf_op jit(solution)/shard_map/ppermute | solution.py:678
  24.4 2.6 %collective-permute-start.10 = (bf16[5,16,128]{2,1,0:T(8,128)(2,1)S(1)}, bf16[5,16,128]{2,1,0:T(8,128)(2,1)S(1)}, u32[]{:S(2)}, u32[]{:S(2)}) collective-permute-start(bf16[5,16,128]{2,1,0:T(8,128)(2,1)S(1)} %get-tuple-element.58), channel_id=1, source_target_pairs={{0,20},{1,21},{2,22},{3,23},{4,16},{5,17},{6,18},{7,19},{8,28},{9,... | collective-permute-start | bytes 61448 | tf_op jit(solution)/shard_map/ppermute | solution.py:678
  27.0 1.5 %collective-permute-start.9 = (bf16[5,16,128]{2,1,0:T(8,128)(2,1)S(1)}, bf16[5,16,128]{2,1,0:T(8,128)(2,1)S(1)}, u32[]{:S(2)}, u32[]{:S(2)}) collective-permute-start(bf16[5,16,128]{2,1,0:T(8,128)(2,1)S(1)} %get-tuple-element.58), channel_id=1, source_target_pairs={{0,16},{1,17},{2,18},{3,19},{4,20},{5,21},{6,22},{7,23},{8,24},{9,... | collective-permute-start | bytes 61448 | tf_op jit(solution)/shard_map/ppermute | solution.py:678
  28.5 0.5 %collective-permute-done.10.refs_2_ = bf16[5,16,128]{2,1,0:T(8,128)(2,1)S(1)} collective-permute-done((bf16[5,16,128]{2,1,0:T(8,128)(2,1)S(1)}, bf16[5,16,128]{2,1,0:T(8,128)(2,1)S(1)}, u32[]{:S(2)}, u32[]{:S(2)}) %collective-permute-start.10) | collective-permute-done | bytes 20512 | tf_op jit(solution)/shard_map/ppermute | solution.py:678
  29.0 1.7 %collective-permute-done.9.refs_3_ = bf16[5,16,128]{2,1,0:T(8,128)(2,1)S(1)} collective-permute-done((bf16[5,16,128]{2,1,0:T(8,128)(2,1)S(1)}, bf16[5,16,128]{2,1,0:T(8,128)(2,1)S(1)}, u32[]{:S(2)}, u32[]{:S(2)}) %collective-permute-start.9) | collective-permute-done | bytes 20512 | tf_op jit(solution)/shard_map/ppermute | solution.py:678
  30.9 0.5 %collective-permute-start.12 = (bf16[128,128]{1,0:T(8,128)(2,1)S(1)}, bf16[128,128]{1,0:T(8,128)(2,1)S(1)}, u32[]{:S(2)}, u32[]{:S(2)}) collective-permute-start(bf16[128,128]{1,0:T(8,128)(2,1)S(1)} %pad_maximum_fusion), channel_id=1, source_target_pairs={{0,1},{1,2},{2,3},{3,0},{4,5},{5,6},{6,7},{7,4},{8,9},{9,10},{10,1... | collective-permute-start | bytes 98312 | tf_op jit(solution)/shard_map/ppermute | solution.py:678
  31.4 1.6 %second_middle.1 = (f32[96,128]{1,0:T(8,128)S(1)}, f32[4,48,128]{2,1,0:T(8,128)S(1)}, bf16[20,240,128]{2,1,0:T(8,128)(2,1)S(1)}) custom-call(s32[4]{0:T(128)S(1)} %pad_add_fusion.flags.refs_0_, bf16[16,80,128]{2,1,0:T(8,128)(2,1)S(1)} %get-tuple-element.54.refs_1_, bf16[5,16,128]{2,1,0:T(8,128)(2,1)S(1)} %collective-permute-done.10.refs_2_, ...), custom_call_target="tpu_custom_call" | custom-call | tf_op jit(solution)/shard_map/second_middle/pallas_call | solution.py:761
  33.0 1.2 %collective-permute-done.12.refs_3_ = bf16[128,128]{1,0:T(8,128)(2,1)S(1)} collective-permute-done((bf16[128,128]{1,0:T(8,128)(2,1)S(1)}, bf16[128,128]{1,0:T(8,128)(2,1)S(1)}, u32[]{:S(2)}, u32[]{:S(2)}) %collective-permute-start.12) | collective-permute-done | bytes 32800 | tf_op jit(solution)/shard_map/ppermute | solution.py:678
  34.3 4.3 %second_step.1 = bf16[80,16,128]{2,1,0:T(8,128)(2,1)} custom-call(s32[4]{0:T(128)S(1)} %pad_add_fusion.flags.refs_0_, bf16[16,80,128]{2,1,0:T(8,128)(2,1)S(1)} %get-tuple-element.54.refs_1_, s32[16,128]{1,0:T(8,128)S(1)} %copy-done.1, bf16[128,128]{1,0:T(8,128)(2,1)S(1)} %collective-permute-done.12.refs_3_, ...), custom_call_target="tpu_custom_call" | custom-call | tf_op jit(solution)/shard_map/second_step/pallas_call | solution.py:761
  (28 shorter events, 0.2 us)
Async XLA Ops:
  0.0 17.4 %copy-start.1 = (s32[16,128]{1,0:T(8,128)S(1)}, s32[16,128]{1,0:T(8,128)}, u32[]{:S(2)}) copy-start(s32[16,128]{1,0:T(8,128)} %refs_2_.3) | copy-start | bytes 24580
  0.0 17.4 %copy-start.2 = (f32[2,4,80]{2,1,0:T(4,128)S(1)}, f32[2,4,80]{2,1,0:T(4,128)}, u32[]{:S(2)}) copy-start(f32[2,4,80]{2,1,0:T(4,128)} %refs_14_.1) | copy-start | bytes 7684
  0.0 17.4 %copy-start = (bf16[80,384]{1,0:T(8,128)(2,1)S(1)}, bf16[80,384]{1,0:T(8,128)(2,1)}, u32[]{:S(2)}) copy-start(bf16[80,384]{1,0:T(8,128)(2,1)} %refs_13_.3) | copy-start | bytes 184324
  2.3 8.7 %collective-permute-start = (bf16[272,128]{1,0:T(8,128)(2,1)S(1)}, bf16[272,128]{1,0:T(8,128)(2,1)S(1)}, u32[]{:S(2)}, u32[]{:S(2)}) collective-permute-start(bf16[272,128]{1,0:T(8,128)(2,1)S(1)} %get-tuple-element.38), channel_id=1, source_target_pairs={{0,4},{1,5},{2,6},{3,7},{4,0},{5,1},{6,2},{7,3},{8,12},{9,13},{10,... | collective-permute-start | bytes 208904 | tf_op jit(solution)/shard_map/ppermute | solution.py:678
  5.4 5.6 %collective-permute-start.1 = (bf16[272,128]{1,0:T(8,128)(2,1)S(1)}, bf16[272,128]{1,0:T(8,128)(2,1)S(1)}, u32[]{:S(2)}, u32[]{:S(2)}) collective-permute-start(bf16[272,128]{1,0:T(8,128)(2,1)S(1)} %get-tuple-element.39), channel_id=1, source_target_pairs={{0,16},{1,17},{2,18},{3,19},{4,8},{5,9},{6,10},{7,11},{8,4},{9,5},... | collective-permute-start | bytes 208904 | tf_op jit(solution)/shard_map/ppermute | solution.py:678
  6.9 4.1 %collective-permute-start.4 = (bf16[5,16,128]{2,1,0:T(8,128)(2,1)S(1)}, bf16[5,16,128]{2,1,0:T(8,128)(2,1)S(1)}, u32[]{:S(2)}, u32[]{:S(2)}) collective-permute-start(bf16[5,16,128]{2,1,0:T(8,128)(2,1)S(1)} %get-tuple-element.40), channel_id=1, source_target_pairs={{0,16},{1,17},{2,18},{3,19},{4,24},{5,25},{6,26},{7,27},{8,20},{9,... | collective-permute-start | bytes 61448 | tf_op jit(solution)/shard_map/ppermute | solution.py:678
  7.4 4.7 %collective-permute-start.3 = (bf16[5,16,128]{2,1,0:T(8,128)(2,1)S(1)}, bf16[5,16,128]{2,1,0:T(8,128)(2,1)S(1)}, u32[]{:S(2)}, u32[]{:S(2)}) collective-permute-start(bf16[5,16,128]{2,1,0:T(8,128)(2,1)S(1)} %get-tuple-element.40), channel_id=1, source_target_pairs={{0,20},{1,21},{2,22},{3,23},{4,16},{5,17},{6,18},{7,19},{8,28},{9,... | collective-permute-start | bytes 61448 | tf_op jit(solution)/shard_map/ppermute | solution.py:678
  9.5 3.8 %collective-permute-start.2 = (bf16[5,16,128]{2,1,0:T(8,128)(2,1)S(1)}, bf16[5,16,128]{2,1,0:T(8,128)(2,1)S(1)}, u32[]{:S(2)}, u32[]{:S(2)}) collective-permute-start(bf16[5,16,128]{2,1,0:T(8,128)(2,1)S(1)} %get-tuple-element.40), channel_id=1, source_target_pairs={{0,16},{1,17},{2,18},{3,19},{4,20},{5,21},{6,22},{7,23},{8,24},{9,... | collective-permute-start | bytes 61448 | tf_op jit(solution)/shard_map/ppermute | solution.py:678
  13.3 2.5 %collective-permute-start.6 = (bf16[176,128]{1,0:T(8,128)(2,1)S(1)}, bf16[176,128]{1,0:T(8,128)(2,1)S(1)}, u32[]{:S(2)}, u32[]{:S(2)}) collective-permute-start(bf16[176,128]{1,0:T(8,128)(2,1)S(1)} %constant_dynamic-update-slice_fusion), channel_id=1, source_target_pairs={{0,3},{1,0},{2,1},{3,2},{4,7},{5,4},{6,5},{7,6},{8,11},{9,8},{10,9... | collective-permute-start | bytes 135176 | tf_op jit(solution)/shard_map/ppermute | solution.py:678
  13.4 4.0 %collective-permute-start.5 = (bf16[176,128]{1,0:T(8,128)(2,1)S(1)}, bf16[176,128]{1,0:T(8,128)(2,1)S(1)}, u32[]{:S(2)}, u32[]{:S(2)}) collective-permute-start(bf16[176,128]{1,0:T(8,128)(2,1)S(1)} %constant_dynamic-update-slice_fusion), channel_id=1, source_target_pairs={{0,1},{1,2},{2,3},{3,0},{4,5},{5,6},{6,7},{7,4},{8,9},{9,10},{10,1... | collective-permute-start | bytes 135176 | tf_op jit(solution)/shard_map/ppermute | solution.py:678
  21.2 7.3 %collective-permute-start.7 = (bf16[240,128]{1,0:T(8,128)(2,1)S(1)}, bf16[240,128]{1,0:T(8,128)(2,1)S(1)}, u32[]{:S(2)}, u32[]{:S(2)}) collective-permute-start(bf16[240,128]{1,0:T(8,128)(2,1)S(1)} %get-tuple-element.56), channel_id=1, source_target_pairs={{0,4},{1,5},{2,6},{3,7},{4,0},{5,1},{6,2},{7,3},{8,12},{9,13},{10,... | collective-permute-start | bytes 184328 | tf_op jit(solution)/shard_map/ppermute | solution.py:678
  22.3 6.1 %collective-permute-start.8 = (bf16[240,128]{1,0:T(8,128)(2,1)S(1)}, bf16[240,128]{1,0:T(8,128)(2,1)S(1)}, u32[]{:S(2)}, u32[]{:S(2)}) collective-permute-start(bf16[240,128]{1,0:T(8,128)(2,1)S(1)} %get-tuple-element.57), channel_id=1, source_target_pairs={{0,16},{1,17},{2,18},{3,19},{4,8},{5,9},{6,10},{7,11},{8,4},{9,5},... | collective-permute-start | bytes 184328 | tf_op jit(solution)/shard_map/ppermute | solution.py:678
  23.9 4.6 %collective-permute-start.11 = (bf16[5,16,128]{2,1,0:T(8,128)(2,1)S(1)}, bf16[5,16,128]{2,1,0:T(8,128)(2,1)S(1)}, u32[]{:S(2)}, u32[]{:S(2)}) collective-permute-start(bf16[5,16,128]{2,1,0:T(8,128)(2,1)S(1)} %get-tuple-element.58), channel_id=1, source_target_pairs={{0,16},{1,17},{2,18},{3,19},{4,24},{5,25},{6,26},{7,27},{8,20},{9,... | collective-permute-start | bytes 61448 | tf_op jit(solution)/shard_map/ppermute | solution.py:678
  24.4 4.7 %collective-permute-start.10 = (bf16[5,16,128]{2,1,0:T(8,128)(2,1)S(1)}, bf16[5,16,128]{2,1,0:T(8,128)(2,1)S(1)}, u32[]{:S(2)}, u32[]{:S(2)}) collective-permute-start(bf16[5,16,128]{2,1,0:T(8,128)(2,1)S(1)} %get-tuple-element.58), channel_id=1, source_target_pairs={{0,20},{1,21},{2,22},{3,23},{4,16},{5,17},{6,18},{7,19},{8,28},{9,... | collective-permute-start | bytes 61448 | tf_op jit(solution)/shard_map/ppermute | solution.py:678
  27.0 3.8 %collective-permute-start.9 = (bf16[5,16,128]{2,1,0:T(8,128)(2,1)S(1)}, bf16[5,16,128]{2,1,0:T(8,128)(2,1)S(1)}, u32[]{:S(2)}, u32[]{:S(2)}) collective-permute-start(bf16[5,16,128]{2,1,0:T(8,128)(2,1)S(1)} %get-tuple-element.58), channel_id=1, source_target_pairs={{0,16},{1,17},{2,18},{3,19},{4,20},{5,21},{6,22},{7,23},{8,24},{9,... | collective-permute-start | bytes 61448 | tf_op jit(solution)/shard_map/ppermute | solution.py:678
  30.8 2.2 %collective-permute-start.13 = (bf16[128,128]{1,0:T(8,128)(2,1)S(1)}, bf16[128,128]{1,0:T(8,128)(2,1)S(1)}, u32[]{:S(2)}, u32[]{:S(2)}) collective-permute-start(bf16[128,128]{1,0:T(8,128)(2,1)S(1)} %pad_maximum_fusion), channel_id=1, source_target_pairs={{0,3},{1,0},{2,1},{3,2},{4,7},{5,4},{6,5},{7,6},{8,11},{9,8},{10,9... | collective-permute-start | bytes 98312 | tf_op jit(solution)/shard_map/ppermute | solution.py:678
  30.9 3.4 %collective-permute-start.12 = (bf16[128,128]{1,0:T(8,128)(2,1)S(1)}, bf16[128,128]{1,0:T(8,128)(2,1)S(1)}, u32[]{:S(2)}, u32[]{:S(2)}) collective-permute-start(bf16[128,128]{1,0:T(8,128)(2,1)S(1)} %pad_maximum_fusion), channel_id=1, source_target_pairs={{0,1},{1,2},{2,3},{3,0},{4,5},{5,6},{6,7},{7,4},{8,9},{9,10},{10,1... | collective-permute-start | bytes 98312 | tf_op jit(solution)/shard_map/ppermute | solution.py:678

commit v9 on v7

--- a/solution.py
+++ b/solution.py
@@ -47,6 +47,7 @@
         self.tiles = -(-(rows + 4) // 8)
         self.tall = 8 * self.tiles
         self.strip = 2 * CH + self.edge_rows
+        self.sent = self.strip + 16 * (NS + 1)
 
 
 def put_edges(ref, at, edges, d):
@@ -118,7 +119,7 @@
     return high, mid, values - high - mid
 
 
-def emit(state, surface, wet, flags, fields, own_edges, one, two, raw, d):
+def emit(state, surface, wet, flags, fields, columns, own_edges, one, two, raw, d):
     half = d.rows // 2
     is_ocean, even = flags[0] != 0, flags[3] == 0
     gap = jnp.zeros((4, CH), F32)
@@ -135,8 +136,9 @@
     keeping = jnp.where(is_ocean, wet[...].astype(F32), 1.0)
     whole = [raw[pl.ds(field, d.rows, stride=8), :] * keeping for field in range(NS)]
     for field in range(NS):
-        fields[field] = whole[field].astype(BF16)
-    fields[NS] = pack_columns(whole, REACH).astype(BF16)
+        fields[field * d.rows : (field + 1) * d.rows, :] = whole[field].astype(BF16)
+    packed = pack_columns(whole, REACH)
+    columns[...] = packed.astype(BF16)
     edges = edge_columns(state, d)
     put_edges(own_edges, 0, edges, d)
     row = lanes(edges.shape) % d.block
@@ -148,6 +150,10 @@
         ref[0:CH, :] = state[first]
         ref[CH : 2 * CH, :] = state[first + 1]
         put_edges(ref, 2 * CH, jnp.where(down, downward, upward), d)
+        for index, values in enumerate(whole + [packed]):
+            part = jnp.where(down, values[d.rows - 16 :], values[:16])
+            at = d.strip + 16 * index
+            ref[at : at + 16, :] = part.astype(BF16)
 
 
 def fetch(sources, targets, sems):
@@ -162,7 +168,7 @@
 
 def start_kernel(
     d, flags, far_given, far_surface, far_wet, far_offsets, far_weights,
-    state, planes, sides, fields, own_edges, one, two,
+    state, planes, sides, fields, columns, own_edges, one, two,
     raw, tall, turned, given, surface, wet, offsets, weights, sems,
 ):
     rows = d.rows
@@ -181,7 +187,7 @@
         state[row] = turned[pl.ds(row, CH, stride=rows), :].astype(BF16)
     for copy in copies[len(pieces) :]:
         copy.wait()
-    emit(state, surface, wet, flags, fields, own_edges, one, two, raw, d)
+    emit(state, surface, wet, flags, fields, columns, own_edges, one, two, raw, d)
     for k in range(NK):
         code = (offsets[0, k] * SPAN + offsets[1, k]).astype(F32)
         tall[k * rows : (k + 1) * rows, :] = code
@@ -193,8 +199,8 @@
     even = flags[3] == 0
     for (ref, first), down in zip(strips(one, two, even, d), (even, jnp.logical_not(even))):
         strip = [tall[pl.ds(first + step, 2 * NK, stride=rows), :] for step in range(2)]
-        ref[d.strip : d.strip + 16, :] = jnp.concatenate(strip, axis=0).astype(BF16)
-        ref[d.strip + 16 : d.strip + 32, :] = jnp.where(
+        ref[d.sent : d.sent + 16, :] = jnp.concatenate(strip, axis=0).astype(BF16)
+        ref[d.sent + 16 : d.sent + 32, :] = jnp.where(
             down, packed[rows - 16 : rows], packed[0:16]
         ).astype(BF16)
 
@@ -518,7 +524,7 @@
 def middle_kernel(d, opening, *refs):
     refs = list(refs)
     take = lambda count: [refs.pop(0) for _ in range(count)]
-    flags, state, field_one, beside, field_two, from_one, from_two = take(7)
+    flags, state, beside, from_one, from_two = take(5)
     if opening:
         planes, *far_weights = take(6)
     else:
@@ -536,7 +542,7 @@
 
         @pl.when(is_ocean != 0)
         def _():
-            base = d.strip
+            base = d.sent
             pair = up_and_down(from_one[base : base + 16, :], from_two[base : base + 16, :])
             plan_x[...] = jnp.zeros_like(plan_x)
             for step, strip in zip((0, rows + 2), pair):
@@ -546,11 +552,14 @@
         for plane in range(2 * NK):
             plan_x[plane * tall + 2 : plane * tall + 2 + rows, :] = planes[plane].astype(F32)
 
+    last = 64 + NS * rows
     for field in range(NS):
-        pair = up_and_down(field_one[field], field_two[field])
-        fields_x[field, 0:16, :] = pair[0][rows - 16 : rows]
-        fields_x[field, 16 : 16 + rows, :] = beside[field].astype(F32)
-        fields_x[field, 16 + rows : 32 + rows, :] = pair[1][0:16]
+        start = field * 16
+        pair = up_and_down(beside[start : start + 16, :], beside[last + start : last + start + 16, :])
+        fields_x[field, 0:16, :] = pair[0]
+        start = 64 + field * rows
+        fields_x[field, 16 : 16 + rows, :] = beside[start : start + rows, :].astype(F32)
+        fields_x[field, 16 + rows : 32 + rows, :] = pair[1]
 
     @pl.when(is_ocean == 0)
     def _():
@@ -571,7 +580,7 @@
 def step_kernel(d, opening, closing, *refs):
     refs = list(refs)
     take = lambda count: [refs.pop(0) for _ in range(count)]
-    flags, state, wet, from_left, from_right = take(5)
+    flags, state, wet, columns_left, columns_right, from_left, from_right = take(7)
     part_x, fields_x, rolled, edges, plan_x, air_in, first, second, atm_out = take(9)
     if not opening:
         (plan_y,) = take(1)
@@ -579,7 +588,7 @@
         (surface,) = take(1)
     (out,) = take(1)
     if not closing:
-        fields, new_edges, one, two = take(4)
+        fields, columns, new_edges, one, two = take(5)
     if opening:
         (plan_y,) = take(1)
     fields_y, forcing_x, forcing_y, stack, hidden, side, raw = take(7)
@@ -592,7 +601,7 @@
         @pl.when(is_ocean != 0)
         def _():
             plan_y[...] = jnp.zeros_like(plan_y)
-            base = rows + 32 + d.edge_rows
+            base = d.edge_rows
             parts = [
                 (ref[base : base + 16, :], ref[base + 16 + rows : base + 32 + rows, :],
                  ref[base + 16 : base + 16 + rows, :])
@@ -610,7 +619,7 @@
 
     parts = [
         (ref[0:16, :], ref[16 + rows : 32 + rows, :], ref[16 : 16 + rows, :])
-        for ref in (from_left, from_right)
+        for ref in (columns_left, columns_right)
     ]
     for field in range(NS):
         first_end, second_end, own = [
@@ -639,7 +648,7 @@
         regrid_beside(
             fields_x, fields_y, plan_x, plan_y, part_x, forcing_x, forcing_y, 0, d.tiles, tall, True
         )
-        joined = [get_edges(ref, rows + 32, d) for ref in (from_left, from_right)]
+        joined = [get_edges(ref, 0, d) for ref in (from_left, from_right)]
         sea(
             state, rolled, get_edges(edges, 0, d), *joined, put, forcing_x, forcing_y,
             first, second, wet, at_top, at_bottom, stack, hidden, side, d,
@@ -648,7 +657,7 @@
     if closing:
         out[...] = raw[...].reshape(CH, rows, 128).astype(BF16)
     else:
-        emit(out, surface, wet, flags, fields, new_edges, one, two, raw, d)
+        emit(out, surface, wet, flags, fields, columns, new_edges, one, two, raw, d)
 
 
 VMEM = pl.BlockSpec(memory_space=pltpu.VMEM)
@@ -676,45 +685,45 @@
     return lax.ppermute(x, names, pairs)
 
 
-def swap_rows(x, turn, across):
+def swap_rows(x, turn):
     count = lax.axis_size("lat")
 
     def move(group, lat, lon):
         other = ((lat + turn) ^ 1) - turn
         if not 0 <= other < count:
             return 1 - group, lat, lon
-        return (1 - group if across else group), other, lon
+        return group, other, lon
 
     return send(x, move)
 
 
-def exchange(fields, own_edges, one, two, sides, d):
-    rows = d.rows
-    from_one = swap_rows(one, 0, False)
-    from_two = swap_rows(two, 1, False)
-    field_one = swap_rows(fields, 0, True)
-    field_two = swap_rows(fields, 1, True)
-    beside = send(fields, lambda g, i, j: (1 - g, i, j))
+def exchange(fields, columns, own_edges, one, two, sides, d):
+    from_one = swap_rows(one, 0)
+    from_two = swap_rows(two, 1)
     lat, count = lax.axis_index("lat"), lax.axis_size("lat")
-    odd = lat % 2 == 1
     edges = own_edges
     for turn, ref in ((0, from_one), (1, from_two)):
         other = ((lat + turn) ^ 1) - turn
         there = (other >= 0) & (other < count)
         edges = edges + jnp.where(there, ref[2 * CH : d.strip], 0)
-    outer = [field_one[NS], field_two[NS]]
-    if rows != 16:
-        outer = [
-            jnp.where(odd, outer[0][rows - 16 :], outer[0][:16]),
-            jnp.where(odd, outer[1][:16], outer[1][rows - 16 :]),
-        ]
-    packed = [outer[0], beside[NS], outer[1], edges]
+    across = d.strip + 16 * NS
+    whole = [from_one[d.strip : across], fields, from_two[d.strip : across]]
+    whole = jnp.concatenate(whole, axis=0)
+    narrow = [from_one[across : d.sent], columns, from_two[across : d.sent]]
+    narrow = jnp.concatenate(narrow, axis=0)
+    packed = edges
     if sides is not None:
-        packed += [from_one[d.strip + 16 :], sides, from_two[d.strip + 16 :]]
-    packed = jnp.concatenate(packed, axis=0)
-    from_left = send(packed, lambda g, i, j: (g, i, j + 1))
-    from_right = send(packed, lambda g, i, j: (g, i, j - 1))
-    return (field_one, beside, field_two, from_one, from_two), (from_left, from_right), edges
+        packed = [edges, from_one[d.sent + 16 :], sides, from_two[d.sent + 16 :]]
+        packed = jnp.concatenate(packed, axis=0)
+    whole, narrow, packed = lax.optimization_barrier((whole, narrow, packed))
+    beside = send(whole, lambda g, i, j: (1 - g, i, j))
+    horizontal = (
+        send(narrow, lambda g, i, j: (1 - g, i, j + 1)),
+        send(narrow, lambda g, i, j: (1 - g, i, j - 1)),
+        send(packed, lambda g, i, j: (g, i, j + 1)),
+        send(packed, lambda g, i, j: (g, i, j - 1)),
+    )
+    return (beside, from_one, from_two), horizontal, edges
 
 
 def local(
@@ -738,10 +747,11 @@
     )
     state_shape = shape(rows, CH, 128)
     emitted = [
-        shape(NS + 1, rows, 128),
+        shape(NS * rows, 128),
+        shape(rows, 128),
         shape(d.edge_rows, 128),
-        shape(d.strip, 128),
-        shape(d.strip, 128),
+        shape(d.sent, 128),
+        shape(d.sent, 128),
     ]
     raw = pltpu.VMEM((rows * 8, 128), F32)
     turned = pltpu.VMEM((CH * rows, 128), F32)
@@ -762,12 +772,12 @@
             name=name,
         )(flags, *operands, *far)
 
-    state, planes, sides, fields, edges, one, two = call(
+    state, planes, sides, *sending = call(
         functools.partial(start_kernel, d),
         (),
         [state_shape, shape(2 * NK, rows, 128), shape(rows, 128)]
-        + emitted[:2]
-        + [shape(d.strip + 32, 128)] * 2,
+        + emitted[:3]
+        + [shape(d.sent + 32, 128)] * 2,
         [raw, pltpu.VMEM((2 * NK * rows, 128), F32), turned],
         "start",
         (coupled_state[0], surface_proj, land_mask, regrid_offsets[0], regrid_weights[0]),
@@ -789,7 +799,7 @@
         pltpu.VMEM((768, d.edge), BF16),
     ]
 
-    vertical, horizontal, edges = exchange(fields, edges, one, two, sides, d)
+    vertical, horizontal, edges = exchange(*sending, sides, d)
     *shared, plan_x, air_in, first, second = call(
         functools.partial(middle_kernel, d, True),
         (state, *vertical, planes),
@@ -799,7 +809,7 @@
         raw_weights,
     )
     weights = (air_in, first, second, atm_out)
-    state, fields, edges, one, two, plan_y = call(
+    state, *sending, plan_y = call(
         functools.partial(step_kernel, d, True, False),
         (state, land_mask, *horizontal, *shared, edges, plan_x, *weights, surface_proj),
         [state_shape] + emitted + [plan],
@@ -807,7 +817,7 @@
         "first_step",
     )
 
-    vertical, horizontal, edges = exchange(fields, edges, one, two, None, d)
+    vertical, horizontal, edges = exchange(*sending, None, d)
     shared = call(
         functools.partial(middle_kernel, d, False),
         (state, *vertical, plan_x),

time: 40.2 us -> 39.2 us (0.975)
  waiting for transfers between devices: 10.1 us -> 8.79 us
    ppermute x14, waiting for transfers between devices: 10.1 us -> 8.79 us  [send(): return lax.ppermute(x, names, pairs)]
where the time goes in v9:
time: 39.2 us; the launch traced here: 38.9 us
  starting transfers between devices  16 us (41%)
  Pallas kernels  13.8 us (35%)
  waiting for transfers between devices  8.79 us (22%)
    ppermute x14, starting transfers between devices, send(): return lax.ppermute(x, names, pairs)  16 us
    pallas_call x5, Pallas kernels, call(): pl.pallas_call(kernel, out_shape=outs, in_specs=[SMEM] + [VMEM] * len(ope...  13.8 us
    ppermute x14, waiting for transfers between devices, send(): return lax.ppermute(x, names, pairs)  8.79 us
  transfers between devices with their start and end apart: 14, of which 7 were waited for; matrix products, arithmetic and copies ran while one was open for 0% of the time, Pallas kernels for 9%

profile of v9, /device:TPU:0, one launch (start us, length us, event | category | flops | bytes accessed | tf_op | source)
XLA Modules:
  0.0 38.9 jit_solution(1274164594787992601)
XLA Ops:
  0.1 2.2 %start.1 = (bf16[16,80,128]{2,1,0:T(8,128)(2,1)S(1)}, bf16[8,16,128]{2,1,0:T(8,128)(2,1)S(1)}, bf16[16,128]{1,0:T(8,128)(2,1)S(1)}, bf16[64,128]{1,0:T(8,128)(2,...) custom-call(s32[4]{0:T(128)S(1)} %pad_add_fusion.flags.refs_0_, ...), custom_call_target="tpu_custom_call" | custom-call | tf_op jit(solution)/shard_map/start/pallas_call | solution.py:765
  2.3 3.1 %collective-permute-start = (bf16[352,128]{1,0:T(8,128)(2,1)S(1)}, bf16[352,128]{1,0:T(8,128)(2,1)S(1)}, u32[]{:S(2)}, u32[]{:S(2)}) collective-permute-start(bf16[352,128]{1,0:T(8,128)(2,1)S(1)} %get-tuple-element.37), channel_id=1, source_target_pairs={{0,4},{1,5},{2,6},{3,7},{4,0},{5,1},{6,2},{7,3},{8,12},{9,13},{10,... | collective-permute-start | bytes 270344 | tf_op jit(solution)/shard_map/ppermute | solution.py:685
  5.4 1.5 %collective-permute-start.1 = (bf16[352,128]{1,0:T(8,128)(2,1)S(1)}, bf16[352,128]{1,0:T(8,128)(2,1)S(1)}, u32[]{:S(2)}, u32[]{:S(2)}) collective-permute-start(bf16[352,128]{1,0:T(8,128)(2,1)S(1)} %get-tuple-element.39), channel_id=1, source_target_pairs={{0,16},{1,17},{2,18},{3,19},{4,8},{5,9},{6,10},{7,11},{8,4},{9,5},... | collective-permute-start | bytes 270344 | tf_op jit(solution)/shard_map/ppermute | solution.py:685
  6.9 1.1 %collective-permute-done.refs_3_ = bf16[352,128]{1,0:T(8,128)(2,1)S(1)} collective-permute-done((bf16[352,128]{1,0:T(8,128)(2,1)S(1)}, bf16[352,128]{1,0:T(8,128)(2,1)S(1)}, u32[]{:S(2)}, u32[]{:S(2)}) %collective-permute-start) | collective-permute-done | bytes 90144 | tf_op jit(solution)/shard_map/ppermute | solution.py:685
  8.0 1.9 %collective-permute-done.1.refs_4_ = bf16[352,128]{1,0:T(8,128)(2,1)S(1)} collective-permute-done((bf16[352,128]{1,0:T(8,128)(2,1)S(1)}, bf16[352,128]{1,0:T(8,128)(2,1)S(1)}, u32[]{:S(2)}, u32[]{:S(2)}) %collective-permute-start.1) | collective-permute-done | bytes 90144 | tf_op jit(solution)/shard_map/ppermute | solution.py:685
  10.0 1.6 %collective-permute-start.6 = (bf16[192,128]{1,0:T(8,128)(2,1)S(1)}, bf16[192,128]{1,0:T(8,128)(2,1)S(1)}, u32[]{:S(2)}, u32[]{:S(2)}) collective-permute-start(bf16[192,128]{1,0:T(8,128)(2,1)S(1)} %pad_maximum_fusion), channel_id=1, source_target_pairs={{0,16},{1,17},{2,18},{3,19},{4,20},{5,21},{6,22},{7,23},{8,24},{9,... | collective-permute-start | bytes 147464 | tf_op jit(solution)/shard_map/ppermute | solution.py:685
  11.5 0.5 %collective-permute-start.4 = (bf16[128,128]{1,0:T(8,128)(2,1)S(1)}, bf16[128,128]{1,0:T(8,128)(2,1)S(1)}, u32[]{:S(2)}, u32[]{:S(2)}) collective-permute-start(bf16[128,128]{1,0:T(8,128)(2,1)S(1)} %pad_maximum_fusion.2), channel_id=1, source_target_pairs={{0,1},{1,2},{2,3},{3,0},{4,5},{5,6},{6,7},{7,4},{8,9},{9,10},{10,1... | collective-permute-start | bytes 98312 | tf_op jit(solution)/shard_map/ppermute | solution.py:685
  12.0 1.2 %collective-permute-start.3 = (bf16[48,128]{1,0:T(8,128)(2,1)S(1)}, bf16[48,128]{1,0:T(8,128)(2,1)S(1)}, u32[]{:S(2)}, u32[]{:S(2)}) collective-permute-start(bf16[48,128]{1,0:T(8,128)(2,1)S(1)} %pad_maximum_fusion.3), channel_id=1, source_target_pairs={{0,19},{1,16},{2,17},{3,18},{4,23},{5,20},{6,21},{7,22},{8,27},{9,... | collective-permute-start | bytes 36872 | tf_op jit(solution)/shard_map/ppermute | solution.py:685
  13.3 0.5 %collective-permute-start.2 = (bf16[48,128]{1,0:T(8,128)(2,1)S(1)}, bf16[48,128]{1,0:T(8,128)(2,1)S(1)}, u32[]{:S(2)}, u32[]{:S(2)}) collective-permute-start(bf16[48,128]{1,0:T(8,128)(2,1)S(1)} %pad_maximum_fusion.3), channel_id=1, source_target_pairs={{0,17},{1,18},{2,19},{3,16},{4,21},{5,22},{6,23},{7,20},{8,25},{9,... | collective-permute-start | bytes 36872 | tf_op jit(solution)/shard_map/ppermute | solution.py:685
  13.8 0.3 collective-permute-done.6.refs_2_
  14.1 1.9 %first_middle.1 = (f32[96,128]{1,0:T(8,128)S(1)}, f32[4,48,128]{2,1,0:T(8,128)S(1)}, bf16[20,240,128]{2,1,0:T(8,128)(2,1)S(1)}, f32[192,128]{1,0:T(8,128)S(1)}, ...) custom-call(s32[4]{0:T(128)S(1)} %pad_add_fusion.flags.refs_0_, ...), custom_call_target="tpu_custom_call" | custom-call | tf_op jit(solution)/shard_map/first_middle/pallas_call | solution.py:765
  16.1 1.2 %collective-permute-done.2.refs_3_ = bf16[48,128]{1,0:T(8,128)(2,1)S(1)} collective-permute-done((bf16[48,128]{1,0:T(8,128)(2,1)S(1)}, bf16[48,128]{1,0:T(8,128)(2,1)S(1)}, u32[]{:S(2)}, u32[]{:S(2)}) %collective-permute-start.2) | collective-permute-done | bytes 12320 | tf_op jit(solution)/shard_map/ppermute | solution.py:685
  17.3 3.8 %first_step.1 = (bf16[16,80,128]{2,1,0:T(8,128)(2,1)S(1)}, bf16[64,128]{1,0:T(8,128)(2,1)S(1)}, bf16[16,128]{1,0:T(8,128)(2,1)S(1)}, bf16[80,128]{1,0:T(8,128)(2...) custom-call(s32[4]{0:T(128)S(1)} %pad_add_fusion.flags.refs_0_, ...), custom_call_target="tpu_custom_call" | custom-call | tf_op jit(solution)/shard_map/first_step/pallas_call | solution.py:765
  21.1 1.2 %collective-permute-start.7 = (bf16[320,128]{1,0:T(8,128)(2,1)S(1)}, bf16[320,128]{1,0:T(8,128)(2,1)S(1)}, u32[]{:S(2)}, u32[]{:S(2)}) collective-permute-start(bf16[320,128]{1,0:T(8,128)(2,1)S(1)} %get-tuple-element.55), channel_id=1, source_target_pairs={{0,4},{1,5},{2,6},{3,7},{4,0},{5,1},{6,2},{7,3},{8,12},{9,13},{10,... | collective-permute-start | bytes 245768 | tf_op jit(solution)/shard_map/ppermute | solution.py:685
  22.3 2.3 %collective-permute-start.8 = (bf16[320,128]{1,0:T(8,128)(2,1)S(1)}, bf16[320,128]{1,0:T(8,128)(2,1)S(1)}, u32[]{:S(2)}, u32[]{:S(2)}) collective-permute-start(bf16[320,128]{1,0:T(8,128)(2,1)S(1)} %get-tuple-element.57), channel_id=1, source_target_pairs={{0,16},{1,17},{2,18},{3,19},{4,8},{5,9},{6,10},{7,11},{8,4},{9,5},... | collective-permute-start | bytes 245768 | tf_op jit(solution)/shard_map/ppermute | solution.py:685
  24.6 1.4 %collective-permute-done.7.refs_3_ = bf16[320,128]{1,0:T(8,128)(2,1)S(1)} collective-permute-done((bf16[320,128]{1,0:T(8,128)(2,1)S(1)}, bf16[320,128]{1,0:T(8,128)(2,1)S(1)}, u32[]{:S(2)}, u32[]{:S(2)}) %collective-permute-start.7) | collective-permute-done | bytes 81952 | tf_op jit(solution)/shard_map/ppermute | solution.py:685
  26.0 1.2 %collective-permute-done.8.refs_4_ = bf16[320,128]{1,0:T(8,128)(2,1)S(1)} collective-permute-done((bf16[320,128]{1,0:T(8,128)(2,1)S(1)}, bf16[320,128]{1,0:T(8,128)(2,1)S(1)}, u32[]{:S(2)}, u32[]{:S(2)}) %collective-permute-start.8) | collective-permute-done | bytes 81952 | tf_op jit(solution)/shard_map/ppermute | solution.py:685
  27.3 1.9 %collective-permute-start.13 = (bf16[192,128]{1,0:T(8,128)(2,1)S(1)}, bf16[192,128]{1,0:T(8,128)(2,1)S(1)}, u32[]{:S(2)}, u32[]{:S(2)}) collective-permute-start(bf16[192,128]{1,0:T(8,128)(2,1)S(1)} %pad_maximum_fusion.1), channel_id=1, source_target_pairs={{0,16},{1,17},{2,18},{3,19},{4,20},{5,21},{6,22},{7,23},{8,24},{9,... | collective-permute-start | bytes 147464 | tf_op jit(solution)/shard_map/ppermute | solution.py:685
  29.2 0.5 %collective-permute-start.11 = (bf16[80,128]{1,0:T(8,128)(2,1)S(1)}, bf16[80,128]{1,0:T(8,128)(2,1)S(1)}, u32[]{:S(2)}, u32[]{:S(2)}) collective-permute-start(bf16[80,128]{1,0:T(8,128)(2,1)S(1)} %fusion.refs_10_), channel_id=1, source_target_pairs={{0,1},{1,2},{2,3},{3,0},{4,5},{5,6},{6,7},{7,4},{8,9},{9,10},{10,1... | collective-permute-start | bytes 61448 | tf_op jit(solution)/shard_map/ppermute | solution.py:685
  29.7 0.9 %collective-permute-start.10 = (bf16[48,128]{1,0:T(8,128)(2,1)S(1)}, bf16[48,128]{1,0:T(8,128)(2,1)S(1)}, u32[]{:S(2)}, u32[]{:S(2)}) collective-permute-start(bf16[48,128]{1,0:T(8,128)(2,1)S(1)} %pad_maximum_fusion.4), channel_id=1, source_target_pairs={{0,19},{1,16},{2,17},{3,18},{4,23},{5,20},{6,21},{7,22},{8,27},{9,... | collective-permute-start | bytes 36872 | tf_op jit(solution)/shard_map/ppermute | solution.py:685
  30.6 0.8 %collective-permute-start.9 = (bf16[48,128]{1,0:T(8,128)(2,1)S(1)}, bf16[48,128]{1,0:T(8,128)(2,1)S(1)}, u32[]{:S(2)}, u32[]{:S(2)}) collective-permute-start(bf16[48,128]{1,0:T(8,128)(2,1)S(1)} %pad_maximum_fusion.4), channel_id=1, source_target_pairs={{0,17},{1,18},{2,19},{3,16},{4,21},{5,22},{6,23},{7,20},{8,25},{9,... | collective-permute-start | bytes 36872 | tf_op jit(solution)/shard_map/ppermute | solution.py:685
  31.5 1.6 %second_middle.1 = (f32[96,128]{1,0:T(8,128)S(1)}, f32[4,48,128]{2,1,0:T(8,128)S(1)}, bf16[20,240,128]{2,1,0:T(8,128)(2,1)S(1)}) custom-call(s32[4]{0:T(128)S(1)} %pad_add_fusion.flags.refs_0_, bf16[16,80,128]{2,1,0:T(8,128)(2,1)S(1)} %get-tuple-element.54.refs_1_, bf16[192,128]{1,0:T(8,128)(2,1)S(1)} %collective-permute-done.13.refs_2_, ...), custom_call_target="tpu_custom_call" | custom-call | tf_op jit(solution)/shard_map/second_middle/pallas_call | solution.py:765
  33.1 1.5 %collective-permute-done.9.refs_3_ = bf16[48,128]{1,0:T(8,128)(2,1)S(1)} collective-permute-done((bf16[48,128]{1,0:T(8,128)(2,1)S(1)}, bf16[48,128]{1,0:T(8,128)(2,1)S(1)}, u32[]{:S(2)}, u32[]{:S(2)}) %collective-permute-start.9) | collective-permute-done | bytes 12320 | tf_op jit(solution)/shard_map/ppermute | solution.py:685
  34.6 4.3 %second_step.1 = bf16[80,16,128]{2,1,0:T(8,128)(2,1)} custom-call(s32[4]{0:T(128)S(1)} %pad_add_fusion.flags.refs_0_, bf16[16,80,128]{2,1,0:T(8,128)(2,1)S(1)} %get-tuple-element.54.refs_1_, s32[16,128]{1,0:T(8,128)S(1)} %copy-done.1, bf16[48,128]{1,0:T(8,128)(2,1)S(1)} %collective-permute-done.9.refs_3_, ...), custom_call_target="tpu_custom_call" | custom-call | tf_op jit(solution)/shard_map/second_step/pallas_call | solution.py:765
  (31 shorter events, 0.2 us)
Async XLA Ops:
  0.0 17.3 %copy-start.1 = (s32[16,128]{1,0:T(8,128)S(1)}, s32[16,128]{1,0:T(8,128)}, u32[]{:S(2)}) copy-start(s32[16,128]{1,0:T(8,128)} %refs_2_.3) | copy-start | bytes 24580
  0.0 17.3 %copy-start.2 = (f32[2,4,80]{2,1,0:T(4,128)S(1)}, f32[2,4,80]{2,1,0:T(4,128)}, u32[]{:S(2)}) copy-start(f32[2,4,80]{2,1,0:T(4,128)} %refs_16_.1) | copy-start | bytes 7684
  0.0 17.3 %copy-start = (bf16[80,384]{1,0:T(8,128)(2,1)S(1)}, bf16[80,384]{1,0:T(8,128)(2,1)}, u32[]{:S(2)}) copy-start(bf16[80,384]{1,0:T(8,128)(2,1)} %refs_15_.3) | copy-start | bytes 184324
  2.3 5.7 %collective-permute-start = (bf16[352,128]{1,0:T(8,128)(2,1)S(1)}, bf16[352,128]{1,0:T(8,128)(2,1)S(1)}, u32[]{:S(2)}, u32[]{:S(2)}) collective-permute-start(bf16[352,128]{1,0:T(8,128)(2,1)S(1)} %get-tuple-element.37), channel_id=1, source_target_pairs={{0,4},{1,5},{2,6},{3,7},{4,0},{5,1},{6,2},{7,3},{8,12},{9,13},{10,... | collective-permute-start | bytes 270344 | tf_op jit(solution)/shard_map/ppermute | solution.py:685
  5.4 4.5 %collective-permute-start.1 = (bf16[352,128]{1,0:T(8,128)(2,1)S(1)}, bf16[352,128]{1,0:T(8,128)(2,1)S(1)}, u32[]{:S(2)}, u32[]{:S(2)}) collective-permute-start(bf16[352,128]{1,0:T(8,128)(2,1)S(1)} %get-tuple-element.39), channel_id=1, source_target_pairs={{0,16},{1,17},{2,18},{3,19},{4,8},{5,9},{6,10},{7,11},{8,4},{9,5},... | collective-permute-start | bytes 270344 | tf_op jit(solution)/shard_map/ppermute | solution.py:685
  10.0 4.2 %collective-permute-start.6 = (bf16[192,128]{1,0:T(8,128)(2,1)S(1)}, bf16[192,128]{1,0:T(8,128)(2,1)S(1)}, u32[]{:S(2)}, u32[]{:S(2)}) collective-permute-start(bf16[192,128]{1,0:T(8,128)(2,1)S(1)} %pad_maximum_fusion), channel_id=1, source_target_pairs={{0,16},{1,17},{2,18},{3,19},{4,20},{5,21},{6,22},{7,23},{8,24},{9,... | collective-permute-start | bytes 147464 | tf_op jit(solution)/shard_map/ppermute | solution.py:685
  11.5 5.8 %collective-permute-start.5 = (bf16[128,128]{1,0:T(8,128)(2,1)S(1)}, bf16[128,128]{1,0:T(8,128)(2,1)S(1)}, u32[]{:S(2)}, u32[]{:S(2)}) collective-permute-start(bf16[128,128]{1,0:T(8,128)(2,1)S(1)} %pad_maximum_fusion.2), channel_id=1, source_target_pairs={{0,3},{1,0},{2,1},{3,2},{4,7},{5,4},{6,5},{7,6},{8,11},{9,8},{10,9... | collective-permute-start | bytes 98312 | tf_op jit(solution)/shard_map/ppermute | solution.py:685
  11.5 5.8 %collective-permute-start.4 = (bf16[128,128]{1,0:T(8,128)(2,1)S(1)}, bf16[128,128]{1,0:T(8,128)(2,1)S(1)}, u32[]{:S(2)}, u32[]{:S(2)}) collective-permute-start(bf16[128,128]{1,0:T(8,128)(2,1)S(1)} %pad_maximum_fusion.2), channel_id=1, source_target_pairs={{0,1},{1,2},{2,3},{3,0},{4,5},{5,6},{6,7},{7,4},{8,9},{9,10},{10,1... | collective-permute-start | bytes 98312 | tf_op jit(solution)/shard_map/ppermute | solution.py:685
  12.0 4.0 %collective-permute-start.3 = (bf16[48,128]{1,0:T(8,128)(2,1)S(1)}, bf16[48,128]{1,0:T(8,128)(2,1)S(1)}, u32[]{:S(2)}, u32[]{:S(2)}) collective-permute-start(bf16[48,128]{1,0:T(8,128)(2,1)S(1)} %pad_maximum_fusion.3), channel_id=1, source_target_pairs={{0,19},{1,16},{2,17},{3,18},{4,23},{5,20},{6,21},{7,22},{8,27},{9,... | collective-permute-start | bytes 36872 | tf_op jit(solution)/shard_map/ppermute | solution.py:685
  13.3 4.1 %collective-permute-start.2 = (bf16[48,128]{1,0:T(8,128)(2,1)S(1)}, bf16[48,128]{1,0:T(8,128)(2,1)S(1)}, u32[]{:S(2)}, u32[]{:S(2)}) collective-permute-start(bf16[48,128]{1,0:T(8,128)(2,1)S(1)} %pad_maximum_fusion.3), channel_id=1, source_target_pairs={{0,17},{1,18},{2,19},{3,16},{4,21},{5,22},{6,23},{7,20},{8,25},{9,... | collective-permute-start | bytes 36872 | tf_op jit(solution)/shard_map/ppermute | solution.py:685
  21.1 4.9 %collective-permute-start.7 = (bf16[320,128]{1,0:T(8,128)(2,1)S(1)}, bf16[320,128]{1,0:T(8,128)(2,1)S(1)}, u32[]{:S(2)}, u32[]{:S(2)}) collective-permute-start(bf16[320,128]{1,0:T(8,128)(2,1)S(1)} %get-tuple-element.55), channel_id=1, source_target_pairs={{0,4},{1,5},{2,6},{3,7},{4,0},{5,1},{6,2},{7,3},{8,12},{9,13},{10,... | collective-permute-start | bytes 245768 | tf_op jit(solution)/shard_map/ppermute | solution.py:685
  22.3 4.9 %collective-permute-start.8 = (bf16[320,128]{1,0:T(8,128)(2,1)S(1)}, bf16[320,128]{1,0:T(8,128)(2,1)S(1)}, u32[]{:S(2)}, u32[]{:S(2)}) collective-permute-start(bf16[320,128]{1,0:T(8,128)(2,1)S(1)} %get-tuple-element.57), channel_id=1, source_target_pairs={{0,16},{1,17},{2,18},{3,19},{4,8},{5,9},{6,10},{7,11},{8,4},{9,5},... | collective-permute-start | bytes 245768 | tf_op jit(solution)/shard_map/ppermute | solution.py:685
  27.3 4.2 %collective-permute-start.13 = (bf16[192,128]{1,0:T(8,128)(2,1)S(1)}, bf16[192,128]{1,0:T(8,128)(2,1)S(1)}, u32[]{:S(2)}, u32[]{:S(2)}) collective-permute-start(bf16[192,128]{1,0:T(8,128)(2,1)S(1)} %pad_maximum_fusion.1), channel_id=1, source_target_pairs={{0,16},{1,17},{2,18},{3,19},{4,20},{5,21},{6,22},{7,23},{8,24},{9,... | collective-permute-start | bytes 147464 | tf_op jit(solution)/shard_map/ppermute | solution.py:685
  29.2 5.4 %collective-permute-start.12 = (bf16[80,128]{1,0:T(8,128)(2,1)S(1)}, bf16[80,128]{1,0:T(8,128)(2,1)S(1)}, u32[]{:S(2)}, u32[]{:S(2)}) collective-permute-start(bf16[80,128]{1,0:T(8,128)(2,1)S(1)} %fusion.refs_10_), channel_id=1, source_target_pairs={{0,3},{1,0},{2,1},{3,2},{4,7},{5,4},{6,5},{7,6},{8,11},{9,8},{10,9... | collective-permute-start | bytes 61448 | tf_op jit(solution)/shard_map/ppermute | solution.py:685
  29.2 5.4 %collective-permute-start.11 = (bf16[80,128]{1,0:T(8,128)(2,1)S(1)}, bf16[80,128]{1,0:T(8,128)(2,1)S(1)}, u32[]{:S(2)}, u32[]{:S(2)}) collective-permute-start(bf16[80,128]{1,0:T(8,128)(2,1)S(1)} %fusion.refs_10_), channel_id=1, source_target_pairs={{0,1},{1,2},{2,3},{3,0},{4,5},{5,6},{6,7},{7,4},{8,9},{9,10},{10,1... | collective-permute-start | bytes 61448 | tf_op jit(solution)/shard_map/ppermute | solution.py:685
  29.7 3.4 %collective-permute-start.10 = (bf16[48,128]{1,0:T(8,128)(2,1)S(1)}, bf16[48,128]{1,0:T(8,128)(2,1)S(1)}, u32[]{:S(2)}, u32[]{:S(2)}) collective-permute-start(bf16[48,128]{1,0:T(8,128)(2,1)S(1)} %pad_maximum_fusion.4), channel_id=1, source_target_pairs={{0,19},{1,16},{2,17},{3,18},{4,23},{5,20},{6,21},{7,22},{8,27},{9,... | collective-permute-start | bytes 36872 | tf_op jit(solution)/shard_map/ppermute | solution.py:685
  30.6 4.0 %collective-permute-start.9 = (bf16[48,128]{1,0:T(8,128)(2,1)S(1)}, bf16[48,128]{1,0:T(8,128)(2,1)S(1)}, u32[]{:S(2)}, u32[]{:S(2)}) collective-permute-start(bf16[48,128]{1,0:T(8,128)(2,1)S(1)} %pad_maximum_fusion.4), channel_id=1, source_target_pairs={{0,17},{1,18},{2,19},{3,16},{4,21},{5,22},{6,23},{7,20},{8,25},{9,... | collective-permute-start | bytes 36872 | tf_op jit(solution)/shard_map/ppermute | solution.py:685

commit v10 on v8

--- a/solution.py
+++ b/solution.py
@@ -14,6 +14,7 @@
 HW = 8
 SPAN = 2 * HW + 1
 REACH = HW + 2
+FIXED = 32767.0
 HIDK = 208
 HIDP = 256
 F32 = jnp.float32
@@ -60,7 +61,7 @@
     )
 
 
-def edge_columns(state, d):
+def edge_places(places, d):
     lane = lanes((1, d.edge))
     block = lane // d.block
     row = lane % d.block - 2
@@ -68,25 +69,14 @@
     own = (row >= 0) & (row < d.rows)
     target = jnp.where(own, column, -1)
     position = subs((128, d.edge))
-    places = [
-        (position == jnp.where(row == step, target, -1)).astype(F32).astype(BF16)
-        for step in range(d.rows)
-    ]
+    for step in range(d.rows):
+        place = (position == jnp.where(row == step, target, -1)).astype(F32).astype(BF16)
+        places[step * 128 : (step + 1) * 128, :] = place
+
+
+def edge_columns(state, places, d):
     whole = jnp.concatenate([state[step] for step in range(d.rows)], axis=1)
-    total = jnp.dot(whole, jnp.concatenate(places, axis=0), preferred_element_type=F32)
-    return total.astype(BF16)
-
-
-def loop(count, unroll, body):
-    while count % unroll:
-        unroll -= 1
-
-    def several(step, carry):
-        for offset in range(unroll):
-            body(step * unroll + offset)
-        return carry
-
-    lax.fori_loop(0, count // unroll, several, 0)
+    return jnp.dot(whole, places[...], preferred_element_type=F32).astype(BF16)
 
 
 def pack_columns(values, reach):
@@ -118,7 +108,7 @@
     return high, mid, values - high - mid
 
 
-def emit(state, surface, wet, flags, fields, own_edges, one, two, raw, d):
+def emit(state, surface, wet, flags, places, fields, own_edges, one, two, raw, d):
     half = d.rows // 2
     is_ocean, even = flags[0] != 0, flags[3] == 0
     gap = jnp.zeros((4, CH), F32)
@@ -137,7 +127,7 @@
     for field in range(NS):
         fields[field] = whole[field].astype(BF16)
     fields[NS] = pack_columns(whole, REACH).astype(BF16)
-    edges = edge_columns(state, d)
+    edges = edge_columns(state, places, d)
     put_edges(own_edges, 0, edges, d)
     row = lanes(edges.shape) % d.block
     downward = jnp.where(row < 2, roll(edges, -d.rows), jnp.zeros_like(edges))
@@ -162,7 +152,7 @@
 
 def start_kernel(
     d, flags, far_given, far_surface, far_wet, far_offsets, far_weights,
-    state, planes, sides, fields, own_edges, one, two,
+    state, planes, sides, places, fields, own_edges, one, two,
     raw, tall, turned, given, surface, wet, offsets, weights, sems,
 ):
     rows = d.rows
@@ -172,6 +162,7 @@
         [given.at[piece] for piece in pieces] + [surface, wet, offsets, weights],
         sems,
     )
+    edge_places(places, d)
     for index, piece in enumerate(pieces):
         copies[index].wait()
         turned[index * 16 * rows : (index + 1) * 16 * rows, :] = (
@@ -181,7 +172,7 @@
         state[row] = turned[pl.ds(row, CH, stride=rows), :].astype(BF16)
     for copy in copies[len(pieces) :]:
         copy.wait()
-    emit(state, surface, wet, flags, fields, own_edges, one, two, raw, d)
+    emit(state, surface, wet, flags, places, fields, own_edges, one, two, raw, d)
     for k in range(NK):
         code = (offsets[0, k] * SPAN + offsets[1, k]).astype(F32)
         tall[k * rows : (k + 1) * rows, :] = code
@@ -218,28 +209,41 @@
     )
 
 
-def select_rows(sources, start, picks):
-    chosen = [[jnp.zeros((8, 128), F32) for _ in range(NS)] for _ in picks]
+def couple(fields, coupled, rows):
+    largest = None
+    for field in range(NS):
+        here = jnp.max(jnp.abs(fields[field]), axis=0, keepdims=True)
+        largest = here if largest is None else jnp.maximum(largest, here)
+    largest = jnp.maximum(jnp.max(largest, axis=1, keepdims=True), 1e-30)
+    scale = FIXED / largest
+    for pair in range(NS // 2):
+        high, low = [
+            jnp.floor(fields[2 * pair + part] * scale + 0.5).astype(jnp.int32) for part in range(2)
+        ]
+        coupled[pair] = high * (1 << 16) + (low + (1 << 15))
+    return largest * (1 / FIXED)
+
+
+def uncouple(values):
+    high = lax.shift_right_arithmetic(values, 16)
+    low = (values & 0xFFFF) - (1 << 15)
+    return high.astype(F32), low.astype(F32)
+
+
+def select_rows(source, start, picks):
+    chosen = [[jnp.full((8, 128), 1 << 15, jnp.int32) for _ in range(NS // 2)] for _ in picks]
     for shift in range(-HW, HW + 1):
         at = pl.ds(start + shift, 8)
-        used = [any(pick[2][index] is not None for pick in picks) for index in range(len(sources))]
-        values = [
-            [source[field, at, :] for field in range(NS)] if use else None
-            for source, use in zip(sources, used)
-        ]
+        values = [source[pair, at, :] for pair in range(NS // 2)]
         for slot, (rows, index, allowed) in enumerate(picks):
-            here = rows == shift
-            for source, within in enumerate(allowed):
-                if within is None:
-                    continue
-                mask = here & within
-                for field in range(NS):
-                    picked = along_lanes(values[source][field], index)
-                    chosen[slot][field] = jnp.where(mask, picked, chosen[slot][field])
-    return chosen
-
-
-def regrid_inside(fields_x, plan_x, part_x, first, tiles, tall):
+            here = (rows == shift) & allowed
+            for pair in range(NS // 2):
+                picked = along_lanes(values[pair], index)
+                chosen[slot][pair] = jnp.where(here, picked, chosen[slot][pair])
+    return [[part for values in pairs for part in uncouple(values)] for pairs in chosen]
+
+
+def regrid_inside(coupled, unit, plan_x, part_x, first, tiles, tall):
     lane = lanes((8, 128))
     for step in range(tiles):
         at = first + step * 8
@@ -247,10 +251,10 @@
         weights = []
         for k in range(NK):
             rows, cols = decode(plan_x[pl.ds(k * tall + at, 8), :])
-            weights.append(plan_x[pl.ds((NK + k) * tall + at, 8), :])
+            weights.append(plan_x[pl.ds((NK + k) * tall + at, 8), :] * unit)
             column = lane + cols
-            picks.append((rows, column & 127, ((column >= 0) & (column < 128),)))
-        chosen = select_rows((fields_x,), at + 14, picks)
+            picks.append((rows, column & 127, (column >= 0) & (column < 128)))
+        chosen = select_rows(coupled, at + 14, picks)
         for field in range(NS):
             total = chosen[0][field] * weights[0]
             for k in range(1, NK):
@@ -258,16 +262,14 @@
             part_x[pl.ds(field * tall + at, 8), :] = total
 
 
-def regrid_beside(
-    fields_x, fields_y, plan_x, plan_y, part_x, forcing_x, forcing_y, first, tiles, tall, sides
-):
+def edge_lanes():
     lane = lanes((8, 128))
-    part = ((lane + 8) & 127) // 32
-    place = ((lane + 8) & 31) - 8
+    return ((lane + 8) & 127) // 32, ((lane + 8) & 31) - 8
+
+
+def plan_edges(plan_x, plan_y, plan_e, first, tiles, tall, sides):
+    part, place = edge_lanes()
     outer = place >= 8
-    inner_column = place & 127
-    outer_column = jnp.where(place < 16, place - 16, place + 112)
-    edge = (lane < 8) | (lane >= 120)
     for step in range(tiles):
         at = first + step * 8
         code = jnp.zeros((8, 128), F32)
@@ -284,11 +286,25 @@
                 )
             code = jnp.where(part == k, edge_code, code)
             weight = jnp.where(part == k, edge_weight, weight)
-        rows, cols = decode(code)
+        plan_e[pl.ds(at, 8), :] = code
+        plan_e[pl.ds(tall + at, 8), :] = weight
+
+
+def regrid_beside(coupled, unit, plan_e, part_x, forcing_x, forcing_y, first, tiles, tall, sides):
+    lane = lanes((8, 128))
+    part, place = edge_lanes()
+    outer = place >= 8
+    inner_column = place & 127
+    outer_column = jnp.where(place < 16, place - 16, place + 112)
+    edge = (lane < 8) | (lane >= 120)
+    for step in range(tiles):
+        at = first + step * 8
+        rows, cols = decode(plan_e[pl.ds(at, 8), :])
+        weight = plan_e[pl.ds(tall + at, 8), :] * unit
         column = jnp.where(outer, outer_column, inner_column) + cols
         within = (column >= 0) & (column < 128)
-        picks = [(rows, column & 127, (within & outer if sides else None, jnp.logical_not(within)))]
-        (chosen,) = select_rows((fields_x, fields_y), at + 14, picks)
+        index = jnp.where(within, column + 32, column) & 127
+        (chosen,) = select_rows(coupled, at + 14, [(rows, index, outer | jnp.logical_not(within))])
         for field in range(NS):
             part_sum = chosen[field] * weight
             extra = part_sum
@@ -303,10 +319,9 @@
                 forcing_y[pl.ds(at * 8 + field + 4, 8, stride=8), :] = extra
 
 
-def gelu(x):
+def twice_gelu(x):
     scale = (2 / jnp.pi) ** 0.5
-    half = 0.5 * x
-    return half + half * jnp.tanh(x * (scale + (scale * 0.044715) * (x * x)))
+    return x + x * jnp.tanh(x * (scale + (scale * 0.044715) * (x * x)))
 
 
 def air(state, out, forcing_x, air_in, atm_out, d):
@@ -322,12 +337,12 @@
 
     for step in range(half):
         pair = jnp.concatenate([inputs(step), inputs(step + half)], axis=1)
-        hidden = gelu(jnp.dot(air_in[...], pair, preferred_element_type=F32)).astype(BF16)
+        hidden = twice_gelu(jnp.dot(air_in[...], pair, preferred_element_type=F32)).astype(BF16)
         update = jnp.dot(atm_out[...], hidden, preferred_element_type=F32)
         for offset in range(2):
             row = step + offset * half
             change = update[:, offset * 128 : (offset + 1) * 128]
-            out(row, state[row].astype(F32) + change)
+            out(row, state[row].astype(F32) + 0.5 * change)
 
 
 def edge_forcing(forcing_x, forcing_y, d):
@@ -425,7 +440,7 @@
             ],
             axis=1,
         )
-        active = gelu(jnp.dot(ocn_in[...], taps, preferred_element_type=F32))
+        active = twice_gelu(jnp.dot(ocn_in[...], taps, preferred_element_type=F32))
         low, high = active[:, :128], active[:, 128:]
         if step == 0:
             low = jnp.where(at_top != 0, 0.0, low)
@@ -440,7 +455,7 @@
     product = jnp.dot(ocn_in[...], side[...], preferred_element_type=F32)
     spot = lanes((1, d.edge)) % block
     gone = ((spot == 0) & (at_top != 0)) | ((spot == rows + 1) & (at_bottom != 0))
-    active = jnp.where(gone, 0.0, gelu(product)).astype(BF16)
+    active = jnp.where(gone, 0.0, twice_gelu(product)).astype(BF16)
     active = jnp.concatenate([active, jnp.zeros((HIDP - HIDK, d.edge), BF16)], axis=0)
 
     def taps_of(slices):
@@ -468,7 +483,7 @@
             total = sums[CH : 2 * CH] + jnp.where(lane == 0, entry, roll(sums[0:CH], 1))
             entry = roll(from_right, 127 - block - row)[:, :128]
             total = total + jnp.where(lane == 127, entry, roll(sums[2 * CH : 3 * CH], -1))
-            update = total * wet[row : row + 1, :].astype(F32)
+            update = total * (0.5 * wet[row : row + 1, :].astype(F32))
             out(row, state[row].astype(F32) + update)
 
 
@@ -526,6 +541,8 @@
     part_x, fields_x, rolled = take(3)
     if opening:
         plan_x, *made_weights = take(4)
+    (coupled,) = take(1)
+    if opening:
         *raw_weights, sems = take(6)
         copies = fetch(far_weights, raw_weights, sems)
     rows, tall = d.rows, d.tall
@@ -552,13 +569,15 @@
         fields_x[field, 16 : 16 + rows, :] = beside[field].astype(F32)
         fields_x[field, 16 + rows : 32 + rows, :] = pair[1][0:16]
 
+    unit = couple(fields_x, coupled, rows)
+
     @pl.when(is_ocean == 0)
     def _():
-        regrid_inside(fields_x, plan_x, part_x, 2, rows // 8, tall)
+        regrid_inside(coupled, unit, plan_x, part_x, 2, rows // 8, tall)
 
     @pl.when(is_ocean != 0)
     def _():
-        regrid_inside(fields_x, plan_x, part_x, 0, d.tiles, tall)
+        regrid_inside(coupled, unit, plan_x, part_x, 0, d.tiles, tall)
         upper, lower = up_and_down(from_one[0 : 2 * CH, :], from_two[0 : 2 * CH, :])
         roll_rows(state, upper.astype(BF16), lower.astype(BF16), rolled, d)
 
@@ -574,15 +593,17 @@
     flags, state, wet, from_left, from_right = take(5)
     part_x, fields_x, rolled, edges, plan_x, air_in, first, second, atm_out = take(9)
     if not opening:
-        (plan_y,) = take(1)
+        (plan_e,) = take(1)
     if not closing:
-        (surface,) = take(1)
+        surface, places = take(2)
     (out,) = take(1)
     if not closing:
         fields, new_edges, one, two = take(4)
     if opening:
+        (plan_e,) = take(1)
+    window, coupled, forcing_x, forcing_y, stack, hidden, side, raw = take(8)
+    if opening:
         (plan_y,) = take(1)
-    fields_y, forcing_x, forcing_y, stack, hidden, side, raw = take(7)
     rows, tall = d.rows, d.tall
     is_ocean, at_top, at_bottom = flags[0], flags[1], flags[2]
     up_and_down = ends(flags)
@@ -619,9 +640,15 @@
             unpack_columns(left, right, field, NS, REACH) for left, right in zip(*parts)
         ]
         above, below = up_and_down(first_end, second_end)
-        fields_y[field, 0:16, :] = above
-        fields_y[field, 16 : 16 + rows, :] = own
-        fields_y[field, 16 + rows : 32 + rows, :] = below
+        for at, values in ((0, above), (16, own), (16 + rows, below)):
+            count = values.shape[0]
+            inside = roll(fields_x[field, at : at + count, :], 32)
+            lane = lanes(values.shape)
+            near = (lane >= 32 - REACH) & (lane < 32 + REACH)
+            far = (lane < REACH) | (lane >= 128 - REACH)
+            kept = jnp.where(near, inside, jnp.where(far, values, 0.0))
+            window[field, at : at + count, :] = kept
+    unit = couple(window, coupled, rows)
 
     def put(row, values):
         if closing:
@@ -631,15 +658,19 @@
 
     @pl.when(is_ocean == 0)
     def _():
+        if opening:
+            plan_edges(plan_x, plan_y, plan_e, 2, rows // 8, tall, False)
         regrid_beside(
-            fields_x, fields_y, plan_x, plan_y, part_x, forcing_x, forcing_y, 2, rows // 8, tall, False
+            coupled, unit, plan_e, part_x, forcing_x, forcing_y, 2, rows // 8, tall, False
         )
         air(state, put, forcing_x, air_in, atm_out, d)
 
     @pl.when(is_ocean != 0)
     def _():
+        if opening:
+            plan_edges(plan_x, plan_y, plan_e, 0, d.tiles, tall, True)
         regrid_beside(
-            fields_x, fields_y, plan_x, plan_y, part_x, forcing_x, forcing_y, 0, d.tiles, tall, True
+            coupled, unit, plan_e, part_x, forcing_x, forcing_y, 0, d.tiles, tall, True
         )
         joined = [get_edges(ref, 0, d) for ref in (from_left, from_right)]
         sea(
@@ -650,7 +681,7 @@
     if closing:
         out[...] = raw[...].reshape(CH, rows, 128).astype(BF16)
     else:
-        emit(out, surface, wet, flags, fields, new_edges, one, two, raw, d)
+        emit(out, surface, wet, flags, places, fields, new_edges, one, two, raw, d)
 
 
 VMEM = pl.BlockSpec(memory_space=pltpu.VMEM)
@@ -768,10 +799,10 @@
             name=name,
         )(flags, *operands, *far)
 
-    state, planes, sides, fields, edges, one, two = call(
+    state, planes, sides, places, fields, edges, one, two = call(
         functools.partial(start_kernel, d),
         (),
-        [state_shape, shape(2 * NK, rows, 128), shape(rows, 128)]
+        [state_shape, shape(2 * NK, rows, 128), shape(rows, 128), shape(rows * 128, d.edge)]
         + emitted[:2]
         + [shape(d.strip + 32, 128)] * 2,
         [raw, pltpu.VMEM((2 * NK * rows, 128), F32), turned],
@@ -786,8 +817,10 @@
         shape(rows + 4, 3 * CH, 128),
     ]
     made = [shape(HA, 128), shape(HIDK, 768), shape(9 * CH, HIDP)]
+    coupled = pltpu.VMEM((NS // 2, rows + 32, 128), jnp.int32)
     scratch = [
         pltpu.VMEM((NS, rows + 32, 128), F32),
+        coupled,
         pltpu.VMEM((d.tall * 8, 128), F32),
         pltpu.VMEM((d.tall * 8, 128), F32),
         pltpu.VMEM((rows + 4, 256, 128), BF16),
@@ -800,16 +833,16 @@
         functools.partial(middle_kernel, d, True),
         (state, *vertical, planes),
         between + [plan] + made,
-        [],
+        [coupled],
         "first_middle",
         raw_weights,
     )
     weights = (air_in, first, second, atm_out)
-    state, fields, edges, one, two, plan_y = call(
+    state, fields, edges, one, two, plan_e = call(
         functools.partial(step_kernel, d, True, False),
-        (state, land_mask, *horizontal, *shared, edges, plan_x, *weights, surface_proj),
-        [state_shape] + emitted + [plan],
-        scratch + [raw],
+        (state, land_mask, *horizontal, *shared, edges, plan_x, *weights, surface_proj, places),
+        [state_shape] + emitted + [shape(2 * d.tall, 128, dtype=F32)],
+        scratch + [raw, pltpu.VMEM(plan.shape, F32)],
         "first_step",
     )
 
@@ -818,12 +851,12 @@
         functools.partial(middle_kernel, d, False),
         (state, *vertical, plan_x),
         between,
-        [],
+        [coupled],
         "second_middle",
     )
     (state,) = call(
         functools.partial(step_kernel, d, False, True),
-        (state, land_mask, *horizontal, *shared, edges, plan_x, *weights, plan_y),
+        (state, land_mask, *horizontal, *shared, edges, plan_x, *weights, plan_e),
         [shape(CH, rows, 128)],
         scratch + [turned],
         "second_step",

time: 38.7 us -> 38.2 us (0.987)
  starting transfers between devices: 17.1 us -> 16.7 us
  Pallas kernels: 13.8 us -> 13.4 us
    ppermute x14, starting transfers between devices: 17.1 us -> 16.7 us  [send(): return lax.ppermute(x, names, pairs)]
where the time goes in v10:
time: 38.2 us; the launch traced here: 38.1 us
  starting transfers between devices  16.7 us (44%)
  Pallas kernels  13.4 us (35%)
  waiting for transfers between devices  7.63 us (20%)
    ppermute x14, starting transfers between devices, send(): return lax.ppermute(x, names, pairs)  16.7 us
    pallas_call x5, Pallas kernels, call(): pl.pallas_call(kernel, out_shape=outs, in_specs=[SMEM] + [VMEM] * len(ope...  13.4 us
    ppermute x14, waiting for transfers between devices, send(): return lax.ppermute(x, names, pairs)  7.63 us
  transfers between devices with their start and end apart: 14, of which 6 were waited for; matrix products, arithmetic and copies ran while one was open for 0% of the time, Pallas kernels for 9%

profile of v10, /device:TPU:0, one launch (start us, length us, event | category | flops | bytes accessed | tf_op | source)
XLA Modules:
  0.0 38.1 jit_solution(13010177330194670836)
XLA Ops:
  0.0 0.1 pad_add_fusion.flags.refs_0_
  0.1 2.2 %start.1 = (bf16[16,80,128]{2,1,0:T(8,128)(2,1)S(1)}, bf16[8,16,128]{2,1,0:T(8,128)(2,1)S(1)}, bf16[16,128]{1,0:T(8,128)(2,1)S(1)}, bf16[2048,128]{1,0:T(8,128)(...) custom-call(s32[4]{0:T(128)S(1)} %pad_add_fusion.flags.refs_0_, ...), custom_call_target="tpu_custom_call" | custom-call | tf_op jit(solution)/shard_map/start/pallas_call | solution.py:792
  2.3 3.1 %collective-permute-start = (bf16[272,128]{1,0:T(8,128)(2,1)S(1)}, bf16[272,128]{1,0:T(8,128)(2,1)S(1)}, u32[]{:S(2)}, u32[]{:S(2)}) collective-permute-start(bf16[272,128]{1,0:T(8,128)(2,1)S(1)} %get-tuple-element.39), channel_id=1, source_target_pairs={{0,4},{1,5},{2,6},{3,7},{4,0},{5,1},{6,2},{7,3},{8,12},{9,13},{10,... | collective-permute-start | bytes 208904 | tf_op jit(solution)/shard_map/ppermute | solution.py:709
  5.4 1.5 %collective-permute-start.1 = (bf16[272,128]{1,0:T(8,128)(2,1)S(1)}, bf16[272,128]{1,0:T(8,128)(2,1)S(1)}, u32[]{:S(2)}, u32[]{:S(2)}) collective-permute-start(bf16[272,128]{1,0:T(8,128)(2,1)S(1)} %get-tuple-element.40), channel_id=1, source_target_pairs={{0,16},{1,17},{2,18},{3,19},{4,8},{5,9},{6,10},{7,11},{8,4},{9,5},... | collective-permute-start | bytes 208904 | tf_op jit(solution)/shard_map/ppermute | solution.py:709
  6.9 0.5 %collective-permute-start.4 = (bf16[5,16,128]{2,1,0:T(8,128)(2,1)S(1)}, bf16[5,16,128]{2,1,0:T(8,128)(2,1)S(1)}, u32[]{:S(2)}, u32[]{:S(2)}) collective-permute-start(bf16[5,16,128]{2,1,0:T(8,128)(2,1)S(1)} %get-tuple-element.41), channel_id=1, source_target_pairs={{0,16},{1,17},{2,18},{3,19},{4,24},{5,25},{6,26},{7,27},{8,20},{9,... | collective-permute-start | bytes 61448 | tf_op jit(solution)/shard_map/ppermute | solution.py:709
  7.4 2.1 %collective-permute-start.3 = (bf16[5,16,128]{2,1,0:T(8,128)(2,1)S(1)}, bf16[5,16,128]{2,1,0:T(8,128)(2,1)S(1)}, u32[]{:S(2)}, u32[]{:S(2)}) collective-permute-start(bf16[5,16,128]{2,1,0:T(8,128)(2,1)S(1)} %get-tuple-element.41), channel_id=1, source_target_pairs={{0,20},{1,21},{2,22},{3,23},{4,16},{5,17},{6,18},{7,19},{8,28},{9,... | collective-permute-start | bytes 61448 | tf_op jit(solution)/shard_map/ppermute | solution.py:709
  9.5 1.5 %collective-permute-start.2 = (bf16[5,16,128]{2,1,0:T(8,128)(2,1)S(1)}, bf16[5,16,128]{2,1,0:T(8,128)(2,1)S(1)}, u32[]{:S(2)}, u32[]{:S(2)}) collective-permute-start(bf16[5,16,128]{2,1,0:T(8,128)(2,1)S(1)} %get-tuple-element.41), channel_id=1, source_target_pairs={{0,16},{1,17},{2,18},{3,19},{4,20},{5,21},{6,22},{7,23},{8,24},{9,... | collective-permute-start | bytes 61448 | tf_op jit(solution)/shard_map/ppermute | solution.py:709
  10.9 1.1 %collective-permute-done.3.refs_2_ = bf16[5,16,128]{2,1,0:T(8,128)(2,1)S(1)} collective-permute-done((bf16[5,16,128]{2,1,0:T(8,128)(2,1)S(1)}, bf16[5,16,128]{2,1,0:T(8,128)(2,1)S(1)}, u32[]{:S(2)}, u32[]{:S(2)}) %collective-permute-start.3) | collective-permute-done | bytes 20512 | tf_op jit(solution)/shard_map/ppermute | solution.py:709
  12.1 1.2 %collective-permute-done.2.refs_3_ = bf16[5,16,128]{2,1,0:T(8,128)(2,1)S(1)} collective-permute-done((bf16[5,16,128]{2,1,0:T(8,128)(2,1)S(1)}, bf16[5,16,128]{2,1,0:T(8,128)(2,1)S(1)}, u32[]{:S(2)}, u32[]{:S(2)}) %collective-permute-start.2) | collective-permute-done | bytes 20512 | tf_op jit(solution)/shard_map/ppermute | solution.py:709
  13.4 0.5 %collective-permute-start.5 = (bf16[176,128]{1,0:T(8,128)(2,1)S(1)}, bf16[176,128]{1,0:T(8,128)(2,1)S(1)}, u32[]{:S(2)}, u32[]{:S(2)}) collective-permute-start(bf16[176,128]{1,0:T(8,128)(2,1)S(1)} %constant_dynamic-update-slice_fusion), channel_id=1, source_target_pairs={{0,1},{1,2},{2,3},{3,0},{4,5},{5,6},{6,7},{7,4},{8,9},{9,10},{10,1... | collective-permute-start | bytes 135176 | tf_op jit(solution)/shard_map/ppermute | solution.py:709
  13.9 1.9 %first_middle.1 = (f32[96,128]{1,0:T(8,128)S(1)}, f32[4,48,128]{2,1,0:T(8,128)S(1)}, bf16[20,240,128]{2,1,0:T(8,128)(2,1)S(1)}, f32[192,128]{1,0:T(8,128)S(1)}, ...) custom-call(s32[4]{0:T(128)S(1)} %pad_add_fusion.flags.refs_0_, ...), custom_call_target="tpu_custom_call" | custom-call | tf_op jit(solution)/shard_map/first_middle/pallas_call | solution.py:792
  15.8 1.6 %collective-permute-done.5.refs_3_ = bf16[176,128]{1,0:T(8,128)(2,1)S(1)} collective-permute-done((bf16[176,128]{1,0:T(8,128)(2,1)S(1)}, bf16[176,128]{1,0:T(8,128)(2,1)S(1)}, u32[]{:S(2)}, u32[]{:S(2)}) %collective-permute-start.5) | collective-permute-done | bytes 45088 | tf_op jit(solution)/shard_map/ppermute | solution.py:709
  17.4 3.7 %first_step.1 = (bf16[16,80,128]{2,1,0:T(8,128)(2,1)S(1)}, bf16[5,16,128]{2,1,0:T(8,128)(2,1)S(1)}, bf16[80,128]{1,0:T(8,128)(2,1)S(1)}, bf16[240,128]{1,0:T(8,1...) custom-call(s32[4]{0:T(128)S(1)} %pad_add_fusion.flags.refs_0_, ...), custom_call_target="tpu_custom_call" | custom-call | tf_op jit(solution)/shard_map/first_step/pallas_call | solution.py:792
  21.1 1.2 %collective-permute-start.7 = (bf16[240,128]{1,0:T(8,128)(2,1)S(1)}, bf16[240,128]{1,0:T(8,128)(2,1)S(1)}, u32[]{:S(2)}, u32[]{:S(2)}) collective-permute-start(bf16[240,128]{1,0:T(8,128)(2,1)S(1)} %get-tuple-element.58), channel_id=1, source_target_pairs={{0,4},{1,5},{2,6},{3,7},{4,0},{5,1},{6,2},{7,3},{8,12},{9,13},{10,... | collective-permute-start | bytes 184328 | tf_op jit(solution)/shard_map/ppermute | solution.py:709
  22.3 1.2 %collective-permute-start.8 = (bf16[240,128]{1,0:T(8,128)(2,1)S(1)}, bf16[240,128]{1,0:T(8,128)(2,1)S(1)}, u32[]{:S(2)}, u32[]{:S(2)}) collective-permute-start(bf16[240,128]{1,0:T(8,128)(2,1)S(1)} %get-tuple-element.59), channel_id=1, source_target_pairs={{0,16},{1,17},{2,18},{3,19},{4,8},{5,9},{6,10},{7,11},{8,4},{9,5},... | collective-permute-start | bytes 184328 | tf_op jit(solution)/shard_map/ppermute | solution.py:709
  23.5 0.8 %collective-permute-start.11 = (bf16[5,16,128]{2,1,0:T(8,128)(2,1)S(1)}, bf16[5,16,128]{2,1,0:T(8,128)(2,1)S(1)}, u32[]{:S(2)}, u32[]{:S(2)}) collective-permute-start(bf16[5,16,128]{2,1,0:T(8,128)(2,1)S(1)} %get-tuple-element.60), channel_id=1, source_target_pairs={{0,16},{1,17},{2,18},{3,19},{4,24},{5,25},{6,26},{7,27},{8,20},{9,... | collective-permute-start | bytes 61448 | tf_op jit(solution)/shard_map/ppermute | solution.py:709
  24.3 2.3 %collective-permute-start.10 = (bf16[5,16,128]{2,1,0:T(8,128)(2,1)S(1)}, bf16[5,16,128]{2,1,0:T(8,128)(2,1)S(1)}, u32[]{:S(2)}, u32[]{:S(2)}) collective-permute-start(bf16[5,16,128]{2,1,0:T(8,128)(2,1)S(1)} %get-tuple-element.60), channel_id=1, source_target_pairs={{0,20},{1,21},{2,22},{3,23},{4,16},{5,17},{6,18},{7,19},{8,28},{9,... | collective-permute-start | bytes 61448 | tf_op jit(solution)/shard_map/ppermute | solution.py:709
  26.6 1.5 %collective-permute-start.9 = (bf16[5,16,128]{2,1,0:T(8,128)(2,1)S(1)}, bf16[5,16,128]{2,1,0:T(8,128)(2,1)S(1)}, u32[]{:S(2)}, u32[]{:S(2)}) collective-permute-start(bf16[5,16,128]{2,1,0:T(8,128)(2,1)S(1)} %get-tuple-element.60), channel_id=1, source_target_pairs={{0,16},{1,17},{2,18},{3,19},{4,20},{5,21},{6,22},{7,23},{8,24},{9,... | collective-permute-start | bytes 61448 | tf_op jit(solution)/shard_map/ppermute | solution.py:709
  28.1 0.9 %collective-permute-done.10.refs_2_ = bf16[5,16,128]{2,1,0:T(8,128)(2,1)S(1)} collective-permute-done((bf16[5,16,128]{2,1,0:T(8,128)(2,1)S(1)}, bf16[5,16,128]{2,1,0:T(8,128)(2,1)S(1)}, u32[]{:S(2)}, u32[]{:S(2)}) %collective-permute-start.10) | collective-permute-done | bytes 20512 | tf_op jit(solution)/shard_map/ppermute | solution.py:709
  29.0 1.4 %collective-permute-done.9.refs_3_ = bf16[5,16,128]{2,1,0:T(8,128)(2,1)S(1)} collective-permute-done((bf16[5,16,128]{2,1,0:T(8,128)(2,1)S(1)}, bf16[5,16,128]{2,1,0:T(8,128)(2,1)S(1)}, u32[]{:S(2)}, u32[]{:S(2)}) %collective-permute-start.9) | collective-permute-done | bytes 20512 | tf_op jit(solution)/shard_map/ppermute | solution.py:709
  30.4 0.5 %collective-permute-start.12 = (bf16[128,128]{1,0:T(8,128)(2,1)S(1)}, bf16[128,128]{1,0:T(8,128)(2,1)S(1)}, u32[]{:S(2)}, u32[]{:S(2)}) collective-permute-start(bf16[128,128]{1,0:T(8,128)(2,1)S(1)} %pad_maximum_fusion), channel_id=1, source_target_pairs={{0,1},{1,2},{2,3},{3,0},{4,5},{5,6},{6,7},{7,4},{8,9},{9,10},{10,1... | collective-permute-start | bytes 98312 | tf_op jit(solution)/shard_map/ppermute | solution.py:709
  30.9 1.4 %second_middle.1 = (f32[96,128]{1,0:T(8,128)S(1)}, f32[4,48,128]{2,1,0:T(8,128)S(1)}, bf16[20,240,128]{2,1,0:T(8,128)(2,1)S(1)}) custom-call(s32[4]{0:T(128)S(1)} %pad_add_fusion.flags.refs_0_, bf16[16,80,128]{2,1,0:T(8,128)(2,1)S(1)} %get-tuple-element.56.refs_1_, bf16[5,16,128]{2,1,0:T(8,128)(2,1)S(1)} %collective-permute-done.10.refs_2_, ...), custom_call_target="tpu_custom_call" | custom-call | tf_op jit(solution)/shard_map/second_middle/pallas_call | solution.py:792
  32.4 1.5 %collective-permute-done.12.refs_3_ = bf16[128,128]{1,0:T(8,128)(2,1)S(1)} collective-permute-done((bf16[128,128]{1,0:T(8,128)(2,1)S(1)}, bf16[128,128]{1,0:T(8,128)(2,1)S(1)}, u32[]{:S(2)}, u32[]{:S(2)}) %collective-permute-start.12) | collective-permute-done | bytes 32800 | tf_op jit(solution)/shard_map/ppermute | solution.py:709
  33.8 4.2 %second_step.1 = bf16[80,16,128]{2,1,0:T(8,128)(2,1)} custom-call(s32[4]{0:T(128)S(1)} %pad_add_fusion.flags.refs_0_, bf16[16,80,128]{2,1,0:T(8,128)(2,1)S(1)} %get-tuple-element.56.refs_1_, s32[16,128]{1,0:T(8,128)S(1)} %copy-done.1, bf16[128,128]{1,0:T(8,128)(2,1)S(1)} %collective-permute-done.12.refs_3_, ...), custom_call_target="tpu_custom_call" | custom-call | tf_op jit(solution)/shard_map/second_step/pallas_call | solution.py:792
  (28 shorter events, 0.2 us)
Async XLA Ops:
  0.0 17.4 %copy-start.1 = (s32[16,128]{1,0:T(8,128)S(1)}, s32[16,128]{1,0:T(8,128)}, u32[]{:S(2)}) copy-start(s32[16,128]{1,0:T(8,128)} %refs_2_.3) | copy-start | bytes 24580
  0.0 17.4 %copy-start.2 = (f32[2,4,80]{2,1,0:T(4,128)S(1)}, f32[2,4,80]{2,1,0:T(4,128)}, u32[]{:S(2)}) copy-start(f32[2,4,80]{2,1,0:T(4,128)} %refs_14_.1) | copy-start | bytes 7684
  0.0 17.4 %copy-start = (bf16[80,384]{1,0:T(8,128)(2,1)S(1)}, bf16[80,384]{1,0:T(8,128)(2,1)}, u32[]{:S(2)}) copy-start(bf16[80,384]{1,0:T(8,128)(2,1)} %refs_13_.3) | copy-start | bytes 184324
  2.3 8.7 %collective-permute-start = (bf16[272,128]{1,0:T(8,128)(2,1)S(1)}, bf16[272,128]{1,0:T(8,128)(2,1)S(1)}, u32[]{:S(2)}, u32[]{:S(2)}) collective-permute-start(bf16[272,128]{1,0:T(8,128)(2,1)S(1)} %get-tuple-element.39), channel_id=1, source_target_pairs={{0,4},{1,5},{2,6},{3,7},{4,0},{5,1},{6,2},{7,3},{8,12},{9,13},{10,... | collective-permute-start | bytes 208904 | tf_op jit(solution)/shard_map/ppermute | solution.py:709
  5.4 5.6 %collective-permute-start.1 = (bf16[272,128]{1,0:T(8,128)(2,1)S(1)}, bf16[272,128]{1,0:T(8,128)(2,1)S(1)}, u32[]{:S(2)}, u32[]{:S(2)}) collective-permute-start(bf16[272,128]{1,0:T(8,128)(2,1)S(1)} %get-tuple-element.40), channel_id=1, source_target_pairs={{0,16},{1,17},{2,18},{3,19},{4,8},{5,9},{6,10},{7,11},{8,4},{9,5},... | collective-permute-start | bytes 208904 | tf_op jit(solution)/shard_map/ppermute | solution.py:709
  6.9 4.1 %collective-permute-start.4 = (bf16[5,16,128]{2,1,0:T(8,128)(2,1)S(1)}, bf16[5,16,128]{2,1,0:T(8,128)(2,1)S(1)}, u32[]{:S(2)}, u32[]{:S(2)}) collective-permute-start(bf16[5,16,128]{2,1,0:T(8,128)(2,1)S(1)} %get-tuple-element.41), channel_id=1, source_target_pairs={{0,16},{1,17},{2,18},{3,19},{4,24},{5,25},{6,26},{7,27},{8,20},{9,... | collective-permute-start | bytes 61448 | tf_op jit(solution)/shard_map/ppermute | solution.py:709
  7.4 4.7 %collective-permute-start.3 = (bf16[5,16,128]{2,1,0:T(8,128)(2,1)S(1)}, bf16[5,16,128]{2,1,0:T(8,128)(2,1)S(1)}, u32[]{:S(2)}, u32[]{:S(2)}) collective-permute-start(bf16[5,16,128]{2,1,0:T(8,128)(2,1)S(1)} %get-tuple-element.41), channel_id=1, source_target_pairs={{0,20},{1,21},{2,22},{3,23},{4,16},{5,17},{6,18},{7,19},{8,28},{9,... | collective-permute-start | bytes 61448 | tf_op jit(solution)/shard_map/ppermute | solution.py:709
  9.5 3.8 %collective-permute-start.2 = (bf16[5,16,128]{2,1,0:T(8,128)(2,1)S(1)}, bf16[5,16,128]{2,1,0:T(8,128)(2,1)S(1)}, u32[]{:S(2)}, u32[]{:S(2)}) collective-permute-start(bf16[5,16,128]{2,1,0:T(8,128)(2,1)S(1)} %get-tuple-element.41), channel_id=1, source_target_pairs={{0,16},{1,17},{2,18},{3,19},{4,20},{5,21},{6,22},{7,23},{8,24},{9,... | collective-permute-start | bytes 61448 | tf_op jit(solution)/shard_map/ppermute | solution.py:709
  13.3 2.5 %collective-permute-start.6 = (bf16[176,128]{1,0:T(8,128)(2,1)S(1)}, bf16[176,128]{1,0:T(8,128)(2,1)S(1)}, u32[]{:S(2)}, u32[]{:S(2)}) collective-permute-start(bf16[176,128]{1,0:T(8,128)(2,1)S(1)} %constant_dynamic-update-slice_fusion), channel_id=1, source_target_pairs={{0,3},{1,0},{2,1},{3,2},{4,7},{5,4},{6,5},{7,6},{8,11},{9,8},{10,9... | collective-permute-start | bytes 135176 | tf_op jit(solution)/shard_map/ppermute | solution.py:709
  13.4 4.0 %collective-permute-start.5 = (bf16[176,128]{1,0:T(8,128)(2,1)S(1)}, bf16[176,128]{1,0:T(8,128)(2,1)S(1)}, u32[]{:S(2)}, u32[]{:S(2)}) collective-permute-start(bf16[176,128]{1,0:T(8,128)(2,1)S(1)} %constant_dynamic-update-slice_fusion), channel_id=1, source_target_pairs={{0,1},{1,2},{2,3},{3,0},{4,5},{5,6},{6,7},{7,4},{8,9},{9,10},{10,1... | collective-permute-start | bytes 135176 | tf_op jit(solution)/shard_map/ppermute | solution.py:709
  21.1 6.9 %collective-permute-start.7 = (bf16[240,128]{1,0:T(8,128)(2,1)S(1)}, bf16[240,128]{1,0:T(8,128)(2,1)S(1)}, u32[]{:S(2)}, u32[]{:S(2)}) collective-permute-start(bf16[240,128]{1,0:T(8,128)(2,1)S(1)} %get-tuple-element.58), channel_id=1, source_target_pairs={{0,4},{1,5},{2,6},{3,7},{4,0},{5,1},{6,2},{7,3},{8,12},{9,13},{10,... | collective-permute-start | bytes 184328 | tf_op jit(solution)/shard_map/ppermute | solution.py:709
  22.3 5.8 %collective-permute-start.8 = (bf16[240,128]{1,0:T(8,128)(2,1)S(1)}, bf16[240,128]{1,0:T(8,128)(2,1)S(1)}, u32[]{:S(2)}, u32[]{:S(2)}) collective-permute-start(bf16[240,128]{1,0:T(8,128)(2,1)S(1)} %get-tuple-element.59), channel_id=1, source_target_pairs={{0,16},{1,17},{2,18},{3,19},{4,8},{5,9},{6,10},{7,11},{8,4},{9,5},... | collective-permute-start | bytes 184328 | tf_op jit(solution)/shard_map/ppermute | solution.py:709
  23.5 4.5 %collective-permute-start.11 = (bf16[5,16,128]{2,1,0:T(8,128)(2,1)S(1)}, bf16[5,16,128]{2,1,0:T(8,128)(2,1)S(1)}, u32[]{:S(2)}, u32[]{:S(2)}) collective-permute-start(bf16[5,16,128]{2,1,0:T(8,128)(2,1)S(1)} %get-tuple-element.60), channel_id=1, source_target_pairs={{0,16},{1,17},{2,18},{3,19},{4,24},{5,25},{6,26},{7,27},{8,20},{9,... | collective-permute-start | bytes 61448 | tf_op jit(solution)/shard_map/ppermute | solution.py:709
  24.3 4.7 %collective-permute-start.10 = (bf16[5,16,128]{2,1,0:T(8,128)(2,1)S(1)}, bf16[5,16,128]{2,1,0:T(8,128)(2,1)S(1)}, u32[]{:S(2)}, u32[]{:S(2)}) collective-permute-start(bf16[5,16,128]{2,1,0:T(8,128)(2,1)S(1)} %get-tuple-element.60), channel_id=1, source_target_pairs={{0,20},{1,21},{2,22},{3,23},{4,16},{5,17},{6,18},{7,19},{8,28},{9,... | collective-permute-start | bytes 61448 | tf_op jit(solution)/shard_map/ppermute | solution.py:709
  26.6 3.8 %collective-permute-start.9 = (bf16[5,16,128]{2,1,0:T(8,128)(2,1)S(1)}, bf16[5,16,128]{2,1,0:T(8,128)(2,1)S(1)}, u32[]{:S(2)}, u32[]{:S(2)}) collective-permute-start(bf16[5,16,128]{2,1,0:T(8,128)(2,1)S(1)} %get-tuple-element.60), channel_id=1, source_target_pairs={{0,16},{1,17},{2,18},{3,19},{4,20},{5,21},{6,22},{7,23},{8,24},{9,... | collective-permute-start | bytes 61448 | tf_op jit(solution)/shard_map/ppermute | solution.py:709
  30.4 2.0 %collective-permute-start.13 = (bf16[128,128]{1,0:T(8,128)(2,1)S(1)}, bf16[128,128]{1,0:T(8,128)(2,1)S(1)}, u32[]{:S(2)}, u32[]{:S(2)}) collective-permute-start(bf16[128,128]{1,0:T(8,128)(2,1)S(1)} %pad_maximum_fusion), channel_id=1, source_target_pairs={{0,3},{1,0},{2,1},{3,2},{4,7},{5,4},{6,5},{7,6},{8,11},{9,8},{10,9... | collective-permute-start | bytes 98312 | tf_op jit(solution)/shard_map/ppermute | solution.py:709
  30.4 3.4 %collective-permute-start.12 = (bf16[128,128]{1,0:T(8,128)(2,1)S(1)}, bf16[128,128]{1,0:T(8,128)(2,1)S(1)}, u32[]{:S(2)}, u32[]{:S(2)}) collective-permute-start(bf16[128,128]{1,0:T(8,128)(2,1)S(1)} %pad_maximum_fusion), channel_id=1, source_target_pairs={{0,1},{1,2},{2,3},{3,0},{4,5},{5,6},{6,7},{7,4},{8,9},{9,10},{10,1... | collective-permute-start | bytes 98312 | tf_op jit(solution)/shard_map/ppermute | solution.py:709

commit v11 on v10

--- a/solution.py
+++ b/solution.py
@@ -108,36 +108,45 @@
     return high, mid, values - high - mid
 
 
-def emit(state, surface, wet, flags, places, fields, own_edges, one, two, raw, d):
-    half = d.rows // 2
-    is_ocean, even = flags[0] != 0, flags[3] == 0
-    gap = jnp.zeros((4, CH), F32)
-    terms = []
-    for term in split_bf16(surface[flags[0]]):
-        terms += [term, gap]
-    proj = jnp.concatenate(terms + [gap, gap], axis=0).astype(BF16)
-    for step in range(half):
-        pair = jnp.concatenate([state[step], state[step + half]], axis=1)
-        parts = jnp.dot(proj, pair, preferred_element_type=F32)
+class Emission:
+    def __init__(self, surface, flags, places, raw, d):
+        gap = jnp.zeros((4, CH), F32)
+        terms = []
+        for term in split_bf16(surface[flags[0]]):
+            terms += [term, gap]
+        self.proj = jnp.concatenate(terms + [gap, gap], axis=0).astype(BF16)
+        self.places, self.raw, self.d, self.flags = places, raw, d, flags
+        self.edges = None
+
+    def add(self, step, low, high):
+        pair = jnp.concatenate([low, high], axis=1)
+        parts = jnp.dot(self.proj, pair, preferred_element_type=F32)
         whole = parts[0:8] + parts[8:16] + parts[16:24]
-        raw[step * 8 : step * 8 + 8, :] = whole[:, :128]
-        raw[(step + half) * 8 : (step + half) * 8 + 8, :] = whole[:, 128:]
-    keeping = jnp.where(is_ocean, wet[...].astype(F32), 1.0)
-    whole = [raw[pl.ds(field, d.rows, stride=8), :] * keeping for field in range(NS)]
-    for field in range(NS):
-        fields[field] = whole[field].astype(BF16)
-    fields[NS] = pack_columns(whole, REACH).astype(BF16)
-    edges = edge_columns(state, places, d)
-    put_edges(own_edges, 0, edges, d)
-    row = lanes(edges.shape) % d.block
-    downward = jnp.where(row < 2, roll(edges, -d.rows), jnp.zeros_like(edges))
-    upward = jnp.where(
-        (row >= d.rows + 2) & (row < d.rows + 4), roll(edges, d.rows), jnp.zeros_like(edges)
-    )
-    for (ref, first), down in zip(strips(one, two, even, d), (even, jnp.logical_not(even))):
-        ref[0:CH, :] = state[first]
-        ref[CH : 2 * CH, :] = state[first + 1]
-        put_edges(ref, 2 * CH, jnp.where(down, downward, upward), d)
+        other = step + self.d.rows // 2
+        self.raw[step * 8 : step * 8 + 8, :] = whole[:, :128]
+        self.raw[other * 8 : other * 8 + 8, :] = whole[:, 128:]
+        places = [self.places[row * 128 : (row + 1) * 128, :] for row in (step, other)]
+        edges = jnp.dot(pair, jnp.concatenate(places, axis=0), preferred_element_type=F32)
+        self.edges = edges if self.edges is None else self.edges + edges
+
+    def close(self, state, wet, fields, own_edges, one, two):
+        d, even = self.d, self.flags[3] == 0
+        keeping = jnp.where(self.flags[0] != 0, wet[...].astype(F32), 1.0)
+        whole = [self.raw[pl.ds(field, d.rows, stride=8), :] * keeping for field in range(NS)]
+        for field in range(NS):
+            fields[field] = whole[field].astype(BF16)
+        fields[NS] = pack_columns(whole, REACH).astype(BF16)
+        edges = self.edges.astype(BF16)
+        put_edges(own_edges, 0, edges, d)
+        row = lanes(edges.shape) % d.block
+        downward = jnp.where(row < 2, roll(edges, -d.rows), jnp.zeros_like(edges))
+        upward = jnp.where(
+            (row >= d.rows + 2) & (row < d.rows + 4), roll(edges, d.rows), jnp.zeros_like(edges)
+        )
+        for (ref, first), down in zip(strips(one, two, even, d), (even, jnp.logical_not(even))):
+            ref[0:CH, :] = state[first]
+            ref[CH : 2 * CH, :] = state[first + 1]
+            put_edges(ref, 2 * CH, jnp.where(down, downward, upward), d)
 
 
 def fetch(sources, targets, sems):
@@ -172,7 +181,10 @@
         state[row] = turned[pl.ds(row, CH, stride=rows), :].astype(BF16)
     for copy in copies[len(pieces) :]:
         copy.wait()
-    emit(state, surface, wet, flags, places, fields, own_edges, one, two, raw, d)
+    emission = Emission(surface, flags, places, raw, d)
+    for step in range(rows // 2):
+        emission.add(step, state[step], state[step + rows // 2])
+    emission.close(state, wet, fields, own_edges, one, two)
     for k in range(NK):
         code = (offsets[0, k] * SPAN + offsets[1, k]).astype(F32)
         tall[k * rows : (k + 1) * rows, :] = code
@@ -231,15 +243,19 @@
 
 
 def select_rows(source, start, picks):
-    chosen = [[jnp.full((8, 128), 1 << 15, jnp.int32) for _ in range(NS // 2)] for _ in picks]
+    parts = source.shape[0]
+    blank = jnp.full((8, 128), 1 << 15, jnp.int32) if parts < NS else jnp.zeros((8, 128), F32)
+    chosen = [[blank for _ in range(parts)] for _ in picks]
     for shift in range(-HW, HW + 1):
         at = pl.ds(start + shift, 8)
-        values = [source[pair, at, :] for pair in range(NS // 2)]
+        values = [source[part, at, :] for part in range(parts)]
         for slot, (rows, index, allowed) in enumerate(picks):
             here = (rows == shift) & allowed
-            for pair in range(NS // 2):
-                picked = along_lanes(values[pair], index)
-                chosen[slot][pair] = jnp.where(here, picked, chosen[slot][pair])
+            for part in range(parts):
+                picked = along_lanes(values[part], index)
+                chosen[slot][part] = jnp.where(here, picked, chosen[slot][part])
+    if parts == NS:
+        return chosen
     return [[part for values in pairs for part in uncouple(values)] for pairs in chosen]
 
 
@@ -290,7 +306,7 @@
         plan_e[pl.ds(tall + at, 8), :] = weight
 
 
-def regrid_beside(coupled, unit, plan_e, part_x, forcing_x, forcing_y, first, tiles, tall, sides):
+def regrid_beside(window, plan_e, part_x, forcing_x, forcing_y, first, tiles, tall, sides):
     lane = lanes((8, 128))
     part, place = edge_lanes()
     outer = place >= 8
@@ -300,11 +316,11 @@
     for step in range(tiles):
         at = first + step * 8
         rows, cols = decode(plan_e[pl.ds(at, 8), :])
-        weight = plan_e[pl.ds(tall + at, 8), :] * unit
+        weight = plan_e[pl.ds(tall + at, 8), :]
         column = jnp.where(outer, outer_column, inner_column) + cols
         within = (column >= 0) & (column < 128)
         index = jnp.where(within, column + 32, column) & 127
-        (chosen,) = select_rows(coupled, at + 14, [(rows, index, outer | jnp.logical_not(within))])
+        (chosen,) = select_rows(window, at + 14, [(rows, index, outer | jnp.logical_not(within))])
         for field in range(NS):
             part_sum = chosen[field] * weight
             extra = part_sum
@@ -339,10 +355,11 @@
         pair = jnp.concatenate([inputs(step), inputs(step + half)], axis=1)
         hidden = twice_gelu(jnp.dot(air_in[...], pair, preferred_element_type=F32)).astype(BF16)
         update = jnp.dot(atm_out[...], hidden, preferred_element_type=F32)
+        news = []
         for offset in range(2):
-            row = step + offset * half
             change = update[:, offset * 128 : (offset + 1) * 128]
-            out(row, state[row].astype(F32) + 0.5 * change)
+            news.append(state[step + offset * half].astype(F32) + 0.5 * change)
+        out(step, *news)
 
 
 def edge_forcing(forcing_x, forcing_y, d):
@@ -476,6 +493,7 @@
                 for tap in range(3)
             ]
         )
+        news = []
         for offset in range(2):
             row = step + offset * half
             sums = product[:, offset * 128 : (offset + 1) * 128]
@@ -484,7 +502,8 @@
             entry = roll(from_right, 127 - block - row)[:, :128]
             total = total + jnp.where(lane == 127, entry, roll(sums[2 * CH : 3 * CH], -1))
             update = total * (0.5 * wet[row : row + 1, :].astype(F32))
-            out(row, state[row].astype(F32) + update)
+            news.append(state[row].astype(F32) + update)
+        out(step, *news)
 
 
 def prepare(atm_in, atm_bias, ocn_in, ocn_bias, ocn_out, air_in, first, second, is_ocean):
@@ -601,7 +620,7 @@
         fields, new_edges, one, two = take(4)
     if opening:
         (plan_e,) = take(1)
-    window, coupled, forcing_x, forcing_y, stack, hidden, side, raw = take(8)
+    window, forcing_x, forcing_y, stack, hidden, side, raw = take(7)
     if opening:
         (plan_y,) = take(1)
     rows, tall = d.rows, d.tall
@@ -648,40 +667,53 @@
             far = (lane < REACH) | (lane >= 128 - REACH)
             kept = jnp.where(near, inside, jnp.where(far, values, 0.0))
             window[field, at : at + count, :] = kept
-    unit = couple(window, coupled, rows)
-
-    def put(row, values):
-        if closing:
-            raw[pl.ds(row, CH, stride=rows), :] = values
-        else:
-            out[row] = values.astype(BF16)
+    def finished():
+        emission = None if closing else Emission(surface, flags, places, raw, d)
+
+        def put(step, low, high):
+            if closing:
+                for row, values in ((step, low), (step + rows // 2, high)):
+                    raw[pl.ds(row, CH, stride=rows), :] = values
+                return
+            low, high = low.astype(BF16), high.astype(BF16)
+            out[step] = low
+            out[step + rows // 2] = high
+            emission.add(step, low, high)
+
+        def close():
+            if not closing:
+                emission.close(out, wet, fields, new_edges, one, two)
+
+        return put, close
 
     @pl.when(is_ocean == 0)
     def _():
         if opening:
             plan_edges(plan_x, plan_y, plan_e, 2, rows // 8, tall, False)
         regrid_beside(
-            coupled, unit, plan_e, part_x, forcing_x, forcing_y, 2, rows // 8, tall, False
+            window, plan_e, part_x, forcing_x, forcing_y, 2, rows // 8, tall, False
         )
+        put, close = finished()
         air(state, put, forcing_x, air_in, atm_out, d)
+        close()
 
     @pl.when(is_ocean != 0)
     def _():
         if opening:
             plan_edges(plan_x, plan_y, plan_e, 0, d.tiles, tall, True)
         regrid_beside(
-            coupled, unit, plan_e, part_x, forcing_x, forcing_y, 0, d.tiles, tall, True
+            window, plan_e, part_x, forcing_x, forcing_y, 0, d.tiles, tall, True
         )
+        put, close = finished()
         joined = [get_edges(ref, 0, d) for ref in (from_left, from_right)]
         sea(
             state, rolled, get_edges(edges, 0, d), *joined, put, forcing_x, forcing_y,
             first, second, wet, at_top, at_bottom, stack, hidden, side, d,
         )
+        close()
 
     if closing:
         out[...] = raw[...].reshape(CH, rows, 128).astype(BF16)
-    else:
-        emit(out, surface, wet, flags, places, fields, new_edges, one, two, raw, d)
 
 
 VMEM = pl.BlockSpec(memory_space=pltpu.VMEM)
@@ -820,7 +852,6 @@
     coupled = pltpu.VMEM((NS // 2, rows + 32, 128), jnp.int32)
     scratch = [
         pltpu.VMEM((NS, rows + 32, 128), F32),
-        coupled,
         pltpu.VMEM((d.tall * 8, 128), F32),
         pltpu.VMEM((d.tall * 8, 128), F32),
         pltpu.VMEM((rows + 4, 256, 128), BF16),

time: 38.2 us -> 40.1 us (1.050)
  starting transfers between devices: 16.7 us -> 18 us
  Pallas kernels: 13.4 us -> 13.9 us
    ppermute x14, starting transfers between devices: 16.7 us -> 18 us  [send(): return lax.ppermute(x, names, pairs)]
    pallas_call x5, Pallas kernels: 13.4 us -> 13.9 us  [call(): pl.pallas_call(kernel, out_shape=outs, in_specs=[SMEM] + [VMEM] * len(ope...]
  transfers between devices with their start and end apart: 14 -> 14, of which waited for: 6 -> 6; matrix products, arithmetic and copies ran while one was open for 0% -> 0% of each run, Pallas kernels for 9% -> 8%
where the time goes in v11:
time: 40.1 us; the launch traced here: 39.9 us
  starting transfers between devices  18 us (45%)
  Pallas kernels  13.9 us (35%)
  waiting for transfers between devices  7.63 us (19%)
    ppermute x14, starting transfers between devices, send(): return lax.ppermute(x, names, pairs)  18 us
    pallas_call x5, Pallas kernels, call(): pl.pallas_call(kernel, out_shape=outs, in_specs=[SMEM] + [VMEM] * len(ope...  13.9 us
    ppermute x14, waiting for transfers between devices, send(): return lax.ppermute(x, names, pairs)  7.63 us
  transfers between devices with their start and end apart: 14, of which 6 were waited for; matrix products, arithmetic and copies ran while one was open for 0% of the time, Pallas kernels for 8%

profile of v11, /device:TPU:0, one launch (start us, length us, event | category | flops | bytes accessed | tf_op | source)
XLA Modules:
  0.0 39.9 jit_solution(8442385655300524731)
XLA Ops:
  0.0 0.1 pad_add_fusion.flags.refs_0_
  0.1 2.2 %start.1 = (bf16[16,80,128]{2,1,0:T(8,128)(2,1)S(1)}, bf16[8,16,128]{2,1,0:T(8,128)(2,1)S(1)}, bf16[16,128]{1,0:T(8,128)(2,1)S(1)}, bf16[2048,128]{1,0:T(8,128)(...) custom-call(s32[4]{0:T(128)S(1)} %pad_add_fusion.flags.refs_0_, ...), custom_call_target="tpu_custom_call" | custom-call | tf_op jit(solution)/shard_map/start/pallas_call | solution.py:824
  2.3 3.1 %collective-permute-start = (bf16[272,128]{1,0:T(8,128)(2,1)S(1)}, bf16[272,128]{1,0:T(8,128)(2,1)S(1)}, u32[]{:S(2)}, u32[]{:S(2)}) collective-permute-start(bf16[272,128]{1,0:T(8,128)(2,1)S(1)} %get-tuple-element.39), channel_id=1, source_target_pairs={{0,4},{1,5},{2,6},{3,7},{4,0},{5,1},{6,2},{7,3},{8,12},{9,13},{10,... | collective-permute-start | bytes 208904 | tf_op jit(solution)/shard_map/ppermute | solution.py:741
  5.4 1.5 %collective-permute-start.1 = (bf16[272,128]{1,0:T(8,128)(2,1)S(1)}, bf16[272,128]{1,0:T(8,128)(2,1)S(1)}, u32[]{:S(2)}, u32[]{:S(2)}) collective-permute-start(bf16[272,128]{1,0:T(8,128)(2,1)S(1)} %get-tuple-element.40), channel_id=1, source_target_pairs={{0,16},{1,17},{2,18},{3,19},{4,8},{5,9},{6,10},{7,11},{8,4},{9,5},... | collective-permute-start | bytes 208904 | tf_op jit(solution)/shard_map/ppermute | solution.py:741
  6.9 0.5 %collective-permute-start.4 = (bf16[5,16,128]{2,1,0:T(8,128)(2,1)S(1)}, bf16[5,16,128]{2,1,0:T(8,128)(2,1)S(1)}, u32[]{:S(2)}, u32[]{:S(2)}) collective-permute-start(bf16[5,16,128]{2,1,0:T(8,128)(2,1)S(1)} %get-tuple-element.41), channel_id=1, source_target_pairs={{0,16},{1,17},{2,18},{3,19},{4,24},{5,25},{6,26},{7,27},{8,20},{9,... | collective-permute-start | bytes 61448 | tf_op jit(solution)/shard_map/ppermute | solution.py:741
  7.4 2.1 %collective-permute-start.3 = (bf16[5,16,128]{2,1,0:T(8,128)(2,1)S(1)}, bf16[5,16,128]{2,1,0:T(8,128)(2,1)S(1)}, u32[]{:S(2)}, u32[]{:S(2)}) collective-permute-start(bf16[5,16,128]{2,1,0:T(8,128)(2,1)S(1)} %get-tuple-element.41), channel_id=1, source_target_pairs={{0,20},{1,21},{2,22},{3,23},{4,16},{5,17},{6,18},{7,19},{8,28},{9,... | collective-permute-start | bytes 61448 | tf_op jit(solution)/shard_map/ppermute | solution.py:741
  9.5 1.5 %collective-permute-start.2 = (bf16[5,16,128]{2,1,0:T(8,128)(2,1)S(1)}, bf16[5,16,128]{2,1,0:T(8,128)(2,1)S(1)}, u32[]{:S(2)}, u32[]{:S(2)}) collective-permute-start(bf16[5,16,128]{2,1,0:T(8,128)(2,1)S(1)} %get-tuple-element.41), channel_id=1, source_target_pairs={{0,16},{1,17},{2,18},{3,19},{4,20},{5,21},{6,22},{7,23},{8,24},{9,... | collective-permute-start | bytes 61448 | tf_op jit(solution)/shard_map/ppermute | solution.py:741
  11.0 1.1 %collective-permute-done.3.refs_2_ = bf16[5,16,128]{2,1,0:T(8,128)(2,1)S(1)} collective-permute-done((bf16[5,16,128]{2,1,0:T(8,128)(2,1)S(1)}, bf16[5,16,128]{2,1,0:T(8,128)(2,1)S(1)}, u32[]{:S(2)}, u32[]{:S(2)}) %collective-permute-start.3) | collective-permute-done | bytes 20512 | tf_op jit(solution)/shard_map/ppermute | solution.py:741
  12.1 1.2 %collective-permute-done.2.refs_3_ = bf16[5,16,128]{2,1,0:T(8,128)(2,1)S(1)} collective-permute-done((bf16[5,16,128]{2,1,0:T(8,128)(2,1)S(1)}, bf16[5,16,128]{2,1,0:T(8,128)(2,1)S(1)}, u32[]{:S(2)}, u32[]{:S(2)}) %collective-permute-start.2) | collective-permute-done | bytes 20512 | tf_op jit(solution)/shard_map/ppermute | solution.py:741
  13.3 0.1 collective-permute-start.6
  13.4 0.5 %collective-permute-start.5 = (bf16[176,128]{1,0:T(8,128)(2,1)S(1)}, bf16[176,128]{1,0:T(8,128)(2,1)S(1)}, u32[]{:S(2)}, u32[]{:S(2)}) collective-permute-start(bf16[176,128]{1,0:T(8,128)(2,1)S(1)} %constant_dynamic-update-slice_fusion), channel_id=1, source_target_pairs={{0,1},{1,2},{2,3},{3,0},{4,5},{5,6},{6,7},{7,4},{8,9},{9,10},{10,1... | collective-permute-start | bytes 135176 | tf_op jit(solution)/shard_map/ppermute | solution.py:741
  13.9 1.9 %first_middle.1 = (f32[96,128]{1,0:T(8,128)S(1)}, f32[4,48,128]{2,1,0:T(8,128)S(1)}, bf16[20,240,128]{2,1,0:T(8,128)(2,1)S(1)}, f32[192,128]{1,0:T(8,128)S(1)}, ...) custom-call(s32[4]{0:T(128)S(1)} %pad_add_fusion.flags.refs_0_, ...), custom_call_target="tpu_custom_call" | custom-call | tf_op jit(solution)/shard_map/first_middle/pallas_call | solution.py:824
  15.8 1.6 %collective-permute-done.5.refs_3_ = bf16[176,128]{1,0:T(8,128)(2,1)S(1)} collective-permute-done((bf16[176,128]{1,0:T(8,128)(2,1)S(1)}, bf16[176,128]{1,0:T(8,128)(2,1)S(1)}, u32[]{:S(2)}, u32[]{:S(2)}) %collective-permute-start.5) | collective-permute-done | bytes 45088 | tf_op jit(solution)/shard_map/ppermute | solution.py:741
  17.4 4.2 %first_step.1 = (bf16[16,80,128]{2,1,0:T(8,128)(2,1)S(1)}, bf16[5,16,128]{2,1,0:T(8,128)(2,1)S(1)}, bf16[80,128]{1,0:T(8,128)(2,1)S(1)}, bf16[240,128]{1,0:T(8,1...) custom-call(s32[4]{0:T(128)S(1)} %pad_add_fusion.flags.refs_0_, ...), custom_call_target="tpu_custom_call" | custom-call | tf_op jit(solution)/shard_map/first_step/pallas_call | solution.py:824
  21.6 1.2 %collective-permute-start.7 = (bf16[240,128]{1,0:T(8,128)(2,1)S(1)}, bf16[240,128]{1,0:T(8,128)(2,1)S(1)}, u32[]{:S(2)}, u32[]{:S(2)}) collective-permute-start(bf16[240,128]{1,0:T(8,128)(2,1)S(1)} %get-tuple-element.58), channel_id=1, source_target_pairs={{0,4},{1,5},{2,6},{3,7},{4,0},{5,1},{6,2},{7,3},{8,12},{9,13},{10,... | collective-permute-start | bytes 184328 | tf_op jit(solution)/shard_map/ppermute | solution.py:741
  22.8 2.5 %collective-permute-start.8 = (bf16[240,128]{1,0:T(8,128)(2,1)S(1)}, bf16[240,128]{1,0:T(8,128)(2,1)S(1)}, u32[]{:S(2)}, u32[]{:S(2)}) collective-permute-start(bf16[240,128]{1,0:T(8,128)(2,1)S(1)} %get-tuple-element.59), channel_id=1, source_target_pairs={{0,16},{1,17},{2,18},{3,19},{4,8},{5,9},{6,10},{7,11},{8,4},{9,5},... | collective-permute-start | bytes 184328 | tf_op jit(solution)/shard_map/ppermute | solution.py:741
  25.4 3.0 %collective-permute-start.10 = (bf16[5,16,128]{2,1,0:T(8,128)(2,1)S(1)}, bf16[5,16,128]{2,1,0:T(8,128)(2,1)S(1)}, u32[]{:S(2)}, u32[]{:S(2)}) collective-permute-start(bf16[5,16,128]{2,1,0:T(8,128)(2,1)S(1)} %get-tuple-element.60), channel_id=1, source_target_pairs={{0,20},{1,21},{2,22},{3,23},{4,16},{5,17},{6,18},{7,19},{8,28},{9,... | collective-permute-start | bytes 61448 | tf_op jit(solution)/shard_map/ppermute | solution.py:741
  28.4 1.5 %collective-permute-start.9 = (bf16[5,16,128]{2,1,0:T(8,128)(2,1)S(1)}, bf16[5,16,128]{2,1,0:T(8,128)(2,1)S(1)}, u32[]{:S(2)}, u32[]{:S(2)}) collective-permute-start(bf16[5,16,128]{2,1,0:T(8,128)(2,1)S(1)} %get-tuple-element.60), channel_id=1, source_target_pairs={{0,16},{1,17},{2,18},{3,19},{4,20},{5,21},{6,22},{7,23},{8,24},{9,... | collective-permute-start | bytes 61448 | tf_op jit(solution)/shard_map/ppermute | solution.py:741
  29.9 0.3 collective-permute-done.10.refs_2_
  30.2 2.0 %collective-permute-done.9.refs_3_ = bf16[5,16,128]{2,1,0:T(8,128)(2,1)S(1)} collective-permute-done((bf16[5,16,128]{2,1,0:T(8,128)(2,1)S(1)}, bf16[5,16,128]{2,1,0:T(8,128)(2,1)S(1)}, u32[]{:S(2)}, u32[]{:S(2)}) %collective-permute-start.9) | collective-permute-done | bytes 20512 | tf_op jit(solution)/shard_map/ppermute | solution.py:741
  32.3 0.5 %collective-permute-start.12 = (bf16[128,128]{1,0:T(8,128)(2,1)S(1)}, bf16[128,128]{1,0:T(8,128)(2,1)S(1)}, u32[]{:S(2)}, u32[]{:S(2)}) collective-permute-start(bf16[128,128]{1,0:T(8,128)(2,1)S(1)} %pad_maximum_fusion), channel_id=1, source_target_pairs={{0,1},{1,2},{2,3},{3,0},{4,5},{5,6},{6,7},{7,4},{8,9},{9,10},{10,1... | collective-permute-start | bytes 98312 | tf_op jit(solution)/shard_map/ppermute | solution.py:741
  32.8 1.4 %second_middle.1 = (f32[96,128]{1,0:T(8,128)S(1)}, f32[4,48,128]{2,1,0:T(8,128)S(1)}, bf16[20,240,128]{2,1,0:T(8,128)(2,1)S(1)}) custom-call(s32[4]{0:T(128)S(1)} %pad_add_fusion.flags.refs_0_, bf16[16,80,128]{2,1,0:T(8,128)(2,1)S(1)} %get-tuple-element.56.refs_1_, bf16[5,16,128]{2,1,0:T(8,128)(2,1)S(1)} %collective-permute-done.10.refs_2_, ...), custom_call_target="tpu_custom_call" | custom-call | tf_op jit(solution)/shard_map/second_middle/pallas_call | solution.py:824
  34.2 1.5 %collective-permute-done.12.refs_3_ = bf16[128,128]{1,0:T(8,128)(2,1)S(1)} collective-permute-done((bf16[128,128]{1,0:T(8,128)(2,1)S(1)}, bf16[128,128]{1,0:T(8,128)(2,1)S(1)}, u32[]{:S(2)}, u32[]{:S(2)}) %collective-permute-start.12) | collective-permute-done | bytes 32800 | tf_op jit(solution)/shard_map/ppermute | solution.py:741
  35.7 4.2 %second_step.1 = bf16[80,16,128]{2,1,0:T(8,128)(2,1)} custom-call(s32[4]{0:T(128)S(1)} %pad_add_fusion.flags.refs_0_, bf16[16,80,128]{2,1,0:T(8,128)(2,1)S(1)} %get-tuple-element.56.refs_1_, s32[16,128]{1,0:T(8,128)S(1)} %copy-done.1, bf16[128,128]{1,0:T(8,128)(2,1)S(1)} %collective-permute-done.12.refs_3_, ...), custom_call_target="tpu_custom_call" | custom-call | tf_op jit(solution)/shard_map/second_step/pallas_call | solution.py:824
  (28 shorter events, 0.2 us)
Async XLA Ops:
  0.0 17.4 %copy-start.1 = (s32[16,128]{1,0:T(8,128)S(1)}, s32[16,128]{1,0:T(8,128)}, u32[]{:S(2)}) copy-start(s32[16,128]{1,0:T(8,128)} %refs_2_.3) | copy-start | bytes 24580
  0.0 17.4 %copy-start.2 = (f32[2,4,80]{2,1,0:T(4,128)S(1)}, f32[2,4,80]{2,1,0:T(4,128)}, u32[]{:S(2)}) copy-start(f32[2,4,80]{2,1,0:T(4,128)} %refs_14_.1) | copy-start | bytes 7684
  0.0 17.4 %copy-start = (bf16[80,384]{1,0:T(8,128)(2,1)S(1)}, bf16[80,384]{1,0:T(8,128)(2,1)}, u32[]{:S(2)}) copy-start(bf16[80,384]{1,0:T(8,128)(2,1)} %refs_13_.3) | copy-start | bytes 184324
  2.3 8.7 %collective-permute-start = (bf16[272,128]{1,0:T(8,128)(2,1)S(1)}, bf16[272,128]{1,0:T(8,128)(2,1)S(1)}, u32[]{:S(2)}, u32[]{:S(2)}) collective-permute-start(bf16[272,128]{1,0:T(8,128)(2,1)S(1)} %get-tuple-element.39), channel_id=1, source_target_pairs={{0,4},{1,5},{2,6},{3,7},{4,0},{5,1},{6,2},{7,3},{8,12},{9,13},{10,... | collective-permute-start | bytes 208904 | tf_op jit(solution)/shard_map/ppermute | solution.py:741
  5.4 5.6 %collective-permute-start.1 = (bf16[272,128]{1,0:T(8,128)(2,1)S(1)}, bf16[272,128]{1,0:T(8,128)(2,1)S(1)}, u32[]{:S(2)}, u32[]{:S(2)}) collective-permute-start(bf16[272,128]{1,0:T(8,128)(2,1)S(1)} %get-tuple-element.40), channel_id=1, source_target_pairs={{0,16},{1,17},{2,18},{3,19},{4,8},{5,9},{6,10},{7,11},{8,4},{9,5},... | collective-permute-start | bytes 208904 | tf_op jit(solution)/shard_map/ppermute | solution.py:741
  6.9 4.1 %collective-permute-start.4 = (bf16[5,16,128]{2,1,0:T(8,128)(2,1)S(1)}, bf16[5,16,128]{2,1,0:T(8,128)(2,1)S(1)}, u32[]{:S(2)}, u32[]{:S(2)}) collective-permute-start(bf16[5,16,128]{2,1,0:T(8,128)(2,1)S(1)} %get-tuple-element.41), channel_id=1, source_target_pairs={{0,16},{1,17},{2,18},{3,19},{4,24},{5,25},{6,26},{7,27},{8,20},{9,... | collective-permute-start | bytes 61448 | tf_op jit(solution)/shard_map/ppermute | solution.py:741
  7.4 4.7 %collective-permute-start.3 = (bf16[5,16,128]{2,1,0:T(8,128)(2,1)S(1)}, bf16[5,16,128]{2,1,0:T(8,128)(2,1)S(1)}, u32[]{:S(2)}, u32[]{:S(2)}) collective-permute-start(bf16[5,16,128]{2,1,0:T(8,128)(2,1)S(1)} %get-tuple-element.41), channel_id=1, source_target_pairs={{0,20},{1,21},{2,22},{3,23},{4,16},{5,17},{6,18},{7,19},{8,28},{9,... | collective-permute-start | bytes 61448 | tf_op jit(solution)/shard_map/ppermute | solution.py:741
  9.5 3.8 %collective-permute-start.2 = (bf16[5,16,128]{2,1,0:T(8,128)(2,1)S(1)}, bf16[5,16,128]{2,1,0:T(8,128)(2,1)S(1)}, u32[]{:S(2)}, u32[]{:S(2)}) collective-permute-start(bf16[5,16,128]{2,1,0:T(8,128)(2,1)S(1)} %get-tuple-element.41), channel_id=1, source_target_pairs={{0,16},{1,17},{2,18},{3,19},{4,20},{5,21},{6,22},{7,23},{8,24},{9,... | collective-permute-start | bytes 61448 | tf_op jit(solution)/shard_map/ppermute | solution.py:741
  13.3 2.5 %collective-permute-start.6 = (bf16[176,128]{1,0:T(8,128)(2,1)S(1)}, bf16[176,128]{1,0:T(8,128)(2,1)S(1)}, u32[]{:S(2)}, u32[]{:S(2)}) collective-permute-start(bf16[176,128]{1,0:T(8,128)(2,1)S(1)} %constant_dynamic-update-slice_fusion), channel_id=1, source_target_pairs={{0,3},{1,0},{2,1},{3,2},{4,7},{5,4},{6,5},{7,6},{8,11},{9,8},{10,9... | collective-permute-start | bytes 135176 | tf_op jit(solution)/shard_map/ppermute | solution.py:741
  13.4 4.0 %collective-permute-start.5 = (bf16[176,128]{1,0:T(8,128)(2,1)S(1)}, bf16[176,128]{1,0:T(8,128)(2,1)S(1)}, u32[]{:S(2)}, u32[]{:S(2)}) collective-permute-start(bf16[176,128]{1,0:T(8,128)(2,1)S(1)} %constant_dynamic-update-slice_fusion), channel_id=1, source_target_pairs={{0,1},{1,2},{2,3},{3,0},{4,5},{5,6},{6,7},{7,4},{8,9},{9,10},{10,1... | collective-permute-start | bytes 135176 | tf_op jit(solution)/shard_map/ppermute | solution.py:741
  21.6 8.3 %collective-permute-start.7 = (bf16[240,128]{1,0:T(8,128)(2,1)S(1)}, bf16[240,128]{1,0:T(8,128)(2,1)S(1)}, u32[]{:S(2)}, u32[]{:S(2)}) collective-permute-start(bf16[240,128]{1,0:T(8,128)(2,1)S(1)} %get-tuple-element.58), channel_id=1, source_target_pairs={{0,4},{1,5},{2,6},{3,7},{4,0},{5,1},{6,2},{7,3},{8,12},{9,13},{10,... | collective-permute-start | bytes 184328 | tf_op jit(solution)/shard_map/ppermute | solution.py:741
  22.8 7.1 %collective-permute-start.8 = (bf16[240,128]{1,0:T(8,128)(2,1)S(1)}, bf16[240,128]{1,0:T(8,128)(2,1)S(1)}, u32[]{:S(2)}, u32[]{:S(2)}) collective-permute-start(bf16[240,128]{1,0:T(8,128)(2,1)S(1)} %get-tuple-element.59), channel_id=1, source_target_pairs={{0,16},{1,17},{2,18},{3,19},{4,8},{5,9},{6,10},{7,11},{8,4},{9,5},... | collective-permute-start | bytes 184328 | tf_op jit(solution)/shard_map/ppermute | solution.py:741
  25.3 4.6 %collective-permute-start.11 = (bf16[5,16,128]{2,1,0:T(8,128)(2,1)S(1)}, bf16[5,16,128]{2,1,0:T(8,128)(2,1)S(1)}, u32[]{:S(2)}, u32[]{:S(2)}) collective-permute-start(bf16[5,16,128]{2,1,0:T(8,128)(2,1)S(1)} %get-tuple-element.60), channel_id=1, source_target_pairs={{0,16},{1,17},{2,18},{3,19},{4,24},{5,25},{6,26},{7,27},{8,20},{9,... | collective-permute-start | bytes 61448 | tf_op jit(solution)/shard_map/ppermute | solution.py:741
  25.4 4.8 %collective-permute-start.10 = (bf16[5,16,128]{2,1,0:T(8,128)(2,1)S(1)}, bf16[5,16,128]{2,1,0:T(8,128)(2,1)S(1)}, u32[]{:S(2)}, u32[]{:S(2)}) collective-permute-start(bf16[5,16,128]{2,1,0:T(8,128)(2,1)S(1)} %get-tuple-element.60), channel_id=1, source_target_pairs={{0,20},{1,21},{2,22},{3,23},{4,16},{5,17},{6,18},{7,19},{8,28},{9,... | collective-permute-start | bytes 61448 | tf_op jit(solution)/shard_map/ppermute | solution.py:741
  28.4 3.8 %collective-permute-start.9 = (bf16[5,16,128]{2,1,0:T(8,128)(2,1)S(1)}, bf16[5,16,128]{2,1,0:T(8,128)(2,1)S(1)}, u32[]{:S(2)}, u32[]{:S(2)}) collective-permute-start(bf16[5,16,128]{2,1,0:T(8,128)(2,1)S(1)} %get-tuple-element.60), channel_id=1, source_target_pairs={{0,16},{1,17},{2,18},{3,19},{4,20},{5,21},{6,22},{7,23},{8,24},{9,... | collective-permute-start | bytes 61448 | tf_op jit(solution)/shard_map/ppermute | solution.py:741
  32.2 2.0 %collective-permute-start.13 = (bf16[128,128]{1,0:T(8,128)(2,1)S(1)}, bf16[128,128]{1,0:T(8,128)(2,1)S(1)}, u32[]{:S(2)}, u32[]{:S(2)}) collective-permute-start(bf16[128,128]{1,0:T(8,128)(2,1)S(1)} %pad_maximum_fusion), channel_id=1, source_target_pairs={{0,3},{1,0},{2,1},{3,2},{4,7},{5,4},{6,5},{7,6},{8,11},{9,8},{10,9... | collective-permute-start | bytes 98312 | tf_op jit(solution)/shard_map/ppermute | solution.py:741
  32.3 3.4 %collective-permute-start.12 = (bf16[128,128]{1,0:T(8,128)(2,1)S(1)}, bf16[128,128]{1,0:T(8,128)(2,1)S(1)}, u32[]{:S(2)}, u32[]{:S(2)}) collective-permute-start(bf16[128,128]{1,0:T(8,128)(2,1)S(1)} %pad_maximum_fusion), channel_id=1, source_target_pairs={{0,1},{1,2},{2,3},{3,0},{4,5},{5,6},{6,7},{7,4},{8,9},{9,10},{10,1... | collective-permute-start | bytes 98312 | tf_op jit(solution)/shard_map/ppermute | solution.py:741

commit v12 on v11

--- a/solution.py
+++ b/solution.py
@@ -116,27 +116,29 @@
             terms += [term, gap]
         self.proj = jnp.concatenate(terms + [gap, gap], axis=0).astype(BF16)
         self.places, self.raw, self.d, self.flags = places, raw, d, flags
-        self.edges = None
-
-    def add(self, step, low, high):
-        pair = jnp.concatenate([low, high], axis=1)
-        parts = jnp.dot(self.proj, pair, preferred_element_type=F32)
-        whole = parts[0:8] + parts[8:16] + parts[16:24]
-        other = step + self.d.rows // 2
-        self.raw[step * 8 : step * 8 + 8, :] = whole[:, :128]
-        self.raw[other * 8 : other * 8 + 8, :] = whole[:, 128:]
-        places = [self.places[row * 128 : (row + 1) * 128, :] for row in (step, other)]
-        edges = jnp.dot(pair, jnp.concatenate(places, axis=0), preferred_element_type=F32)
-        self.edges = edges if self.edges is None else self.edges + edges
+
+    def project(self, state):
+        half = self.d.rows // 2
+        products = []
+        for step in range(half):
+            pair = jnp.concatenate([state[step], state[step + half]], axis=1)
+            products.append(jnp.dot(self.proj, pair, preferred_element_type=F32))
+        whole = jnp.concatenate([state[step] for step in range(2 * half)], axis=1)
+        edges = jnp.dot(whole, self.places[...], preferred_element_type=F32)
+        for step, parts in enumerate(products):
+            parts = parts[0:8] + parts[8:16] + parts[16:24]
+            self.raw[step * 8 : step * 8 + 8, :] = parts[:, :128]
+            self.raw[(step + half) * 8 : (step + half) * 8 + 8, :] = parts[:, 128:]
+        return edges.astype(BF16)
 
     def close(self, state, wet, fields, own_edges, one, two):
         d, even = self.d, self.flags[3] == 0
+        edges = self.project(state)
         keeping = jnp.where(self.flags[0] != 0, wet[...].astype(F32), 1.0)
         whole = [self.raw[pl.ds(field, d.rows, stride=8), :] * keeping for field in range(NS)]
         for field in range(NS):
             fields[field] = whole[field].astype(BF16)
         fields[NS] = pack_columns(whole, REACH).astype(BF16)
-        edges = self.edges.astype(BF16)
         put_edges(own_edges, 0, edges, d)
         row = lanes(edges.shape) % d.block
         downward = jnp.where(row < 2, roll(edges, -d.rows), jnp.zeros_like(edges))
@@ -182,8 +184,6 @@
     for copy in copies[len(pieces) :]:
         copy.wait()
     emission = Emission(surface, flags, places, raw, d)
-    for step in range(rows // 2):
-        emission.add(step, state[step], state[step + rows // 2])
     emission.close(state, wet, fields, own_edges, one, two)
     for k in range(NK):
         code = (offsets[0, k] * SPAN + offsets[1, k]).astype(F32)
@@ -340,26 +340,45 @@
     return x + x * jnp.tanh(x * (scale + (scale * 0.044715) * (x * x)))
 
 
+def staggered(count, *stages):
+    values = [{} for _ in stages]
+    for turn in range(count + len(stages) - 1):
+        for index, stage in enumerate(stages):
+            step = turn - index
+            if 0 <= step < count:
+                given = values[index - 1].pop(step) if index else None
+                values[index][step] = stage(step, given)
+
+
 def air(state, out, forcing_x, air_in, atm_out, d):
     half = d.rows // 2
-    first = subs((8, 128)) < 4
+    leading = subs((8, 128)) < 4
     blank = jnp.zeros((32, 128), BF16)
 
     def inputs(row):
         at = (row + 2) * 8
-        forced = jnp.where(first, forcing_x[at : at + 8, :], 1.0)
+        forced = jnp.where(leading, forcing_x[at : at + 8, :], 1.0)
         forced = jnp.concatenate([forced, jnp.zeros_like(forced)], axis=0).astype(BF16)
         return jnp.concatenate([state[row], forced, blank], axis=0)
 
-    for step in range(half):
+    def first(step, _):
         pair = jnp.concatenate([inputs(step), inputs(step + half)], axis=1)
-        hidden = twice_gelu(jnp.dot(air_in[...], pair, preferred_element_type=F32)).astype(BF16)
-        update = jnp.dot(atm_out[...], hidden, preferred_element_type=F32)
+        return jnp.dot(air_in[...], pair, preferred_element_type=F32)
+
+    def middle(step, product):
+        return twice_gelu(product).astype(BF16)
+
+    def second(step, hidden):
+        return jnp.dot(atm_out[...], hidden, preferred_element_type=F32)
+
+    def last(step, update):
         news = []
         for offset in range(2):
             change = update[:, offset * 128 : (offset + 1) * 128]
             news.append(state[step + offset * half].astype(F32) + 0.5 * change)
         out(step, *news)
+
+    staggered(half, first, middle, second, last)
 
 
 def edge_forcing(forcing_x, forcing_y, d):
@@ -449,7 +468,7 @@
 
     pairs = (rows + 2) // 2
 
-    for step in range(pairs):
+    def first(step, _):
         taps = jnp.concatenate(
             [
                 stack[step : step + 3].reshape(3 * 256, 128),
@@ -457,7 +476,10 @@
             ],
             axis=1,
         )
-        active = twice_gelu(jnp.dot(ocn_in[...], taps, preferred_element_type=F32))
+        return jnp.dot(ocn_in[...], taps, preferred_element_type=F32)
+
+    def activate(step, product):
+        active = twice_gelu(product)
         low, high = active[:, :128], active[:, 128:]
         if step == 0:
             low = jnp.where(at_top != 0, 0.0, low)
@@ -469,6 +491,7 @@
         hidden[step, HIDK:HIDP, :] = blank
         hidden[step + pairs, HIDK:HIDP, :] = blank
 
+    staggered(pairs, first, activate)
     product = jnp.dot(ocn_in[...], side[...], preferred_element_type=F32)
     spot = lanes((1, d.edge)) % block
     gone = ((spot == 0) & (at_top != 0)) | ((spot == rows + 1) & (at_bottom != 0))
@@ -486,13 +509,16 @@
     partial = taps_of([roll(active, -tap) for tap in range(3)])
     from_left, from_right = partial[0:CH], partial[2 * CH : 3 * CH]
     half = rows // 2
-    for step in range(half):
-        product = taps_of(
+
+    def second(step, _):
+        return taps_of(
             [
                 jnp.concatenate([hidden[step + tap], hidden[step + half + tap]], axis=1)
                 for tap in range(3)
             ]
         )
+
+    def last(step, product):
         news = []
         for offset in range(2):
             row = step + offset * half
@@ -504,6 +530,8 @@
             update = total * (0.5 * wet[row : row + 1, :].astype(F32))
             news.append(state[row].astype(F32) + update)
         out(step, *news)
+
+    staggered(half, second, last)
 
 
 def prepare(atm_in, atm_bias, ocn_in, ocn_bias, ocn_out, air_in, first, second, is_ocean):
@@ -675,10 +703,8 @@
                 for row, values in ((step, low), (step + rows // 2, high)):
                     raw[pl.ds(row, CH, stride=rows), :] = values
                 return
-            low, high = low.astype(BF16), high.astype(BF16)
-            out[step] = low
-            out[step + rows // 2] = high
-            emission.add(step, low, high)
+            out[step] = low.astype(BF16)
+            out[step + rows // 2] = high.astype(BF16)
 
         def close():
             if not closing:

time: 40.1 us -> 37.2 us (0.928)
  Pallas kernels: 13.9 us -> 11.5 us
    pallas_call x5, Pallas kernels: 13.9 us -> 11.5 us  [call(): pl.pallas_call(kernel, out_shape=outs, in_specs=[SMEM] + [VMEM] * len(ope...]
  transfers between devices with their start and end apart: 14 -> 14, of which waited for: 6 -> 6; matrix products, arithmetic and copies ran while one was open for 0% -> 0% of each run, Pallas kernels for 8% -> 9%
where the time goes in v12:
time: 37.2 us; the launch traced here: 37 us
  starting transfers between devices  17.6 us (47%)
  Pallas kernels  11.5 us (31%)
  waiting for transfers between devices  7.63 us (21%)
    ppermute x14, starting transfers between devices, send(): return lax.ppermute(x, names, pairs)  17.6 us
    pallas_call x5, Pallas kernels, call(): pl.pallas_call(kernel, out_shape=outs, in_specs=[SMEM] + [VMEM] * len(ope...  11.5 us
    ppermute x14, waiting for transfers between devices, send(): return lax.ppermute(x, names, pairs)  7.63 us
  transfers between devices with their start and end apart: 14, of which 6 were waited for; matrix products, arithmetic and copies ran while one was open for 0% of the time, Pallas kernels for 9%

profile of v12, /device:TPU:0, one launch (start us, length us, event | category | flops | bytes accessed | tf_op | source)
XLA Modules:
  0.0 37.0 jit_solution(11260989395634477675)
XLA Ops:
  0.0 0.1 pad_add_fusion.flags.refs_0_
  0.1 2.2 %start.1 = (bf16[16,80,128]{2,1,0:T(8,128)(2,1)S(1)}, bf16[8,16,128]{2,1,0:T(8,128)(2,1)S(1)}, bf16[16,128]{1,0:T(8,128)(2,1)S(1)}, bf16[2048,128]{1,0:T(8,128)(...) custom-call(s32[4]{0:T(128)S(1)} %pad_add_fusion.flags.refs_0_, ...), custom_call_target="tpu_custom_call" | custom-call | tf_op jit(solution)/shard_map/start/pallas_call | solution.py:850
  2.3 3.1 %collective-permute-start = (bf16[272,128]{1,0:T(8,128)(2,1)S(1)}, bf16[272,128]{1,0:T(8,128)(2,1)S(1)}, u32[]{:S(2)}, u32[]{:S(2)}) collective-permute-start(bf16[272,128]{1,0:T(8,128)(2,1)S(1)} %get-tuple-element.39), channel_id=1, source_target_pairs={{0,4},{1,5},{2,6},{3,7},{4,0},{5,1},{6,2},{7,3},{8,12},{9,13},{10,... | collective-permute-start | bytes 208904 | tf_op jit(solution)/shard_map/ppermute | solution.py:767
  5.4 1.5 %collective-permute-start.1 = (bf16[272,128]{1,0:T(8,128)(2,1)S(1)}, bf16[272,128]{1,0:T(8,128)(2,1)S(1)}, u32[]{:S(2)}, u32[]{:S(2)}) collective-permute-start(bf16[272,128]{1,0:T(8,128)(2,1)S(1)} %get-tuple-element.40), channel_id=1, source_target_pairs={{0,16},{1,17},{2,18},{3,19},{4,8},{5,9},{6,10},{7,11},{8,4},{9,5},... | collective-permute-start | bytes 208904 | tf_op jit(solution)/shard_map/ppermute | solution.py:767
  6.9 0.5 %collective-permute-start.4 = (bf16[5,16,128]{2,1,0:T(8,128)(2,1)S(1)}, bf16[5,16,128]{2,1,0:T(8,128)(2,1)S(1)}, u32[]{:S(2)}, u32[]{:S(2)}) collective-permute-start(bf16[5,16,128]{2,1,0:T(8,128)(2,1)S(1)} %get-tuple-element.41), channel_id=1, source_target_pairs={{0,16},{1,17},{2,18},{3,19},{4,24},{5,25},{6,26},{7,27},{8,20},{9,... | collective-permute-start | bytes 61448 | tf_op jit(solution)/shard_map/ppermute | solution.py:767
  7.4 2.1 %collective-permute-start.3 = (bf16[5,16,128]{2,1,0:T(8,128)(2,1)S(1)}, bf16[5,16,128]{2,1,0:T(8,128)(2,1)S(1)}, u32[]{:S(2)}, u32[]{:S(2)}) collective-permute-start(bf16[5,16,128]{2,1,0:T(8,128)(2,1)S(1)} %get-tuple-element.41), channel_id=1, source_target_pairs={{0,20},{1,21},{2,22},{3,23},{4,16},{5,17},{6,18},{7,19},{8,28},{9,... | collective-permute-start | bytes 61448 | tf_op jit(solution)/shard_map/ppermute | solution.py:767
  9.5 1.5 %collective-permute-start.2 = (bf16[5,16,128]{2,1,0:T(8,128)(2,1)S(1)}, bf16[5,16,128]{2,1,0:T(8,128)(2,1)S(1)}, u32[]{:S(2)}, u32[]{:S(2)}) collective-permute-start(bf16[5,16,128]{2,1,0:T(8,128)(2,1)S(1)} %get-tuple-element.41), channel_id=1, source_target_pairs={{0,16},{1,17},{2,18},{3,19},{4,20},{5,21},{6,22},{7,23},{8,24},{9,... | collective-permute-start | bytes 61448 | tf_op jit(solution)/shard_map/ppermute | solution.py:767
  11.0 1.1 %collective-permute-done.3.refs_2_ = bf16[5,16,128]{2,1,0:T(8,128)(2,1)S(1)} collective-permute-done((bf16[5,16,128]{2,1,0:T(8,128)(2,1)S(1)}, bf16[5,16,128]{2,1,0:T(8,128)(2,1)S(1)}, u32[]{:S(2)}, u32[]{:S(2)}) %collective-permute-start.3) | collective-permute-done | bytes 20512 | tf_op jit(solution)/shard_map/ppermute | solution.py:767
  12.1 1.2 %collective-permute-done.2.refs_3_ = bf16[5,16,128]{2,1,0:T(8,128)(2,1)S(1)} collective-permute-done((bf16[5,16,128]{2,1,0:T(8,128)(2,1)S(1)}, bf16[5,16,128]{2,1,0:T(8,128)(2,1)S(1)}, u32[]{:S(2)}, u32[]{:S(2)}) %collective-permute-start.2) | collective-permute-done | bytes 20512 | tf_op jit(solution)/shard_map/ppermute | solution.py:767
  13.3 0.1 collective-permute-start.6
  13.4 0.5 %collective-permute-start.5 = (bf16[176,128]{1,0:T(8,128)(2,1)S(1)}, bf16[176,128]{1,0:T(8,128)(2,1)S(1)}, u32[]{:S(2)}, u32[]{:S(2)}) collective-permute-start(bf16[176,128]{1,0:T(8,128)(2,1)S(1)} %constant_dynamic-update-slice_fusion), channel_id=1, source_target_pairs={{0,1},{1,2},{2,3},{3,0},{4,5},{5,6},{6,7},{7,4},{8,9},{9,10},{10,1... | collective-permute-start | bytes 135176 | tf_op jit(solution)/shard_map/ppermute | solution.py:767
  13.9 1.9 %first_middle.1 = (f32[96,128]{1,0:T(8,128)S(1)}, f32[4,48,128]{2,1,0:T(8,128)S(1)}, bf16[20,240,128]{2,1,0:T(8,128)(2,1)S(1)}, f32[192,128]{1,0:T(8,128)S(1)}, ...) custom-call(s32[4]{0:T(128)S(1)} %pad_add_fusion.flags.refs_0_, ...), custom_call_target="tpu_custom_call" | custom-call | tf_op jit(solution)/shard_map/first_middle/pallas_call | solution.py:850
  15.8 1.6 %collective-permute-done.5.refs_3_ = bf16[176,128]{1,0:T(8,128)(2,1)S(1)} collective-permute-done((bf16[176,128]{1,0:T(8,128)(2,1)S(1)}, bf16[176,128]{1,0:T(8,128)(2,1)S(1)}, u32[]{:S(2)}, u32[]{:S(2)}) %collective-permute-start.5) | collective-permute-done | bytes 45088 | tf_op jit(solution)/shard_map/ppermute | solution.py:767
  17.4 2.7 %first_step.1 = (bf16[16,80,128]{2,1,0:T(8,128)(2,1)S(1)}, bf16[5,16,128]{2,1,0:T(8,128)(2,1)S(1)}, bf16[80,128]{1,0:T(8,128)(2,1)S(1)}, bf16[240,128]{1,0:T(8,1...) custom-call(s32[4]{0:T(128)S(1)} %pad_add_fusion.flags.refs_0_, ...), custom_call_target="tpu_custom_call" | custom-call | tf_op jit(solution)/shard_map/first_step/pallas_call | solution.py:850
  20.1 1.2 %collective-permute-start.7 = (bf16[240,128]{1,0:T(8,128)(2,1)S(1)}, bf16[240,128]{1,0:T(8,128)(2,1)S(1)}, u32[]{:S(2)}, u32[]{:S(2)}) collective-permute-start(bf16[240,128]{1,0:T(8,128)(2,1)S(1)} %get-tuple-element.58), channel_id=1, source_target_pairs={{0,4},{1,5},{2,6},{3,7},{4,0},{5,1},{6,2},{7,3},{8,12},{9,13},{10,... | collective-permute-start | bytes 184328 | tf_op jit(solution)/shard_map/ppermute | solution.py:767
  21.3 2.1 %collective-permute-start.8 = (bf16[240,128]{1,0:T(8,128)(2,1)S(1)}, bf16[240,128]{1,0:T(8,128)(2,1)S(1)}, u32[]{:S(2)}, u32[]{:S(2)}) collective-permute-start(bf16[240,128]{1,0:T(8,128)(2,1)S(1)} %get-tuple-element.59), channel_id=1, source_target_pairs={{0,16},{1,17},{2,18},{3,19},{4,8},{5,9},{6,10},{7,11},{8,4},{9,5},... | collective-permute-start | bytes 184328 | tf_op jit(solution)/shard_map/ppermute | solution.py:767
  23.4 3.0 %collective-permute-start.10 = (bf16[5,16,128]{2,1,0:T(8,128)(2,1)S(1)}, bf16[5,16,128]{2,1,0:T(8,128)(2,1)S(1)}, u32[]{:S(2)}, u32[]{:S(2)}) collective-permute-start(bf16[5,16,128]{2,1,0:T(8,128)(2,1)S(1)} %get-tuple-element.60), channel_id=1, source_target_pairs={{0,20},{1,21},{2,22},{3,23},{4,16},{5,17},{6,18},{7,19},{8,28},{9,... | collective-permute-start | bytes 61448 | tf_op jit(solution)/shard_map/ppermute | solution.py:767
  26.5 1.5 %collective-permute-start.9 = (bf16[5,16,128]{2,1,0:T(8,128)(2,1)S(1)}, bf16[5,16,128]{2,1,0:T(8,128)(2,1)S(1)}, u32[]{:S(2)}, u32[]{:S(2)}) collective-permute-start(bf16[5,16,128]{2,1,0:T(8,128)(2,1)S(1)} %get-tuple-element.60), channel_id=1, source_target_pairs={{0,16},{1,17},{2,18},{3,19},{4,20},{5,21},{6,22},{7,23},{8,24},{9,... | collective-permute-start | bytes 61448 | tf_op jit(solution)/shard_map/ppermute | solution.py:767
  28.0 0.3 collective-permute-done.10.refs_2_
  28.3 2.0 %collective-permute-done.9.refs_3_ = bf16[5,16,128]{2,1,0:T(8,128)(2,1)S(1)} collective-permute-done((bf16[5,16,128]{2,1,0:T(8,128)(2,1)S(1)}, bf16[5,16,128]{2,1,0:T(8,128)(2,1)S(1)}, u32[]{:S(2)}, u32[]{:S(2)}) %collective-permute-start.9) | collective-permute-done | bytes 20512 | tf_op jit(solution)/shard_map/ppermute | solution.py:767
  30.4 0.5 %collective-permute-start.12 = (bf16[128,128]{1,0:T(8,128)(2,1)S(1)}, bf16[128,128]{1,0:T(8,128)(2,1)S(1)}, u32[]{:S(2)}, u32[]{:S(2)}) collective-permute-start(bf16[128,128]{1,0:T(8,128)(2,1)S(1)} %pad_maximum_fusion), channel_id=1, source_target_pairs={{0,1},{1,2},{2,3},{3,0},{4,5},{5,6},{6,7},{7,4},{8,9},{9,10},{10,1... | collective-permute-start | bytes 98312 | tf_op jit(solution)/shard_map/ppermute | solution.py:767
  30.9 1.4 %second_middle.1 = (f32[96,128]{1,0:T(8,128)S(1)}, f32[4,48,128]{2,1,0:T(8,128)S(1)}, bf16[20,240,128]{2,1,0:T(8,128)(2,1)S(1)}) custom-call(s32[4]{0:T(128)S(1)} %pad_add_fusion.flags.refs_0_, bf16[16,80,128]{2,1,0:T(8,128)(2,1)S(1)} %get-tuple-element.56.refs_1_, bf16[5,16,128]{2,1,0:T(8,128)(2,1)S(1)} %collective-permute-done.10.refs_2_, ...), custom_call_target="tpu_custom_call" | custom-call | tf_op jit(solution)/shard_map/second_middle/pallas_call | solution.py:850
  32.3 1.5 %collective-permute-done.12.refs_3_ = bf16[128,128]{1,0:T(8,128)(2,1)S(1)} collective-permute-done((bf16[128,128]{1,0:T(8,128)(2,1)S(1)}, bf16[128,128]{1,0:T(8,128)(2,1)S(1)}, u32[]{:S(2)}, u32[]{:S(2)}) %collective-permute-start.12) | collective-permute-done | bytes 32800 | tf_op jit(solution)/shard_map/ppermute | solution.py:767
  33.8 3.3 %second_step.1 = bf16[80,16,128]{2,1,0:T(8,128)(2,1)} custom-call(s32[4]{0:T(128)S(1)} %pad_add_fusion.flags.refs_0_, bf16[16,80,128]{2,1,0:T(8,128)(2,1)S(1)} %get-tuple-element.56.refs_1_, s32[16,128]{1,0:T(8,128)S(1)} %copy-done.1, bf16[128,128]{1,0:T(8,128)(2,1)S(1)} %collective-permute-done.12.refs_3_, ...), custom_call_target="tpu_custom_call" | custom-call | tf_op jit(solution)/shard_map/second_step/pallas_call | solution.py:850
  (28 shorter events, 0.2 us)
Async XLA Ops:
  0.0 17.4 %copy-start.1 = (s32[16,128]{1,0:T(8,128)S(1)}, s32[16,128]{1,0:T(8,128)}, u32[]{:S(2)}) copy-start(s32[16,128]{1,0:T(8,128)} %refs_2_.3) | copy-start | bytes 24580
  0.0 17.4 %copy-start.2 = (f32[2,4,80]{2,1,0:T(4,128)S(1)}, f32[2,4,80]{2,1,0:T(4,128)}, u32[]{:S(2)}) copy-start(f32[2,4,80]{2,1,0:T(4,128)} %refs_14_.1) | copy-start | bytes 7684
  0.0 17.4 %copy-start = (bf16[80,384]{1,0:T(8,128)(2,1)S(1)}, bf16[80,384]{1,0:T(8,128)(2,1)}, u32[]{:S(2)}) copy-start(bf16[80,384]{1,0:T(8,128)(2,1)} %refs_13_.3) | copy-start | bytes 184324
  2.3 8.7 %collective-permute-start = (bf16[272,128]{1,0:T(8,128)(2,1)S(1)}, bf16[272,128]{1,0:T(8,128)(2,1)S(1)}, u32[]{:S(2)}, u32[]{:S(2)}) collective-permute-start(bf16[272,128]{1,0:T(8,128)(2,1)S(1)} %get-tuple-element.39), channel_id=1, source_target_pairs={{0,4},{1,5},{2,6},{3,7},{4,0},{5,1},{6,2},{7,3},{8,12},{9,13},{10,... | collective-permute-start | bytes 208904 | tf_op jit(solution)/shard_map/ppermute | solution.py:767
  5.4 5.6 %collective-permute-start.1 = (bf16[272,128]{1,0:T(8,128)(2,1)S(1)}, bf16[272,128]{1,0:T(8,128)(2,1)S(1)}, u32[]{:S(2)}, u32[]{:S(2)}) collective-permute-start(bf16[272,128]{1,0:T(8,128)(2,1)S(1)} %get-tuple-element.40), channel_id=1, source_target_pairs={{0,16},{1,17},{2,18},{3,19},{4,8},{5,9},{6,10},{7,11},{8,4},{9,5},... | collective-permute-start | bytes 208904 | tf_op jit(solution)/shard_map/ppermute | solution.py:767
  6.9 4.1 %collective-permute-start.4 = (bf16[5,16,128]{2,1,0:T(8,128)(2,1)S(1)}, bf16[5,16,128]{2,1,0:T(8,128)(2,1)S(1)}, u32[]{:S(2)}, u32[]{:S(2)}) collective-permute-start(bf16[5,16,128]{2,1,0:T(8,128)(2,1)S(1)} %get-tuple-element.41), channel_id=1, source_target_pairs={{0,16},{1,17},{2,18},{3,19},{4,24},{5,25},{6,26},{7,27},{8,20},{9,... | collective-permute-start | bytes 61448 | tf_op jit(solution)/shard_map/ppermute | solution.py:767
  7.4 4.7 %collective-permute-start.3 = (bf16[5,16,128]{2,1,0:T(8,128)(2,1)S(1)}, bf16[5,16,128]{2,1,0:T(8,128)(2,1)S(1)}, u32[]{:S(2)}, u32[]{:S(2)}) collective-permute-start(bf16[5,16,128]{2,1,0:T(8,128)(2,1)S(1)} %get-tuple-element.41), channel_id=1, source_target_pairs={{0,20},{1,21},{2,22},{3,23},{4,16},{5,17},{6,18},{7,19},{8,28},{9,... | collective-permute-start | bytes 61448 | tf_op jit(solution)/shard_map/ppermute | solution.py:767
  9.5 3.8 %collective-permute-start.2 = (bf16[5,16,128]{2,1,0:T(8,128)(2,1)S(1)}, bf16[5,16,128]{2,1,0:T(8,128)(2,1)S(1)}, u32[]{:S(2)}, u32[]{:S(2)}) collective-permute-start(bf16[5,16,128]{2,1,0:T(8,128)(2,1)S(1)} %get-tuple-element.41), channel_id=1, source_target_pairs={{0,16},{1,17},{2,18},{3,19},{4,20},{5,21},{6,22},{7,23},{8,24},{9,... | collective-permute-start | bytes 61448 | tf_op jit(solution)/shard_map/ppermute | solution.py:767
  13.3 2.5 %collective-permute-start.6 = (bf16[176,128]{1,0:T(8,128)(2,1)S(1)}, bf16[176,128]{1,0:T(8,128)(2,1)S(1)}, u32[]{:S(2)}, u32[]{:S(2)}) collective-permute-start(bf16[176,128]{1,0:T(8,128)(2,1)S(1)} %constant_dynamic-update-slice_fusion), channel_id=1, source_target_pairs={{0,3},{1,0},{2,1},{3,2},{4,7},{5,4},{6,5},{7,6},{8,11},{9,8},{10,9... | collective-permute-start | bytes 135176 | tf_op jit(solution)/shard_map/ppermute | solution.py:767
  13.4 4.0 %collective-permute-start.5 = (bf16[176,128]{1,0:T(8,128)(2,1)S(1)}, bf16[176,128]{1,0:T(8,128)(2,1)S(1)}, u32[]{:S(2)}, u32[]{:S(2)}) collective-permute-start(bf16[176,128]{1,0:T(8,128)(2,1)S(1)} %constant_dynamic-update-slice_fusion), channel_id=1, source_target_pairs={{0,1},{1,2},{2,3},{3,0},{4,5},{5,6},{6,7},{7,4},{8,9},{9,10},{10,1... | collective-permute-start | bytes 135176 | tf_op jit(solution)/shard_map/ppermute | solution.py:767
  20.1 7.9 %collective-permute-start.7 = (bf16[240,128]{1,0:T(8,128)(2,1)S(1)}, bf16[240,128]{1,0:T(8,128)(2,1)S(1)}, u32[]{:S(2)}, u32[]{:S(2)}) collective-permute-start(bf16[240,128]{1,0:T(8,128)(2,1)S(1)} %get-tuple-element.58), channel_id=1, source_target_pairs={{0,4},{1,5},{2,6},{3,7},{4,0},{5,1},{6,2},{7,3},{8,12},{9,13},{10,... | collective-permute-start | bytes 184328 | tf_op jit(solution)/shard_map/ppermute | solution.py:767
  21.3 6.7 %collective-permute-start.8 = (bf16[240,128]{1,0:T(8,128)(2,1)S(1)}, bf16[240,128]{1,0:T(8,128)(2,1)S(1)}, u32[]{:S(2)}, u32[]{:S(2)}) collective-permute-start(bf16[240,128]{1,0:T(8,128)(2,1)S(1)} %get-tuple-element.59), channel_id=1, source_target_pairs={{0,16},{1,17},{2,18},{3,19},{4,8},{5,9},{6,10},{7,11},{8,4},{9,5},... | collective-permute-start | bytes 184328 | tf_op jit(solution)/shard_map/ppermute | solution.py:767
  23.4 4.6 %collective-permute-start.11 = (bf16[5,16,128]{2,1,0:T(8,128)(2,1)S(1)}, bf16[5,16,128]{2,1,0:T(8,128)(2,1)S(1)}, u32[]{:S(2)}, u32[]{:S(2)}) collective-permute-start(bf16[5,16,128]{2,1,0:T(8,128)(2,1)S(1)} %get-tuple-element.60), channel_id=1, source_target_pairs={{0,16},{1,17},{2,18},{3,19},{4,24},{5,25},{6,26},{7,27},{8,20},{9,... | collective-permute-start | bytes 61448 | tf_op jit(solution)/shard_map/ppermute | solution.py:767
  23.4 4.8 %collective-permute-start.10 = (bf16[5,16,128]{2,1,0:T(8,128)(2,1)S(1)}, bf16[5,16,128]{2,1,0:T(8,128)(2,1)S(1)}, u32[]{:S(2)}, u32[]{:S(2)}) collective-permute-start(bf16[5,16,128]{2,1,0:T(8,128)(2,1)S(1)} %get-tuple-element.60), channel_id=1, source_target_pairs={{0,20},{1,21},{2,22},{3,23},{4,16},{5,17},{6,18},{7,19},{8,28},{9,... | collective-permute-start | bytes 61448 | tf_op jit(solution)/shard_map/ppermute | solution.py:767
  26.5 3.8 %collective-permute-start.9 = (bf16[5,16,128]{2,1,0:T(8,128)(2,1)S(1)}, bf16[5,16,128]{2,1,0:T(8,128)(2,1)S(1)}, u32[]{:S(2)}, u32[]{:S(2)}) collective-permute-start(bf16[5,16,128]{2,1,0:T(8,128)(2,1)S(1)} %get-tuple-element.60), channel_id=1, source_target_pairs={{0,16},{1,17},{2,18},{3,19},{4,20},{5,21},{6,22},{7,23},{8,24},{9,... | collective-permute-start | bytes 61448 | tf_op jit(solution)/shard_map/ppermute | solution.py:767
  30.3 2.0 %collective-permute-start.13 = (bf16[128,128]{1,0:T(8,128)(2,1)S(1)}, bf16[128,128]{1,0:T(8,128)(2,1)S(1)}, u32[]{:S(2)}, u32[]{:S(2)}) collective-permute-start(bf16[128,128]{1,0:T(8,128)(2,1)S(1)} %pad_maximum_fusion), channel_id=1, source_target_pairs={{0,3},{1,0},{2,1},{3,2},{4,7},{5,4},{6,5},{7,6},{8,11},{9,8},{10,9... | collective-permute-start | bytes 98312 | tf_op jit(solution)/shard_map/ppermute | solution.py:767
  30.4 3.4 %collective-permute-start.12 = (bf16[128,128]{1,0:T(8,128)(2,1)S(1)}, bf16[128,128]{1,0:T(8,128)(2,1)S(1)}, u32[]{:S(2)}, u32[]{:S(2)}) collective-permute-start(bf16[128,128]{1,0:T(8,128)(2,1)S(1)} %pad_maximum_fusion), channel_id=1, source_target_pairs={{0,1},{1,2},{2,3},{3,0},{4,5},{5,6},{6,7},{7,4},{8,9},{9,10},{10,1... | collective-permute-start | bytes 98312 | tf_op jit(solution)/shard_map/ppermute | solution.py:767

commit v13 on v12

--- a/solution.py
+++ b/solution.py
@@ -768,13 +768,14 @@
 
 
 def swap_rows(x, turn, across):
-    count = lax.axis_size("lat")
+    count, columns = lax.axis_size("lat"), lax.axis_size("lon")
 
     def move(group, lat, lon):
         other = ((lat + turn) ^ 1) - turn
-        if not 0 <= other < count:
-            return 1 - group, lat, lon
-        return (1 - group if across else group), other, lon
+        if 0 <= other < count and (across or group == 1):
+            return (1 - group if across else group), other, lon
+        beside = lon ^ 1
+        return group, lat, beside if beside < columns else lon
 
     return send(x, move)
 

time: 37.2 us -> 37.2 us (level)
  no operation moved by 1% of the time
where the time goes in v13:
time: 37.2 us; the launch traced here: 37 us
  starting transfers between devices  17.6 us (47%)
  Pallas kernels  11.5 us (31%)
  waiting for transfers between devices  7.63 us (21%)
    ppermute x14, starting transfers between devices, send(): return lax.ppermute(x, names, pairs)  17.6 us
    pallas_call x5, Pallas kernels, call(): pl.pallas_call(kernel, out_shape=outs, in_specs=[SMEM] + [VMEM] * len(ope...  11.5 us
    ppermute x14, waiting for transfers between devices, send(): return lax.ppermute(x, names, pairs)  7.63 us
  transfers between devices with their start and end apart: 14, of which 6 were waited for; matrix products, arithmetic and copies ran while one was open for 0% of the time, Pallas kernels for 9%

profile of v13, /device:TPU:0, one launch (start us, length us, event | category | flops | bytes accessed | tf_op | source)
XLA Modules:
  0.0 37.0 jit_solution(412314425557345191)
XLA Ops:
  0.0 0.1 pad_add_fusion.flags.refs_0_
  0.1 2.2 %start.1 = (bf16[16,80,128]{2,1,0:T(8,128)(2,1)S(1)}, bf16[8,16,128]{2,1,0:T(8,128)(2,1)S(1)}, bf16[16,128]{1,0:T(8,128)(2,1)S(1)}, bf16[2048,128]{1,0:T(8,128)(...) custom-call(s32[4]{0:T(128)S(1)} %pad_add_fusion.flags.refs_0_, ...), custom_call_target="tpu_custom_call" | custom-call | tf_op jit(solution)/shard_map/start/pallas_call | solution.py:851
  2.3 0.5 %collective-permute-start = (bf16[272,128]{1,0:T(8,128)(2,1)S(1)}, bf16[272,128]{1,0:T(8,128)(2,1)S(1)}, u32[]{:S(2)}, u32[]{:S(2)}) collective-permute-start(bf16[272,128]{1,0:T(8,128)(2,1)S(1)} %get-tuple-element.39), channel_id=1, source_target_pairs={{0,1},{1,0},{2,3},{3,2},{4,5},{5,4},{6,7},{7,6},{8,9},{9,8},{10,11... | collective-permute-start | bytes 208904 | tf_op jit(solution)/shard_map/ppermute | solution.py:767
  2.8 0.1 collective-permute-start.1
  2.9 0.4 %collective-permute-start.4 = (bf16[5,16,128]{2,1,0:T(8,128)(2,1)S(1)}, bf16[5,16,128]{2,1,0:T(8,128)(2,1)S(1)}, u32[]{:S(2)}, u32[]{:S(2)}) collective-permute-start(bf16[5,16,128]{2,1,0:T(8,128)(2,1)S(1)} %get-tuple-element.41), channel_id=1, source_target_pairs={{0,1},{1,0},{2,3},{3,2},{4,24},{5,25},{6,26},{7,27},{8,20},{9,21},... | collective-permute-start | bytes 61448 | tf_op jit(solution)/shard_map/ppermute | solution.py:767
  3.3 6.1 %collective-permute-start.3 = (bf16[5,16,128]{2,1,0:T(8,128)(2,1)S(1)}, bf16[5,16,128]{2,1,0:T(8,128)(2,1)S(1)}, u32[]{:S(2)}, u32[]{:S(2)}) collective-permute-start(bf16[5,16,128]{2,1,0:T(8,128)(2,1)S(1)} %get-tuple-element.41), channel_id=1, source_target_pairs={{0,20},{1,21},{2,22},{3,23},{4,16},{5,17},{6,18},{7,19},{8,28},{9,... | collective-permute-start | bytes 61448 | tf_op jit(solution)/shard_map/ppermute | solution.py:767
  9.5 1.5 %collective-permute-start.2 = (bf16[5,16,128]{2,1,0:T(8,128)(2,1)S(1)}, bf16[5,16,128]{2,1,0:T(8,128)(2,1)S(1)}, u32[]{:S(2)}, u32[]{:S(2)}) collective-permute-start(bf16[5,16,128]{2,1,0:T(8,128)(2,1)S(1)} %get-tuple-element.41), channel_id=1, source_target_pairs={{0,16},{1,17},{2,18},{3,19},{4,20},{5,21},{6,22},{7,23},{8,24},{9,... | collective-permute-start | bytes 61448 | tf_op jit(solution)/shard_map/ppermute | solution.py:767
  11.0 0.3 collective-permute-done.3.refs_2_
  11.2 2.0 %collective-permute-done.2.refs_3_ = bf16[5,16,128]{2,1,0:T(8,128)(2,1)S(1)} collective-permute-done((bf16[5,16,128]{2,1,0:T(8,128)(2,1)S(1)}, bf16[5,16,128]{2,1,0:T(8,128)(2,1)S(1)}, u32[]{:S(2)}, u32[]{:S(2)}) %collective-permute-start.2) | collective-permute-done | bytes 20512 | tf_op jit(solution)/shard_map/ppermute | solution.py:767
  13.4 0.5 %collective-permute-start.5 = (bf16[176,128]{1,0:T(8,128)(2,1)S(1)}, bf16[176,128]{1,0:T(8,128)(2,1)S(1)}, u32[]{:S(2)}, u32[]{:S(2)}) collective-permute-start(bf16[176,128]{1,0:T(8,128)(2,1)S(1)} %constant_dynamic-update-slice_fusion), channel_id=1, source_target_pairs={{0,1},{1,2},{2,3},{3,0},{4,5},{5,6},{6,7},{7,4},{8,9},{9,10},{10,1... | collective-permute-start | bytes 135176 | tf_op jit(solution)/shard_map/ppermute | solution.py:767
  13.9 1.9 %first_middle.1 = (f32[96,128]{1,0:T(8,128)S(1)}, f32[4,48,128]{2,1,0:T(8,128)S(1)}, bf16[20,240,128]{2,1,0:T(8,128)(2,1)S(1)}, f32[192,128]{1,0:T(8,128)S(1)}, ...) custom-call(s32[4]{0:T(128)S(1)} %pad_add_fusion.flags.refs_0_, ...), custom_call_target="tpu_custom_call" | custom-call | tf_op jit(solution)/shard_map/first_middle/pallas_call | solution.py:851
  15.8 1.6 %collective-permute-done.5.refs_3_ = bf16[176,128]{1,0:T(8,128)(2,1)S(1)} collective-permute-done((bf16[176,128]{1,0:T(8,128)(2,1)S(1)}, bf16[176,128]{1,0:T(8,128)(2,1)S(1)}, u32[]{:S(2)}, u32[]{:S(2)}) %collective-permute-start.5) | collective-permute-done | bytes 45088 | tf_op jit(solution)/shard_map/ppermute | solution.py:767
  17.4 2.7 %first_step.1 = (bf16[16,80,128]{2,1,0:T(8,128)(2,1)S(1)}, bf16[5,16,128]{2,1,0:T(8,128)(2,1)S(1)}, bf16[80,128]{1,0:T(8,128)(2,1)S(1)}, bf16[240,128]{1,0:T(8,1...) custom-call(s32[4]{0:T(128)S(1)} %pad_add_fusion.flags.refs_0_, ...), custom_call_target="tpu_custom_call" | custom-call | tf_op jit(solution)/shard_map/first_step/pallas_call | solution.py:851
  20.1 0.2 collective-permute-start.7
  20.3 0.4 %collective-permute-start.8 = (bf16[240,128]{1,0:T(8,128)(2,1)S(1)}, bf16[240,128]{1,0:T(8,128)(2,1)S(1)}, u32[]{:S(2)}, u32[]{:S(2)}) collective-permute-start(bf16[240,128]{1,0:T(8,128)(2,1)S(1)} %get-tuple-element.59), channel_id=1, source_target_pairs={{0,1},{1,0},{2,3},{3,2},{4,5},{5,4},{6,7},{7,6},{8,9},{9,8},{10,11... | collective-permute-start | bytes 184328 | tf_op jit(solution)/shard_map/ppermute | solution.py:767
  20.7 0.1 collective-permute-start.11
  20.8 5.7 %collective-permute-start.10 = (bf16[5,16,128]{2,1,0:T(8,128)(2,1)S(1)}, bf16[5,16,128]{2,1,0:T(8,128)(2,1)S(1)}, u32[]{:S(2)}, u32[]{:S(2)}) collective-permute-start(bf16[5,16,128]{2,1,0:T(8,128)(2,1)S(1)} %get-tuple-element.60), channel_id=1, source_target_pairs={{0,20},{1,21},{2,22},{3,23},{4,16},{5,17},{6,18},{7,19},{8,28},{9,... | collective-permute-start | bytes 61448 | tf_op jit(solution)/shard_map/ppermute | solution.py:767
  26.5 1.5 %collective-permute-start.9 = (bf16[5,16,128]{2,1,0:T(8,128)(2,1)S(1)}, bf16[5,16,128]{2,1,0:T(8,128)(2,1)S(1)}, u32[]{:S(2)}, u32[]{:S(2)}) collective-permute-start(bf16[5,16,128]{2,1,0:T(8,128)(2,1)S(1)} %get-tuple-element.60), channel_id=1, source_target_pairs={{0,16},{1,17},{2,18},{3,19},{4,20},{5,21},{6,22},{7,23},{8,24},{9,... | collective-permute-start | bytes 61448 | tf_op jit(solution)/shard_map/ppermute | solution.py:767
  28.0 0.3 collective-permute-done.10.refs_2_
  28.3 2.0 %collective-permute-done.9.refs_3_ = bf16[5,16,128]{2,1,0:T(8,128)(2,1)S(1)} collective-permute-done((bf16[5,16,128]{2,1,0:T(8,128)(2,1)S(1)}, bf16[5,16,128]{2,1,0:T(8,128)(2,1)S(1)}, u32[]{:S(2)}, u32[]{:S(2)}) %collective-permute-start.9) | collective-permute-done | bytes 20512 | tf_op jit(solution)/shard_map/ppermute | solution.py:767
  30.4 0.5 %collective-permute-start.12 = (bf16[128,128]{1,0:T(8,128)(2,1)S(1)}, bf16[128,128]{1,0:T(8,128)(2,1)S(1)}, u32[]{:S(2)}, u32[]{:S(2)}) collective-permute-start(bf16[128,128]{1,0:T(8,128)(2,1)S(1)} %pad_maximum_fusion), channel_id=1, source_target_pairs={{0,1},{1,2},{2,3},{3,0},{4,5},{5,6},{6,7},{7,4},{8,9},{9,10},{10,1... | collective-permute-start | bytes 98312 | tf_op jit(solution)/shard_map/ppermute | solution.py:767
  30.9 1.4 %second_middle.1 = (f32[96,128]{1,0:T(8,128)S(1)}, f32[4,48,128]{2,1,0:T(8,128)S(1)}, bf16[20,240,128]{2,1,0:T(8,128)(2,1)S(1)}) custom-call(s32[4]{0:T(128)S(1)} %pad_add_fusion.flags.refs_0_, bf16[16,80,128]{2,1,0:T(8,128)(2,1)S(1)} %get-tuple-element.56.refs_1_, bf16[5,16,128]{2,1,0:T(8,128)(2,1)S(1)} %collective-permute-done.10.refs_2_, ...), custom_call_target="tpu_custom_call" | custom-call | tf_op jit(solution)/shard_map/second_middle/pallas_call | solution.py:851
  32.3 1.5 %collective-permute-done.12.refs_3_ = bf16[128,128]{1,0:T(8,128)(2,1)S(1)} collective-permute-done((bf16[128,128]{1,0:T(8,128)(2,1)S(1)}, bf16[128,128]{1,0:T(8,128)(2,1)S(1)}, u32[]{:S(2)}, u32[]{:S(2)}) %collective-permute-start.12) | collective-permute-done | bytes 32800 | tf_op jit(solution)/shard_map/ppermute | solution.py:767
  33.8 3.3 %second_step.1 = bf16[80,16,128]{2,1,0:T(8,128)(2,1)} custom-call(s32[4]{0:T(128)S(1)} %pad_add_fusion.flags.refs_0_, bf16[16,80,128]{2,1,0:T(8,128)(2,1)S(1)} %get-tuple-element.56.refs_1_, s32[16,128]{1,0:T(8,128)S(1)} %copy-done.1, bf16[128,128]{1,0:T(8,128)(2,1)S(1)} %collective-permute-done.12.refs_3_, ...), custom_call_target="tpu_custom_call" | custom-call | tf_op jit(solution)/shard_map/second_step/pallas_call | solution.py:851
  (28 shorter events, 0.2 us)
Async XLA Ops:
  0.0 17.4 %copy-start.1 = (s32[16,128]{1,0:T(8,128)S(1)}, s32[16,128]{1,0:T(8,128)}, u32[]{:S(2)}) copy-start(s32[16,128]{1,0:T(8,128)} %refs_2_.3) | copy-start | bytes 24580
  0.0 17.4 %copy-start.2 = (f32[2,4,80]{2,1,0:T(4,128)S(1)}, f32[2,4,80]{2,1,0:T(4,128)}, u32[]{:S(2)}) copy-start(f32[2,4,80]{2,1,0:T(4,128)} %refs_14_.1) | copy-start | bytes 7684
  0.0 17.4 %copy-start = (bf16[80,384]{1,0:T(8,128)(2,1)S(1)}, bf16[80,384]{1,0:T(8,128)(2,1)}, u32[]{:S(2)}) copy-start(bf16[80,384]{1,0:T(8,128)(2,1)} %refs_13_.3) | copy-start | bytes 184324
  2.3 8.7 %collective-permute-start = (bf16[272,128]{1,0:T(8,128)(2,1)S(1)}, bf16[272,128]{1,0:T(8,128)(2,1)S(1)}, u32[]{:S(2)}, u32[]{:S(2)}) collective-permute-start(bf16[272,128]{1,0:T(8,128)(2,1)S(1)} %get-tuple-element.39), channel_id=1, source_target_pairs={{0,1},{1,0},{2,3},{3,2},{4,5},{5,4},{6,7},{7,6},{8,9},{9,8},{10,11... | collective-permute-start | bytes 208904 | tf_op jit(solution)/shard_map/ppermute | solution.py:767
  2.8 8.1 %collective-permute-start.1 = (bf16[272,128]{1,0:T(8,128)(2,1)S(1)}, bf16[272,128]{1,0:T(8,128)(2,1)S(1)}, u32[]{:S(2)}, u32[]{:S(2)}) collective-permute-start(bf16[272,128]{1,0:T(8,128)(2,1)S(1)} %get-tuple-element.40), channel_id=1, source_target_pairs={{0,1},{1,0},{2,3},{3,2},{4,5},{5,4},{6,7},{7,6},{8,9},{9,8},{10,11... | collective-permute-start | bytes 208904 | tf_op jit(solution)/shard_map/ppermute | solution.py:767
  2.9 8.1 %collective-permute-start.4 = (bf16[5,16,128]{2,1,0:T(8,128)(2,1)S(1)}, bf16[5,16,128]{2,1,0:T(8,128)(2,1)S(1)}, u32[]{:S(2)}, u32[]{:S(2)}) collective-permute-start(bf16[5,16,128]{2,1,0:T(8,128)(2,1)S(1)} %get-tuple-element.41), channel_id=1, source_target_pairs={{0,1},{1,0},{2,3},{3,2},{4,24},{5,25},{6,26},{7,27},{8,20},{9,21},... | collective-permute-start | bytes 61448 | tf_op jit(solution)/shard_map/ppermute | solution.py:767
  3.3 7.9 %collective-permute-start.3 = (bf16[5,16,128]{2,1,0:T(8,128)(2,1)S(1)}, bf16[5,16,128]{2,1,0:T(8,128)(2,1)S(1)}, u32[]{:S(2)}, u32[]{:S(2)}) collective-permute-start(bf16[5,16,128]{2,1,0:T(8,128)(2,1)S(1)} %get-tuple-element.41), channel_id=1, source_target_pairs={{0,20},{1,21},{2,22},{3,23},{4,16},{5,17},{6,18},{7,19},{8,28},{9,... | collective-permute-start | bytes 61448 | tf_op jit(solution)/shard_map/ppermute | solution.py:767
  9.5 3.8 %collective-permute-start.2 = (bf16[5,16,128]{2,1,0:T(8,128)(2,1)S(1)}, bf16[5,16,128]{2,1,0:T(8,128)(2,1)S(1)}, u32[]{:S(2)}, u32[]{:S(2)}) collective-permute-start(bf16[5,16,128]{2,1,0:T(8,128)(2,1)S(1)} %get-tuple-element.41), channel_id=1, source_target_pairs={{0,16},{1,17},{2,18},{3,19},{4,20},{5,21},{6,22},{7,23},{8,24},{9,... | collective-permute-start | bytes 61448 | tf_op jit(solution)/shard_map/ppermute | solution.py:767
  13.3 2.5 %collective-permute-start.6 = (bf16[176,128]{1,0:T(8,128)(2,1)S(1)}, bf16[176,128]{1,0:T(8,128)(2,1)S(1)}, u32[]{:S(2)}, u32[]{:S(2)}) collective-permute-start(bf16[176,128]{1,0:T(8,128)(2,1)S(1)} %constant_dynamic-update-slice_fusion), channel_id=1, source_target_pairs={{0,3},{1,0},{2,1},{3,2},{4,7},{5,4},{6,5},{7,6},{8,11},{9,8},{10,9... | collective-permute-start | bytes 135176 | tf_op jit(solution)/shard_map/ppermute | solution.py:767
  13.4 4.0 %collective-permute-start.5 = (bf16[176,128]{1,0:T(8,128)(2,1)S(1)}, bf16[176,128]{1,0:T(8,128)(2,1)S(1)}, u32[]{:S(2)}, u32[]{:S(2)}) collective-permute-start(bf16[176,128]{1,0:T(8,128)(2,1)S(1)} %constant_dynamic-update-slice_fusion), channel_id=1, source_target_pairs={{0,1},{1,2},{2,3},{3,0},{4,5},{5,6},{6,7},{7,4},{8,9},{9,10},{10,1... | collective-permute-start | bytes 135176 | tf_op jit(solution)/shard_map/ppermute | solution.py:767
  20.1 7.9 %collective-permute-start.7 = (bf16[240,128]{1,0:T(8,128)(2,1)S(1)}, bf16[240,128]{1,0:T(8,128)(2,1)S(1)}, u32[]{:S(2)}, u32[]{:S(2)}) collective-permute-start(bf16[240,128]{1,0:T(8,128)(2,1)S(1)} %get-tuple-element.58), channel_id=1, source_target_pairs={{0,1},{1,0},{2,3},{3,2},{4,5},{5,4},{6,7},{7,6},{8,9},{9,8},{10,11... | collective-permute-start | bytes 184328 | tf_op jit(solution)/shard_map/ppermute | solution.py:767
  20.3 7.7 %collective-permute-start.8 = (bf16[240,128]{1,0:T(8,128)(2,1)S(1)}, bf16[240,128]{1,0:T(8,128)(2,1)S(1)}, u32[]{:S(2)}, u32[]{:S(2)}) collective-permute-start(bf16[240,128]{1,0:T(8,128)(2,1)S(1)} %get-tuple-element.59), channel_id=1, source_target_pairs={{0,1},{1,0},{2,3},{3,2},{4,5},{5,4},{6,7},{7,6},{8,9},{9,8},{10,11... | collective-permute-start | bytes 184328 | tf_op jit(solution)/shard_map/ppermute | solution.py:767
  20.7 7.3 %collective-permute-start.11 = (bf16[5,16,128]{2,1,0:T(8,128)(2,1)S(1)}, bf16[5,16,128]{2,1,0:T(8,128)(2,1)S(1)}, u32[]{:S(2)}, u32[]{:S(2)}) collective-permute-start(bf16[5,16,128]{2,1,0:T(8,128)(2,1)S(1)} %get-tuple-element.60), channel_id=1, source_target_pairs={{0,1},{1,0},{2,3},{3,2},{4,24},{5,25},{6,26},{7,27},{8,20},{9,21},... | collective-permute-start | bytes 61448 | tf_op jit(solution)/shard_map/ppermute | solution.py:767
  20.8 7.5 %collective-permute-start.10 = (bf16[5,16,128]{2,1,0:T(8,128)(2,1)S(1)}, bf16[5,16,128]{2,1,0:T(8,128)(2,1)S(1)}, u32[]{:S(2)}, u32[]{:S(2)}) collective-permute-start(bf16[5,16,128]{2,1,0:T(8,128)(2,1)S(1)} %get-tuple-element.60), channel_id=1, source_target_pairs={{0,20},{1,21},{2,22},{3,23},{4,16},{5,17},{6,18},{7,19},{8,28},{9,... | collective-permute-start | bytes 61448 | tf_op jit(solution)/shard_map/ppermute | solution.py:767
  26.5 3.8 %collective-permute-start.9 = (bf16[5,16,128]{2,1,0:T(8,128)(2,1)S(1)}, bf16[5,16,128]{2,1,0:T(8,128)(2,1)S(1)}, u32[]{:S(2)}, u32[]{:S(2)}) collective-permute-start(bf16[5,16,128]{2,1,0:T(8,128)(2,1)S(1)} %get-tuple-element.60), channel_id=1, source_target_pairs={{0,16},{1,17},{2,18},{3,19},{4,20},{5,21},{6,22},{7,23},{8,24},{9,... | collective-permute-start | bytes 61448 | tf_op jit(solution)/shard_map/ppermute | solution.py:767
  30.3 2.0 %collective-permute-start.13 = (bf16[128,128]{1,0:T(8,128)(2,1)S(1)}, bf16[128,128]{1,0:T(8,128)(2,1)S(1)}, u32[]{:S(2)}, u32[]{:S(2)}) collective-permute-start(bf16[128,128]{1,0:T(8,128)(2,1)S(1)} %pad_maximum_fusion), channel_id=1, source_target_pairs={{0,3},{1,0},{2,1},{3,2},{4,7},{5,4},{6,5},{7,6},{8,11},{9,8},{10,9... | collective-permute-start | bytes 98312 | tf_op jit(solution)/shard_map/ppermute | solution.py:767
  30.4 3.4 %collective-permute-start.12 = (bf16[128,128]{1,0:T(8,128)(2,1)S(1)}, bf16[128,128]{1,0:T(8,128)(2,1)S(1)}, u32[]{:S(2)}, u32[]{:S(2)}) collective-permute-start(bf16[128,128]{1,0:T(8,128)(2,1)S(1)} %pad_maximum_fusion), channel_id=1, source_target_pairs={{0,1},{1,2},{2,3},{3,0},{4,5},{5,6},{6,7},{7,4},{8,9},{9,10},{10,1... | collective-permute-start | bytes 98312 | tf_op jit(solution)/shard_map/ppermute | solution.py:767

commit v14 on v13

--- a/solution.py
+++ b/solution.py
@@ -64,12 +64,10 @@
 def edge_places(places, d):
     lane = lanes((1, d.edge))
     block = lane // d.block
-    row = lane % d.block - 2
-    column = jnp.where(block == 0, 126, jnp.where(block == 1, 0, jnp.where(block == 2, 127, 1)))
-    own = (row >= 0) & (row < d.rows)
-    target = jnp.where(own, column, -1)
+    row = lane % d.block
+    target = jnp.where(block == 0, 126, jnp.where(block == 1, 0, jnp.where(block == 2, 127, 1)))
     position = subs((128, d.edge))
-    for step in range(d.rows):
+    for step in range(d.rows + 4):
         place = (position == jnp.where(row == step, target, -1)).astype(F32).astype(BF16)
         places[step * 128 : (step + 1) * 128, :] = place
 
@@ -124,7 +122,8 @@
             pair = jnp.concatenate([state[step], state[step + half]], axis=1)
             products.append(jnp.dot(self.proj, pair, preferred_element_type=F32))
         whole = jnp.concatenate([state[step] for step in range(2 * half)], axis=1)
-        edges = jnp.dot(whole, self.places[...], preferred_element_type=F32)
+        own = self.places[256 : 256 + 256 * half, :]
+        edges = jnp.dot(whole, own, preferred_element_type=F32)
         for step, parts in enumerate(products):
             parts = parts[0:8] + parts[8:16] + parts[16:24]
             self.raw[step * 8 : step * 8 + 8, :] = parts[:, :128]
@@ -340,7 +339,8 @@
     return x + x * jnp.tanh(x * (scale + (scale * 0.044715) * (x * x)))
 
 
-def staggered(count, *stages):
+def staggered(count, *stages, between=()):
+    between = list(between)
     values = [{} for _ in stages]
     for turn in range(count + len(stages) - 1):
         for index, stage in enumerate(stages):
@@ -348,6 +348,10 @@
             if 0 <= step < count:
                 given = values[index - 1].pop(step) if index else None
                 values[index][step] = stage(step, given)
+        if between:
+            between.pop(0)()
+    for extra in between:
+        extra()
 
 
 def air(state, out, forcing_x, air_in, atm_out, d):
@@ -381,24 +385,23 @@
     staggered(half, first, middle, second, last)
 
 
-def edge_forcing(forcing_x, forcing_y, d):
-    lane = lanes((8, d.edge))
-    block = lane // d.block
-    row = lane % d.block
-
-    inner = outer = jnp.zeros((8, d.edge), F32)
+def spread(edges, places, first, second):
+    chosen = [places[row * 128 : (row + 1) * 128, :] for row in (first, second)]
+    terms = edges.shape[1] // places.shape[1]
+    chosen = jnp.concatenate([jnp.concatenate(chosen, axis=0)] * terms, axis=1)
+    return lax.dot_general(
+        edges, chosen, (((1,), (1,)), ((), ())), preferred_element_type=F32
+    )
+
+
+def edge_forcing(forcing_x, forcing_y, places, d):
+    rows = []
     for step in range(d.rows + 4):
         at = pl.ds(step * 8, 8)
-        pad = [jnp.zeros((8, 128), F32)] * (d.pieces - 1)
-        here = jnp.concatenate([forcing_x[at, :]] + pad, axis=1)
-        there = jnp.concatenate([forcing_y[at, :]] + pad, axis=1)
-        for index, column in enumerate((126, 0, 127, 1)):
-            shift = step + index * d.block - column
-            match = (block == index) & (row == step)
-            if column in (0, 127):
-                inner = jnp.where(match, roll(here, shift), inner)
-            outer = jnp.where(match, roll(there, shift), outer)
-    return inner, outer
+        rows.append(jnp.concatenate([forcing_x[at, :], forcing_y[at, :]], axis=0).astype(BF16))
+    whole = jnp.concatenate(rows, axis=1)
+    edges = jnp.dot(whole, places[...], preferred_element_type=F32)
+    return edges[0:8], edges[8:16]
 
 
 def roll_rows(state, upper, lower, rolled, d):
@@ -416,7 +419,7 @@
 
 def sea(
     state, rolled, edges, left, right, out, forcing_x, forcing_y, ocn_in, ocn_out, wet,
-    at_top, at_bottom, stack, hidden, side, d,
+    at_top, at_bottom, stack, hidden, side, places, d,
 ):
     rows, block = d.rows, d.block
     lane = lanes((CH, 128))
@@ -434,8 +437,12 @@
         )
 
     beside = sides_of(inner, outer, spot)
-    middle = beside[1]
-    force_in, force_out = edge_forcing(forcing_x, forcing_y, d)
+    middle = jnp.where((spot >= block) & (spot < 3 * block), roll(beside[1], block), 0)
+    entries = []
+    for row in range(0, rows + 4, 2):
+        pair = spread(middle, places, row, row + 1).astype(BF16)
+        entries += [pair[:, :128], pair[:, 128:]]
+    force_in, force_out = edge_forcing(forcing_x, forcing_y, places, d)
     beside_forcing = sides_of(force_in, force_out, lanes((8, d.edge)))
     sub = subs((8, d.edge))
     ones = jnp.ones((8, d.edge), F32)
@@ -454,10 +461,9 @@
     lane_row = lanes((8, 128))
 
     for row in range(rows + 4):
-        entry = roll(middle, -row)[:, :128]
+        entry = entries[row]
         stack[row, 0:CH, :] = jnp.where(lane == 0, entry, rolled[row, 0:CH, :])
         stack[row, CH : 2 * CH, :] = rolled[row, CH : 2 * CH, :]
-        entry = roll(middle, 127 - block - row)[:, :128]
         stack[row, 2 * CH : 3 * CH, :] = jnp.where(lane == 127, entry, rolled[row, 2 * CH : 3 * CH, :])
         here, there = forcing_x[row * 8 : row * 8 + 8, :], forcing_y[row * 8 : row * 8 + 8, :]
         before = roll(jnp.where(lane_row == 127, there, here), 1)
@@ -491,12 +497,32 @@
         hidden[step, HIDK:HIDP, :] = blank
         hidden[step + pairs, HIDK:HIDP, :] = blank
 
-    staggered(pairs, first, activate)
-    product = jnp.dot(ocn_in[...], side[...], preferred_element_type=F32)
-    spot = lanes((1, d.edge)) % block
-    gone = ((spot == 0) & (at_top != 0)) | ((spot == rows + 1) & (at_bottom != 0))
-    active = jnp.where(gone, 0.0, twice_gelu(product)).astype(BF16)
-    active = jnp.concatenate([active, jnp.zeros((HIDP - HIDK, d.edge), BF16)], axis=0)
+    held = {}
+
+    def edge_first():
+        held["product"] = jnp.dot(ocn_in[...], side[...], preferred_element_type=F32)
+
+    def edge_activate():
+        spot = lanes((1, d.edge)) % block
+        gone = ((spot == 0) & (at_top != 0)) | ((spot == rows + 1) & (at_bottom != 0))
+        active = jnp.where(gone, 0.0, twice_gelu(held["product"])).astype(BF16)
+        active = jnp.concatenate([active, jnp.zeros((HIDP - HIDK, d.edge), BF16)], axis=0)
+        held["taps"] = [roll(active, -tap) for tap in range(3)]
+
+    def edge_second():
+        held["partial"] = taps_of(held["taps"])
+
+    def edge_spread():
+        spot = lanes((CH, d.edge))
+        row = spot % block - 2
+        inside = (row >= 0) & (row < rows)
+        left = (spot >= block) & (spot < 2 * block) & inside
+        right = (spot >= 2 * block) & (spot < 3 * block) & inside
+        from_left = roll(held["partial"][0:CH], block + 2)
+        from_right = roll(held["partial"][2 * CH : 3 * CH], block + 2)
+        sums = jnp.where(left, from_left, jnp.where(right, from_right, 0.0))
+        high = sums.astype(BF16)
+        held["sums"] = jnp.concatenate([high, (sums - high.astype(F32)).astype(BF16)], axis=1)
 
     def taps_of(slices):
         total = None
@@ -506,27 +532,31 @@
             total = product if total is None else total + product
         return total
 
-    partial = taps_of([roll(active, -tap) for tap in range(3)])
-    from_left, from_right = partial[0:CH], partial[2 * CH : 3 * CH]
+    wait = lambda: None
+    staggered(
+        pairs, first, activate,
+        between=(edge_first, wait, edge_activate, wait, edge_second, wait, edge_spread),
+    )
     half = rows // 2
 
     def second(step, _):
-        return taps_of(
+        product = taps_of(
             [
                 jnp.concatenate([hidden[step + tap], hidden[step + half + tap]], axis=1)
                 for tap in range(3)
             ]
         )
-
-    def last(step, product):
+        return product, spread(held["sums"], places, step + 2, step + half + 2)
+
+    def last(step, products):
+        product, entries = products
         news = []
         for offset in range(2):
             row = step + offset * half
             sums = product[:, offset * 128 : (offset + 1) * 128]
-            entry = roll(from_left, -row)[:, :128]
-            total = sums[CH : 2 * CH] + jnp.where(lane == 0, entry, roll(sums[0:CH], 1))
-            entry = roll(from_right, 127 - block - row)[:, :128]
-            total = total + jnp.where(lane == 127, entry, roll(sums[2 * CH : 3 * CH], -1))
+            total = sums[CH : 2 * CH] + entries[:, offset * 128 : (offset + 1) * 128]
+            total = total + jnp.where(lane == 0, 0.0, roll(sums[0:CH], 1))
+            total = total + jnp.where(lane == 127, 0.0, roll(sums[2 * CH : 3 * CH], -1))
             update = total * (0.5 * wet[row : row + 1, :].astype(F32))
             news.append(state[row].astype(F32) + update)
         out(step, *news)
@@ -641,8 +671,9 @@
     part_x, fields_x, rolled, edges, plan_x, air_in, first, second, atm_out = take(9)
     if not opening:
         (plan_e,) = take(1)
+    (places,) = take(1)
     if not closing:
-        surface, places = take(2)
+        (surface,) = take(1)
     (out,) = take(1)
     if not closing:
         fields, new_edges, one, two = take(4)
@@ -734,7 +765,7 @@
         joined = [get_edges(ref, 0, d) for ref in (from_left, from_right)]
         sea(
             state, rolled, get_edges(edges, 0, d), *joined, put, forcing_x, forcing_y,
-            first, second, wet, at_top, at_bottom, stack, hidden, side, d,
+            first, second, wet, at_top, at_bottom, stack, hidden, side, places, d,
         )
         close()
 
@@ -861,7 +892,7 @@
     state, planes, sides, places, fields, edges, one, two = call(
         functools.partial(start_kernel, d),
         (),
-        [state_shape, shape(2 * NK, rows, 128), shape(rows, 128), shape(rows * 128, d.edge)]
+        [state_shape, shape(2 * NK, rows, 128), shape(rows, 128), shape((rows + 4) * 128, d.edge)]
         + emitted[:2]
         + [shape(d.strip + 32, 128)] * 2,
         [raw, pltpu.VMEM((2 * NK * rows, 128), F32), turned],
@@ -898,7 +929,7 @@
     weights = (air_in, first, second, atm_out)
     state, fields, edges, one, two, plan_e = call(
         functools.partial(step_kernel, d, True, False),
-        (state, land_mask, *horizontal, *shared, edges, plan_x, *weights, surface_proj, places),
+        (state, land_mask, *horizontal, *shared, edges, plan_x, *weights, places, surface_proj),
         [state_shape] + emitted + [shape(2 * d.tall, 128, dtype=F32)],
         scratch + [raw, pltpu.VMEM(plan.shape, F32)],
         "first_step",
@@ -914,7 +945,7 @@
     )
     (state,) = call(
         functools.partial(step_kernel, d, False, True),
-        (state, land_mask, *horizontal, *shared, edges, plan_x, *weights, plan_e),
+        (state, land_mask, *horizontal, *shared, edges, plan_x, *weights, plan_e, places),
         [shape(CH, rows, 128)],
         scratch + [turned],
         "second_step",

time: 37.2 us -> 37.4 us (level)
  no operation moved by 1% of the time
where the time goes in v14:
time: 37.4 us; the launch traced here: 37.2 us
  starting transfers between devices  17.8 us (48%)
  Pallas kernels  11.5 us (31%)
  waiting for transfers between devices  7.63 us (20%)
    ppermute x14, starting transfers between devices, send(): return lax.ppermute(x, names, pairs)  17.8 us
    pallas_call x5, Pallas kernels, call(): pl.pallas_call(kernel, out_shape=outs, in_specs=[SMEM] + [VMEM] * len(ope...  11.5 us
    ppermute x14, waiting for transfers between devices, send(): return lax.ppermute(x, names, pairs)  7.63 us
  transfers between devices with their start and end apart: 14, of which 6 were waited for; matrix products, arithmetic and copies ran while one was open for 0% of the time, Pallas kernels for 9%

profile of v14, /device:TPU:0, one launch (start us, length us, event | category | flops | bytes accessed | tf_op | source)
XLA Modules:
  0.0 37.2 jit_solution(5178726941414052118)
XLA Ops:
  0.0 0.1 pad_add_fusion.flags.refs_0_
  0.1 2.2 %start.1 = (bf16[16,80,128]{2,1,0:T(8,128)(2,1)S(1)}, bf16[8,16,128]{2,1,0:T(8,128)(2,1)S(1)}, bf16[16,128]{1,0:T(8,128)(2,1)S(1)}, bf16[2560,128]{1,0:T(8,128)(...) custom-call(s32[4]{0:T(128)S(1)} %pad_add_fusion.flags.refs_0_, ...), custom_call_target="tpu_custom_call" | custom-call | tf_op jit(solution)/shard_map/start/pallas_call | solution.py:882
  2.3 0.5 %collective-permute-start = (bf16[272,128]{1,0:T(8,128)(2,1)S(1)}, bf16[272,128]{1,0:T(8,128)(2,1)S(1)}, u32[]{:S(2)}, u32[]{:S(2)}) collective-permute-start(bf16[272,128]{1,0:T(8,128)(2,1)S(1)} %get-tuple-element.39), channel_id=1, source_target_pairs={{0,1},{1,0},{2,3},{3,2},{4,5},{5,4},{6,7},{7,6},{8,9},{9,8},{10,11... | collective-permute-start | bytes 208904 | tf_op jit(solution)/shard_map/ppermute | solution.py:798
  2.8 0.1 collective-permute-start.1
  2.9 0.4 %collective-permute-start.4 = (bf16[5,16,128]{2,1,0:T(8,128)(2,1)S(1)}, bf16[5,16,128]{2,1,0:T(8,128)(2,1)S(1)}, u32[]{:S(2)}, u32[]{:S(2)}) collective-permute-start(bf16[5,16,128]{2,1,0:T(8,128)(2,1)S(1)} %get-tuple-element.41), channel_id=1, source_target_pairs={{0,1},{1,0},{2,3},{3,2},{4,24},{5,25},{6,26},{7,27},{8,20},{9,21},... | collective-permute-start | bytes 61448 | tf_op jit(solution)/shard_map/ppermute | solution.py:798
  3.3 6.1 %collective-permute-start.3 = (bf16[5,16,128]{2,1,0:T(8,128)(2,1)S(1)}, bf16[5,16,128]{2,1,0:T(8,128)(2,1)S(1)}, u32[]{:S(2)}, u32[]{:S(2)}) collective-permute-start(bf16[5,16,128]{2,1,0:T(8,128)(2,1)S(1)} %get-tuple-element.41), channel_id=1, source_target_pairs={{0,20},{1,21},{2,22},{3,23},{4,16},{5,17},{6,18},{7,19},{8,28},{9,... | collective-permute-start | bytes 61448 | tf_op jit(solution)/shard_map/ppermute | solution.py:798
  9.5 1.5 %collective-permute-start.2 = (bf16[5,16,128]{2,1,0:T(8,128)(2,1)S(1)}, bf16[5,16,128]{2,1,0:T(8,128)(2,1)S(1)}, u32[]{:S(2)}, u32[]{:S(2)}) collective-permute-start(bf16[5,16,128]{2,1,0:T(8,128)(2,1)S(1)} %get-tuple-element.41), channel_id=1, source_target_pairs={{0,16},{1,17},{2,18},{3,19},{4,20},{5,21},{6,22},{7,23},{8,24},{9,... | collective-permute-start | bytes 61448 | tf_op jit(solution)/shard_map/ppermute | solution.py:798
  11.0 0.3 collective-permute-done.3.refs_2_
  11.2 2.0 %collective-permute-done.2.refs_3_ = bf16[5,16,128]{2,1,0:T(8,128)(2,1)S(1)} collective-permute-done((bf16[5,16,128]{2,1,0:T(8,128)(2,1)S(1)}, bf16[5,16,128]{2,1,0:T(8,128)(2,1)S(1)}, u32[]{:S(2)}, u32[]{:S(2)}) %collective-permute-start.2) | collective-permute-done | bytes 20512 | tf_op jit(solution)/shard_map/ppermute | solution.py:798
  13.4 0.5 %collective-permute-start.5 = (bf16[176,128]{1,0:T(8,128)(2,1)S(1)}, bf16[176,128]{1,0:T(8,128)(2,1)S(1)}, u32[]{:S(2)}, u32[]{:S(2)}) collective-permute-start(bf16[176,128]{1,0:T(8,128)(2,1)S(1)} %constant_dynamic-update-slice_fusion), channel_id=1, source_target_pairs={{0,1},{1,2},{2,3},{3,0},{4,5},{5,6},{6,7},{7,4},{8,9},{9,10},{10,1... | collective-permute-start | bytes 135176 | tf_op jit(solution)/shard_map/ppermute | solution.py:798
  13.9 1.9 %first_middle.1 = (f32[96,128]{1,0:T(8,128)S(1)}, f32[4,48,128]{2,1,0:T(8,128)S(1)}, bf16[20,240,128]{2,1,0:T(8,128)(2,1)S(1)}, f32[192,128]{1,0:T(8,128)S(1)}, ...) custom-call(s32[4]{0:T(128)S(1)} %pad_add_fusion.flags.refs_0_, ...), custom_call_target="tpu_custom_call" | custom-call | tf_op jit(solution)/shard_map/first_middle/pallas_call | solution.py:882
  15.8 1.6 %collective-permute-done.5.refs_3_ = bf16[176,128]{1,0:T(8,128)(2,1)S(1)} collective-permute-done((bf16[176,128]{1,0:T(8,128)(2,1)S(1)}, bf16[176,128]{1,0:T(8,128)(2,1)S(1)}, u32[]{:S(2)}, u32[]{:S(2)}) %collective-permute-start.5) | collective-permute-done | bytes 45088 | tf_op jit(solution)/shard_map/ppermute | solution.py:798
  17.4 2.7 %first_step.1 = (bf16[16,80,128]{2,1,0:T(8,128)(2,1)S(1)}, bf16[5,16,128]{2,1,0:T(8,128)(2,1)S(1)}, bf16[80,128]{1,0:T(8,128)(2,1)S(1)}, bf16[240,128]{1,0:T(8,1...) custom-call(s32[4]{0:T(128)S(1)} %pad_add_fusion.flags.refs_0_, ...), custom_call_target="tpu_custom_call" | custom-call | tf_op jit(solution)/shard_map/first_step/pallas_call | solution.py:882
  20.1 0.2 collective-permute-start.7
  20.3 0.4 %collective-permute-start.8 = (bf16[240,128]{1,0:T(8,128)(2,1)S(1)}, bf16[240,128]{1,0:T(8,128)(2,1)S(1)}, u32[]{:S(2)}, u32[]{:S(2)}) collective-permute-start(bf16[240,128]{1,0:T(8,128)(2,1)S(1)} %get-tuple-element.59), channel_id=1, source_target_pairs={{0,1},{1,0},{2,3},{3,2},{4,5},{5,4},{6,7},{7,6},{8,9},{9,8},{10,11... | collective-permute-start | bytes 184328 | tf_op jit(solution)/shard_map/ppermute | solution.py:798
  20.7 0.1 collective-permute-start.11
  20.8 5.9 %collective-permute-start.10 = (bf16[5,16,128]{2,1,0:T(8,128)(2,1)S(1)}, bf16[5,16,128]{2,1,0:T(8,128)(2,1)S(1)}, u32[]{:S(2)}, u32[]{:S(2)}) collective-permute-start(bf16[5,16,128]{2,1,0:T(8,128)(2,1)S(1)} %get-tuple-element.60), channel_id=1, source_target_pairs={{0,20},{1,21},{2,22},{3,23},{4,16},{5,17},{6,18},{7,19},{8,28},{9,... | collective-permute-start | bytes 61448 | tf_op jit(solution)/shard_map/ppermute | solution.py:798
  26.7 1.5 %collective-permute-start.9 = (bf16[5,16,128]{2,1,0:T(8,128)(2,1)S(1)}, bf16[5,16,128]{2,1,0:T(8,128)(2,1)S(1)}, u32[]{:S(2)}, u32[]{:S(2)}) collective-permute-start(bf16[5,16,128]{2,1,0:T(8,128)(2,1)S(1)} %get-tuple-element.60), channel_id=1, source_target_pairs={{0,16},{1,17},{2,18},{3,19},{4,20},{5,21},{6,22},{7,23},{8,24},{9,... | collective-permute-start | bytes 61448 | tf_op jit(solution)/shard_map/ppermute | solution.py:798
  28.1 0.3 collective-permute-done.10.refs_2_
  28.4 2.0 %collective-permute-done.9.refs_3_ = bf16[5,16,128]{2,1,0:T(8,128)(2,1)S(1)} collective-permute-done((bf16[5,16,128]{2,1,0:T(8,128)(2,1)S(1)}, bf16[5,16,128]{2,1,0:T(8,128)(2,1)S(1)}, u32[]{:S(2)}, u32[]{:S(2)}) %collective-permute-start.9) | collective-permute-done | bytes 20512 | tf_op jit(solution)/shard_map/ppermute | solution.py:798
  30.5 0.5 %collective-permute-start.12 = (bf16[128,128]{1,0:T(8,128)(2,1)S(1)}, bf16[128,128]{1,0:T(8,128)(2,1)S(1)}, u32[]{:S(2)}, u32[]{:S(2)}) collective-permute-start(bf16[128,128]{1,0:T(8,128)(2,1)S(1)} %pad_maximum_fusion), channel_id=1, source_target_pairs={{0,1},{1,2},{2,3},{3,0},{4,5},{5,6},{6,7},{7,4},{8,9},{9,10},{10,1... | collective-permute-start | bytes 98312 | tf_op jit(solution)/shard_map/ppermute | solution.py:798
  31.0 1.4 %second_middle.1 = (f32[96,128]{1,0:T(8,128)S(1)}, f32[4,48,128]{2,1,0:T(8,128)S(1)}, bf16[20,240,128]{2,1,0:T(8,128)(2,1)S(1)}) custom-call(s32[4]{0:T(128)S(1)} %pad_add_fusion.flags.refs_0_, bf16[16,80,128]{2,1,0:T(8,128)(2,1)S(1)} %get-tuple-element.56.refs_1_, bf16[5,16,128]{2,1,0:T(8,128)(2,1)S(1)} %collective-permute-done.10.refs_2_, ...), custom_call_target="tpu_custom_call" | custom-call | tf_op jit(solution)/shard_map/second_middle/pallas_call | solution.py:882
  32.4 1.5 %collective-permute-done.12.refs_3_ = bf16[128,128]{1,0:T(8,128)(2,1)S(1)} collective-permute-done((bf16[128,128]{1,0:T(8,128)(2,1)S(1)}, bf16[128,128]{1,0:T(8,128)(2,1)S(1)}, u32[]{:S(2)}, u32[]{:S(2)}) %collective-permute-start.12) | collective-permute-done | bytes 32800 | tf_op jit(solution)/shard_map/ppermute | solution.py:798
  33.9 3.3 %second_step.1 = bf16[80,16,128]{2,1,0:T(8,128)(2,1)} custom-call(s32[4]{0:T(128)S(1)} %pad_add_fusion.flags.refs_0_, bf16[16,80,128]{2,1,0:T(8,128)(2,1)S(1)} %get-tuple-element.56.refs_1_, s32[16,128]{1,0:T(8,128)S(1)} %copy-done.1, bf16[128,128]{1,0:T(8,128)(2,1)S(1)} %collective-permute-done.12.refs_3_, ...), custom_call_target="tpu_custom_call" | custom-call | tf_op jit(solution)/shard_map/second_step/pallas_call | solution.py:882
  (28 shorter events, 0.2 us)
Async XLA Ops:
  0.0 17.4 %copy-start.1 = (s32[16,128]{1,0:T(8,128)S(1)}, s32[16,128]{1,0:T(8,128)}, u32[]{:S(2)}) copy-start(s32[16,128]{1,0:T(8,128)} %refs_2_.3) | copy-start | bytes 24580
  0.0 17.4 %copy-start.2 = (f32[2,4,80]{2,1,0:T(4,128)S(1)}, f32[2,4,80]{2,1,0:T(4,128)}, u32[]{:S(2)}) copy-start(f32[2,4,80]{2,1,0:T(4,128)} %refs_15_.1) | copy-start | bytes 7684
  0.0 17.4 %copy-start = (bf16[80,384]{1,0:T(8,128)(2,1)S(1)}, bf16[80,384]{1,0:T(8,128)(2,1)}, u32[]{:S(2)}) copy-start(bf16[80,384]{1,0:T(8,128)(2,1)} %refs_13_.3) | copy-start | bytes 184324
  2.3 8.7 %collective-permute-start = (bf16[272,128]{1,0:T(8,128)(2,1)S(1)}, bf16[272,128]{1,0:T(8,128)(2,1)S(1)}, u32[]{:S(2)}, u32[]{:S(2)}) collective-permute-start(bf16[272,128]{1,0:T(8,128)(2,1)S(1)} %get-tuple-element.39), channel_id=1, source_target_pairs={{0,1},{1,0},{2,3},{3,2},{4,5},{5,4},{6,7},{7,6},{8,9},{9,8},{10,11... | collective-permute-start | bytes 208904 | tf_op jit(solution)/shard_map/ppermute | solution.py:798
  2.8 8.1 %collective-permute-start.1 = (bf16[272,128]{1,0:T(8,128)(2,1)S(1)}, bf16[272,128]{1,0:T(8,128)(2,1)S(1)}, u32[]{:S(2)}, u32[]{:S(2)}) collective-permute-start(bf16[272,128]{1,0:T(8,128)(2,1)S(1)} %get-tuple-element.40), channel_id=1, source_target_pairs={{0,1},{1,0},{2,3},{3,2},{4,5},{5,4},{6,7},{7,6},{8,9},{9,8},{10,11... | collective-permute-start | bytes 208904 | tf_op jit(solution)/shard_map/ppermute | solution.py:798
  2.9 8.1 %collective-permute-start.4 = (bf16[5,16,128]{2,1,0:T(8,128)(2,1)S(1)}, bf16[5,16,128]{2,1,0:T(8,128)(2,1)S(1)}, u32[]{:S(2)}, u32[]{:S(2)}) collective-permute-start(bf16[5,16,128]{2,1,0:T(8,128)(2,1)S(1)} %get-tuple-element.41), channel_id=1, source_target_pairs={{0,1},{1,0},{2,3},{3,2},{4,24},{5,25},{6,26},{7,27},{8,20},{9,21},... | collective-permute-start | bytes 61448 | tf_op jit(solution)/shard_map/ppermute | solution.py:798
  3.3 7.9 %collective-permute-start.3 = (bf16[5,16,128]{2,1,0:T(8,128)(2,1)S(1)}, bf16[5,16,128]{2,1,0:T(8,128)(2,1)S(1)}, u32[]{:S(2)}, u32[]{:S(2)}) collective-permute-start(bf16[5,16,128]{2,1,0:T(8,128)(2,1)S(1)} %get-tuple-element.41), channel_id=1, source_target_pairs={{0,20},{1,21},{2,22},{3,23},{4,16},{5,17},{6,18},{7,19},{8,28},{9,... | collective-permute-start | bytes 61448 | tf_op jit(solution)/shard_map/ppermute | solution.py:798
  9.5 3.8 %collective-permute-start.2 = (bf16[5,16,128]{2,1,0:T(8,128)(2,1)S(1)}, bf16[5,16,128]{2,1,0:T(8,128)(2,1)S(1)}, u32[]{:S(2)}, u32[]{:S(2)}) collective-permute-start(bf16[5,16,128]{2,1,0:T(8,128)(2,1)S(1)} %get-tuple-element.41), channel_id=1, source_target_pairs={{0,16},{1,17},{2,18},{3,19},{4,20},{5,21},{6,22},{7,23},{8,24},{9,... | collective-permute-start | bytes 61448 | tf_op jit(solution)/shard_map/ppermute | solution.py:798
  13.3 2.5 %collective-permute-start.6 = (bf16[176,128]{1,0:T(8,128)(2,1)S(1)}, bf16[176,128]{1,0:T(8,128)(2,1)S(1)}, u32[]{:S(2)}, u32[]{:S(2)}) collective-permute-start(bf16[176,128]{1,0:T(8,128)(2,1)S(1)} %constant_dynamic-update-slice_fusion), channel_id=1, source_target_pairs={{0,3},{1,0},{2,1},{3,2},{4,7},{5,4},{6,5},{7,6},{8,11},{9,8},{10,9... | collective-permute-start | bytes 135176 | tf_op jit(solution)/shard_map/ppermute | solution.py:798
  13.4 4.0 %collective-permute-start.5 = (bf16[176,128]{1,0:T(8,128)(2,1)S(1)}, bf16[176,128]{1,0:T(8,128)(2,1)S(1)}, u32[]{:S(2)}, u32[]{:S(2)}) collective-permute-start(bf16[176,128]{1,0:T(8,128)(2,1)S(1)} %constant_dynamic-update-slice_fusion), channel_id=1, source_target_pairs={{0,1},{1,2},{2,3},{3,0},{4,5},{5,6},{6,7},{7,4},{8,9},{9,10},{10,1... | collective-permute-start | bytes 135176 | tf_op jit(solution)/shard_map/ppermute | solution.py:798
  20.1 8.0 %collective-permute-start.7 = (bf16[240,128]{1,0:T(8,128)(2,1)S(1)}, bf16[240,128]{1,0:T(8,128)(2,1)S(1)}, u32[]{:S(2)}, u32[]{:S(2)}) collective-permute-start(bf16[240,128]{1,0:T(8,128)(2,1)S(1)} %get-tuple-element.58), channel_id=1, source_target_pairs={{0,1},{1,0},{2,3},{3,2},{4,5},{5,4},{6,7},{7,6},{8,9},{9,8},{10,11... | collective-permute-start | bytes 184328 | tf_op jit(solution)/shard_map/ppermute | solution.py:798
  20.3 7.9 %collective-permute-start.8 = (bf16[240,128]{1,0:T(8,128)(2,1)S(1)}, bf16[240,128]{1,0:T(8,128)(2,1)S(1)}, u32[]{:S(2)}, u32[]{:S(2)}) collective-permute-start(bf16[240,128]{1,0:T(8,128)(2,1)S(1)} %get-tuple-element.59), channel_id=1, source_target_pairs={{0,1},{1,0},{2,3},{3,2},{4,5},{5,4},{6,7},{7,6},{8,9},{9,8},{10,11... | collective-permute-start | bytes 184328 | tf_op jit(solution)/shard_map/ppermute | solution.py:798
  20.7 7.5 %collective-permute-start.11 = (bf16[5,16,128]{2,1,0:T(8,128)(2,1)S(1)}, bf16[5,16,128]{2,1,0:T(8,128)(2,1)S(1)}, u32[]{:S(2)}, u32[]{:S(2)}) collective-permute-start(bf16[5,16,128]{2,1,0:T(8,128)(2,1)S(1)} %get-tuple-element.60), channel_id=1, source_target_pairs={{0,1},{1,0},{2,3},{3,2},{4,24},{5,25},{6,26},{7,27},{8,20},{9,21},... | collective-permute-start | bytes 61448 | tf_op jit(solution)/shard_map/ppermute | solution.py:798
  20.8 7.6 %collective-permute-start.10 = (bf16[5,16,128]{2,1,0:T(8,128)(2,1)S(1)}, bf16[5,16,128]{2,1,0:T(8,128)(2,1)S(1)}, u32[]{:S(2)}, u32[]{:S(2)}) collective-permute-start(bf16[5,16,128]{2,1,0:T(8,128)(2,1)S(1)} %get-tuple-element.60), channel_id=1, source_target_pairs={{0,20},{1,21},{2,22},{3,23},{4,16},{5,17},{6,18},{7,19},{8,28},{9,... | collective-permute-start | bytes 61448 | tf_op jit(solution)/shard_map/ppermute | solution.py:798
  26.7 3.8 %collective-permute-start.9 = (bf16[5,16,128]{2,1,0:T(8,128)(2,1)S(1)}, bf16[5,16,128]{2,1,0:T(8,128)(2,1)S(1)}, u32[]{:S(2)}, u32[]{:S(2)}) collective-permute-start(bf16[5,16,128]{2,1,0:T(8,128)(2,1)S(1)} %get-tuple-element.60), channel_id=1, source_target_pairs={{0,16},{1,17},{2,18},{3,19},{4,20},{5,21},{6,22},{7,23},{8,24},{9,... | collective-permute-start | bytes 61448 | tf_op jit(solution)/shard_map/ppermute | solution.py:798
  30.5 2.0 %collective-permute-start.13 = (bf16[128,128]{1,0:T(8,128)(2,1)S(1)}, bf16[128,128]{1,0:T(8,128)(2,1)S(1)}, u32[]{:S(2)}, u32[]{:S(2)}) collective-permute-start(bf16[128,128]{1,0:T(8,128)(2,1)S(1)} %pad_maximum_fusion), channel_id=1, source_target_pairs={{0,3},{1,0},{2,1},{3,2},{4,7},{5,4},{6,5},{7,6},{8,11},{9,8},{10,9... | collective-permute-start | bytes 98312 | tf_op jit(solution)/shard_map/ppermute | solution.py:798
  30.5 3.4 %collective-permute-start.12 = (bf16[128,128]{1,0:T(8,128)(2,1)S(1)}, bf16[128,128]{1,0:T(8,128)(2,1)S(1)}, u32[]{:S(2)}, u32[]{:S(2)}) collective-permute-start(bf16[128,128]{1,0:T(8,128)(2,1)S(1)} %pad_maximum_fusion), channel_id=1, source_target_pairs={{0,1},{1,2},{2,3},{3,0},{4,5},{5,6},{6,7},{7,4},{8,9},{9,10},{10,1... | collective-permute-start | bytes 98312 | tf_op jit(solution)/shard_map/ppermute | solution.py:798

commit v15 on v13

--- a/solution.py
+++ b/solution.py
@@ -782,11 +782,17 @@
 
 def exchange(fields, own_edges, one, two, sides, d):
     rows = d.rows
+    scale = jnp.where(lax.axis_index("grp") > 1, 0, 1).astype(BF16)
     from_one = swap_rows(one, 0, False)
-    from_two = swap_rows(two, 1, False)
     field_one = swap_rows(fields, 0, True)
+    from_two = swap_rows(two * scale, 1, False)
+    fields = fields * scale
     field_two = swap_rows(fields, 1, True)
     beside = send(fields, lambda g, i, j: (1 - g, i, j))
+    field_one, from_one = lax.optimization_barrier((field_one, from_one))
+    from_two, field_one = lax.optimization_barrier((from_two, field_one))
+    field_two, from_two = lax.optimization_barrier((field_two, from_two))
+    beside, field_two = lax.optimization_barrier((beside, field_two))
     lat, count = lax.axis_index("lat"), lax.axis_size("lat")
     odd = lat % 2 == 1
     edges = own_edges
@@ -794,9 +800,6 @@
         other = ((lat + turn) ^ 1) - turn
         there = (other >= 0) & (other < count)
         edges = edges + jnp.where(there, ref[2 * CH : d.strip], 0)
-    edges, beside, field_one, field_two = lax.optimization_barrier(
-        (edges, beside, field_one, field_two)
-    )
     outer = [field_one[NS], field_two[NS]]
     if rows != 16:
         outer = [

time: 37.2 us -> 34.4 us (0.925)
  starting transfers between devices: 17.6 us -> 14.2 us
  waiting for transfers between devices: 7.63 us -> 8.2 us
    ppermute x14, starting transfers between devices: 17.6 us -> 14.2 us  [send(): return lax.ppermute(x, names, pairs)]
    ppermute x14, waiting for transfers between devices: 7.63 us -> 8.2 us  [send(): return lax.ppermute(x, names, pairs)]
  transfers between devices with their start and end apart: 14 -> 14, of which waited for: 6 -> 5; matrix products, arithmetic and copies ran while one was open for 0% -> 0% of each run, Pallas kernels for 9% -> 10%
where the time goes in v15:
time: 34.4 us; the launch traced here: 34.2 us
  starting transfers between devices  14.2 us (41%)
  Pallas kernels  11.5 us (33%)
  waiting for transfers between devices  8.2 us (24%)
    ppermute x14, starting transfers between devices, send(): return lax.ppermute(x, names, pairs)  14.2 us
    pallas_call x5, Pallas kernels, call(): pl.pallas_call(kernel, out_shape=outs, in_specs=[SMEM] + [VMEM] * len(ope...  11.5 us
    ppermute x14, waiting for transfers between devices, send(): return lax.ppermute(x, names, pairs)  8.2 us
  transfers between devices with their start and end apart: 14, of which 5 were waited for; matrix products, arithmetic and copies ran while one was open for 0% of the time, Pallas kernels for 10%

profile of v15, /device:TPU:0, one launch (start us, length us, event | category | flops | bytes accessed | tf_op | source)
XLA Modules:
  0.0 34.2 jit_solution(16984541425198244177)
XLA Ops:
  0.0 0.1 pad_add_fusion.flags.refs_0_
  0.1 2.2 %start.1 = (bf16[16,80,128]{2,1,0:T(8,128)(2,1)S(1)}, bf16[8,16,128]{2,1,0:T(8,128)(2,1)S(1)}, bf16[16,128]{1,0:T(8,128)(2,1)S(1)}, bf16[2048,128]{1,0:T(8,128)(...) custom-call(s32[4]{0:T(128)S(1)} %pad_add_fusion.flags.refs_0_, ...), custom_call_target="tpu_custom_call" | custom-call | tf_op jit(solution)/shard_map/start/pallas_call | solution.py:854
  2.3 4.0 %collective-permute-start = (bf16[5,16,128]{2,1,0:T(8,128)(2,1)S(1)}, bf16[5,16,128]{2,1,0:T(8,128)(2,1)S(1)}, u32[]{:S(2)}, u32[]{:S(2)}) collective-permute-start(bf16[5,16,128]{2,1,0:T(8,128)(2,1)S(1)} %get-tuple-element.47), channel_id=1, source_target_pairs={{0,20},{1,21},{2,22},{3,23},{4,16},{5,17},{6,18},{7,19},{8,28},{9,... | collective-permute-start | bytes 61448 | tf_op jit(solution)/shard_map/ppermute | solution.py:767
  6.3 0.1 collective-permute-start.3
  6.4 0.5 %collective-permute-start.1 = (bf16[272,128]{1,0:T(8,128)(2,1)S(1)}, bf16[272,128]{1,0:T(8,128)(2,1)S(1)}, u32[]{:S(2)}, u32[]{:S(2)}) collective-permute-start(bf16[272,128]{1,0:T(8,128)(2,1)S(1)} %get-tuple-element.48), channel_id=1, source_target_pairs={{0,1},{1,0},{2,3},{3,2},{4,5},{5,4},{6,7},{7,6},{8,9},{9,8},{10,11... | collective-permute-start | bytes 208904 | tf_op jit(solution)/shard_map/ppermute | solution.py:767
  6.9 0.1 collective-permute-start.2
  7.0 3.2 %collective-permute-start.4 = (bf16[5,16,128]{2,1,0:T(8,128)(2,1)S(1)}, bf16[5,16,128]{2,1,0:T(8,128)(2,1)S(1)}, u32[]{:S(2)}, u32[]{:S(2)}) collective-permute-start(bf16[5,16,128]{2,1,0:T(8,128)(2,1)S(1)} %broadcast_multiply_fusion.3), channel_id=1, source_target_pairs={{0,16},{1,17},{2,18},{3,19},{4,20},{5,21},{6,22},{7,23},{8,24},{9,... | collective-permute-start | bytes 61448 | tf_op jit(solution)/shard_map/ppermute | solution.py:767
  10.2 0.0 collective-permute-done.3.refs_6_
  10.2 1.7 %collective-permute-done.4.refs_3_ = bf16[5,16,128]{2,1,0:T(8,128)(2,1)S(1)} collective-permute-done((bf16[5,16,128]{2,1,0:T(8,128)(2,1)S(1)}, bf16[5,16,128]{2,1,0:T(8,128)(2,1)S(1)}, u32[]{:S(2)}, u32[]{:S(2)}) %collective-permute-start.4) | collective-permute-done | bytes 20512 | tf_op jit(solution)/shard_map/ppermute | solution.py:767
  12.0 0.7 %collective-permute-start.6 = (bf16[176,128]{1,0:T(8,128)(2,1)S(1)}, bf16[176,128]{1,0:T(8,128)(2,1)S(1)}, u32[]{:S(2)}, u32[]{:S(2)}) collective-permute-start(bf16[176,128]{1,0:T(8,128)(2,1)S(1)} %constant_dynamic-update-slice_fusion), channel_id=1, source_target_pairs={{0,3},{1,0},{2,1},{3,2},{4,7},{5,4},{6,5},{7,6},{8,11},{9,8},{10,9... | collective-permute-start | bytes 135176 | tf_op jit(solution)/shard_map/ppermute | solution.py:767
  12.8 1.9 %first_middle.1 = (f32[96,128]{1,0:T(8,128)S(1)}, f32[4,48,128]{2,1,0:T(8,128)S(1)}, bf16[20,240,128]{2,1,0:T(8,128)(2,1)S(1)}, f32[192,128]{1,0:T(8,128)S(1)}, ...) custom-call(s32[4]{0:T(128)S(1)} %pad_add_fusion.flags.refs_0_, ...), custom_call_target="tpu_custom_call" | custom-call | tf_op jit(solution)/shard_map/first_middle/pallas_call | solution.py:854
  14.7 1.5 %collective-permute-done.5.refs_3_ = bf16[176,128]{1,0:T(8,128)(2,1)S(1)} collective-permute-done((bf16[176,128]{1,0:T(8,128)(2,1)S(1)}, bf16[176,128]{1,0:T(8,128)(2,1)S(1)}, u32[]{:S(2)}, u32[]{:S(2)}) %collective-permute-start.5) | collective-permute-done | bytes 45088 | tf_op jit(solution)/shard_map/ppermute | solution.py:767
  16.2 2.7 %first_step.1 = (bf16[16,80,128]{2,1,0:T(8,128)(2,1)S(1)}, bf16[5,16,128]{2,1,0:T(8,128)(2,1)S(1)}, bf16[80,128]{1,0:T(8,128)(2,1)S(1)}, bf16[240,128]{1,0:T(8,1...) custom-call(s32[4]{0:T(128)S(1)} %pad_add_fusion.flags.refs_0_, ...), custom_call_target="tpu_custom_call" | custom-call | tf_op jit(solution)/shard_map/first_step/pallas_call | solution.py:854
  19.0 4.1 %collective-permute-start.7 = (bf16[5,16,128]{2,1,0:T(8,128)(2,1)S(1)}, bf16[5,16,128]{2,1,0:T(8,128)(2,1)S(1)}, u32[]{:S(2)}, u32[]{:S(2)}) collective-permute-start(bf16[5,16,128]{2,1,0:T(8,128)(2,1)S(1)} %get-tuple-element.70), channel_id=1, source_target_pairs={{0,20},{1,21},{2,22},{3,23},{4,16},{5,17},{6,18},{7,19},{8,28},{9,... | collective-permute-start | bytes 61448 | tf_op jit(solution)/shard_map/ppermute | solution.py:767
  23.1 0.5 %collective-permute-start.8 = (bf16[240,128]{1,0:T(8,128)(2,1)S(1)}, bf16[240,128]{1,0:T(8,128)(2,1)S(1)}, u32[]{:S(2)}, u32[]{:S(2)}) collective-permute-start(bf16[240,128]{1,0:T(8,128)(2,1)S(1)} %get-tuple-element.71), channel_id=1, source_target_pairs={{0,1},{1,0},{2,3},{3,2},{4,5},{5,4},{6,7},{7,6},{8,9},{9,8},{10,11... | collective-permute-start | bytes 184328 | tf_op jit(solution)/shard_map/ppermute | solution.py:767
  23.6 0.1 collective-permute-start.9
  23.7 0.3 collective-permute-start.11
  24.0 0.8 %collective-permute-done.7.refs_2_ = bf16[5,16,128]{2,1,0:T(8,128)(2,1)S(1)} collective-permute-done((bf16[5,16,128]{2,1,0:T(8,128)(2,1)S(1)}, bf16[5,16,128]{2,1,0:T(8,128)(2,1)S(1)}, u32[]{:S(2)}, u32[]{:S(2)}) %collective-permute-start.7) | collective-permute-done | bytes 20512 | tf_op jit(solution)/shard_map/ppermute | solution.py:767
  24.9 2.6 %collective-permute-done.11.refs_3_ = bf16[5,16,128]{2,1,0:T(8,128)(2,1)S(1)} collective-permute-done((bf16[5,16,128]{2,1,0:T(8,128)(2,1)S(1)}, bf16[5,16,128]{2,1,0:T(8,128)(2,1)S(1)}, u32[]{:S(2)}, u32[]{:S(2)}) %collective-permute-start.11) | collective-permute-done | bytes 20512 | tf_op jit(solution)/shard_map/ppermute | solution.py:767
  27.5 0.1 collective-permute-start.13
  27.6 0.5 %collective-permute-start.12 = (bf16[128,128]{1,0:T(8,128)(2,1)S(1)}, bf16[128,128]{1,0:T(8,128)(2,1)S(1)}, u32[]{:S(2)}, u32[]{:S(2)}) collective-permute-start(bf16[128,128]{1,0:T(8,128)(2,1)S(1)} %pad_maximum_fusion), channel_id=1, source_target_pairs={{0,1},{1,2},{2,3},{3,0},{4,5},{5,6},{6,7},{7,4},{8,9},{9,10},{10,1... | collective-permute-start | bytes 98312 | tf_op jit(solution)/shard_map/ppermute | solution.py:767
  28.1 1.4 %second_middle.1 = (f32[96,128]{1,0:T(8,128)S(1)}, f32[4,48,128]{2,1,0:T(8,128)S(1)}, bf16[20,240,128]{2,1,0:T(8,128)(2,1)S(1)}) custom-call(s32[4]{0:T(128)S(1)} %pad_add_fusion.flags.refs_0_, bf16[16,80,128]{2,1,0:T(8,128)(2,1)S(1)} %get-tuple-element.68.refs_1_, bf16[5,16,128]{2,1,0:T(8,128)(2,1)S(1)} %collective-permute-done.7.refs_2_, ...), custom_call_target="tpu_custom_call" | custom-call | tf_op jit(solution)/shard_map/second_middle/pallas_call | solution.py:854
  29.5 1.5 %collective-permute-done.12.refs_3_ = bf16[128,128]{1,0:T(8,128)(2,1)S(1)} collective-permute-done((bf16[128,128]{1,0:T(8,128)(2,1)S(1)}, bf16[128,128]{1,0:T(8,128)(2,1)S(1)}, u32[]{:S(2)}, u32[]{:S(2)}) %collective-permute-start.12) | collective-permute-done | bytes 32800 | tf_op jit(solution)/shard_map/ppermute | solution.py:767
  30.9 3.3 %second_step.1 = bf16[80,16,128]{2,1,0:T(8,128)(2,1)} custom-call(s32[4]{0:T(128)S(1)} %pad_add_fusion.flags.refs_0_, bf16[16,80,128]{2,1,0:T(8,128)(2,1)S(1)} %get-tuple-element.68.refs_1_, s32[16,128]{1,0:T(8,128)S(1)} %copy-done.1, bf16[128,128]{1,0:T(8,128)(2,1)S(1)} %collective-permute-done.12.refs_3_, ...), custom_call_target="tpu_custom_call" | custom-call | tf_op jit(solution)/shard_map/second_step/pallas_call | solution.py:854
  (31 shorter events, 0.2 us)
Async XLA Ops:
  0.0 16.2 %copy-start.1 = (s32[16,128]{1,0:T(8,128)S(1)}, s32[16,128]{1,0:T(8,128)}, u32[]{:S(2)}) copy-start(s32[16,128]{1,0:T(8,128)} %refs_2_.3) | copy-start | bytes 24580
  0.0 16.2 %copy-start.2 = (f32[2,4,80]{2,1,0:T(4,128)S(1)}, f32[2,4,80]{2,1,0:T(4,128)}, u32[]{:S(2)}) copy-start(f32[2,4,80]{2,1,0:T(4,128)} %refs_14_.1) | copy-start | bytes 7684
  0.0 16.2 %copy-start = (bf16[80,384]{1,0:T(8,128)(2,1)S(1)}, bf16[80,384]{1,0:T(8,128)(2,1)}, u32[]{:S(2)}) copy-start(bf16[80,384]{1,0:T(8,128)(2,1)} %refs_13_.3) | copy-start | bytes 184324
  2.3 7.9 %collective-permute-start = (bf16[5,16,128]{2,1,0:T(8,128)(2,1)S(1)}, bf16[5,16,128]{2,1,0:T(8,128)(2,1)S(1)}, u32[]{:S(2)}, u32[]{:S(2)}) collective-permute-start(bf16[5,16,128]{2,1,0:T(8,128)(2,1)S(1)} %get-tuple-element.47), channel_id=1, source_target_pairs={{0,20},{1,21},{2,22},{3,23},{4,16},{5,17},{6,18},{7,19},{8,28},{9,... | collective-permute-start | bytes 61448 | tf_op jit(solution)/shard_map/ppermute | solution.py:767
  6.3 3.8 %collective-permute-start.3 = (bf16[272,128]{1,0:T(8,128)(2,1)S(1)}, bf16[272,128]{1,0:T(8,128)(2,1)S(1)}, u32[]{:S(2)}, u32[]{:S(2)}) collective-permute-start(bf16[272,128]{1,0:T(8,128)(2,1)S(1)} %broadcast_multiply_fusion), channel_id=1, source_target_pairs={{0,1},{1,0},{2,3},{3,2},{4,5},{5,4},{6,7},{7,6},{8,9},{9,8},{10,11... | collective-permute-start | bytes 208904 | tf_op jit(solution)/shard_map/ppermute | solution.py:767
  6.4 3.7 %collective-permute-start.1 = (bf16[272,128]{1,0:T(8,128)(2,1)S(1)}, bf16[272,128]{1,0:T(8,128)(2,1)S(1)}, u32[]{:S(2)}, u32[]{:S(2)}) collective-permute-start(bf16[272,128]{1,0:T(8,128)(2,1)S(1)} %get-tuple-element.48), channel_id=1, source_target_pairs={{0,1},{1,0},{2,3},{3,2},{4,5},{5,4},{6,7},{7,6},{8,9},{9,8},{10,11... | collective-permute-start | bytes 208904 | tf_op jit(solution)/shard_map/ppermute | solution.py:767
  6.9 3.3 %collective-permute-start.2 = (bf16[5,16,128]{2,1,0:T(8,128)(2,1)S(1)}, bf16[5,16,128]{2,1,0:T(8,128)(2,1)S(1)}, u32[]{:S(2)}, u32[]{:S(2)}) collective-permute-start(bf16[5,16,128]{2,1,0:T(8,128)(2,1)S(1)} %broadcast_multiply_fusion.3), channel_id=1, source_target_pairs={{0,1},{1,0},{2,3},{3,2},{4,24},{5,25},{6,26},{7,27},{8,20},{9,21},... | collective-permute-start | bytes 61448 | tf_op jit(solution)/shard_map/ppermute | solution.py:767
  7.0 4.9 %collective-permute-start.4 = (bf16[5,16,128]{2,1,0:T(8,128)(2,1)S(1)}, bf16[5,16,128]{2,1,0:T(8,128)(2,1)S(1)}, u32[]{:S(2)}, u32[]{:S(2)}) collective-permute-start(bf16[5,16,128]{2,1,0:T(8,128)(2,1)S(1)} %broadcast_multiply_fusion.3), channel_id=1, source_target_pairs={{0,16},{1,17},{2,18},{3,19},{4,20},{5,21},{6,22},{7,23},{8,24},{9,... | collective-permute-start | bytes 61448 | tf_op jit(solution)/shard_map/ppermute | solution.py:767
  12.0 2.7 %collective-permute-start.6 = (bf16[176,128]{1,0:T(8,128)(2,1)S(1)}, bf16[176,128]{1,0:T(8,128)(2,1)S(1)}, u32[]{:S(2)}, u32[]{:S(2)}) collective-permute-start(bf16[176,128]{1,0:T(8,128)(2,1)S(1)} %constant_dynamic-update-slice_fusion), channel_id=1, source_target_pairs={{0,3},{1,0},{2,1},{3,2},{4,7},{5,4},{6,5},{7,6},{8,11},{9,8},{10,9... | collective-permute-start | bytes 135176 | tf_op jit(solution)/shard_map/ppermute | solution.py:767
  12.7 3.5 %collective-permute-start.5 = (bf16[176,128]{1,0:T(8,128)(2,1)S(1)}, bf16[176,128]{1,0:T(8,128)(2,1)S(1)}, u32[]{:S(2)}, u32[]{:S(2)}) collective-permute-start(bf16[176,128]{1,0:T(8,128)(2,1)S(1)} %constant_dynamic-update-slice_fusion), channel_id=1, source_target_pairs={{0,1},{1,2},{2,3},{3,0},{4,5},{5,6},{6,7},{7,4},{8,9},{9,10},{10,1... | collective-permute-start | bytes 135176 | tf_op jit(solution)/shard_map/ppermute | solution.py:767
  19.0 5.9 %collective-permute-start.7 = (bf16[5,16,128]{2,1,0:T(8,128)(2,1)S(1)}, bf16[5,16,128]{2,1,0:T(8,128)(2,1)S(1)}, u32[]{:S(2)}, u32[]{:S(2)}) collective-permute-start(bf16[5,16,128]{2,1,0:T(8,128)(2,1)S(1)} %get-tuple-element.70), channel_id=1, source_target_pairs={{0,20},{1,21},{2,22},{3,23},{4,16},{5,17},{6,18},{7,19},{8,28},{9,... | collective-permute-start | bytes 61448 | tf_op jit(solution)/shard_map/ppermute | solution.py:767
  23.1 1.8 %collective-permute-start.10 = (bf16[240,128]{1,0:T(8,128)(2,1)S(1)}, bf16[240,128]{1,0:T(8,128)(2,1)S(1)}, u32[]{:S(2)}, u32[]{:S(2)}) collective-permute-start(bf16[240,128]{1,0:T(8,128)(2,1)S(1)} %broadcast_multiply_fusion.1), channel_id=1, source_target_pairs={{0,1},{1,0},{2,3},{3,2},{4,5},{5,4},{6,7},{7,6},{8,9},{9,8},{10,11... | collective-permute-start | bytes 184328 | tf_op jit(solution)/shard_map/ppermute | solution.py:767
  23.1 1.8 %collective-permute-start.8 = (bf16[240,128]{1,0:T(8,128)(2,1)S(1)}, bf16[240,128]{1,0:T(8,128)(2,1)S(1)}, u32[]{:S(2)}, u32[]{:S(2)}) collective-permute-start(bf16[240,128]{1,0:T(8,128)(2,1)S(1)} %get-tuple-element.71), channel_id=1, source_target_pairs={{0,1},{1,0},{2,3},{3,2},{4,5},{5,4},{6,7},{7,6},{8,9},{9,8},{10,11... | collective-permute-start | bytes 184328 | tf_op jit(solution)/shard_map/ppermute | solution.py:767
  23.6 1.3 %collective-permute-start.9 = (bf16[5,16,128]{2,1,0:T(8,128)(2,1)S(1)}, bf16[5,16,128]{2,1,0:T(8,128)(2,1)S(1)}, u32[]{:S(2)}, u32[]{:S(2)}) collective-permute-start(bf16[5,16,128]{2,1,0:T(8,128)(2,1)S(1)} %broadcast_multiply_fusion.2), channel_id=1, source_target_pairs={{0,1},{1,0},{2,3},{3,2},{4,24},{5,25},{6,26},{7,27},{8,20},{9,21},... | collective-permute-start | bytes 61448 | tf_op jit(solution)/shard_map/ppermute | solution.py:767
  23.7 3.8 %collective-permute-start.11 = (bf16[5,16,128]{2,1,0:T(8,128)(2,1)S(1)}, bf16[5,16,128]{2,1,0:T(8,128)(2,1)S(1)}, u32[]{:S(2)}, u32[]{:S(2)}) collective-permute-start(bf16[5,16,128]{2,1,0:T(8,128)(2,1)S(1)} %broadcast_multiply_fusion.2), channel_id=1, source_target_pairs={{0,16},{1,17},{2,18},{3,19},{4,20},{5,21},{6,22},{7,23},{8,24},{9,... | collective-permute-start | bytes 61448 | tf_op jit(solution)/shard_map/ppermute | solution.py:767
  27.5 2.0 %collective-permute-start.13 = (bf16[128,128]{1,0:T(8,128)(2,1)S(1)}, bf16[128,128]{1,0:T(8,128)(2,1)S(1)}, u32[]{:S(2)}, u32[]{:S(2)}) collective-permute-start(bf16[128,128]{1,0:T(8,128)(2,1)S(1)} %pad_maximum_fusion), channel_id=1, source_target_pairs={{0,3},{1,0},{2,1},{3,2},{4,7},{5,4},{6,5},{7,6},{8,11},{9,8},{10,9... | collective-permute-start | bytes 98312 | tf_op jit(solution)/shard_map/ppermute | solution.py:767
  27.6 3.4 %collective-permute-start.12 = (bf16[128,128]{1,0:T(8,128)(2,1)S(1)}, bf16[128,128]{1,0:T(8,128)(2,1)S(1)}, u32[]{:S(2)}, u32[]{:S(2)}) collective-permute-start(bf16[128,128]{1,0:T(8,128)(2,1)S(1)} %pad_maximum_fusion), channel_id=1, source_target_pairs={{0,1},{1,2},{2,3},{3,0},{4,5},{5,6},{6,7},{7,4},{8,9},{9,10},{10,1... | collective-permute-start | bytes 98312 | tf_op jit(solution)/shard_map/ppermute | solution.py:767

commit v16 on v13

--- a/solution.py
+++ b/solution.py
@@ -782,11 +782,17 @@
 
 def exchange(fields, own_edges, one, two, sides, d):
     rows = d.rows
+    scale = jnp.where(lax.axis_index("grp") > 1, 0, 1).astype(BF16)
+    later = fields * scale
+    beside = send(fields, lambda g, i, j: (1 - g, i, j))
     from_one = swap_rows(one, 0, False)
     from_two = swap_rows(two, 1, False)
-    field_one = swap_rows(fields, 0, True)
-    field_two = swap_rows(fields, 1, True)
-    beside = send(fields, lambda g, i, j: (1 - g, i, j))
+    field_one = swap_rows(later, 0, True)
+    field_two = swap_rows(later, 1, True)
+    beside, from_one = lax.optimization_barrier((beside, from_one))
+    from_two, beside = lax.optimization_barrier((from_two, beside))
+    field_one, from_two = lax.optimization_barrier((field_one, from_two))
+    field_two, field_one = lax.optimization_barrier((field_two, field_one))
     lat, count = lax.axis_index("lat"), lax.axis_size("lat")
     odd = lat % 2 == 1
     edges = own_edges
@@ -794,9 +800,6 @@
         other = ((lat + turn) ^ 1) - turn
         there = (other >= 0) & (other < count)
         edges = edges + jnp.where(there, ref[2 * CH : d.strip], 0)
-    edges, beside, field_one, field_two = lax.optimization_barrier(
-        (edges, beside, field_one, field_two)
-    )
     outer = [field_one[NS], field_two[NS]]
     if rows != 16:
         outer = [

time: 37.2 us -> 34 us (0.914)
  the two profiles are of different devices: /device:TPU:0 before, /device:TPU:8 now
where the time goes in v16:
time: 34 us; the launch traced here: 33.8 us
  starting transfers between devices  12.2 us (36%)
  Pallas kernels  11.5 us (34%)
  waiting for transfers between devices  9.79 us (29%)
    ppermute x14, starting transfers between devices, send(): return lax.ppermute(x, names, pairs)  12.2 us
    pallas_call x5, Pallas kernels, call(): pl.pallas_call(kernel, out_shape=outs, in_specs=[SMEM] + [VMEM] * len(ope...  11.5 us
    ppermute x14, waiting for transfers between devices, send(): return lax.ppermute(x, names, pairs)  9.79 us
  transfers between devices with their start and end apart: 14, of which 6 were waited for; matrix products, arithmetic and copies ran while one was open for 0% of the time, Pallas kernels for 10%

profile of v16, /device:TPU:8, one launch (start us, length us, event | category | flops | bytes accessed | tf_op | source)
XLA Modules:
  0.0 33.8 jit_solution(4637572778850616898)
XLA Ops:
  0.0 0.1 pad_add_fusion.flags.refs_0_
  0.1 2.2 %start.1 = (bf16[16,80,128]{2,1,0:T(8,128)(2,1)S(1)}, bf16[8,16,128]{2,1,0:T(8,128)(2,1)S(1)}, bf16[16,128]{1,0:T(8,128)(2,1)S(1)}, bf16[2048,128]{1,0:T(8,128)(...) custom-call(s32[4]{0:T(128)S(1)} %pad_add_fusion.flags.refs_0_, ...), custom_call_target="tpu_custom_call" | custom-call | tf_op jit(solution)/shard_map/start/pallas_call | solution.py:854
  2.3 1.6 %collective-permute-start = (bf16[5,16,128]{2,1,0:T(8,128)(2,1)S(1)}, bf16[5,16,128]{2,1,0:T(8,128)(2,1)S(1)}, u32[]{:S(2)}, u32[]{:S(2)}) collective-permute-start(bf16[5,16,128]{2,1,0:T(8,128)(2,1)S(1)} %get-tuple-element.47), channel_id=1, source_target_pairs={{0,16},{1,17},{2,18},{3,19},{4,20},{5,21},{6,22},{7,23},{8,24},{9,... | collective-permute-start | bytes 61448 | tf_op jit(solution)/shard_map/ppermute | solution.py:767
  3.9 0.5 %collective-permute-start.3 = (bf16[272,128]{1,0:T(8,128)(2,1)S(1)}, bf16[272,128]{1,0:T(8,128)(2,1)S(1)}, u32[]{:S(2)}, u32[]{:S(2)}) collective-permute-start(bf16[272,128]{1,0:T(8,128)(2,1)S(1)} %get-tuple-element.50), channel_id=1, source_target_pairs={{0,1},{1,0},{2,3},{3,2},{4,5},{5,4},{6,7},{7,6},{8,9},{9,8},{10,11... | collective-permute-start | bytes 208904 | tf_op jit(solution)/shard_map/ppermute | solution.py:767
  4.4 1.5 %collective-permute-start.2 = (bf16[5,16,128]{2,1,0:T(8,128)(2,1)S(1)}, bf16[5,16,128]{2,1,0:T(8,128)(2,1)S(1)}, u32[]{:S(2)}, u32[]{:S(2)}) collective-permute-start(bf16[5,16,128]{2,1,0:T(8,128)(2,1)S(1)} %broadcast_multiply_fusion.1), channel_id=1, source_target_pairs={{0,20},{1,21},{2,22},{3,23},{4,16},{5,17},{6,18},{7,19},{8,28},{9,... | collective-permute-start | bytes 61448 | tf_op jit(solution)/shard_map/ppermute | solution.py:767
  5.9 2.5 %collective-permute-start.4 = (bf16[5,16,128]{2,1,0:T(8,128)(2,1)S(1)}, bf16[5,16,128]{2,1,0:T(8,128)(2,1)S(1)}, u32[]{:S(2)}, u32[]{:S(2)}) collective-permute-start(bf16[5,16,128]{2,1,0:T(8,128)(2,1)S(1)} %broadcast_multiply_fusion.1), channel_id=1, source_target_pairs={{0,1},{1,0},{2,3},{3,2},{4,24},{5,25},{6,26},{7,27},{8,20},{9,21},... | collective-permute-start | bytes 61448 | tf_op jit(solution)/shard_map/ppermute | solution.py:767
  8.4 0.6 %collective-permute-done.2.refs_2_ = bf16[5,16,128]{2,1,0:T(8,128)(2,1)S(1)} collective-permute-done((bf16[5,16,128]{2,1,0:T(8,128)(2,1)S(1)}, bf16[5,16,128]{2,1,0:T(8,128)(2,1)S(1)}, u32[]{:S(2)}, u32[]{:S(2)}) %collective-permute-start.2) | collective-permute-done | bytes 20512 | tf_op jit(solution)/shard_map/ppermute | solution.py:767
  9.1 1.5 %collective-permute-done.4.refs_4_ = bf16[5,16,128]{2,1,0:T(8,128)(2,1)S(1)} collective-permute-done((bf16[5,16,128]{2,1,0:T(8,128)(2,1)S(1)}, bf16[5,16,128]{2,1,0:T(8,128)(2,1)S(1)}, u32[]{:S(2)}, u32[]{:S(2)}) %collective-permute-start.4) | collective-permute-done | bytes 20512 | tf_op jit(solution)/shard_map/ppermute | solution.py:767
  10.7 0.2 collective-permute-start.6
  10.9 0.4 %collective-permute-start.5 = (bf16[176,128]{1,0:T(8,128)(2,1)S(1)}, bf16[176,128]{1,0:T(8,128)(2,1)S(1)}, u32[]{:S(2)}, u32[]{:S(2)}) collective-permute-start(bf16[176,128]{1,0:T(8,128)(2,1)S(1)} %constant_dynamic-update-slice_fusion), channel_id=1, source_target_pairs={{0,1},{1,2},{2,3},{3,0},{4,5},{5,6},{6,7},{7,4},{8,9},{9,10},{10,1... | collective-permute-start | bytes 135176 | tf_op jit(solution)/shard_map/ppermute | solution.py:767
  11.3 1.9 %first_middle.1 = (f32[96,128]{1,0:T(8,128)S(1)}, f32[4,48,128]{2,1,0:T(8,128)S(1)}, bf16[20,240,128]{2,1,0:T(8,128)(2,1)S(1)}, f32[192,128]{1,0:T(8,128)S(1)}, ...) custom-call(s32[4]{0:T(128)S(1)} %pad_add_fusion.flags.refs_0_, ...), custom_call_target="tpu_custom_call" | custom-call | tf_op jit(solution)/shard_map/first_middle/pallas_call | solution.py:854
  13.2 1.6 %collective-permute-done.5.refs_3_ = bf16[176,128]{1,0:T(8,128)(2,1)S(1)} collective-permute-done((bf16[176,128]{1,0:T(8,128)(2,1)S(1)}, bf16[176,128]{1,0:T(8,128)(2,1)S(1)}, u32[]{:S(2)}, u32[]{:S(2)}) %collective-permute-start.5) | collective-permute-done | bytes 45088 | tf_op jit(solution)/shard_map/ppermute | solution.py:767
  14.8 2.7 %first_step.1 = (bf16[16,80,128]{2,1,0:T(8,128)(2,1)S(1)}, bf16[5,16,128]{2,1,0:T(8,128)(2,1)S(1)}, bf16[80,128]{1,0:T(8,128)(2,1)S(1)}, bf16[240,128]{1,0:T(8,1...) custom-call(s32[4]{0:T(128)S(1)} %pad_add_fusion.flags.refs_0_, ...), custom_call_target="tpu_custom_call" | custom-call | tf_op jit(solution)/shard_map/first_step/pallas_call | solution.py:854
  17.5 3.3 %collective-permute-start.7 = (bf16[5,16,128]{2,1,0:T(8,128)(2,1)S(1)}, bf16[5,16,128]{2,1,0:T(8,128)(2,1)S(1)}, u32[]{:S(2)}, u32[]{:S(2)}) collective-permute-start(bf16[5,16,128]{2,1,0:T(8,128)(2,1)S(1)} %get-tuple-element.70), channel_id=1, source_target_pairs={{0,16},{1,17},{2,18},{3,19},{4,20},{5,21},{6,22},{7,23},{8,24},{9,... | collective-permute-start | bytes 61448 | tf_op jit(solution)/shard_map/ppermute | solution.py:767
  20.8 0.5 %collective-permute-start.10 = (bf16[240,128]{1,0:T(8,128)(2,1)S(1)}, bf16[240,128]{1,0:T(8,128)(2,1)S(1)}, u32[]{:S(2)}, u32[]{:S(2)}) collective-permute-start(bf16[240,128]{1,0:T(8,128)(2,1)S(1)} %get-tuple-element.73), channel_id=1, source_target_pairs={{0,1},{1,0},{2,3},{3,2},{4,5},{5,4},{6,7},{7,6},{8,9},{9,8},{10,11... | collective-permute-start | bytes 184328 | tf_op jit(solution)/shard_map/ppermute | solution.py:767
  21.3 1.1 %collective-permute-start.9 = (bf16[5,16,128]{2,1,0:T(8,128)(2,1)S(1)}, bf16[5,16,128]{2,1,0:T(8,128)(2,1)S(1)}, u32[]{:S(2)}, u32[]{:S(2)}) collective-permute-start(bf16[5,16,128]{2,1,0:T(8,128)(2,1)S(1)} %broadcast_multiply_fusion), channel_id=1, source_target_pairs={{0,20},{1,21},{2,22},{3,23},{4,16},{5,17},{6,18},{7,19},{8,28},{9,... | collective-permute-start | bytes 61448 | tf_op jit(solution)/shard_map/ppermute | solution.py:767
  22.4 0.1 collective-permute-start.11
  22.5 3.4 %collective-permute-done.9.refs_2_ = bf16[5,16,128]{2,1,0:T(8,128)(2,1)S(1)} collective-permute-done((bf16[5,16,128]{2,1,0:T(8,128)(2,1)S(1)}, bf16[5,16,128]{2,1,0:T(8,128)(2,1)S(1)}, u32[]{:S(2)}, u32[]{:S(2)}) %collective-permute-start.9) | collective-permute-done | bytes 20512 | tf_op jit(solution)/shard_map/ppermute | solution.py:767
  26.0 1.1 %collective-permute-done.11.refs_4_ = bf16[5,16,128]{2,1,0:T(8,128)(2,1)S(1)} collective-permute-done((bf16[5,16,128]{2,1,0:T(8,128)(2,1)S(1)}, bf16[5,16,128]{2,1,0:T(8,128)(2,1)S(1)}, u32[]{:S(2)}, u32[]{:S(2)}) %collective-permute-start.11) | collective-permute-done | bytes 20512 | tf_op jit(solution)/shard_map/ppermute | solution.py:767
  27.1 0.1 collective-permute-start.13
  27.2 0.5 %collective-permute-start.12 = (bf16[128,128]{1,0:T(8,128)(2,1)S(1)}, bf16[128,128]{1,0:T(8,128)(2,1)S(1)}, u32[]{:S(2)}, u32[]{:S(2)}) collective-permute-start(bf16[128,128]{1,0:T(8,128)(2,1)S(1)} %pad_maximum_fusion), channel_id=1, source_target_pairs={{0,1},{1,2},{2,3},{3,0},{4,5},{5,6},{6,7},{7,4},{8,9},{9,10},{10,1... | collective-permute-start | bytes 98312 | tf_op jit(solution)/shard_map/ppermute | solution.py:767
  27.7 1.4 %second_middle.1 = (f32[96,128]{1,0:T(8,128)S(1)}, f32[4,48,128]{2,1,0:T(8,128)S(1)}, bf16[20,240,128]{2,1,0:T(8,128)(2,1)S(1)}) custom-call(s32[4]{0:T(128)S(1)} %pad_add_fusion.flags.refs_0_, bf16[16,80,128]{2,1,0:T(8,128)(2,1)S(1)} %get-tuple-element.68.refs_1_, bf16[5,16,128]{2,1,0:T(8,128)(2,1)S(1)} %collective-permute-done.9.refs_2_, ...), custom_call_target="tpu_custom_call" | custom-call | tf_op jit(solution)/shard_map/second_middle/pallas_call | solution.py:854
  29.1 1.5 %collective-permute-done.12.refs_3_ = bf16[128,128]{1,0:T(8,128)(2,1)S(1)} collective-permute-done((bf16[128,128]{1,0:T(8,128)(2,1)S(1)}, bf16[128,128]{1,0:T(8,128)(2,1)S(1)}, u32[]{:S(2)}, u32[]{:S(2)}) %collective-permute-start.12) | collective-permute-done | bytes 32800 | tf_op jit(solution)/shard_map/ppermute | solution.py:767
  30.6 3.3 %second_step.1 = bf16[80,16,128]{2,1,0:T(8,128)(2,1)} custom-call(s32[4]{0:T(128)S(1)} %pad_add_fusion.flags.refs_0_, bf16[16,80,128]{2,1,0:T(8,128)(2,1)S(1)} %get-tuple-element.68.refs_1_, s32[16,128]{1,0:T(8,128)S(1)} %copy-done.1, bf16[128,128]{1,0:T(8,128)(2,1)S(1)} %collective-permute-done.12.refs_3_, ...), custom_call_target="tpu_custom_call" | custom-call | tf_op jit(solution)/shard_map/second_step/pallas_call | solution.py:854
  (29 shorter events, 0.2 us)
Async XLA Ops:
  0.0 14.8 %copy-start.1 = (s32[16,128]{1,0:T(8,128)S(1)}, s32[16,128]{1,0:T(8,128)}, u32[]{:S(2)}) copy-start(s32[16,128]{1,0:T(8,128)} %refs_2_.3) | copy-start | bytes 24580
  0.0 14.8 %copy-start.2 = (f32[2,4,80]{2,1,0:T(4,128)S(1)}, f32[2,4,80]{2,1,0:T(4,128)}, u32[]{:S(2)}) copy-start(f32[2,4,80]{2,1,0:T(4,128)} %refs_14_.1) | copy-start | bytes 7684
  0.0 14.8 %copy-start = (bf16[80,384]{1,0:T(8,128)(2,1)S(1)}, bf16[80,384]{1,0:T(8,128)(2,1)}, u32[]{:S(2)}) copy-start(bf16[80,384]{1,0:T(8,128)(2,1)} %refs_13_.3) | copy-start | bytes 184324
  2.3 6.1 %collective-permute-start = (bf16[5,16,128]{2,1,0:T(8,128)(2,1)S(1)}, bf16[5,16,128]{2,1,0:T(8,128)(2,1)S(1)}, u32[]{:S(2)}, u32[]{:S(2)}) collective-permute-start(bf16[5,16,128]{2,1,0:T(8,128)(2,1)S(1)} %get-tuple-element.47), channel_id=1, source_target_pairs={{0,16},{1,17},{2,18},{3,19},{4,20},{5,21},{6,22},{7,23},{8,24},{9,... | collective-permute-start | bytes 61448 | tf_op jit(solution)/shard_map/ppermute | solution.py:767
  3.9 4.6 %collective-permute-start.1 = (bf16[272,128]{1,0:T(8,128)(2,1)S(1)}, bf16[272,128]{1,0:T(8,128)(2,1)S(1)}, u32[]{:S(2)}, u32[]{:S(2)}) collective-permute-start(bf16[272,128]{1,0:T(8,128)(2,1)S(1)} %get-tuple-element.48), channel_id=1, source_target_pairs={{0,1},{1,0},{2,3},{3,2},{4,5},{5,4},{6,7},{7,6},{8,9},{9,8},{10,11... | collective-permute-start | bytes 208904 | tf_op jit(solution)/shard_map/ppermute | solution.py:767
  3.9 4.6 %collective-permute-start.3 = (bf16[272,128]{1,0:T(8,128)(2,1)S(1)}, bf16[272,128]{1,0:T(8,128)(2,1)S(1)}, u32[]{:S(2)}, u32[]{:S(2)}) collective-permute-start(bf16[272,128]{1,0:T(8,128)(2,1)S(1)} %get-tuple-element.50), channel_id=1, source_target_pairs={{0,1},{1,0},{2,3},{3,2},{4,5},{5,4},{6,7},{7,6},{8,9},{9,8},{10,11... | collective-permute-start | bytes 208904 | tf_op jit(solution)/shard_map/ppermute | solution.py:767
  4.4 4.7 %collective-permute-start.2 = (bf16[5,16,128]{2,1,0:T(8,128)(2,1)S(1)}, bf16[5,16,128]{2,1,0:T(8,128)(2,1)S(1)}, u32[]{:S(2)}, u32[]{:S(2)}) collective-permute-start(bf16[5,16,128]{2,1,0:T(8,128)(2,1)S(1)} %broadcast_multiply_fusion.1), channel_id=1, source_target_pairs={{0,20},{1,21},{2,22},{3,23},{4,16},{5,17},{6,18},{7,19},{8,28},{9,... | collective-permute-start | bytes 61448 | tf_op jit(solution)/shard_map/ppermute | solution.py:767
  5.9 4.7 %collective-permute-start.4 = (bf16[5,16,128]{2,1,0:T(8,128)(2,1)S(1)}, bf16[5,16,128]{2,1,0:T(8,128)(2,1)S(1)}, u32[]{:S(2)}, u32[]{:S(2)}) collective-permute-start(bf16[5,16,128]{2,1,0:T(8,128)(2,1)S(1)} %broadcast_multiply_fusion.1), channel_id=1, source_target_pairs={{0,1},{1,0},{2,3},{3,2},{4,24},{5,25},{6,26},{7,27},{8,20},{9,21},... | collective-permute-start | bytes 61448 | tf_op jit(solution)/shard_map/ppermute | solution.py:767
  10.7 2.5 %collective-permute-start.6 = (bf16[176,128]{1,0:T(8,128)(2,1)S(1)}, bf16[176,128]{1,0:T(8,128)(2,1)S(1)}, u32[]{:S(2)}, u32[]{:S(2)}) collective-permute-start(bf16[176,128]{1,0:T(8,128)(2,1)S(1)} %constant_dynamic-update-slice_fusion), channel_id=1, source_target_pairs={{0,3},{1,0},{2,1},{3,2},{4,7},{5,4},{6,5},{7,6},{8,11},{9,8},{10,9... | collective-permute-start | bytes 135176 | tf_op jit(solution)/shard_map/ppermute | solution.py:767
  10.9 3.9 %collective-permute-start.5 = (bf16[176,128]{1,0:T(8,128)(2,1)S(1)}, bf16[176,128]{1,0:T(8,128)(2,1)S(1)}, u32[]{:S(2)}, u32[]{:S(2)}) collective-permute-start(bf16[176,128]{1,0:T(8,128)(2,1)S(1)} %constant_dynamic-update-slice_fusion), channel_id=1, source_target_pairs={{0,1},{1,2},{2,3},{3,0},{4,5},{5,6},{6,7},{7,4},{8,9},{9,10},{10,1... | collective-permute-start | bytes 135176 | tf_op jit(solution)/shard_map/ppermute | solution.py:767
  17.5 5.0 %collective-permute-start.7 = (bf16[5,16,128]{2,1,0:T(8,128)(2,1)S(1)}, bf16[5,16,128]{2,1,0:T(8,128)(2,1)S(1)}, u32[]{:S(2)}, u32[]{:S(2)}) collective-permute-start(bf16[5,16,128]{2,1,0:T(8,128)(2,1)S(1)} %get-tuple-element.70), channel_id=1, source_target_pairs={{0,16},{1,17},{2,18},{3,19},{4,20},{5,21},{6,22},{7,23},{8,24},{9,... | collective-permute-start | bytes 61448 | tf_op jit(solution)/shard_map/ppermute | solution.py:767
  20.8 1.8 %collective-permute-start.8 = (bf16[240,128]{1,0:T(8,128)(2,1)S(1)}, bf16[240,128]{1,0:T(8,128)(2,1)S(1)}, u32[]{:S(2)}, u32[]{:S(2)}) collective-permute-start(bf16[240,128]{1,0:T(8,128)(2,1)S(1)} %get-tuple-element.71), channel_id=1, source_target_pairs={{0,1},{1,0},{2,3},{3,2},{4,5},{5,4},{6,7},{7,6},{8,9},{9,8},{10,11... | collective-permute-start | bytes 184328 | tf_op jit(solution)/shard_map/ppermute | solution.py:767
  20.8 1.8 %collective-permute-start.10 = (bf16[240,128]{1,0:T(8,128)(2,1)S(1)}, bf16[240,128]{1,0:T(8,128)(2,1)S(1)}, u32[]{:S(2)}, u32[]{:S(2)}) collective-permute-start(bf16[240,128]{1,0:T(8,128)(2,1)S(1)} %get-tuple-element.73), channel_id=1, source_target_pairs={{0,1},{1,0},{2,3},{3,2},{4,5},{5,4},{6,7},{7,6},{8,9},{9,8},{10,11... | collective-permute-start | bytes 184328 | tf_op jit(solution)/shard_map/ppermute | solution.py:767
  21.3 4.7 %collective-permute-start.9 = (bf16[5,16,128]{2,1,0:T(8,128)(2,1)S(1)}, bf16[5,16,128]{2,1,0:T(8,128)(2,1)S(1)}, u32[]{:S(2)}, u32[]{:S(2)}) collective-permute-start(bf16[5,16,128]{2,1,0:T(8,128)(2,1)S(1)} %broadcast_multiply_fusion), channel_id=1, source_target_pairs={{0,20},{1,21},{2,22},{3,23},{4,16},{5,17},{6,18},{7,19},{8,28},{9,... | collective-permute-start | bytes 61448 | tf_op jit(solution)/shard_map/ppermute | solution.py:767
  22.4 4.7 %collective-permute-start.11 = (bf16[5,16,128]{2,1,0:T(8,128)(2,1)S(1)}, bf16[5,16,128]{2,1,0:T(8,128)(2,1)S(1)}, u32[]{:S(2)}, u32[]{:S(2)}) collective-permute-start(bf16[5,16,128]{2,1,0:T(8,128)(2,1)S(1)} %broadcast_multiply_fusion), channel_id=1, source_target_pairs={{0,1},{1,0},{2,3},{3,2},{4,24},{5,25},{6,26},{7,27},{8,20},{9,21},... | collective-permute-start | bytes 61448 | tf_op jit(solution)/shard_map/ppermute | solution.py:767
  27.1 2.0 %collective-permute-start.13 = (bf16[128,128]{1,0:T(8,128)(2,1)S(1)}, bf16[128,128]{1,0:T(8,128)(2,1)S(1)}, u32[]{:S(2)}, u32[]{:S(2)}) collective-permute-start(bf16[128,128]{1,0:T(8,128)(2,1)S(1)} %pad_maximum_fusion), channel_id=1, source_target_pairs={{0,3},{1,0},{2,1},{3,2},{4,7},{5,4},{6,5},{7,6},{8,11},{9,8},{10,9... | collective-permute-start | bytes 98312 | tf_op jit(solution)/shard_map/ppermute | solution.py:767
  27.2 3.4 %collective-permute-start.12 = (bf16[128,128]{1,0:T(8,128)(2,1)S(1)}, bf16[128,128]{1,0:T(8,128)(2,1)S(1)}, u32[]{:S(2)}, u32[]{:S(2)}) collective-permute-start(bf16[128,128]{1,0:T(8,128)(2,1)S(1)} %pad_maximum_fusion), channel_id=1, source_target_pairs={{0,1},{1,2},{2,3},{3,0},{4,5},{5,6},{6,7},{7,4},{8,9},{9,10},{10,1... | collective-permute-start | bytes 98312 | tf_op jit(solution)/shard_map/ppermute | solution.py:767

commit v17 on v13

--- a/solution.py
+++ b/solution.py
@@ -47,7 +47,8 @@
         self.edge_rows = CH * self.pieces
         self.tiles = -(-(rows + 4) // 8)
         self.tall = 8 * self.tiles
-        self.strip = 2 * CH + self.edge_rows
+        self.strip = 2 * CH + 16
+        self.lead = self.edge_rows + 32
 
 
 def put_edges(ref, at, edges, d):
@@ -95,6 +96,23 @@
     at = index * (128 // count)
     left = roll(left.astype(F32), 128 - at - 2 * reach)
     return jnp.where(lanes(left.shape) < 64, roll(right.astype(F32), -at), left)
+
+
+def corner_lane(index):
+    block = index // 2
+    column = jnp.where(block == 0, 126, jnp.where(block == 1, 0, jnp.where(block == 2, 127, 1)))
+    return jnp.where(index < 8, column + 128 * (index % 2), -1)
+
+
+def join_corners(own, above, below, d):
+    index = subs((16, d.edge))
+    spot = (index % 8 // 2) * d.block + index % 2 + jnp.where(index < 8, 0, d.rows + 2)
+    place = (lanes((16, d.edge)) == spot).astype(F32).astype(BF16)
+    corners = jnp.concatenate([above[0:8], below[0:8]], axis=0).astype(BF16)
+    corners = lax.dot_general(
+        corners, place, (((0,), (0,)), ((), ())), preferred_element_type=F32
+    )
+    return own + corners[:CH].astype(BF16)
 
 
 def strips(one, two, even, d):
@@ -140,15 +158,19 @@
             fields[field] = whole[field].astype(BF16)
         fields[NS] = pack_columns(whole, REACH).astype(BF16)
         put_edges(own_edges, 0, edges, d)
-        row = lanes(edges.shape) % d.block
-        downward = jnp.where(row < 2, roll(edges, -d.rows), jnp.zeros_like(edges))
-        upward = jnp.where(
-            (row >= d.rows + 2) & (row < d.rows + 4), roll(edges, d.rows), jnp.zeros_like(edges)
-        )
-        for (ref, first), down in zip(strips(one, two, even, d), (even, jnp.logical_not(even))):
+        pick = (lanes((16, 256)) == corner_lane(subs((16, 256)))).astype(F32).astype(BF16)
+        rest = jnp.zeros((128 - CH, 256), BF16)
+        for ref, first in strips(one, two, even, d):
             ref[0:CH, :] = state[first]
             ref[CH : 2 * CH, :] = state[first + 1]
-            put_edges(ref, 2 * CH, jnp.where(down, downward, upward), d)
+            pair = jnp.concatenate([state[first], state[first + 1]], axis=1)
+            corners = lax.dot_general(
+                pick,
+                jnp.concatenate([pair, rest], axis=0),
+                (((1,), (1,)), ((), ())),
+                preferred_element_type=F32,
+            )
+            ref[2 * CH : d.strip, :] = corners.astype(BF16)
 
 
 def fetch(sources, targets, sems):
@@ -169,22 +191,13 @@
     rows = d.rows
     pieces = [pl.ds(at, 16) for at in range(0, CH, 16)]
     copies = fetch(
-        [far_given.at[piece] for piece in pieces] + [far_surface, far_wet, far_offsets, far_weights],
-        [given.at[piece] for piece in pieces] + [surface, wet, offsets, weights],
+        [far_offsets, far_weights, far_surface, far_wet] + [far_given.at[piece] for piece in pieces],
+        [offsets, weights, surface, wet] + [given.at[piece] for piece in pieces],
         sems,
     )
     edge_places(places, d)
-    for index, piece in enumerate(pieces):
-        copies[index].wait()
-        turned[index * 16 * rows : (index + 1) * 16 * rows, :] = (
-            given[piece].astype(F32).reshape(16 * rows, 128)
-        )
-    for row in range(rows):
-        state[row] = turned[pl.ds(row, CH, stride=rows), :].astype(BF16)
-    for copy in copies[len(pieces) :]:
+    for copy in copies[:4]:
         copy.wait()
-    emission = Emission(surface, flags, places, raw, d)
-    emission.close(state, wet, fields, own_edges, one, two)
     for k in range(NK):
         code = (offsets[0, k] * SPAN + offsets[1, k]).astype(F32)
         tall[k * rows : (k + 1) * rows, :] = code
@@ -200,6 +213,15 @@
         ref[d.strip + 16 : d.strip + 32, :] = jnp.where(
             down, packed[rows - 16 : rows], packed[0:16]
         ).astype(BF16)
+    for index, piece in enumerate(pieces):
+        copies[4 + index].wait()
+        turned[index * 16 * rows : (index + 1) * 16 * rows, :] = (
+            given[piece].astype(F32).reshape(16 * rows, 128)
+        )
+    for row in range(rows):
+        state[row] = turned[pl.ds(row, CH, stride=rows), :].astype(BF16)
+    emission = Emission(surface, flags, places, raw, d)
+    emission.close(state, wet, fields, own_edges, one, two)
 
 
 def decode(code):
@@ -637,7 +659,7 @@
 def step_kernel(d, opening, closing, *refs):
     refs = list(refs)
     take = lambda count: [refs.pop(0) for _ in range(count)]
-    flags, state, wet, from_left, from_right = take(5)
+    flags, state, wet, from_one, from_two, from_left, from_right = take(7)
     part_x, fields_x, rolled, edges, plan_x, air_in, first, second, atm_out = take(9)
     if not opening:
         (plan_e,) = take(1)
@@ -660,7 +682,7 @@
         @pl.when(is_ocean != 0)
         def _():
             plan_y[...] = jnp.zeros_like(plan_y)
-            base = d.edge_rows
+            base = d.lead
             parts = [
                 (ref[base : base + 16, :], ref[base + 16 + rows : base + 32 + rows, :],
                  ref[base + 16 : base + 16 + rows, :])
@@ -676,7 +698,7 @@
                 plan_y[at + 2 : at + 2 + rows, :] = own
                 plan_y[at + 2 + rows : at + 4 + rows, :] = below[0:2]
 
-    base = d.edge_rows + (rows + 32 if opening else 0)
+    base = d.lead + (rows + 32 if opening else 0)
     parts = [
         (ref[base : base + 16, :], ref[base + 16 + rows : base + 32 + rows, :],
          ref[base + 16 : base + 16 + rows, :])
@@ -731,9 +753,17 @@
             window, plan_e, part_x, forcing_x, forcing_y, 0, d.tiles, tall, True
         )
         put, close = finished()
-        joined = [get_edges(ref, 0, d) for ref in (from_left, from_right)]
+        at, end = d.edge_rows, d.edge_rows + 16
+        joined = [
+            join_corners(
+                get_edges(ref, 0, d), *up_and_down(ref[at:end, :], ref[end : end + 16, :]), d
+            )
+            for ref in (from_left, from_right)
+        ]
+        corners = up_and_down(from_one[2 * CH : d.strip, :], from_two[2 * CH : d.strip, :])
+        own = join_corners(get_edges(edges, 0, d), *corners, d)
         sea(
-            state, rolled, get_edges(edges, 0, d), *joined, put, forcing_x, forcing_y,
+            state, rolled, own, *joined, put, forcing_x, forcing_y,
             first, second, wet, at_top, at_bottom, stack, hidden, side, d,
         )
         close()
@@ -782,35 +812,42 @@
 
 def exchange(fields, own_edges, one, two, sides, d):
     rows = d.rows
-    from_one = swap_rows(one, 0, False)
-    from_two = swap_rows(two, 1, False)
-    field_one = swap_rows(fields, 0, True)
-    field_two = swap_rows(fields, 1, True)
-    beside = send(fields, lambda g, i, j: (1 - g, i, j))
-    lat, count = lax.axis_index("lat"), lax.axis_size("lat")
-    odd = lat % 2 == 1
-    edges = own_edges
-    for turn, ref in ((0, from_one), (1, from_two)):
-        other = ((lat + turn) ^ 1) - turn
-        there = (other >= 0) & (other < count)
-        edges = edges + jnp.where(there, ref[2 * CH : d.strip], 0)
-    edges, beside, field_one, field_two = lax.optimization_barrier(
-        (edges, beside, field_one, field_two)
-    )
+    rest = fields * jnp.where(lax.axis_index("grp") > 1, 0, 1).astype(BF16)
+    if sides is not None:
+        field_two = swap_rows(fields, 1, True)
+        from_one = swap_rows(one, 0, False)
+        from_two = swap_rows(two, 1, False)
+        field_one = swap_rows(rest, 0, True)
+        beside = send(rest, lambda g, i, j: (1 - g, i, j))
+        from_one, field_two = lax.optimization_barrier((from_one, field_two))
+        from_two, from_one = lax.optimization_barrier((from_two, from_one))
+        field_one, from_two = lax.optimization_barrier((field_one, from_two))
+        beside, field_one, own_edges = lax.optimization_barrier((beside, field_one, own_edges))
+    else:
+        field_one = swap_rows(fields, 0, True)
+        from_two = swap_rows(two, 1, False)
+        from_one = swap_rows(one, 0, False)
+        field_two = swap_rows(rest, 1, True)
+        beside = send(rest, lambda g, i, j: (1 - g, i, j))
+        from_two, field_one = lax.optimization_barrier((from_two, field_one))
+        from_one, from_two = lax.optimization_barrier((from_one, from_two))
+        field_two, from_one = lax.optimization_barrier((field_two, from_one))
+        beside, field_two, own_edges = lax.optimization_barrier((beside, field_two, own_edges))
+    odd = lax.axis_index("lat") % 2 == 1
     outer = [field_one[NS], field_two[NS]]
     if rows != 16:
         outer = [
             jnp.where(odd, outer[0][rows - 16 :], outer[0][:16]),
             jnp.where(odd, outer[1][:16], outer[1][rows - 16 :]),
         ]
-    packed = [edges]
+    packed = [own_edges, from_one[2 * CH : d.strip], from_two[2 * CH : d.strip]]
     if sides is not None:
         packed += [from_one[d.strip + 16 :], sides, from_two[d.strip + 16 :]]
     packed += [outer[0], beside[NS], outer[1]]
     packed = jnp.concatenate(packed, axis=0)
     from_left = send(packed, lambda g, i, j: (g, i, j + 1))
     from_right = send(packed, lambda g, i, j: (g, i, j - 1))
-    return (field_one, beside, field_two, from_one, from_two), (from_left, from_right), edges
+    return (field_one, beside, field_two, from_one, from_two), (from_one, from_two, from_left, from_right)
 
 
 def local(
@@ -886,7 +923,7 @@
         pltpu.VMEM((768, d.edge), BF16),
     ]
 
-    vertical, horizontal, edges = exchange(fields, edges, one, two, sides, d)
+    vertical, horizontal = exchange(fields, edges, one, two, sides, d)
     *shared, plan_x, air_in, first, second = call(
         functools.partial(middle_kernel, d, True),
         (state, *vertical, planes),
@@ -904,7 +941,7 @@
         "first_step",
     )
 
-    vertical, horizontal, edges = exchange(fields, edges, one, two, None, d)
+    vertical, horizontal = exchange(fields, edges, one, two, None, d)
     shared = call(
         functools.partial(middle_kernel, d, False),
         (state, *vertical, plan_x),

time: 37.2 us -> 35.1 us (0.944)
  the two profiles are of different devices: /device:TPU:0 before, /device:TPU:10 now
where the time goes in v17:
time: 35.1 us; the launch traced here: 34.9 us
  Pallas kernels  15.3 us (44%)
  starting transfers between devices  12.2 us (35%)
  waiting for transfers between devices  7.12 us (20%)
    pallas_call x5, Pallas kernels, call(): pl.pallas_call(kernel, out_shape=outs, in_specs=[SMEM] + [VMEM] * len(ope...  15.3 us
    ppermute x14, starting transfers between devices, send(): return lax.ppermute(x, names, pairs)  12.2 us
    ppermute x14, waiting for transfers between devices, send(): return lax.ppermute(x, names, pairs)  7.12 us
  transfers between devices with their start and end apart: 14, of which 8 were waited for; matrix products, arithmetic and copies ran while one was open for 0% of the time, Pallas kernels for 12%

profile of v17, /device:TPU:10, one launch (start us, length us, event | category | flops | bytes accessed | tf_op | source)
XLA Modules:
  0.0 34.9 jit_solution(6318143783983105518)
XLA Ops:
  0.0 0.1 pad_add_fusion.flags.refs_0_
  0.1 2.2 %start.1 = (bf16[16,80,128]{2,1,0:T(8,128)(2,1)S(1)}, bf16[8,16,128]{2,1,0:T(8,128)(2,1)S(1)}, bf16[16,128]{1,0:T(8,128)(2,1)S(1)}, bf16[2048,128]{1,0:T(8,128)(...) custom-call(s32[4]{0:T(128)S(1)} %pad_add_fusion.flags.refs_0_, ...), custom_call_target="tpu_custom_call" | custom-call | tf_op jit(solution)/shard_map/start/pallas_call | solution.py:888
  2.4 1.6 %collective-permute-start.2 = (bf16[5,16,128]{2,1,0:T(8,128)(2,1)S(1)}, bf16[5,16,128]{2,1,0:T(8,128)(2,1)S(1)}, u32[]{:S(2)}, u32[]{:S(2)}) collective-permute-start(bf16[5,16,128]{2,1,0:T(8,128)(2,1)S(1)} %get-tuple-element.50), channel_id=1, source_target_pairs={{0,1},{1,0},{2,3},{3,2},{4,24},{5,25},{6,26},{7,27},{8,20},{9,21},... | collective-permute-start | bytes 61448 | tf_op jit(solution)/shard_map/ppermute | solution.py:797
  4.0 0.4 %collective-permute-start = (bf16[208,128]{1,0:T(8,128)(2,1)S(1)}, bf16[208,128]{1,0:T(8,128)(2,1)S(1)}, u32[]{:S(2)}, u32[]{:S(2)}) collective-permute-start(bf16[208,128]{1,0:T(8,128)(2,1)S(1)} %get-tuple-element.48), channel_id=1, source_target_pairs={{0,1},{1,0},{2,3},{3,2},{4,5},{5,4},{6,7},{7,6},{8,9},{9,8},{10,11... | collective-permute-start | bytes 159752 | tf_op jit(solution)/shard_map/ppermute | solution.py:797
  4.5 3.4 %collective-permute-start.4 = (bf16[5,16,128]{2,1,0:T(8,128)(2,1)S(1)}, bf16[5,16,128]{2,1,0:T(8,128)(2,1)S(1)}, u32[]{:S(2)}, u32[]{:S(2)}) collective-permute-start(bf16[5,16,128]{2,1,0:T(8,128)(2,1)S(1)} %broadcast_multiply_fusion.1), channel_id=1, source_target_pairs={{0,16},{1,17},{2,18},{3,19},{4,20},{5,21},{6,22},{7,23},{8,24},{9,... | collective-permute-start | bytes 61448 | tf_op jit(solution)/shard_map/ppermute | solution.py:797
  7.9 0.9 %collective-permute-done.1.refs_5_.refs_3_ = bf16[208,128]{1,0:T(8,128)(2,1)S(1)} collective-permute-done((bf16[208,128]{1,0:T(8,128)(2,1)S(1)}, bf16[208,128]{1,0:T(8,128)(2,1)S(1)}, u32[]{:S(2)}, u32[]{:S(2)}) %collective-permute-start.1) | collective-permute-done | bytes 53280 | tf_op jit(solution)/shard_map/ppermute | solution.py:797
  8.8 0.4 %collective-permute-done.3.refs_2_ = bf16[5,16,128]{2,1,0:T(8,128)(2,1)S(1)} collective-permute-done((bf16[5,16,128]{2,1,0:T(8,128)(2,1)S(1)}, bf16[5,16,128]{2,1,0:T(8,128)(2,1)S(1)}, u32[]{:S(2)}, u32[]{:S(2)}) %collective-permute-start.3) | collective-permute-done | bytes 20512 | tf_op jit(solution)/shard_map/ppermute | solution.py:797
  9.2 0.5 %collective-permute-done.4.refs_3_ = bf16[5,16,128]{2,1,0:T(8,128)(2,1)S(1)} collective-permute-done((bf16[5,16,128]{2,1,0:T(8,128)(2,1)S(1)}, bf16[5,16,128]{2,1,0:T(8,128)(2,1)S(1)}, u32[]{:S(2)}, u32[]{:S(2)}) %collective-permute-start.4) | collective-permute-done | bytes 20512 | tf_op jit(solution)/shard_map/ppermute | solution.py:797
  9.8 0.5 %collective-permute-start.5 = (bf16[208,128]{1,0:T(8,128)(2,1)S(1)}, bf16[208,128]{1,0:T(8,128)(2,1)S(1)}, u32[]{:S(2)}, u32[]{:S(2)}) collective-permute-start(bf16[208,128]{1,0:T(8,128)(2,1)S(1)} %constant_dynamic-update-slice_fusion), channel_id=1, source_target_pairs={{0,1},{1,2},{2,3},{3,0},{4,5},{5,6},{6,7},{7,4},{8,9},{9,10},{10,1... | collective-permute-start | bytes 159752 | tf_op jit(solution)/shard_map/ppermute | solution.py:797
  10.3 2.3 %first_middle.1 = (f32[96,128]{1,0:T(8,128)S(1)}, f32[4,48,128]{2,1,0:T(8,128)S(1)}, bf16[20,240,128]{2,1,0:T(8,128)(2,1)S(1)}, f32[192,128]{1,0:T(8,128)S(1)}, ...) custom-call(s32[4]{0:T(128)S(1)} %pad_add_fusion.flags.refs_0_, ...), custom_call_target="tpu_custom_call" | custom-call | tf_op jit(solution)/shard_map/first_middle/pallas_call | solution.py:888
  12.6 1.4 %collective-permute-done.5.refs_5_ = bf16[208,128]{1,0:T(8,128)(2,1)S(1)} collective-permute-done((bf16[208,128]{1,0:T(8,128)(2,1)S(1)}, bf16[208,128]{1,0:T(8,128)(2,1)S(1)}, u32[]{:S(2)}, u32[]{:S(2)}) %collective-permute-start.5) | collective-permute-done | bytes 53280 | tf_op jit(solution)/shard_map/ppermute | solution.py:797
  14.0 4.2 %first_step.1 = (bf16[16,80,128]{2,1,0:T(8,128)(2,1)S(1)}, bf16[5,16,128]{2,1,0:T(8,128)(2,1)S(1)}, bf16[80,128]{1,0:T(8,128)(2,1)S(1)}, bf16[176,128]{1,0:T(8,1...) custom-call(s32[4]{0:T(128)S(1)} %pad_add_fusion.flags.refs_0_, ...), custom_call_target="tpu_custom_call" | custom-call | tf_op jit(solution)/shard_map/first_step/pallas_call | solution.py:888
  18.2 0.1 collective-permute-start.10
  18.2 1.9 %collective-permute-start.8 = (bf16[176,128]{1,0:T(8,128)(2,1)S(1)}, bf16[176,128]{1,0:T(8,128)(2,1)S(1)}, u32[]{:S(2)}, u32[]{:S(2)}) collective-permute-start(bf16[176,128]{1,0:T(8,128)(2,1)S(1)} %get-tuple-element.73), channel_id=1, source_target_pairs={{0,1},{1,0},{2,3},{3,2},{4,5},{5,4},{6,7},{7,6},{8,9},{9,8},{10,11... | collective-permute-start | bytes 135176 | tf_op jit(solution)/shard_map/ppermute | solution.py:797
  20.2 1.6 %collective-permute-start.9 = (bf16[176,128]{1,0:T(8,128)(2,1)S(1)}, bf16[176,128]{1,0:T(8,128)(2,1)S(1)}, u32[]{:S(2)}, u32[]{:S(2)}) collective-permute-start(bf16[176,128]{1,0:T(8,128)(2,1)S(1)} %get-tuple-element.74), channel_id=1, source_target_pairs={{0,1},{1,0},{2,3},{3,2},{4,5},{5,4},{6,7},{7,6},{8,9},{9,8},{10,11... | collective-permute-start | bytes 135176 | tf_op jit(solution)/shard_map/ppermute | solution.py:797
  21.8 0.9 %collective-permute-start.7 = (bf16[5,16,128]{2,1,0:T(8,128)(2,1)S(1)}, bf16[5,16,128]{2,1,0:T(8,128)(2,1)S(1)}, u32[]{:S(2)}, u32[]{:S(2)}) collective-permute-start(bf16[5,16,128]{2,1,0:T(8,128)(2,1)S(1)} %broadcast_multiply_fusion), channel_id=1, source_target_pairs={{0,1},{1,0},{2,3},{3,2},{4,24},{5,25},{6,26},{7,27},{8,20},{9,21},... | collective-permute-start | bytes 61448 | tf_op jit(solution)/shard_map/ppermute | solution.py:797
  22.7 1.0 %collective-permute-start.11 = (bf16[5,16,128]{2,1,0:T(8,128)(2,1)S(1)}, bf16[5,16,128]{2,1,0:T(8,128)(2,1)S(1)}, u32[]{:S(2)}, u32[]{:S(2)}) collective-permute-start(bf16[5,16,128]{2,1,0:T(8,128)(2,1)S(1)} %broadcast_multiply_fusion), channel_id=1, source_target_pairs={{0,16},{1,17},{2,18},{3,19},{4,20},{5,21},{6,22},{7,23},{8,24},{9,... | collective-permute-start | bytes 61448 | tf_op jit(solution)/shard_map/ppermute | solution.py:797
  23.7 0.8 %collective-permute-done.9.refs_6_.refs_4_ = bf16[176,128]{1,0:T(8,128)(2,1)S(1)} collective-permute-done((bf16[176,128]{1,0:T(8,128)(2,1)S(1)}, bf16[176,128]{1,0:T(8,128)(2,1)S(1)}, u32[]{:S(2)}, u32[]{:S(2)}) %collective-permute-start.9) | collective-permute-done | bytes 45088 | tf_op jit(solution)/shard_map/ppermute | solution.py:797
  24.5 2.0 %collective-permute-done.7.refs_4_ = bf16[5,16,128]{2,1,0:T(8,128)(2,1)S(1)} collective-permute-done((bf16[5,16,128]{2,1,0:T(8,128)(2,1)S(1)}, bf16[5,16,128]{2,1,0:T(8,128)(2,1)S(1)}, u32[]{:S(2)}, u32[]{:S(2)}) %collective-permute-start.7) | collective-permute-done | bytes 20512 | tf_op jit(solution)/shard_map/ppermute | solution.py:797
  26.5 0.2 collective-permute-done.11.refs_3_
  26.8 0.5 %collective-permute-start.12 = (bf16[160,128]{1,0:T(8,128)(2,1)S(1)}, bf16[160,128]{1,0:T(8,128)(2,1)S(1)}, u32[]{:S(2)}, u32[]{:S(2)}) collective-permute-start(bf16[160,128]{1,0:T(8,128)(2,1)S(1)} %constant_dynamic-update-slice_fusion.9), channel_id=1, source_target_pairs={{0,1},{1,2},{2,3},{3,0},{4,5},{5,6},{6,7},{7,4},{8,9},{9,10},{10,1... | collective-permute-start | bytes 122888 | tf_op jit(solution)/shard_map/ppermute | solution.py:797
  27.3 2.0 %second_middle.1 = (f32[96,128]{1,0:T(8,128)S(1)}, f32[4,48,128]{2,1,0:T(8,128)S(1)}, bf16[20,240,128]{2,1,0:T(8,128)(2,1)S(1)}) custom-call(s32[4]{0:T(128)S(1)} %pad_add_fusion.flags.refs_0_, bf16[16,80,128]{2,1,0:T(8,128)(2,1)S(1)} %get-tuple-element.71.refs_1_, bf16[5,16,128]{2,1,0:T(8,128)(2,1)S(1)} %collective-permute-done.10.refs_2_, ...), custom_call_target="tpu_custom_call" | custom-call | tf_op jit(solution)/shard_map/second_middle/pallas_call | solution.py:888
  29.3 1.0 %collective-permute-done.12.refs_5_ = bf16[160,128]{1,0:T(8,128)(2,1)S(1)} collective-permute-done((bf16[160,128]{1,0:T(8,128)(2,1)S(1)}, bf16[160,128]{1,0:T(8,128)(2,1)S(1)}, u32[]{:S(2)}, u32[]{:S(2)}) %collective-permute-start.12) | collective-permute-done | bytes 40992 | tf_op jit(solution)/shard_map/ppermute | solution.py:797
  30.3 4.7 %second_step.1 = bf16[80,16,128]{2,1,0:T(8,128)(2,1)} custom-call(s32[4]{0:T(128)S(1)} %pad_add_fusion.flags.refs_0_, bf16[16,80,128]{2,1,0:T(8,128)(2,1)S(1)} %get-tuple-element.71.refs_1_, s32[16,128]{1,0:T(8,128)S(1)} %copy-done.1, bf16[176,128]{1,0:T(8,128)(2,1)S(1)} %collective-permute-done.8.refs_5_.refs_3_, ...), custom_call_target="tpu_custom_call" | custom-call | tf_op jit(solution)/shard_map/second_step/pallas_call | solution.py:888
  (33 shorter events, 0.3 us)
Async XLA Ops:
  0.0 14.0 %copy-start.1 = (s32[16,128]{1,0:T(8,128)S(1)}, s32[16,128]{1,0:T(8,128)}, u32[]{:S(2)}) copy-start(s32[16,128]{1,0:T(8,128)} %refs_2_.3) | copy-start | bytes 24580
  0.0 14.0 %copy-start.2 = (f32[2,4,80]{2,1,0:T(4,128)S(1)}, f32[2,4,80]{2,1,0:T(4,128)}, u32[]{:S(2)}) copy-start(f32[2,4,80]{2,1,0:T(4,128)} %refs_16_.1) | copy-start | bytes 7684
  0.0 14.0 %copy-start = (bf16[80,384]{1,0:T(8,128)(2,1)S(1)}, bf16[80,384]{1,0:T(8,128)(2,1)}, u32[]{:S(2)}) copy-start(bf16[80,384]{1,0:T(8,128)(2,1)} %refs_15_.3) | copy-start | bytes 184324
  2.4 5.6 %collective-permute-start.2 = (bf16[5,16,128]{2,1,0:T(8,128)(2,1)S(1)}, bf16[5,16,128]{2,1,0:T(8,128)(2,1)S(1)}, u32[]{:S(2)}, u32[]{:S(2)}) collective-permute-start(bf16[5,16,128]{2,1,0:T(8,128)(2,1)S(1)} %get-tuple-element.50), channel_id=1, source_target_pairs={{0,1},{1,0},{2,3},{3,2},{4,24},{5,25},{6,26},{7,27},{8,20},{9,21},... | collective-permute-start | bytes 61448 | tf_op jit(solution)/shard_map/ppermute | solution.py:797
  4.0 4.8 %collective-permute-start = (bf16[208,128]{1,0:T(8,128)(2,1)S(1)}, bf16[208,128]{1,0:T(8,128)(2,1)S(1)}, u32[]{:S(2)}, u32[]{:S(2)}) collective-permute-start(bf16[208,128]{1,0:T(8,128)(2,1)S(1)} %get-tuple-element.48), channel_id=1, source_target_pairs={{0,1},{1,0},{2,3},{3,2},{4,5},{5,4},{6,7},{7,6},{8,9},{9,8},{10,11... | collective-permute-start | bytes 159752 | tf_op jit(solution)/shard_map/ppermute | solution.py:797
  4.4 4.4 %collective-permute-start.1 = (bf16[208,128]{1,0:T(8,128)(2,1)S(1)}, bf16[208,128]{1,0:T(8,128)(2,1)S(1)}, u32[]{:S(2)}, u32[]{:S(2)}) collective-permute-start(bf16[208,128]{1,0:T(8,128)(2,1)S(1)} %get-tuple-element.49), channel_id=1, source_target_pairs={{0,1},{1,0},{2,3},{3,2},{4,5},{5,4},{6,7},{7,6},{8,9},{9,8},{10,11... | collective-permute-start | bytes 159752 | tf_op jit(solution)/shard_map/ppermute | solution.py:797
  4.4 4.7 %collective-permute-start.3 = (bf16[5,16,128]{2,1,0:T(8,128)(2,1)S(1)}, bf16[5,16,128]{2,1,0:T(8,128)(2,1)S(1)}, u32[]{:S(2)}, u32[]{:S(2)}) collective-permute-start(bf16[5,16,128]{2,1,0:T(8,128)(2,1)S(1)} %broadcast_multiply_fusion.1), channel_id=1, source_target_pairs={{0,20},{1,21},{2,22},{3,23},{4,16},{5,17},{6,18},{7,19},{8,28},{9,... | collective-permute-start | bytes 61448 | tf_op jit(solution)/shard_map/ppermute | solution.py:797
  4.5 5.2 %collective-permute-start.4 = (bf16[5,16,128]{2,1,0:T(8,128)(2,1)S(1)}, bf16[5,16,128]{2,1,0:T(8,128)(2,1)S(1)}, u32[]{:S(2)}, u32[]{:S(2)}) collective-permute-start(bf16[5,16,128]{2,1,0:T(8,128)(2,1)S(1)} %broadcast_multiply_fusion.1), channel_id=1, source_target_pairs={{0,16},{1,17},{2,18},{3,19},{4,20},{5,21},{6,22},{7,23},{8,24},{9,... | collective-permute-start | bytes 61448 | tf_op jit(solution)/shard_map/ppermute | solution.py:797
  9.8 2.9 %collective-permute-start.6 = (bf16[208,128]{1,0:T(8,128)(2,1)S(1)}, bf16[208,128]{1,0:T(8,128)(2,1)S(1)}, u32[]{:S(2)}, u32[]{:S(2)}) collective-permute-start(bf16[208,128]{1,0:T(8,128)(2,1)S(1)} %constant_dynamic-update-slice_fusion), channel_id=1, source_target_pairs={{0,3},{1,0},{2,1},{3,2},{4,7},{5,4},{6,5},{7,6},{8,11},{9,8},{10,9... | collective-permute-start | bytes 159752 | tf_op jit(solution)/shard_map/ppermute | solution.py:797
  9.8 4.2 %collective-permute-start.5 = (bf16[208,128]{1,0:T(8,128)(2,1)S(1)}, bf16[208,128]{1,0:T(8,128)(2,1)S(1)}, u32[]{:S(2)}, u32[]{:S(2)}) collective-permute-start(bf16[208,128]{1,0:T(8,128)(2,1)S(1)} %constant_dynamic-update-slice_fusion), channel_id=1, source_target_pairs={{0,1},{1,2},{2,3},{3,0},{4,5},{5,6},{6,7},{7,4},{8,9},{9,10},{10,1... | collective-permute-start | bytes 159752 | tf_op jit(solution)/shard_map/ppermute | solution.py:797
  18.2 5.5 %collective-permute-start.10 = (bf16[5,16,128]{2,1,0:T(8,128)(2,1)S(1)}, bf16[5,16,128]{2,1,0:T(8,128)(2,1)S(1)}, u32[]{:S(2)}, u32[]{:S(2)}) collective-permute-start(bf16[5,16,128]{2,1,0:T(8,128)(2,1)S(1)} %get-tuple-element.72), channel_id=1, source_target_pairs={{0,20},{1,21},{2,22},{3,23},{4,16},{5,17},{6,18},{7,19},{8,28},{9,... | collective-permute-start | bytes 61448 | tf_op jit(solution)/shard_map/ppermute | solution.py:797
  18.2 6.2 %collective-permute-start.8 = (bf16[176,128]{1,0:T(8,128)(2,1)S(1)}, bf16[176,128]{1,0:T(8,128)(2,1)S(1)}, u32[]{:S(2)}, u32[]{:S(2)}) collective-permute-start(bf16[176,128]{1,0:T(8,128)(2,1)S(1)} %get-tuple-element.73), channel_id=1, source_target_pairs={{0,1},{1,0},{2,3},{3,2},{4,5},{5,4},{6,7},{7,6},{8,9},{9,8},{10,11... | collective-permute-start | bytes 135176 | tf_op jit(solution)/shard_map/ppermute | solution.py:797
  20.2 4.3 %collective-permute-start.9 = (bf16[176,128]{1,0:T(8,128)(2,1)S(1)}, bf16[176,128]{1,0:T(8,128)(2,1)S(1)}, u32[]{:S(2)}, u32[]{:S(2)}) collective-permute-start(bf16[176,128]{1,0:T(8,128)(2,1)S(1)} %get-tuple-element.74), channel_id=1, source_target_pairs={{0,1},{1,0},{2,3},{3,2},{4,5},{5,4},{6,7},{7,6},{8,9},{9,8},{10,11... | collective-permute-start | bytes 135176 | tf_op jit(solution)/shard_map/ppermute | solution.py:797
  21.8 4.7 %collective-permute-start.7 = (bf16[5,16,128]{2,1,0:T(8,128)(2,1)S(1)}, bf16[5,16,128]{2,1,0:T(8,128)(2,1)S(1)}, u32[]{:S(2)}, u32[]{:S(2)}) collective-permute-start(bf16[5,16,128]{2,1,0:T(8,128)(2,1)S(1)} %broadcast_multiply_fusion), channel_id=1, source_target_pairs={{0,1},{1,0},{2,3},{3,2},{4,24},{5,25},{6,26},{7,27},{8,20},{9,21},... | collective-permute-start | bytes 61448 | tf_op jit(solution)/shard_map/ppermute | solution.py:797
  22.7 4.0 %collective-permute-start.11 = (bf16[5,16,128]{2,1,0:T(8,128)(2,1)S(1)}, bf16[5,16,128]{2,1,0:T(8,128)(2,1)S(1)}, u32[]{:S(2)}, u32[]{:S(2)}) collective-permute-start(bf16[5,16,128]{2,1,0:T(8,128)(2,1)S(1)} %broadcast_multiply_fusion), channel_id=1, source_target_pairs={{0,16},{1,17},{2,18},{3,19},{4,20},{5,21},{6,22},{7,23},{8,24},{9,... | collective-permute-start | bytes 61448 | tf_op jit(solution)/shard_map/ppermute | solution.py:797
  26.7 2.5 %collective-permute-start.13 = (bf16[160,128]{1,0:T(8,128)(2,1)S(1)}, bf16[160,128]{1,0:T(8,128)(2,1)S(1)}, u32[]{:S(2)}, u32[]{:S(2)}) collective-permute-start(bf16[160,128]{1,0:T(8,128)(2,1)S(1)} %constant_dynamic-update-slice_fusion.9), channel_id=1, source_target_pairs={{0,3},{1,0},{2,1},{3,2},{4,7},{5,4},{6,5},{7,6},{8,11},{9,8},{10,9... | collective-permute-start | bytes 122888 | tf_op jit(solution)/shard_map/ppermute | solution.py:797
  26.8 3.5 %collective-permute-start.12 = (bf16[160,128]{1,0:T(8,128)(2,1)S(1)}, bf16[160,128]{1,0:T(8,128)(2,1)S(1)}, u32[]{:S(2)}, u32[]{:S(2)}) collective-permute-start(bf16[160,128]{1,0:T(8,128)(2,1)S(1)} %constant_dynamic-update-slice_fusion.9), channel_id=1, source_target_pairs={{0,1},{1,2},{2,3},{3,0},{4,5},{5,6},{6,7},{7,4},{8,9},{9,10},{10,1... | collective-permute-start | bytes 122888 | tf_op jit(solution)/shard_map/ppermute | solution.py:797

commit v18 on v16

--- a/solution.py
+++ b/solution.py
@@ -498,25 +498,20 @@
     active = jnp.where(gone, 0.0, twice_gelu(product)).astype(BF16)
     active = jnp.concatenate([active, jnp.zeros((HIDP - HIDK, d.edge), BF16)], axis=0)
 
-    def taps_of(slices):
-        total = None
-        for tap, values in enumerate(slices):
-            weights = ocn_out[tap * 3 * CH : (tap + 1) * 3 * CH, :]
-            product = jnp.dot(weights, values, preferred_element_type=F32)
-            total = product if total is None else total + product
-        return total
-
-    partial = taps_of([roll(active, -tap) for tap in range(3)])
-    from_left, from_right = partial[0:CH], partial[2 * CH : 3 * CH]
+    taps = jnp.concatenate([roll(active, -tap) for tap in range(3)], axis=0)
+    from_left = jnp.dot(ocn_out[0:CH, :], taps, preferred_element_type=F32)
+    from_right = jnp.dot(ocn_out[2 * CH : 3 * CH, :], taps, preferred_element_type=F32)
     half = rows // 2
 
     def second(step, _):
-        return taps_of(
+        taps = jnp.concatenate(
             [
-                jnp.concatenate([hidden[step + tap], hidden[step + half + tap]], axis=1)
-                for tap in range(3)
-            ]
+                hidden[step : step + 3].reshape(3 * HIDP, 128),
+                hidden[step + half : step + half + 3].reshape(3 * HIDP, 128),
+            ],
+            axis=1,
         )
+        return jnp.dot(ocn_out[...], taps, preferred_element_type=F32)
 
     def last(step, product):
         news = []
@@ -561,7 +556,8 @@
             first[:, tap * 256 : (tap + 1) * 256] = columns[:HIDK].astype(BF16)
         for tap in range(9):
             values = ocn_out[tap].astype(F32)
-            second[tap * CH : (tap + 1) * CH, :] = jnp.pad(
+            at, column = tap // 3 * HIDP, tap % 3
+            second[column * CH : (column + 1) * CH, at : at + HIDP] = jnp.pad(
                 values, ((0, 0), (0, HIDP - count))
             ).astype(BF16)
 
@@ -878,7 +874,7 @@
         shape(NS, rows + 32, 128, dtype=F32),
         shape(rows + 4, 3 * CH, 128),
     ]
-    made = [shape(HA, 128), shape(HIDK, 768), shape(9 * CH, HIDP)]
+    made = [shape(HA, 128), shape(HIDK, 768), shape(3 * CH, 3 * HIDP)]
     coupled = pltpu.VMEM((NS // 2, rows + 32, 128), jnp.int32)
     scratch = [
         pltpu.VMEM((NS, rows + 32, 128), F32),

time: 34 us -> 34.1 us (level)
  no operation moved by 1% of the time
where the time goes in v18:
time: 34.1 us; the launch traced here: 33.9 us
  starting transfers between devices  12.3 us (36%)
  Pallas kernels  11.5 us (34%)
  waiting for transfers between devices  9.79 us (29%)
    ppermute x14, starting transfers between devices, send(): return lax.ppermute(x, names, pairs)  12.3 us
    pallas_call x5, Pallas kernels, call(): pl.pallas_call(kernel, out_shape=outs, in_specs=[SMEM] + [VMEM] * len(ope...  11.5 us
    ppermute x14, waiting for transfers between devices, send(): return lax.ppermute(x, names, pairs)  9.79 us
  transfers between devices with their start and end apart: 14, of which 6 were waited for; matrix products, arithmetic and copies ran while one was open for 0% of the time, Pallas kernels for 10%

profile of v18, /device:TPU:8, one launch (start us, length us, event | category | flops | bytes accessed | tf_op | source)
XLA Modules:
  0.0 33.9 jit_solution(1526090201882048363)
XLA Ops:
  0.0 0.1 pad_add_fusion.flags.refs_0_
  0.1 2.2 %start.1 = (bf16[16,80,128]{2,1,0:T(8,128)(2,1)S(1)}, bf16[8,16,128]{2,1,0:T(8,128)(2,1)S(1)}, bf16[16,128]{1,0:T(8,128)(2,1)S(1)}, bf16[2048,128]{1,0:T(8,128)(...) custom-call(s32[4]{0:T(128)S(1)} %pad_add_fusion.flags.refs_0_, ...), custom_call_target="tpu_custom_call" | custom-call | tf_op jit(solution)/shard_map/start/pallas_call | solution.py:850
  2.3 1.6 %collective-permute-start = (bf16[5,16,128]{2,1,0:T(8,128)(2,1)S(1)}, bf16[5,16,128]{2,1,0:T(8,128)(2,1)S(1)}, u32[]{:S(2)}, u32[]{:S(2)}) collective-permute-start(bf16[5,16,128]{2,1,0:T(8,128)(2,1)S(1)} %get-tuple-element.47), channel_id=1, source_target_pairs={{0,16},{1,17},{2,18},{3,19},{4,20},{5,21},{6,22},{7,23},{8,24},{9,... | collective-permute-start | bytes 61448 | tf_op jit(solution)/shard_map/ppermute | solution.py:763
  3.9 0.5 %collective-permute-start.3 = (bf16[272,128]{1,0:T(8,128)(2,1)S(1)}, bf16[272,128]{1,0:T(8,128)(2,1)S(1)}, u32[]{:S(2)}, u32[]{:S(2)}) collective-permute-start(bf16[272,128]{1,0:T(8,128)(2,1)S(1)} %get-tuple-element.50), channel_id=1, source_target_pairs={{0,1},{1,0},{2,3},{3,2},{4,5},{5,4},{6,7},{7,6},{8,9},{9,8},{10,11... | collective-permute-start | bytes 208904 | tf_op jit(solution)/shard_map/ppermute | solution.py:763
  4.4 1.5 %collective-permute-start.2 = (bf16[5,16,128]{2,1,0:T(8,128)(2,1)S(1)}, bf16[5,16,128]{2,1,0:T(8,128)(2,1)S(1)}, u32[]{:S(2)}, u32[]{:S(2)}) collective-permute-start(bf16[5,16,128]{2,1,0:T(8,128)(2,1)S(1)} %broadcast_multiply_fusion.1), channel_id=1, source_target_pairs={{0,20},{1,21},{2,22},{3,23},{4,16},{5,17},{6,18},{7,19},{8,28},{9,... | collective-permute-start | bytes 61448 | tf_op jit(solution)/shard_map/ppermute | solution.py:763
  5.9 2.5 %collective-permute-start.4 = (bf16[5,16,128]{2,1,0:T(8,128)(2,1)S(1)}, bf16[5,16,128]{2,1,0:T(8,128)(2,1)S(1)}, u32[]{:S(2)}, u32[]{:S(2)}) collective-permute-start(bf16[5,16,128]{2,1,0:T(8,128)(2,1)S(1)} %broadcast_multiply_fusion.1), channel_id=1, source_target_pairs={{0,1},{1,0},{2,3},{3,2},{4,24},{5,25},{6,26},{7,27},{8,20},{9,21},... | collective-permute-start | bytes 61448 | tf_op jit(solution)/shard_map/ppermute | solution.py:763
  8.4 0.6 %collective-permute-done.2.refs_2_ = bf16[5,16,128]{2,1,0:T(8,128)(2,1)S(1)} collective-permute-done((bf16[5,16,128]{2,1,0:T(8,128)(2,1)S(1)}, bf16[5,16,128]{2,1,0:T(8,128)(2,1)S(1)}, u32[]{:S(2)}, u32[]{:S(2)}) %collective-permute-start.2) | collective-permute-done | bytes 20512 | tf_op jit(solution)/shard_map/ppermute | solution.py:763
  9.1 1.5 %collective-permute-done.4.refs_4_ = bf16[5,16,128]{2,1,0:T(8,128)(2,1)S(1)} collective-permute-done((bf16[5,16,128]{2,1,0:T(8,128)(2,1)S(1)}, bf16[5,16,128]{2,1,0:T(8,128)(2,1)S(1)}, u32[]{:S(2)}, u32[]{:S(2)}) %collective-permute-start.4) | collective-permute-done | bytes 20512 | tf_op jit(solution)/shard_map/ppermute | solution.py:763
  10.7 0.2 collective-permute-start.6
  10.9 0.4 %collective-permute-start.5 = (bf16[176,128]{1,0:T(8,128)(2,1)S(1)}, bf16[176,128]{1,0:T(8,128)(2,1)S(1)}, u32[]{:S(2)}, u32[]{:S(2)}) collective-permute-start(bf16[176,128]{1,0:T(8,128)(2,1)S(1)} %constant_dynamic-update-slice_fusion), channel_id=1, source_target_pairs={{0,1},{1,2},{2,3},{3,0},{4,5},{5,6},{6,7},{7,4},{8,9},{9,10},{10,1... | collective-permute-start | bytes 135176 | tf_op jit(solution)/shard_map/ppermute | solution.py:763
  11.3 1.9 %first_middle.1 = (f32[96,128]{1,0:T(8,128)S(1)}, f32[4,48,128]{2,1,0:T(8,128)S(1)}, bf16[20,240,128]{2,1,0:T(8,128)(2,1)S(1)}, f32[192,128]{1,0:T(8,128)S(1)}, ...) custom-call(s32[4]{0:T(128)S(1)} %pad_add_fusion.flags.refs_0_, ...), custom_call_target="tpu_custom_call" | custom-call | tf_op jit(solution)/shard_map/first_middle/pallas_call | solution.py:850
  13.2 1.6 %collective-permute-done.5.refs_3_ = bf16[176,128]{1,0:T(8,128)(2,1)S(1)} collective-permute-done((bf16[176,128]{1,0:T(8,128)(2,1)S(1)}, bf16[176,128]{1,0:T(8,128)(2,1)S(1)}, u32[]{:S(2)}, u32[]{:S(2)}) %collective-permute-start.5) | collective-permute-done | bytes 45088 | tf_op jit(solution)/shard_map/ppermute | solution.py:763
  14.8 2.7 %first_step.1 = (bf16[16,80,128]{2,1,0:T(8,128)(2,1)S(1)}, bf16[5,16,128]{2,1,0:T(8,128)(2,1)S(1)}, bf16[80,128]{1,0:T(8,128)(2,1)S(1)}, bf16[240,128]{1,0:T(8,1...) custom-call(s32[4]{0:T(128)S(1)} %pad_add_fusion.flags.refs_0_, ...), custom_call_target="tpu_custom_call" | custom-call | tf_op jit(solution)/shard_map/first_step/pallas_call | solution.py:850
  17.5 3.3 %collective-permute-start.7 = (bf16[5,16,128]{2,1,0:T(8,128)(2,1)S(1)}, bf16[5,16,128]{2,1,0:T(8,128)(2,1)S(1)}, u32[]{:S(2)}, u32[]{:S(2)}) collective-permute-start(bf16[5,16,128]{2,1,0:T(8,128)(2,1)S(1)} %get-tuple-element.70), channel_id=1, source_target_pairs={{0,16},{1,17},{2,18},{3,19},{4,20},{5,21},{6,22},{7,23},{8,24},{9,... | collective-permute-start | bytes 61448 | tf_op jit(solution)/shard_map/ppermute | solution.py:763
  20.8 0.5 %collective-permute-start.10 = (bf16[240,128]{1,0:T(8,128)(2,1)S(1)}, bf16[240,128]{1,0:T(8,128)(2,1)S(1)}, u32[]{:S(2)}, u32[]{:S(2)}) collective-permute-start(bf16[240,128]{1,0:T(8,128)(2,1)S(1)} %get-tuple-element.73), channel_id=1, source_target_pairs={{0,1},{1,0},{2,3},{3,2},{4,5},{5,4},{6,7},{7,6},{8,9},{9,8},{10,11... | collective-permute-start | bytes 184328 | tf_op jit(solution)/shard_map/ppermute | solution.py:763
  21.3 1.1 %collective-permute-start.9 = (bf16[5,16,128]{2,1,0:T(8,128)(2,1)S(1)}, bf16[5,16,128]{2,1,0:T(8,128)(2,1)S(1)}, u32[]{:S(2)}, u32[]{:S(2)}) collective-permute-start(bf16[5,16,128]{2,1,0:T(8,128)(2,1)S(1)} %broadcast_multiply_fusion), channel_id=1, source_target_pairs={{0,20},{1,21},{2,22},{3,23},{4,16},{5,17},{6,18},{7,19},{8,28},{9,... | collective-permute-start | bytes 61448 | tf_op jit(solution)/shard_map/ppermute | solution.py:763
  22.4 0.1 collective-permute-start.11
  22.6 3.4 %collective-permute-done.9.refs_2_ = bf16[5,16,128]{2,1,0:T(8,128)(2,1)S(1)} collective-permute-done((bf16[5,16,128]{2,1,0:T(8,128)(2,1)S(1)}, bf16[5,16,128]{2,1,0:T(8,128)(2,1)S(1)}, u32[]{:S(2)}, u32[]{:S(2)}) %collective-permute-start.9) | collective-permute-done | bytes 20512 | tf_op jit(solution)/shard_map/ppermute | solution.py:763
  26.0 1.1 %collective-permute-done.11.refs_4_ = bf16[5,16,128]{2,1,0:T(8,128)(2,1)S(1)} collective-permute-done((bf16[5,16,128]{2,1,0:T(8,128)(2,1)S(1)}, bf16[5,16,128]{2,1,0:T(8,128)(2,1)S(1)}, u32[]{:S(2)}, u32[]{:S(2)}) %collective-permute-start.11) | collective-permute-done | bytes 20512 | tf_op jit(solution)/shard_map/ppermute | solution.py:763
  27.1 0.1 collective-permute-start.13
  27.2 0.5 %collective-permute-start.12 = (bf16[128,128]{1,0:T(8,128)(2,1)S(1)}, bf16[128,128]{1,0:T(8,128)(2,1)S(1)}, u32[]{:S(2)}, u32[]{:S(2)}) collective-permute-start(bf16[128,128]{1,0:T(8,128)(2,1)S(1)} %pad_maximum_fusion), channel_id=1, source_target_pairs={{0,1},{1,2},{2,3},{3,0},{4,5},{5,6},{6,7},{7,4},{8,9},{9,10},{10,1... | collective-permute-start | bytes 98312 | tf_op jit(solution)/shard_map/ppermute | solution.py:763
  27.7 1.4 %second_middle.1 = (f32[96,128]{1,0:T(8,128)S(1)}, f32[4,48,128]{2,1,0:T(8,128)S(1)}, bf16[20,240,128]{2,1,0:T(8,128)(2,1)S(1)}) custom-call(s32[4]{0:T(128)S(1)} %pad_add_fusion.flags.refs_0_, bf16[16,80,128]{2,1,0:T(8,128)(2,1)S(1)} %get-tuple-element.68.refs_1_, bf16[5,16,128]{2,1,0:T(8,128)(2,1)S(1)} %collective-permute-done.9.refs_2_, ...), custom_call_target="tpu_custom_call" | custom-call | tf_op jit(solution)/shard_map/second_middle/pallas_call | solution.py:850
  29.1 1.5 %collective-permute-done.12.refs_3_ = bf16[128,128]{1,0:T(8,128)(2,1)S(1)} collective-permute-done((bf16[128,128]{1,0:T(8,128)(2,1)S(1)}, bf16[128,128]{1,0:T(8,128)(2,1)S(1)}, u32[]{:S(2)}, u32[]{:S(2)}) %collective-permute-start.12) | collective-permute-done | bytes 32800 | tf_op jit(solution)/shard_map/ppermute | solution.py:763
  30.6 3.3 %second_step.1 = bf16[80,16,128]{2,1,0:T(8,128)(2,1)} custom-call(s32[4]{0:T(128)S(1)} %pad_add_fusion.flags.refs_0_, bf16[16,80,128]{2,1,0:T(8,128)(2,1)S(1)} %get-tuple-element.68.refs_1_, s32[16,128]{1,0:T(8,128)S(1)} %copy-done.1, bf16[128,128]{1,0:T(8,128)(2,1)S(1)} %collective-permute-done.12.refs_3_, ...), custom_call_target="tpu_custom_call" | custom-call | tf_op jit(solution)/shard_map/second_step/pallas_call | solution.py:850
  (29 shorter events, 0.2 us)
Async XLA Ops:
  0.0 14.8 %copy-start.1 = (s32[16,128]{1,0:T(8,128)S(1)}, s32[16,128]{1,0:T(8,128)}, u32[]{:S(2)}) copy-start(s32[16,128]{1,0:T(8,128)} %refs_2_.3) | copy-start | bytes 24580
  0.0 14.8 %copy-start.2 = (f32[2,4,80]{2,1,0:T(4,128)S(1)}, f32[2,4,80]{2,1,0:T(4,128)}, u32[]{:S(2)}) copy-start(f32[2,4,80]{2,1,0:T(4,128)} %refs_14_.1) | copy-start | bytes 7684
  0.0 14.8 %copy-start = (bf16[80,384]{1,0:T(8,128)(2,1)S(1)}, bf16[80,384]{1,0:T(8,128)(2,1)}, u32[]{:S(2)}) copy-start(bf16[80,384]{1,0:T(8,128)(2,1)} %refs_13_.3) | copy-start | bytes 184324
  2.3 6.1 %collective-permute-start = (bf16[5,16,128]{2,1,0:T(8,128)(2,1)S(1)}, bf16[5,16,128]{2,1,0:T(8,128)(2,1)S(1)}, u32[]{:S(2)}, u32[]{:S(2)}) collective-permute-start(bf16[5,16,128]{2,1,0:T(8,128)(2,1)S(1)} %get-tuple-element.47), channel_id=1, source_target_pairs={{0,16},{1,17},{2,18},{3,19},{4,20},{5,21},{6,22},{7,23},{8,24},{9,... | collective-permute-start | bytes 61448 | tf_op jit(solution)/shard_map/ppermute | solution.py:763
  3.9 4.6 %collective-permute-start.1 = (bf16[272,128]{1,0:T(8,128)(2,1)S(1)}, bf16[272,128]{1,0:T(8,128)(2,1)S(1)}, u32[]{:S(2)}, u32[]{:S(2)}) collective-permute-start(bf16[272,128]{1,0:T(8,128)(2,1)S(1)} %get-tuple-element.48), channel_id=1, source_target_pairs={{0,1},{1,0},{2,3},{3,2},{4,5},{5,4},{6,7},{7,6},{8,9},{9,8},{10,11... | collective-permute-start | bytes 208904 | tf_op jit(solution)/shard_map/ppermute | solution.py:763
  3.9 4.6 %collective-permute-start.3 = (bf16[272,128]{1,0:T(8,128)(2,1)S(1)}, bf16[272,128]{1,0:T(8,128)(2,1)S(1)}, u32[]{:S(2)}, u32[]{:S(2)}) collective-permute-start(bf16[272,128]{1,0:T(8,128)(2,1)S(1)} %get-tuple-element.50), channel_id=1, source_target_pairs={{0,1},{1,0},{2,3},{3,2},{4,5},{5,4},{6,7},{7,6},{8,9},{9,8},{10,11... | collective-permute-start | bytes 208904 | tf_op jit(solution)/shard_map/ppermute | solution.py:763
  4.4 4.7 %collective-permute-start.2 = (bf16[5,16,128]{2,1,0:T(8,128)(2,1)S(1)}, bf16[5,16,128]{2,1,0:T(8,128)(2,1)S(1)}, u32[]{:S(2)}, u32[]{:S(2)}) collective-permute-start(bf16[5,16,128]{2,1,0:T(8,128)(2,1)S(1)} %broadcast_multiply_fusion.1), channel_id=1, source_target_pairs={{0,20},{1,21},{2,22},{3,23},{4,16},{5,17},{6,18},{7,19},{8,28},{9,... | collective-permute-start | bytes 61448 | tf_op jit(solution)/shard_map/ppermute | solution.py:763
  5.9 4.7 %collective-permute-start.4 = (bf16[5,16,128]{2,1,0:T(8,128)(2,1)S(1)}, bf16[5,16,128]{2,1,0:T(8,128)(2,1)S(1)}, u32[]{:S(2)}, u32[]{:S(2)}) collective-permute-start(bf16[5,16,128]{2,1,0:T(8,128)(2,1)S(1)} %broadcast_multiply_fusion.1), channel_id=1, source_target_pairs={{0,1},{1,0},{2,3},{3,2},{4,24},{5,25},{6,26},{7,27},{8,20},{9,21},... | collective-permute-start | bytes 61448 | tf_op jit(solution)/shard_map/ppermute | solution.py:763
  10.7 2.5 %collective-permute-start.6 = (bf16[176,128]{1,0:T(8,128)(2,1)S(1)}, bf16[176,128]{1,0:T(8,128)(2,1)S(1)}, u32[]{:S(2)}, u32[]{:S(2)}) collective-permute-start(bf16[176,128]{1,0:T(8,128)(2,1)S(1)} %constant_dynamic-update-slice_fusion), channel_id=1, source_target_pairs={{0,3},{1,0},{2,1},{3,2},{4,7},{5,4},{6,5},{7,6},{8,11},{9,8},{10,9... | collective-permute-start | bytes 135176 | tf_op jit(solution)/shard_map/ppermute | solution.py:763
  10.9 3.9 %collective-permute-start.5 = (bf16[176,128]{1,0:T(8,128)(2,1)S(1)}, bf16[176,128]{1,0:T(8,128)(2,1)S(1)}, u32[]{:S(2)}, u32[]{:S(2)}) collective-permute-start(bf16[176,128]{1,0:T(8,128)(2,1)S(1)} %constant_dynamic-update-slice_fusion), channel_id=1, source_target_pairs={{0,1},{1,2},{2,3},{3,0},{4,5},{5,6},{6,7},{7,4},{8,9},{9,10},{10,1... | collective-permute-start | bytes 135176 | tf_op jit(solution)/shard_map/ppermute | solution.py:763
  17.5 5.1 %collective-permute-start.7 = (bf16[5,16,128]{2,1,0:T(8,128)(2,1)S(1)}, bf16[5,16,128]{2,1,0:T(8,128)(2,1)S(1)}, u32[]{:S(2)}, u32[]{:S(2)}) collective-permute-start(bf16[5,16,128]{2,1,0:T(8,128)(2,1)S(1)} %get-tuple-element.70), channel_id=1, source_target_pairs={{0,16},{1,17},{2,18},{3,19},{4,20},{5,21},{6,22},{7,23},{8,24},{9,... | collective-permute-start | bytes 61448 | tf_op jit(solution)/shard_map/ppermute | solution.py:763
  20.8 1.8 %collective-permute-start.8 = (bf16[240,128]{1,0:T(8,128)(2,1)S(1)}, bf16[240,128]{1,0:T(8,128)(2,1)S(1)}, u32[]{:S(2)}, u32[]{:S(2)}) collective-permute-start(bf16[240,128]{1,0:T(8,128)(2,1)S(1)} %get-tuple-element.71), channel_id=1, source_target_pairs={{0,1},{1,0},{2,3},{3,2},{4,5},{5,4},{6,7},{7,6},{8,9},{9,8},{10,11... | collective-permute-start | bytes 184328 | tf_op jit(solution)/shard_map/ppermute | solution.py:763
  20.8 1.8 %collective-permute-start.10 = (bf16[240,128]{1,0:T(8,128)(2,1)S(1)}, bf16[240,128]{1,0:T(8,128)(2,1)S(1)}, u32[]{:S(2)}, u32[]{:S(2)}) collective-permute-start(bf16[240,128]{1,0:T(8,128)(2,1)S(1)} %get-tuple-element.73), channel_id=1, source_target_pairs={{0,1},{1,0},{2,3},{3,2},{4,5},{5,4},{6,7},{7,6},{8,9},{9,8},{10,11... | collective-permute-start | bytes 184328 | tf_op jit(solution)/shard_map/ppermute | solution.py:763
  21.3 4.7 %collective-permute-start.9 = (bf16[5,16,128]{2,1,0:T(8,128)(2,1)S(1)}, bf16[5,16,128]{2,1,0:T(8,128)(2,1)S(1)}, u32[]{:S(2)}, u32[]{:S(2)}) collective-permute-start(bf16[5,16,128]{2,1,0:T(8,128)(2,1)S(1)} %broadcast_multiply_fusion), channel_id=1, source_target_pairs={{0,20},{1,21},{2,22},{3,23},{4,16},{5,17},{6,18},{7,19},{8,28},{9,... | collective-permute-start | bytes 61448 | tf_op jit(solution)/shard_map/ppermute | solution.py:763
  22.4 4.7 %collective-permute-start.11 = (bf16[5,16,128]{2,1,0:T(8,128)(2,1)S(1)}, bf16[5,16,128]{2,1,0:T(8,128)(2,1)S(1)}, u32[]{:S(2)}, u32[]{:S(2)}) collective-permute-start(bf16[5,16,128]{2,1,0:T(8,128)(2,1)S(1)} %broadcast_multiply_fusion), channel_id=1, source_target_pairs={{0,1},{1,0},{2,3},{3,2},{4,24},{5,25},{6,26},{7,27},{8,20},{9,21},... | collective-permute-start | bytes 61448 | tf_op jit(solution)/shard_map/ppermute | solution.py:763
  27.1 2.0 %collective-permute-start.13 = (bf16[128,128]{1,0:T(8,128)(2,1)S(1)}, bf16[128,128]{1,0:T(8,128)(2,1)S(1)}, u32[]{:S(2)}, u32[]{:S(2)}) collective-permute-start(bf16[128,128]{1,0:T(8,128)(2,1)S(1)} %pad_maximum_fusion), channel_id=1, source_target_pairs={{0,3},{1,0},{2,1},{3,2},{4,7},{5,4},{6,5},{7,6},{8,11},{9,8},{10,9... | collective-permute-start | bytes 98312 | tf_op jit(solution)/shard_map/ppermute | solution.py:763
  27.2 3.4 %collective-permute-start.12 = (bf16[128,128]{1,0:T(8,128)(2,1)S(1)}, bf16[128,128]{1,0:T(8,128)(2,1)S(1)}, u32[]{:S(2)}, u32[]{:S(2)}) collective-permute-start(bf16[128,128]{1,0:T(8,128)(2,1)S(1)} %pad_maximum_fusion), channel_id=1, source_target_pairs={{0,1},{1,2},{2,3},{3,0},{4,5},{5,6},{6,7},{7,4},{8,9},{9,10},{10,1... | collective-permute-start | bytes 98312 | tf_op jit(solution)/shard_map/ppermute | solution.py:763

commit v19 on v18

--- a/solution.py
+++ b/solution.py
@@ -340,7 +340,8 @@
     return x + x * jnp.tanh(x * (scale + (scale * 0.044715) * (x * x)))
 
 
-def staggered(count, *stages):
+def staggered(count, *stages, between=()):
+    between = list(between)
     values = [{} for _ in stages]
     for turn in range(count + len(stages) - 1):
         for index, stage in enumerate(stages):
@@ -348,6 +349,10 @@
             if 0 <= step < count:
                 given = values[index - 1].pop(step) if index else None
                 values[index][step] = stage(step, given)
+        if between:
+            between.pop(0)()
+    for extra in between:
+        extra()
 
 
 def air(state, out, forcing_x, air_in, atm_out, d):
@@ -491,16 +496,29 @@
         hidden[step, HIDK:HIDP, :] = blank
         hidden[step + pairs, HIDK:HIDP, :] = blank
 
-    staggered(pairs, first, activate)
-    product = jnp.dot(ocn_in[...], side[...], preferred_element_type=F32)
-    spot = lanes((1, d.edge)) % block
-    gone = ((spot == 0) & (at_top != 0)) | ((spot == rows + 1) & (at_bottom != 0))
-    active = jnp.where(gone, 0.0, twice_gelu(product)).astype(BF16)
-    active = jnp.concatenate([active, jnp.zeros((HIDP - HIDK, d.edge), BF16)], axis=0)
-
-    taps = jnp.concatenate([roll(active, -tap) for tap in range(3)], axis=0)
-    from_left = jnp.dot(ocn_out[0:CH, :], taps, preferred_element_type=F32)
-    from_right = jnp.dot(ocn_out[2 * CH : 3 * CH, :], taps, preferred_element_type=F32)
+    held = {}
+
+    def edge_first():
+        held["product"] = jnp.dot(ocn_in[...], side[...], preferred_element_type=F32)
+
+    def edge_activate():
+        spot = lanes((1, d.edge)) % block
+        gone = ((spot == 0) & (at_top != 0)) | ((spot == rows + 1) & (at_bottom != 0))
+        active = jnp.where(gone, 0.0, twice_gelu(held["product"])).astype(BF16)
+        active = jnp.concatenate([active, jnp.zeros((HIDP - HIDK, d.edge), BF16)], axis=0)
+        held["taps"] = jnp.concatenate([roll(active, -tap) for tap in range(3)], axis=0)
+
+    def edge_second():
+        held["left"] = jnp.dot(ocn_out[0:CH, :], held["taps"], preferred_element_type=F32)
+        held["right"] = jnp.dot(
+            ocn_out[2 * CH : 3 * CH, :], held["taps"], preferred_element_type=F32
+        )
+
+    wait = lambda: None
+    staggered(
+        pairs, first, activate, between=(edge_first, wait, edge_activate, wait, edge_second)
+    )
+    from_left, from_right = held["left"], held["right"]
     half = rows // 2
 
     def second(step, _):

time: 34.1 us -> 34 us (level)
  no operation moved by 1% of the time
where the time goes in v19:
time: 34 us; the launch traced here: 33.8 us
  starting transfers between devices  12.2 us (36%)
  Pallas kernels  11.5 us (34%)
  waiting for transfers between devices  9.79 us (29%)
    ppermute x14, starting transfers between devices, send(): return lax.ppermute(x, names, pairs)  12.2 us
    pallas_call x5, Pallas kernels, call(): pl.pallas_call(kernel, out_shape=outs, in_specs=[SMEM] + [VMEM] * len(ope...  11.5 us
    ppermute x14, waiting for transfers between devices, send(): return lax.ppermute(x, names, pairs)  9.79 us
  transfers between devices with their start and end apart: 14, of which 6 were waited for; matrix products, arithmetic and copies ran while one was open for 0% of the time, Pallas kernels for 10%

profile of v19, /device:TPU:8, one launch (start us, length us, event | category | flops | bytes accessed | tf_op | source)
XLA Modules:
  0.0 33.8 jit_solution(5959927659846283736)
XLA Ops:
  0.0 0.1 pad_add_fusion.flags.refs_0_
  0.1 2.2 %start.1 = (bf16[16,80,128]{2,1,0:T(8,128)(2,1)S(1)}, bf16[8,16,128]{2,1,0:T(8,128)(2,1)S(1)}, bf16[16,128]{1,0:T(8,128)(2,1)S(1)}, bf16[2048,128]{1,0:T(8,128)(...) custom-call(s32[4]{0:T(128)S(1)} %pad_add_fusion.flags.refs_0_, ...), custom_call_target="tpu_custom_call" | custom-call | tf_op jit(solution)/shard_map/start/pallas_call | solution.py:868
  2.3 1.6 %collective-permute-start = (bf16[5,16,128]{2,1,0:T(8,128)(2,1)S(1)}, bf16[5,16,128]{2,1,0:T(8,128)(2,1)S(1)}, u32[]{:S(2)}, u32[]{:S(2)}) collective-permute-start(bf16[5,16,128]{2,1,0:T(8,128)(2,1)S(1)} %get-tuple-element.47), channel_id=1, source_target_pairs={{0,16},{1,17},{2,18},{3,19},{4,20},{5,21},{6,22},{7,23},{8,24},{9,... | collective-permute-start | bytes 61448 | tf_op jit(solution)/shard_map/ppermute | solution.py:781
  3.9 0.5 %collective-permute-start.3 = (bf16[272,128]{1,0:T(8,128)(2,1)S(1)}, bf16[272,128]{1,0:T(8,128)(2,1)S(1)}, u32[]{:S(2)}, u32[]{:S(2)}) collective-permute-start(bf16[272,128]{1,0:T(8,128)(2,1)S(1)} %get-tuple-element.50), channel_id=1, source_target_pairs={{0,1},{1,0},{2,3},{3,2},{4,5},{5,4},{6,7},{7,6},{8,9},{9,8},{10,11... | collective-permute-start | bytes 208904 | tf_op jit(solution)/shard_map/ppermute | solution.py:781
  4.4 1.5 %collective-permute-start.2 = (bf16[5,16,128]{2,1,0:T(8,128)(2,1)S(1)}, bf16[5,16,128]{2,1,0:T(8,128)(2,1)S(1)}, u32[]{:S(2)}, u32[]{:S(2)}) collective-permute-start(bf16[5,16,128]{2,1,0:T(8,128)(2,1)S(1)} %broadcast_multiply_fusion.1), channel_id=1, source_target_pairs={{0,20},{1,21},{2,22},{3,23},{4,16},{5,17},{6,18},{7,19},{8,28},{9,... | collective-permute-start | bytes 61448 | tf_op jit(solution)/shard_map/ppermute | solution.py:781
  5.9 2.5 %collective-permute-start.4 = (bf16[5,16,128]{2,1,0:T(8,128)(2,1)S(1)}, bf16[5,16,128]{2,1,0:T(8,128)(2,1)S(1)}, u32[]{:S(2)}, u32[]{:S(2)}) collective-permute-start(bf16[5,16,128]{2,1,0:T(8,128)(2,1)S(1)} %broadcast_multiply_fusion.1), channel_id=1, source_target_pairs={{0,1},{1,0},{2,3},{3,2},{4,24},{5,25},{6,26},{7,27},{8,20},{9,21},... | collective-permute-start | bytes 61448 | tf_op jit(solution)/shard_map/ppermute | solution.py:781
  8.4 0.6 %collective-permute-done.2.refs_2_ = bf16[5,16,128]{2,1,0:T(8,128)(2,1)S(1)} collective-permute-done((bf16[5,16,128]{2,1,0:T(8,128)(2,1)S(1)}, bf16[5,16,128]{2,1,0:T(8,128)(2,1)S(1)}, u32[]{:S(2)}, u32[]{:S(2)}) %collective-permute-start.2) | collective-permute-done | bytes 20512 | tf_op jit(solution)/shard_map/ppermute | solution.py:781
  9.1 1.5 %collective-permute-done.4.refs_4_ = bf16[5,16,128]{2,1,0:T(8,128)(2,1)S(1)} collective-permute-done((bf16[5,16,128]{2,1,0:T(8,128)(2,1)S(1)}, bf16[5,16,128]{2,1,0:T(8,128)(2,1)S(1)}, u32[]{:S(2)}, u32[]{:S(2)}) %collective-permute-start.4) | collective-permute-done | bytes 20512 | tf_op jit(solution)/shard_map/ppermute | solution.py:781
  10.7 0.2 collective-permute-start.6
  10.9 0.4 %collective-permute-start.5 = (bf16[176,128]{1,0:T(8,128)(2,1)S(1)}, bf16[176,128]{1,0:T(8,128)(2,1)S(1)}, u32[]{:S(2)}, u32[]{:S(2)}) collective-permute-start(bf16[176,128]{1,0:T(8,128)(2,1)S(1)} %constant_dynamic-update-slice_fusion), channel_id=1, source_target_pairs={{0,1},{1,2},{2,3},{3,0},{4,5},{5,6},{6,7},{7,4},{8,9},{9,10},{10,1... | collective-permute-start | bytes 135176 | tf_op jit(solution)/shard_map/ppermute | solution.py:781
  11.3 1.9 %first_middle.1 = (f32[96,128]{1,0:T(8,128)S(1)}, f32[4,48,128]{2,1,0:T(8,128)S(1)}, bf16[20,240,128]{2,1,0:T(8,128)(2,1)S(1)}, f32[192,128]{1,0:T(8,128)S(1)}, ...) custom-call(s32[4]{0:T(128)S(1)} %pad_add_fusion.flags.refs_0_, ...), custom_call_target="tpu_custom_call" | custom-call | tf_op jit(solution)/shard_map/first_middle/pallas_call | solution.py:868
  13.2 1.6 %collective-permute-done.5.refs_3_ = bf16[176,128]{1,0:T(8,128)(2,1)S(1)} collective-permute-done((bf16[176,128]{1,0:T(8,128)(2,1)S(1)}, bf16[176,128]{1,0:T(8,128)(2,1)S(1)}, u32[]{:S(2)}, u32[]{:S(2)}) %collective-permute-start.5) | collective-permute-done | bytes 45088 | tf_op jit(solution)/shard_map/ppermute | solution.py:781
  14.8 2.7 %first_step.1 = (bf16[16,80,128]{2,1,0:T(8,128)(2,1)S(1)}, bf16[5,16,128]{2,1,0:T(8,128)(2,1)S(1)}, bf16[80,128]{1,0:T(8,128)(2,1)S(1)}, bf16[240,128]{1,0:T(8,1...) custom-call(s32[4]{0:T(128)S(1)} %pad_add_fusion.flags.refs_0_, ...), custom_call_target="tpu_custom_call" | custom-call | tf_op jit(solution)/shard_map/first_step/pallas_call | solution.py:868
  17.5 3.3 %collective-permute-start.7 = (bf16[5,16,128]{2,1,0:T(8,128)(2,1)S(1)}, bf16[5,16,128]{2,1,0:T(8,128)(2,1)S(1)}, u32[]{:S(2)}, u32[]{:S(2)}) collective-permute-start(bf16[5,16,128]{2,1,0:T(8,128)(2,1)S(1)} %get-tuple-element.70), channel_id=1, source_target_pairs={{0,16},{1,17},{2,18},{3,19},{4,20},{5,21},{6,22},{7,23},{8,24},{9,... | collective-permute-start | bytes 61448 | tf_op jit(solution)/shard_map/ppermute | solution.py:781
  20.8 0.5 %collective-permute-start.10 = (bf16[240,128]{1,0:T(8,128)(2,1)S(1)}, bf16[240,128]{1,0:T(8,128)(2,1)S(1)}, u32[]{:S(2)}, u32[]{:S(2)}) collective-permute-start(bf16[240,128]{1,0:T(8,128)(2,1)S(1)} %get-tuple-element.73), channel_id=1, source_target_pairs={{0,1},{1,0},{2,3},{3,2},{4,5},{5,4},{6,7},{7,6},{8,9},{9,8},{10,11... | collective-permute-start | bytes 184328 | tf_op jit(solution)/shard_map/ppermute | solution.py:781
  21.3 1.1 %collective-permute-start.9 = (bf16[5,16,128]{2,1,0:T(8,128)(2,1)S(1)}, bf16[5,16,128]{2,1,0:T(8,128)(2,1)S(1)}, u32[]{:S(2)}, u32[]{:S(2)}) collective-permute-start(bf16[5,16,128]{2,1,0:T(8,128)(2,1)S(1)} %broadcast_multiply_fusion), channel_id=1, source_target_pairs={{0,20},{1,21},{2,22},{3,23},{4,16},{5,17},{6,18},{7,19},{8,28},{9,... | collective-permute-start | bytes 61448 | tf_op jit(solution)/shard_map/ppermute | solution.py:781
  22.4 0.1 collective-permute-start.11
  22.5 3.4 %collective-permute-done.9.refs_2_ = bf16[5,16,128]{2,1,0:T(8,128)(2,1)S(1)} collective-permute-done((bf16[5,16,128]{2,1,0:T(8,128)(2,1)S(1)}, bf16[5,16,128]{2,1,0:T(8,128)(2,1)S(1)}, u32[]{:S(2)}, u32[]{:S(2)}) %collective-permute-start.9) | collective-permute-done | bytes 20512 | tf_op jit(solution)/shard_map/ppermute | solution.py:781
  25.9 1.1 %collective-permute-done.11.refs_4_ = bf16[5,16,128]{2,1,0:T(8,128)(2,1)S(1)} collective-permute-done((bf16[5,16,128]{2,1,0:T(8,128)(2,1)S(1)}, bf16[5,16,128]{2,1,0:T(8,128)(2,1)S(1)}, u32[]{:S(2)}, u32[]{:S(2)}) %collective-permute-start.11) | collective-permute-done | bytes 20512 | tf_op jit(solution)/shard_map/ppermute | solution.py:781
  27.1 0.1 collective-permute-start.13
  27.1 0.5 %collective-permute-start.12 = (bf16[128,128]{1,0:T(8,128)(2,1)S(1)}, bf16[128,128]{1,0:T(8,128)(2,1)S(1)}, u32[]{:S(2)}, u32[]{:S(2)}) collective-permute-start(bf16[128,128]{1,0:T(8,128)(2,1)S(1)} %pad_maximum_fusion), channel_id=1, source_target_pairs={{0,1},{1,2},{2,3},{3,0},{4,5},{5,6},{6,7},{7,4},{8,9},{9,10},{10,1... | collective-permute-start | bytes 98312 | tf_op jit(solution)/shard_map/ppermute | solution.py:781
  27.6 1.4 %second_middle.1 = (f32[96,128]{1,0:T(8,128)S(1)}, f32[4,48,128]{2,1,0:T(8,128)S(1)}, bf16[20,240,128]{2,1,0:T(8,128)(2,1)S(1)}) custom-call(s32[4]{0:T(128)S(1)} %pad_add_fusion.flags.refs_0_, bf16[16,80,128]{2,1,0:T(8,128)(2,1)S(1)} %get-tuple-element.68.refs_1_, bf16[5,16,128]{2,1,0:T(8,128)(2,1)S(1)} %collective-permute-done.9.refs_2_, ...), custom_call_target="tpu_custom_call" | custom-call | tf_op jit(solution)/shard_map/second_middle/pallas_call | solution.py:868
  29.1 1.5 %collective-permute-done.12.refs_3_ = bf16[128,128]{1,0:T(8,128)(2,1)S(1)} collective-permute-done((bf16[128,128]{1,0:T(8,128)(2,1)S(1)}, bf16[128,128]{1,0:T(8,128)(2,1)S(1)}, u32[]{:S(2)}, u32[]{:S(2)}) %collective-permute-start.12) | collective-permute-done | bytes 32800 | tf_op jit(solution)/shard_map/ppermute | solution.py:781
  30.5 3.3 %second_step.1 = bf16[80,16,128]{2,1,0:T(8,128)(2,1)} custom-call(s32[4]{0:T(128)S(1)} %pad_add_fusion.flags.refs_0_, bf16[16,80,128]{2,1,0:T(8,128)(2,1)S(1)} %get-tuple-element.68.refs_1_, s32[16,128]{1,0:T(8,128)S(1)} %copy-done.1, bf16[128,128]{1,0:T(8,128)(2,1)S(1)} %collective-permute-done.12.refs_3_, ...), custom_call_target="tpu_custom_call" | custom-call | tf_op jit(solution)/shard_map/second_step/pallas_call | solution.py:868
  (29 shorter events, 0.2 us)
Async XLA Ops:
  0.0 14.8 %copy-start.1 = (s32[16,128]{1,0:T(8,128)S(1)}, s32[16,128]{1,0:T(8,128)}, u32[]{:S(2)}) copy-start(s32[16,128]{1,0:T(8,128)} %refs_2_.3) | copy-start | bytes 24580
  0.0 14.8 %copy-start.2 = (f32[2,4,80]{2,1,0:T(4,128)S(1)}, f32[2,4,80]{2,1,0:T(4,128)}, u32[]{:S(2)}) copy-start(f32[2,4,80]{2,1,0:T(4,128)} %refs_14_.1) | copy-start | bytes 7684
  0.0 14.8 %copy-start = (bf16[80,384]{1,0:T(8,128)(2,1)S(1)}, bf16[80,384]{1,0:T(8,128)(2,1)}, u32[]{:S(2)}) copy-start(bf16[80,384]{1,0:T(8,128)(2,1)} %refs_13_.3) | copy-start | bytes 184324
  2.3 6.1 %collective-permute-start = (bf16[5,16,128]{2,1,0:T(8,128)(2,1)S(1)}, bf16[5,16,128]{2,1,0:T(8,128)(2,1)S(1)}, u32[]{:S(2)}, u32[]{:S(2)}) collective-permute-start(bf16[5,16,128]{2,1,0:T(8,128)(2,1)S(1)} %get-tuple-element.47), channel_id=1, source_target_pairs={{0,16},{1,17},{2,18},{3,19},{4,20},{5,21},{6,22},{7,23},{8,24},{9,... | collective-permute-start | bytes 61448 | tf_op jit(solution)/shard_map/ppermute | solution.py:781
  3.9 4.6 %collective-permute-start.1 = (bf16[272,128]{1,0:T(8,128)(2,1)S(1)}, bf16[272,128]{1,0:T(8,128)(2,1)S(1)}, u32[]{:S(2)}, u32[]{:S(2)}) collective-permute-start(bf16[272,128]{1,0:T(8,128)(2,1)S(1)} %get-tuple-element.48), channel_id=1, source_target_pairs={{0,1},{1,0},{2,3},{3,2},{4,5},{5,4},{6,7},{7,6},{8,9},{9,8},{10,11... | collective-permute-start | bytes 208904 | tf_op jit(solution)/shard_map/ppermute | solution.py:781
  3.9 4.6 %collective-permute-start.3 = (bf16[272,128]{1,0:T(8,128)(2,1)S(1)}, bf16[272,128]{1,0:T(8,128)(2,1)S(1)}, u32[]{:S(2)}, u32[]{:S(2)}) collective-permute-start(bf16[272,128]{1,0:T(8,128)(2,1)S(1)} %get-tuple-element.50), channel_id=1, source_target_pairs={{0,1},{1,0},{2,3},{3,2},{4,5},{5,4},{6,7},{7,6},{8,9},{9,8},{10,11... | collective-permute-start | bytes 208904 | tf_op jit(solution)/shard_map/ppermute | solution.py:781
  4.4 4.7 %collective-permute-start.2 = (bf16[5,16,128]{2,1,0:T(8,128)(2,1)S(1)}, bf16[5,16,128]{2,1,0:T(8,128)(2,1)S(1)}, u32[]{:S(2)}, u32[]{:S(2)}) collective-permute-start(bf16[5,16,128]{2,1,0:T(8,128)(2,1)S(1)} %broadcast_multiply_fusion.1), channel_id=1, source_target_pairs={{0,20},{1,21},{2,22},{3,23},{4,16},{5,17},{6,18},{7,19},{8,28},{9,... | collective-permute-start | bytes 61448 | tf_op jit(solution)/shard_map/ppermute | solution.py:781
  5.9 4.7 %collective-permute-start.4 = (bf16[5,16,128]{2,1,0:T(8,128)(2,1)S(1)}, bf16[5,16,128]{2,1,0:T(8,128)(2,1)S(1)}, u32[]{:S(2)}, u32[]{:S(2)}) collective-permute-start(bf16[5,16,128]{2,1,0:T(8,128)(2,1)S(1)} %broadcast_multiply_fusion.1), channel_id=1, source_target_pairs={{0,1},{1,0},{2,3},{3,2},{4,24},{5,25},{6,26},{7,27},{8,20},{9,21},... | collective-permute-start | bytes 61448 | tf_op jit(solution)/shard_map/ppermute | solution.py:781
  10.7 2.5 %collective-permute-start.6 = (bf16[176,128]{1,0:T(8,128)(2,1)S(1)}, bf16[176,128]{1,0:T(8,128)(2,1)S(1)}, u32[]{:S(2)}, u32[]{:S(2)}) collective-permute-start(bf16[176,128]{1,0:T(8,128)(2,1)S(1)} %constant_dynamic-update-slice_fusion), channel_id=1, source_target_pairs={{0,3},{1,0},{2,1},{3,2},{4,7},{5,4},{6,5},{7,6},{8,11},{9,8},{10,9... | collective-permute-start | bytes 135176 | tf_op jit(solution)/shard_map/ppermute | solution.py:781
  10.9 3.9 %collective-permute-start.5 = (bf16[176,128]{1,0:T(8,128)(2,1)S(1)}, bf16[176,128]{1,0:T(8,128)(2,1)S(1)}, u32[]{:S(2)}, u32[]{:S(2)}) collective-permute-start(bf16[176,128]{1,0:T(8,128)(2,1)S(1)} %constant_dynamic-update-slice_fusion), channel_id=1, source_target_pairs={{0,1},{1,2},{2,3},{3,0},{4,5},{5,6},{6,7},{7,4},{8,9},{9,10},{10,1... | collective-permute-start | bytes 135176 | tf_op jit(solution)/shard_map/ppermute | solution.py:781
  17.5 5.0 %collective-permute-start.7 = (bf16[5,16,128]{2,1,0:T(8,128)(2,1)S(1)}, bf16[5,16,128]{2,1,0:T(8,128)(2,1)S(1)}, u32[]{:S(2)}, u32[]{:S(2)}) collective-permute-start(bf16[5,16,128]{2,1,0:T(8,128)(2,1)S(1)} %get-tuple-element.70), channel_id=1, source_target_pairs={{0,16},{1,17},{2,18},{3,19},{4,20},{5,21},{6,22},{7,23},{8,24},{9,... | collective-permute-start | bytes 61448 | tf_op jit(solution)/shard_map/ppermute | solution.py:781
  20.7 1.8 %collective-permute-start.8 = (bf16[240,128]{1,0:T(8,128)(2,1)S(1)}, bf16[240,128]{1,0:T(8,128)(2,1)S(1)}, u32[]{:S(2)}, u32[]{:S(2)}) collective-permute-start(bf16[240,128]{1,0:T(8,128)(2,1)S(1)} %get-tuple-element.71), channel_id=1, source_target_pairs={{0,1},{1,0},{2,3},{3,2},{4,5},{5,4},{6,7},{7,6},{8,9},{9,8},{10,11... | collective-permute-start | bytes 184328 | tf_op jit(solution)/shard_map/ppermute | solution.py:781
  20.8 1.8 %collective-permute-start.10 = (bf16[240,128]{1,0:T(8,128)(2,1)S(1)}, bf16[240,128]{1,0:T(8,128)(2,1)S(1)}, u32[]{:S(2)}, u32[]{:S(2)}) collective-permute-start(bf16[240,128]{1,0:T(8,128)(2,1)S(1)} %get-tuple-element.73), channel_id=1, source_target_pairs={{0,1},{1,0},{2,3},{3,2},{4,5},{5,4},{6,7},{7,6},{8,9},{9,8},{10,11... | collective-permute-start | bytes 184328 | tf_op jit(solution)/shard_map/ppermute | solution.py:781
  21.3 4.7 %collective-permute-start.9 = (bf16[5,16,128]{2,1,0:T(8,128)(2,1)S(1)}, bf16[5,16,128]{2,1,0:T(8,128)(2,1)S(1)}, u32[]{:S(2)}, u32[]{:S(2)}) collective-permute-start(bf16[5,16,128]{2,1,0:T(8,128)(2,1)S(1)} %broadcast_multiply_fusion), channel_id=1, source_target_pairs={{0,20},{1,21},{2,22},{3,23},{4,16},{5,17},{6,18},{7,19},{8,28},{9,... | collective-permute-start | bytes 61448 | tf_op jit(solution)/shard_map/ppermute | solution.py:781
  22.4 4.7 %collective-permute-start.11 = (bf16[5,16,128]{2,1,0:T(8,128)(2,1)S(1)}, bf16[5,16,128]{2,1,0:T(8,128)(2,1)S(1)}, u32[]{:S(2)}, u32[]{:S(2)}) collective-permute-start(bf16[5,16,128]{2,1,0:T(8,128)(2,1)S(1)} %broadcast_multiply_fusion), channel_id=1, source_target_pairs={{0,1},{1,0},{2,3},{3,2},{4,24},{5,25},{6,26},{7,27},{8,20},{9,21},... | collective-permute-start | bytes 61448 | tf_op jit(solution)/shard_map/ppermute | solution.py:781
  27.1 2.0 %collective-permute-start.13 = (bf16[128,128]{1,0:T(8,128)(2,1)S(1)}, bf16[128,128]{1,0:T(8,128)(2,1)S(1)}, u32[]{:S(2)}, u32[]{:S(2)}) collective-permute-start(bf16[128,128]{1,0:T(8,128)(2,1)S(1)} %pad_maximum_fusion), channel_id=1, source_target_pairs={{0,3},{1,0},{2,1},{3,2},{4,7},{5,4},{6,5},{7,6},{8,11},{9,8},{10,9... | collective-permute-start | bytes 98312 | tf_op jit(solution)/shard_map/ppermute | solution.py:781
  27.1 3.4 %collective-permute-start.12 = (bf16[128,128]{1,0:T(8,128)(2,1)S(1)}, bf16[128,128]{1,0:T(8,128)(2,1)S(1)}, u32[]{:S(2)}, u32[]{:S(2)}) collective-permute-start(bf16[128,128]{1,0:T(8,128)(2,1)S(1)} %pad_maximum_fusion), channel_id=1, source_target_pairs={{0,1},{1,2},{2,3},{3,0},{4,5},{5,6},{6,7},{7,4},{8,9},{9,10},{10,1... | collective-permute-start | bytes 98312 | tf_op jit(solution)/shard_map/ppermute | solution.py:781

commit v20 on v18

--- a/solution.py
+++ b/solution.py
@@ -697,7 +697,7 @@
         def put(step, low, high):
             if closing:
                 for row, values in ((step, low), (step + rows // 2, high)):
-                    raw[pl.ds(row, CH, stride=rows), :] = values
+                    raw[row * CH : (row + 1) * CH, :] = values
                 return
             out[step] = low.astype(BF16)
             out[step + rows // 2] = high.astype(BF16)
@@ -735,7 +735,8 @@
         close()
 
     if closing:
-        out[...] = raw[...].reshape(CH, rows, 128).astype(BF16)
+        for channel in range(CH):
+            out[channel] = raw[pl.ds(channel, rows, stride=CH), :].astype(BF16)
 
 
 VMEM = pl.BlockSpec(memory_space=pltpu.VMEM)

time: 34.1 us -> 34.2 us (level)
  no operation moved by 1% of the time
where the time goes in v20:
time: 34.2 us; the launch traced here: 34 us
  starting transfers between devices  12.3 us (36%)
  Pallas kernels  11.6 us (34%)
  waiting for transfers between devices  9.79 us (29%)
    ppermute x14, starting transfers between devices, send(): return lax.ppermute(x, names, pairs)  12.3 us
    pallas_call x5, Pallas kernels, call(): pl.pallas_call(kernel, out_shape=outs, in_specs=[SMEM] + [VMEM] * len(ope...  11.6 us
    ppermute x14, waiting for transfers between devices, send(): return lax.ppermute(x, names, pairs)  9.79 us
  transfers between devices with their start and end apart: 14, of which 6 were waited for; matrix products, arithmetic and copies ran while one was open for 0% of the time, Pallas kernels for 10%

profile of v20, /device:TPU:8, one launch (start us, length us, event | category | flops | bytes accessed | tf_op | source)
XLA Modules:
  0.0 34.0 jit_solution(5423253685360320267)
XLA Ops:
  0.0 0.1 pad_add_fusion.flags.refs_0_
  0.1 2.2 %start.1 = (bf16[16,80,128]{2,1,0:T(8,128)(2,1)S(1)}, bf16[8,16,128]{2,1,0:T(8,128)(2,1)S(1)}, bf16[16,128]{1,0:T(8,128)(2,1)S(1)}, bf16[2048,128]{1,0:T(8,128)(...) custom-call(s32[4]{0:T(128)S(1)} %pad_add_fusion.flags.refs_0_, ...), custom_call_target="tpu_custom_call" | custom-call | tf_op jit(solution)/shard_map/start/pallas_call | solution.py:851
  2.3 1.6 %collective-permute-start = (bf16[5,16,128]{2,1,0:T(8,128)(2,1)S(1)}, bf16[5,16,128]{2,1,0:T(8,128)(2,1)S(1)}, u32[]{:S(2)}, u32[]{:S(2)}) collective-permute-start(bf16[5,16,128]{2,1,0:T(8,128)(2,1)S(1)} %get-tuple-element.47), channel_id=1, source_target_pairs={{0,16},{1,17},{2,18},{3,19},{4,20},{5,21},{6,22},{7,23},{8,24},{9,... | collective-permute-start | bytes 61448 | tf_op jit(solution)/shard_map/ppermute | solution.py:764
  3.9 0.5 %collective-permute-start.3 = (bf16[272,128]{1,0:T(8,128)(2,1)S(1)}, bf16[272,128]{1,0:T(8,128)(2,1)S(1)}, u32[]{:S(2)}, u32[]{:S(2)}) collective-permute-start(bf16[272,128]{1,0:T(8,128)(2,1)S(1)} %get-tuple-element.50), channel_id=1, source_target_pairs={{0,1},{1,0},{2,3},{3,2},{4,5},{5,4},{6,7},{7,6},{8,9},{9,8},{10,11... | collective-permute-start | bytes 208904 | tf_op jit(solution)/shard_map/ppermute | solution.py:764
  4.4 1.5 %collective-permute-start.2 = (bf16[5,16,128]{2,1,0:T(8,128)(2,1)S(1)}, bf16[5,16,128]{2,1,0:T(8,128)(2,1)S(1)}, u32[]{:S(2)}, u32[]{:S(2)}) collective-permute-start(bf16[5,16,128]{2,1,0:T(8,128)(2,1)S(1)} %broadcast_multiply_fusion.1), channel_id=1, source_target_pairs={{0,20},{1,21},{2,22},{3,23},{4,16},{5,17},{6,18},{7,19},{8,28},{9,... | collective-permute-start | bytes 61448 | tf_op jit(solution)/shard_map/ppermute | solution.py:764
  5.9 2.5 %collective-permute-start.4 = (bf16[5,16,128]{2,1,0:T(8,128)(2,1)S(1)}, bf16[5,16,128]{2,1,0:T(8,128)(2,1)S(1)}, u32[]{:S(2)}, u32[]{:S(2)}) collective-permute-start(bf16[5,16,128]{2,1,0:T(8,128)(2,1)S(1)} %broadcast_multiply_fusion.1), channel_id=1, source_target_pairs={{0,1},{1,0},{2,3},{3,2},{4,24},{5,25},{6,26},{7,27},{8,20},{9,21},... | collective-permute-start | bytes 61448 | tf_op jit(solution)/shard_map/ppermute | solution.py:764
  8.4 0.6 %collective-permute-done.2.refs_2_ = bf16[5,16,128]{2,1,0:T(8,128)(2,1)S(1)} collective-permute-done((bf16[5,16,128]{2,1,0:T(8,128)(2,1)S(1)}, bf16[5,16,128]{2,1,0:T(8,128)(2,1)S(1)}, u32[]{:S(2)}, u32[]{:S(2)}) %collective-permute-start.2) | collective-permute-done | bytes 20512 | tf_op jit(solution)/shard_map/ppermute | solution.py:764
  9.1 1.5 %collective-permute-done.4.refs_4_ = bf16[5,16,128]{2,1,0:T(8,128)(2,1)S(1)} collective-permute-done((bf16[5,16,128]{2,1,0:T(8,128)(2,1)S(1)}, bf16[5,16,128]{2,1,0:T(8,128)(2,1)S(1)}, u32[]{:S(2)}, u32[]{:S(2)}) %collective-permute-start.4) | collective-permute-done | bytes 20512 | tf_op jit(solution)/shard_map/ppermute | solution.py:764
  10.7 0.2 collective-permute-start.6
  10.9 0.4 %collective-permute-start.5 = (bf16[176,128]{1,0:T(8,128)(2,1)S(1)}, bf16[176,128]{1,0:T(8,128)(2,1)S(1)}, u32[]{:S(2)}, u32[]{:S(2)}) collective-permute-start(bf16[176,128]{1,0:T(8,128)(2,1)S(1)} %constant_dynamic-update-slice_fusion), channel_id=1, source_target_pairs={{0,1},{1,2},{2,3},{3,0},{4,5},{5,6},{6,7},{7,4},{8,9},{9,10},{10,1... | collective-permute-start | bytes 135176 | tf_op jit(solution)/shard_map/ppermute | solution.py:764
  11.3 1.9 %first_middle.1 = (f32[96,128]{1,0:T(8,128)S(1)}, f32[4,48,128]{2,1,0:T(8,128)S(1)}, bf16[20,240,128]{2,1,0:T(8,128)(2,1)S(1)}, f32[192,128]{1,0:T(8,128)S(1)}, ...) custom-call(s32[4]{0:T(128)S(1)} %pad_add_fusion.flags.refs_0_, ...), custom_call_target="tpu_custom_call" | custom-call | tf_op jit(solution)/shard_map/first_middle/pallas_call | solution.py:851
  13.2 1.6 %collective-permute-done.5.refs_3_ = bf16[176,128]{1,0:T(8,128)(2,1)S(1)} collective-permute-done((bf16[176,128]{1,0:T(8,128)(2,1)S(1)}, bf16[176,128]{1,0:T(8,128)(2,1)S(1)}, u32[]{:S(2)}, u32[]{:S(2)}) %collective-permute-start.5) | collective-permute-done | bytes 45088 | tf_op jit(solution)/shard_map/ppermute | solution.py:764
  14.8 2.7 %first_step.1 = (bf16[16,80,128]{2,1,0:T(8,128)(2,1)S(1)}, bf16[5,16,128]{2,1,0:T(8,128)(2,1)S(1)}, bf16[80,128]{1,0:T(8,128)(2,1)S(1)}, bf16[240,128]{1,0:T(8,1...) custom-call(s32[4]{0:T(128)S(1)} %pad_add_fusion.flags.refs_0_, ...), custom_call_target="tpu_custom_call" | custom-call | tf_op jit(solution)/shard_map/first_step/pallas_call | solution.py:851
  17.5 3.3 %collective-permute-start.7 = (bf16[5,16,128]{2,1,0:T(8,128)(2,1)S(1)}, bf16[5,16,128]{2,1,0:T(8,128)(2,1)S(1)}, u32[]{:S(2)}, u32[]{:S(2)}) collective-permute-start(bf16[5,16,128]{2,1,0:T(8,128)(2,1)S(1)} %get-tuple-element.70), channel_id=1, source_target_pairs={{0,16},{1,17},{2,18},{3,19},{4,20},{5,21},{6,22},{7,23},{8,24},{9,... | collective-permute-start | bytes 61448 | tf_op jit(solution)/shard_map/ppermute | solution.py:764
  20.8 0.5 %collective-permute-start.10 = (bf16[240,128]{1,0:T(8,128)(2,1)S(1)}, bf16[240,128]{1,0:T(8,128)(2,1)S(1)}, u32[]{:S(2)}, u32[]{:S(2)}) collective-permute-start(bf16[240,128]{1,0:T(8,128)(2,1)S(1)} %get-tuple-element.73), channel_id=1, source_target_pairs={{0,1},{1,0},{2,3},{3,2},{4,5},{5,4},{6,7},{7,6},{8,9},{9,8},{10,11... | collective-permute-start | bytes 184328 | tf_op jit(solution)/shard_map/ppermute | solution.py:764
  21.3 1.1 %collective-permute-start.9 = (bf16[5,16,128]{2,1,0:T(8,128)(2,1)S(1)}, bf16[5,16,128]{2,1,0:T(8,128)(2,1)S(1)}, u32[]{:S(2)}, u32[]{:S(2)}) collective-permute-start(bf16[5,16,128]{2,1,0:T(8,128)(2,1)S(1)} %broadcast_multiply_fusion), channel_id=1, source_target_pairs={{0,20},{1,21},{2,22},{3,23},{4,16},{5,17},{6,18},{7,19},{8,28},{9,... | collective-permute-start | bytes 61448 | tf_op jit(solution)/shard_map/ppermute | solution.py:764
  22.4 0.1 collective-permute-start.11
  22.6 3.4 %collective-permute-done.9.refs_2_ = bf16[5,16,128]{2,1,0:T(8,128)(2,1)S(1)} collective-permute-done((bf16[5,16,128]{2,1,0:T(8,128)(2,1)S(1)}, bf16[5,16,128]{2,1,0:T(8,128)(2,1)S(1)}, u32[]{:S(2)}, u32[]{:S(2)}) %collective-permute-start.9) | collective-permute-done | bytes 20512 | tf_op jit(solution)/shard_map/ppermute | solution.py:764
  26.0 1.1 %collective-permute-done.11.refs_4_ = bf16[5,16,128]{2,1,0:T(8,128)(2,1)S(1)} collective-permute-done((bf16[5,16,128]{2,1,0:T(8,128)(2,1)S(1)}, bf16[5,16,128]{2,1,0:T(8,128)(2,1)S(1)}, u32[]{:S(2)}, u32[]{:S(2)}) %collective-permute-start.11) | collective-permute-done | bytes 20512 | tf_op jit(solution)/shard_map/ppermute | solution.py:764
  27.1 0.1 collective-permute-start.13
  27.2 0.5 %collective-permute-start.12 = (bf16[128,128]{1,0:T(8,128)(2,1)S(1)}, bf16[128,128]{1,0:T(8,128)(2,1)S(1)}, u32[]{:S(2)}, u32[]{:S(2)}) collective-permute-start(bf16[128,128]{1,0:T(8,128)(2,1)S(1)} %pad_maximum_fusion), channel_id=1, source_target_pairs={{0,1},{1,2},{2,3},{3,0},{4,5},{5,6},{6,7},{7,4},{8,9},{9,10},{10,1... | collective-permute-start | bytes 98312 | tf_op jit(solution)/shard_map/ppermute | solution.py:764
  27.7 1.4 %second_middle.1 = (f32[96,128]{1,0:T(8,128)S(1)}, f32[4,48,128]{2,1,0:T(8,128)S(1)}, bf16[20,240,128]{2,1,0:T(8,128)(2,1)S(1)}) custom-call(s32[4]{0:T(128)S(1)} %pad_add_fusion.flags.refs_0_, bf16[16,80,128]{2,1,0:T(8,128)(2,1)S(1)} %get-tuple-element.68.refs_1_, bf16[5,16,128]{2,1,0:T(8,128)(2,1)S(1)} %collective-permute-done.9.refs_2_, ...), custom_call_target="tpu_custom_call" | custom-call | tf_op jit(solution)/shard_map/second_middle/pallas_call | solution.py:851
  29.1 1.5 %collective-permute-done.12.refs_3_ = bf16[128,128]{1,0:T(8,128)(2,1)S(1)} collective-permute-done((bf16[128,128]{1,0:T(8,128)(2,1)S(1)}, bf16[128,128]{1,0:T(8,128)(2,1)S(1)}, u32[]{:S(2)}, u32[]{:S(2)}) %collective-permute-start.12) | collective-permute-done | bytes 32800 | tf_op jit(solution)/shard_map/ppermute | solution.py:764
  30.6 3.4 %second_step.1 = bf16[80,16,128]{2,1,0:T(8,128)(2,1)} custom-call(s32[4]{0:T(128)S(1)} %pad_add_fusion.flags.refs_0_, bf16[16,80,128]{2,1,0:T(8,128)(2,1)S(1)} %get-tuple-element.68.refs_1_, s32[16,128]{1,0:T(8,128)S(1)} %copy-done.1, bf16[128,128]{1,0:T(8,128)(2,1)S(1)} %collective-permute-done.12.refs_3_, ...), custom_call_target="tpu_custom_call" | custom-call | tf_op jit(solution)/shard_map/second_step/pallas_call | solution.py:851
  (29 shorter events, 0.2 us)
Async XLA Ops:
  0.0 14.8 %copy-start.1 = (s32[16,128]{1,0:T(8,128)S(1)}, s32[16,128]{1,0:T(8,128)}, u32[]{:S(2)}) copy-start(s32[16,128]{1,0:T(8,128)} %refs_2_.3) | copy-start | bytes 24580
  0.0 14.8 %copy-start.2 = (f32[2,4,80]{2,1,0:T(4,128)S(1)}, f32[2,4,80]{2,1,0:T(4,128)}, u32[]{:S(2)}) copy-start(f32[2,4,80]{2,1,0:T(4,128)} %refs_14_.1) | copy-start | bytes 7684
  0.0 14.8 %copy-start = (bf16[80,384]{1,0:T(8,128)(2,1)S(1)}, bf16[80,384]{1,0:T(8,128)(2,1)}, u32[]{:S(2)}) copy-start(bf16[80,384]{1,0:T(8,128)(2,1)} %refs_13_.3) | copy-start | bytes 184324
  2.3 6.1 %collective-permute-start = (bf16[5,16,128]{2,1,0:T(8,128)(2,1)S(1)}, bf16[5,16,128]{2,1,0:T(8,128)(2,1)S(1)}, u32[]{:S(2)}, u32[]{:S(2)}) collective-permute-start(bf16[5,16,128]{2,1,0:T(8,128)(2,1)S(1)} %get-tuple-element.47), channel_id=1, source_target_pairs={{0,16},{1,17},{2,18},{3,19},{4,20},{5,21},{6,22},{7,23},{8,24},{9,... | collective-permute-start | bytes 61448 | tf_op jit(solution)/shard_map/ppermute | solution.py:764
  3.9 4.6 %collective-permute-start.1 = (bf16[272,128]{1,0:T(8,128)(2,1)S(1)}, bf16[272,128]{1,0:T(8,128)(2,1)S(1)}, u32[]{:S(2)}, u32[]{:S(2)}) collective-permute-start(bf16[272,128]{1,0:T(8,128)(2,1)S(1)} %get-tuple-element.48), channel_id=1, source_target_pairs={{0,1},{1,0},{2,3},{3,2},{4,5},{5,4},{6,7},{7,6},{8,9},{9,8},{10,11... | collective-permute-start | bytes 208904 | tf_op jit(solution)/shard_map/ppermute | solution.py:764
  3.9 4.6 %collective-permute-start.3 = (bf16[272,128]{1,0:T(8,128)(2,1)S(1)}, bf16[272,128]{1,0:T(8,128)(2,1)S(1)}, u32[]{:S(2)}, u32[]{:S(2)}) collective-permute-start(bf16[272,128]{1,0:T(8,128)(2,1)S(1)} %get-tuple-element.50), channel_id=1, source_target_pairs={{0,1},{1,0},{2,3},{3,2},{4,5},{5,4},{6,7},{7,6},{8,9},{9,8},{10,11... | collective-permute-start | bytes 208904 | tf_op jit(solution)/shard_map/ppermute | solution.py:764
  4.4 4.7 %collective-permute-start.2 = (bf16[5,16,128]{2,1,0:T(8,128)(2,1)S(1)}, bf16[5,16,128]{2,1,0:T(8,128)(2,1)S(1)}, u32[]{:S(2)}, u32[]{:S(2)}) collective-permute-start(bf16[5,16,128]{2,1,0:T(8,128)(2,1)S(1)} %broadcast_multiply_fusion.1), channel_id=1, source_target_pairs={{0,20},{1,21},{2,22},{3,23},{4,16},{5,17},{6,18},{7,19},{8,28},{9,... | collective-permute-start | bytes 61448 | tf_op jit(solution)/shard_map/ppermute | solution.py:764
  5.9 4.7 %collective-permute-start.4 = (bf16[5,16,128]{2,1,0:T(8,128)(2,1)S(1)}, bf16[5,16,128]{2,1,0:T(8,128)(2,1)S(1)}, u32[]{:S(2)}, u32[]{:S(2)}) collective-permute-start(bf16[5,16,128]{2,1,0:T(8,128)(2,1)S(1)} %broadcast_multiply_fusion.1), channel_id=1, source_target_pairs={{0,1},{1,0},{2,3},{3,2},{4,24},{5,25},{6,26},{7,27},{8,20},{9,21},... | collective-permute-start | bytes 61448 | tf_op jit(solution)/shard_map/ppermute | solution.py:764
  10.7 2.5 %collective-permute-start.6 = (bf16[176,128]{1,0:T(8,128)(2,1)S(1)}, bf16[176,128]{1,0:T(8,128)(2,1)S(1)}, u32[]{:S(2)}, u32[]{:S(2)}) collective-permute-start(bf16[176,128]{1,0:T(8,128)(2,1)S(1)} %constant_dynamic-update-slice_fusion), channel_id=1, source_target_pairs={{0,3},{1,0},{2,1},{3,2},{4,7},{5,4},{6,5},{7,6},{8,11},{9,8},{10,9... | collective-permute-start | bytes 135176 | tf_op jit(solution)/shard_map/ppermute | solution.py:764
  10.9 3.9 %collective-permute-start.5 = (bf16[176,128]{1,0:T(8,128)(2,1)S(1)}, bf16[176,128]{1,0:T(8,128)(2,1)S(1)}, u32[]{:S(2)}, u32[]{:S(2)}) collective-permute-start(bf16[176,128]{1,0:T(8,128)(2,1)S(1)} %constant_dynamic-update-slice_fusion), channel_id=1, source_target_pairs={{0,1},{1,2},{2,3},{3,0},{4,5},{5,6},{6,7},{7,4},{8,9},{9,10},{10,1... | collective-permute-start | bytes 135176 | tf_op jit(solution)/shard_map/ppermute | solution.py:764
  17.5 5.1 %collective-permute-start.7 = (bf16[5,16,128]{2,1,0:T(8,128)(2,1)S(1)}, bf16[5,16,128]{2,1,0:T(8,128)(2,1)S(1)}, u32[]{:S(2)}, u32[]{:S(2)}) collective-permute-start(bf16[5,16,128]{2,1,0:T(8,128)(2,1)S(1)} %get-tuple-element.70), channel_id=1, source_target_pairs={{0,16},{1,17},{2,18},{3,19},{4,20},{5,21},{6,22},{7,23},{8,24},{9,... | collective-permute-start | bytes 61448 | tf_op jit(solution)/shard_map/ppermute | solution.py:764
  20.8 1.8 %collective-permute-start.8 = (bf16[240,128]{1,0:T(8,128)(2,1)S(1)}, bf16[240,128]{1,0:T(8,128)(2,1)S(1)}, u32[]{:S(2)}, u32[]{:S(2)}) collective-permute-start(bf16[240,128]{1,0:T(8,128)(2,1)S(1)} %get-tuple-element.71), channel_id=1, source_target_pairs={{0,1},{1,0},{2,3},{3,2},{4,5},{5,4},{6,7},{7,6},{8,9},{9,8},{10,11... | collective-permute-start | bytes 184328 | tf_op jit(solution)/shard_map/ppermute | solution.py:764
  20.8 1.8 %collective-permute-start.10 = (bf16[240,128]{1,0:T(8,128)(2,1)S(1)}, bf16[240,128]{1,0:T(8,128)(2,1)S(1)}, u32[]{:S(2)}, u32[]{:S(2)}) collective-permute-start(bf16[240,128]{1,0:T(8,128)(2,1)S(1)} %get-tuple-element.73), channel_id=1, source_target_pairs={{0,1},{1,0},{2,3},{3,2},{4,5},{5,4},{6,7},{7,6},{8,9},{9,8},{10,11... | collective-permute-start | bytes 184328 | tf_op jit(solution)/shard_map/ppermute | solution.py:764
  21.3 4.7 %collective-permute-start.9 = (bf16[5,16,128]{2,1,0:T(8,128)(2,1)S(1)}, bf16[5,16,128]{2,1,0:T(8,128)(2,1)S(1)}, u32[]{:S(2)}, u32[]{:S(2)}) collective-permute-start(bf16[5,16,128]{2,1,0:T(8,128)(2,1)S(1)} %broadcast_multiply_fusion), channel_id=1, source_target_pairs={{0,20},{1,21},{2,22},{3,23},{4,16},{5,17},{6,18},{7,19},{8,28},{9,... | collective-permute-start | bytes 61448 | tf_op jit(solution)/shard_map/ppermute | solution.py:764
  22.4 4.7 %collective-permute-start.11 = (bf16[5,16,128]{2,1,0:T(8,128)(2,1)S(1)}, bf16[5,16,128]{2,1,0:T(8,128)(2,1)S(1)}, u32[]{:S(2)}, u32[]{:S(2)}) collective-permute-start(bf16[5,16,128]{2,1,0:T(8,128)(2,1)S(1)} %broadcast_multiply_fusion), channel_id=1, source_target_pairs={{0,1},{1,0},{2,3},{3,2},{4,24},{5,25},{6,26},{7,27},{8,20},{9,21},... | collective-permute-start | bytes 61448 | tf_op jit(solution)/shard_map/ppermute | solution.py:764
  27.1 2.0 %collective-permute-start.13 = (bf16[128,128]{1,0:T(8,128)(2,1)S(1)}, bf16[128,128]{1,0:T(8,128)(2,1)S(1)}, u32[]{:S(2)}, u32[]{:S(2)}) collective-permute-start(bf16[128,128]{1,0:T(8,128)(2,1)S(1)} %pad_maximum_fusion), channel_id=1, source_target_pairs={{0,3},{1,0},{2,1},{3,2},{4,7},{5,4},{6,5},{7,6},{8,11},{9,8},{10,9... | collective-permute-start | bytes 98312 | tf_op jit(solution)/shard_map/ppermute | solution.py:764
  27.2 3.4 %collective-permute-start.12 = (bf16[128,128]{1,0:T(8,128)(2,1)S(1)}, bf16[128,128]{1,0:T(8,128)(2,1)S(1)}, u32[]{:S(2)}, u32[]{:S(2)}) collective-permute-start(bf16[128,128]{1,0:T(8,128)(2,1)S(1)} %pad_maximum_fusion), channel_id=1, source_target_pairs={{0,1},{1,2},{2,3},{3,0},{4,5},{5,6},{6,7},{7,4},{8,9},{9,10},{10,1... | collective-permute-start | bytes 98312 | tf_op jit(solution)/shard_map/ppermute | solution.py:764
